TPU v7x, 32 devices: a whole 2x2x4 slice. The times are simulated.
32 devices in a mesh: dp: 8 (over y, x, core), row: 4 (over z).
Axes of the slice: x: 2, y: 2, z: 4, core: 2. Of those that a mesh axis runs over, the one named last changes fastest.
Arguments:
- small_nodes: bfloat16 [96, 32, 512], P(('dp', 'row')), may hold values from -6 to 6
- small_edges: bfloat16 [96, 32, 2048], P(('dp', 'row')), may hold values from -6 to 6
- small_counts: int32 [96], P(('dp', 'row')), may hold values from 16 to 32
- big_nodes: bfloat16 [64, 64, 512], P('dp', 'row'), may hold values from -6 to 6
- big_edges: bfloat16 [64, 64, 4096], P('dp', 'row'), may hold values from -6 to 6
- big_counts: int32 [64], P('dp'), may hold values from 32 to 64
- small_node_cot: bfloat16 [96, 32, 512], P(('dp', 'row')), may hold values from -6 to 6
- small_edge_cot: bfloat16 [96, 32, 2048], P(('dp', 'row')), may hold values from -6 to 6
- big_node_cot: bfloat16 [64, 64, 512], P('dp', 'row'), may hold values from -6 to 6
- big_edge_cot: bfloat16 [64, 64, 4096], P('dp', 'row'), may hold values from -6 to 6
- master: float32 [66320, 128], P('dp'), may hold values from -3 to 3
- first_moment: float32 [66320, 128], P('dp')
- second_moment: float32 [66320, 128], P('dp'), as said below
- owner: int32 [8], replicated, may hold values from 0 to 7, as said below
- segment_rows: int32 [8], replicated, may hold values from 1 to 8290, as said below
- step_count: int32 [1], replicated, may hold values from 1 to 20
Outputs:
- small_nodes_out: bfloat16 [96, 32, 512], P(('dp', 'row'))
- small_edges_out: bfloat16 [96, 32, 2048], P(('dp', 'row'))
- big_nodes_out: bfloat16 [64, 64, 512], P('dp', 'row')
- big_edges_out: bfloat16 [64, 64, 4096], P('dp', 'row')
- small_nodes_grad: bfloat16 [96, 32, 512], P(('dp', 'row'))
- small_edges_grad: bfloat16 [96, 32, 2048], P(('dp', 'row'))
- big_nodes_grad: bfloat16 [64, 64, 512], P('dp', 'row')
- big_edges_grad: bfloat16 [64, 64, 4096], P('dp', 'row')
- new_master: float32 [66320, 128], P('dp')
- new_first: float32 [66320, 128], P('dp')
- new_second: float32 [66320, 128], P('dp')
- norm_grads: float32 [8, 576], replicated
Inputs may be any that keep to these rules, and one draw needn't show every extreme that they name: owner[j] is the segment kept by index j of dp; every segment is named once. `segment_rows`: segments follow one another in order of s and together cover 33156 rows; one segment has exactly 8290 rows. `second_moment`: second moments are positive.
All inputs are finite; a program needn't handle non-finite values.
Results may differ from a plain program's by a relative error of at most 0.02.
Values may be sent and summed in bfloat16 or wider, within the bound.
No kernel may reach another device: no remote copies, remote signals or barrier semaphores. Data moves between devices by JAX's collectives and lax.ppermute only.
A program may use at most 256 MiB of HBM per device.

v0:
```python
import jax
import jax.numpy as jnp
from jax import lax
from jax.sharding import PartitionSpec as P

D = 512
H = 32
DE = 64
FF = 1024
FFE = 128
PARAMS = 4243968
TOTAL_ROWS = 33156


NORM_EPS = 1e-05
BETA_ONE = 0.9
BETA_TWO = 0.95
WEIGHT_DECAY = 0.1
ADAM_EPS = 1e-08
PAD_RATE = 0.05
MASK_FILL = -1e30
SET_PIECES = 13


def layer_shapes():
    return [
        (D, D),
        (D, D),
        (D, D),
        (D, D),
        (D, FF),
        (FF, D),
        (DE, H),
        (DE, H),
        (H, DE),
        (DE, FFE),
        (FFE, DE),
        (4, D),
        (4, DE),
    ]


def piece_shapes():
    return layer_shapes() + layer_shapes()


def piece_rates():
    one_set = [
        0.5 * D ** (-0.5),
        0.5 * D ** (-0.5),
        0.5 * D ** (-0.5),
        2.0 * D ** (-0.5),
        0.5 * D ** (-0.5),
        0.5 * FF ** (-0.5),
        0.5 * DE ** (-0.5),
        0.5 * DE ** (-0.5),
        0.5 * H ** (-0.5),
        0.5 * DE ** (-0.5),
        0.5 * FFE ** (-0.5),
        0.25,
        0.25,
    ]
    return one_set + one_set


def unpack(flat_all):
    result = []
    offset = 0
    for piece_shape in piece_shapes():
        entries = piece_shape[0] * piece_shape[1]
        result.append(flat_all[offset : offset + entries].reshape(piece_shape))
        offset += entries
    return result


def lookup(table, index):
    slot_ids = jnp.arange(table.shape[0], dtype=jnp.int32)
    return jnp.sum(jnp.where(index[:, None] == slot_ids[None, :], table[None, :], 0), axis=1)


def segment_bounds(segment_rows):
    ends = jnp.cumsum(segment_rows)
    return (ends - segment_rows, ends)


def target_rows(owner, segment_rows, held_rows):
    starts, ends = segment_bounds(segment_rows)
    start_of = lookup(starts, owner)
    length_of = lookup(segment_rows, owner)
    inside = jnp.arange(held_rows, dtype=jnp.int32)
    targets = start_of[:, None] + inside[None, :]
    live = inside[None, :] < length_of[:, None]
    return (jnp.minimum(targets, TOTAL_ROWS - 1).reshape(-1), live.reshape(-1))


def source_rows(owner, segment_rows, held_rows):
    starts, ends = segment_bounds(segment_rows)
    flat_ids = jnp.arange(TOTAL_ROWS, dtype=jnp.int32)
    segment_of = jnp.sum((ends[None, :] <= flat_ids[:, None]).astype(jnp.int32), axis=1)
    slot_ids = jnp.arange(owner.shape[0], dtype=jnp.int32)
    holder = jnp.sum(jnp.where(owner[None, :] == slot_ids[:, None], slot_ids[None, :], 0), axis=1)
    return lookup(holder, segment_of) * held_rows + flat_ids - lookup(starts, segment_of)


def rate_table(positions):
    entry_rates = jnp.full(positions.shape, PAD_RATE, jnp.float32)
    start_at = 0
    for piece_shape, piece_rate in zip(piece_shapes(), piece_rates()):
        entries = piece_shape[0] * piece_shape[1]
        inside = (positions >= start_at) & (positions < start_at + entries)
        entry_rates = jnp.where(inside, piece_rate, entry_rates)
        start_at += entries
    return entry_rates


def layer_norm(values, norm_gain, norm_bias):
    centred = values - jnp.mean(values, axis=-1, keepdims=True)
    spread = jnp.mean(centred * centred, axis=-1, keepdims=True)
    return centred * lax.rsqrt(spread + NORM_EPS) * norm_gain + norm_bias


def smooth_gate(values):
    return jax.nn.gelu(values, approximate=True)


def forward_dot(values, weight):
    return jnp.dot(values, weight, preferred_element_type=jnp.float32)


def weight_grad(inputs, grad_rows):
    flat_in = inputs.reshape(-1, inputs.shape[-1])
    flat_back = grad_rows.reshape(-1, grad_rows.shape[-1])
    return lax.dot_general(
        flat_in, flat_back, (((0,), (0,)), ((), ())), preferred_element_type=jnp.float32
    )


def back_through(grad_rows, weight):
    return lax.dot_general(
        grad_rows,
        weight,
        (((grad_rows.ndim - 1,), (1,)), ((), ())),
        preferred_element_type=jnp.float32,
    )


def attention_scores(queries_heads, keys_heads, edge_low, w_bias):
    score_scale = (D // H) ** (-0.5)
    products = jnp.einsum(
        "grhd,gkhd->grkh", queries_heads, keys_heads, preferred_element_type=jnp.float32
    )
    return products * score_scale + forward_dot(edge_low, w_bias)


def mask_scores(scores, counts):
    valid_keys = jnp.arange(scores.shape[2], dtype=jnp.int32)[None, :] < counts[:, None]
    return jnp.where(valid_keys[:, None, :, None], scores, MASK_FILL)


def graph_layer(node_rows, edge_rows, counts, params, split_rows):
    (
        w_query,
        w_key,
        w_value,
        w_out,
        w_up,
        w_down,
        w_bias,
        w_gate,
        w_edge,
        w_edge_up,
        w_edge_down,
        node_norms,
        edge_norms,
    ) = params
    norms_node = node_norms.astype(jnp.float32)
    norms_edge = edge_norms.astype(jnp.float32)
    graphs, rows_here, _ = node_rows.shape
    keys_total = edge_rows.shape[2] // DE
    head_dim = D // H
    score_scale = head_dim ** (-0.5)
    inputs = node_rows.astype(jnp.float32)
    normed, norm_one_back = jax.vjp(layer_norm, inputs, norms_node[0], norms_node[1])
    normed_low = normed.astype(jnp.bfloat16)
    queries = forward_dot(normed_low, w_query).astype(jnp.bfloat16)
    keys_own = forward_dot(normed_low, w_key).astype(jnp.bfloat16)
    values_own = forward_dot(normed_low, w_value).astype(jnp.bfloat16)
    if split_rows:
        keys_all, values_all = (
            lax.all_gather(keys_own, "row", axis=1, tiled=True),
            lax.all_gather(values_own, "row", axis=1, tiled=True),
        )
    else:
        keys_all, values_all = (keys_own, values_own)
    queries_heads = queries.reshape(graphs, rows_here, H, head_dim)
    keys_heads = keys_all.reshape(graphs, keys_total, H, head_dim)
    values_heads = values_all.reshape(graphs, keys_total, H, head_dim)
    edge_in = edge_rows.astype(jnp.float32).reshape(graphs, rows_here, keys_total, DE)
    edge_normed, edge_one_back = jax.vjp(layer_norm, edge_in, norms_edge[0], norms_edge[1])
    edge_low = edge_normed.astype(jnp.bfloat16)
    gate_open = jax.nn.sigmoid(forward_dot(edge_low, w_gate))
    scores = attention_scores(queries_heads, keys_heads, edge_low, w_bias)
    masked = mask_scores(scores, counts)
    top_score = jnp.max(masked, axis=2, keepdims=True)
    log_total = top_score + jnp.log(jnp.sum(jnp.exp(masked - top_score), axis=2, keepdims=True))
    weights_low = (jnp.exp(masked - log_total) * gate_open).astype(jnp.bfloat16)
    mixed_heads = jnp.einsum(
        "grkh,gkhd->grhd", weights_low, values_heads, preferred_element_type=jnp.float32
    )
    mixed_low = mixed_heads.astype(jnp.bfloat16).reshape(graphs, rows_here, D)
    hidden = inputs + forward_dot(mixed_low, w_out)
    ffn_in, norm_two_back = jax.vjp(layer_norm, hidden, norms_node[2], norms_node[3])
    ffn_low = ffn_in.astype(jnp.bfloat16)
    ffn_act, gate_back = jax.vjp(smooth_gate, forward_dot(ffn_low, w_up))
    act_low = ffn_act.astype(jnp.bfloat16)
    node_out = (hidden + forward_dot(act_low, w_down)).astype(jnp.bfloat16)
    edge_mid = edge_in + forward_dot(scores.astype(jnp.bfloat16), w_edge)
    edge_ffn_in, edge_two_back = jax.vjp(layer_norm, edge_mid, norms_edge[2], norms_edge[3])
    edge_ffn_low = edge_ffn_in.astype(jnp.bfloat16)
    edge_act, edge_gate_back = jax.vjp(smooth_gate, forward_dot(edge_ffn_low, w_edge_up))
    edge_act_low = edge_act.astype(jnp.bfloat16)
    edge_out = (edge_mid + forward_dot(edge_act_low, w_edge_down)).astype(jnp.bfloat16)
    edge_out = edge_out.reshape(graphs, rows_here, keys_total * DE)

    def backward(node_cot, edge_cot):
        grad_down = weight_grad(act_low, node_cot)
        (act_back,) = gate_back(back_through(node_cot, w_down))
        up_low = act_back.astype(jnp.bfloat16)
        grad_up = weight_grad(ffn_low, up_low)
        hidden_norm_back, gain_two, bias_two = norm_two_back(back_through(up_low, w_up))
        hidden_grad = node_cot.astype(jnp.float32) + hidden_norm_back
        hidden_low = hidden_grad.astype(jnp.bfloat16)
        grad_out = weight_grad(mixed_low, hidden_low)
        mixed_back = (
            back_through(hidden_low, w_out)
            .astype(jnp.bfloat16)
            .reshape(graphs, rows_here, H, head_dim)
        )
        edge_cot_rows = edge_cot.reshape(graphs, rows_here, keys_total, DE)
        grad_edge_down = weight_grad(edge_act_low, edge_cot_rows)
        (edge_act_back,) = edge_gate_back(back_through(edge_cot_rows, w_edge_down))
        edge_up_low = edge_act_back.astype(jnp.bfloat16)
        grad_edge_up = weight_grad(edge_ffn_low, edge_up_low)
        mid_norm_back, gain_edge_two, bias_edge_two = edge_two_back(
            back_through(edge_up_low, w_edge_up)
        )
        mid_grad = edge_cot_rows.astype(jnp.float32) + mid_norm_back
        mid_low = mid_grad.astype(jnp.bfloat16)
        keys_back, values_back = (keys_all, values_all)
        if split_rows:
            keys_back, values_back = (keys_all, values_all)
        keys_again_heads = keys_back.reshape(graphs, keys_total, H, head_dim)
        values_again_heads = values_back.reshape(graphs, keys_total, H, head_dim)
        scores_again = attention_scores(queries_heads, keys_again_heads, edge_low, w_bias)
        attn_probs = jnp.exp(mask_scores(scores_again, counts) - log_total)
        grad_edge = weight_grad(scores_again.astype(jnp.bfloat16), mid_low)
        score_from_edge = back_through(mid_low, w_edge)
        weight_back = jnp.einsum(
            "grhd,gkhd->grkh", mixed_back, values_again_heads, preferred_element_type=jnp.float32
        )
        values_part = jnp.einsum(
            "grkh,grhd->gkhd", weights_low, mixed_back, preferred_element_type=jnp.float32
        )
        prob_back = weight_back * gate_open
        gate_low = (weight_back * attn_probs * gate_open * (1.0 - gate_open)).astype(jnp.bfloat16)
        score_grad = (
            attn_probs * (prob_back - jnp.sum(attn_probs * prob_back, axis=2, keepdims=True))
            + score_from_edge
        )
        score_low = score_grad.astype(jnp.bfloat16)
        query_low = (
            jnp.einsum(
                "grkh,gkhd->grhd", score_low, keys_again_heads, preferred_element_type=jnp.float32
            )
            * score_scale
        )
        query_low = query_low.astype(jnp.bfloat16).reshape(graphs, rows_here, D)
        keys_part = (
            jnp.einsum(
                "grkh,grhd->gkhd", score_low, queries_heads, preferred_element_type=jnp.float32
            )
            * score_scale
        )
        keys_part = keys_part.reshape(graphs, keys_total, D)
        values_part = values_part.reshape(graphs, keys_total, D)
        if split_rows:
            keys_sum, values_sum = (
                lax.psum_scatter(
                    keys_part.astype(jnp.bfloat16), "row", scatter_dimension=1, tiled=True
                ).astype(jnp.float32),
                lax.psum_scatter(
                    values_part.astype(jnp.bfloat16), "row", scatter_dimension=1, tiled=True
                ).astype(jnp.float32),
            )
        else:
            keys_sum, values_sum = (keys_part, values_part)
        key_low = keys_sum.astype(jnp.bfloat16)
        value_low = values_sum.astype(jnp.bfloat16)
        grad_bias = weight_grad(edge_low, score_low)
        grad_gate = weight_grad(edge_low, gate_low)
        edge_norm_back, gain_edge_one, bias_edge_one = edge_one_back(
            back_through(score_low, w_bias) + back_through(gate_low, w_gate)
        )
        edge_grad = (
            (mid_grad + edge_norm_back)
            .astype(jnp.bfloat16)
            .reshape(graphs, rows_here, keys_total * DE)
        )
        grad_query = weight_grad(normed_low, query_low)
        grad_key = weight_grad(normed_low, key_low)
        grad_value = weight_grad(normed_low, value_low)
        normed_back = (
            back_through(query_low, w_query)
            + back_through(key_low, w_key)
            + back_through(value_low, w_value)
        )
        input_norm_back, gain_one, bias_one = norm_one_back(normed_back)
        node_grad = (hidden_grad + input_norm_back).astype(jnp.bfloat16)
        weight_grads = [
            grad_query,
            grad_key,
            grad_value,
            grad_out,
            grad_up,
            grad_down,
            grad_bias,
            grad_gate,
            grad_edge,
            grad_edge_up,
            grad_edge_down,
            jnp.stack([gain_one, bias_one, gain_two, bias_two]),
            jnp.stack([gain_edge_one, bias_edge_one, gain_edge_two, bias_edge_two]),
        ]
        return ((node_grad, edge_grad), weight_grads)

    return (node_out, edge_out, backward)


def per_device(
    small_nodes,
    small_edges,
    small_counts,
    big_nodes,
    big_edges,
    big_counts,
    small_node_cot,
    small_edge_cot,
    big_node_cot,
    big_edge_cot,
    master,
    first_moment,
    second_moment,
    owner,
    segment_rows,
    step_count,
):
    held_rows = master.shape[0]
    gathered = lax.all_gather(master.astype(jnp.bfloat16), "dp", axis=0, tiled=True)
    param_rows = jnp.take(gathered, source_rows(owner, segment_rows, held_rows), axis=0)
    params = unpack(param_rows.reshape(-1))
    first_set = params[:SET_PIECES]
    second_set = params[SET_PIECES:]
    small_first = graph_layer(small_nodes, small_edges, small_counts, first_set, False)
    big_first = graph_layer(big_nodes, big_edges, big_counts, first_set, True)
    small_second = graph_layer(small_first[0], small_first[1], small_counts, second_set, False)
    (small_mid_nodes, small_mid_edges), small_grads_two = small_second[2](
        small_node_cot, small_edge_cot
    )
    (small_node_grad, small_edge_grad), small_grads_one = small_first[2](
        small_mid_nodes, small_mid_edges
    )
    share = big_nodes.shape[0] // lax.axis_size("row")
    whole_nodes, whole_edges, whole_node_cot, whole_edge_cot = (
        lax.all_to_all(big_first[0], "row", split_axis=0, concat_axis=1, tiled=True),
        lax.all_to_all(big_first[1], "row", split_axis=0, concat_axis=1, tiled=True),
        lax.all_to_all(big_node_cot, "row", split_axis=0, concat_axis=1, tiled=True),
        lax.all_to_all(big_edge_cot, "row", split_axis=0, concat_axis=1, tiled=True),
    )
    own_counts = lax.dynamic_slice_in_dim(big_counts, lax.axis_index("row") * share, share)
    big_second = graph_layer(whole_nodes, whole_edges, own_counts, second_set, False)
    (whole_node_grad, whole_edge_grad), big_grads_two = big_second[2](
        whole_node_cot, whole_edge_cot
    )
    big_node_out, big_edge_out, big_mid_nodes, big_mid_edges = (
        lax.all_to_all(big_second[0], "row", split_axis=1, concat_axis=0, tiled=True),
        lax.all_to_all(big_second[1], "row", split_axis=1, concat_axis=0, tiled=True),
        lax.all_to_all(whole_node_grad, "row", split_axis=1, concat_axis=0, tiled=True),
        lax.all_to_all(whole_edge_grad, "row", split_axis=1, concat_axis=0, tiled=True),
    )
    (big_node_grad, big_edge_grad), big_grads_one = big_first[2](big_mid_nodes, big_mid_edges)
    all_grads = [a + b for a, b in zip(small_grads_one, big_grads_one)] + [
        a + b for a, b in zip(small_grads_two, big_grads_two)
    ]
    norm_part = jnp.concatenate(
        [
            jnp.concatenate([all_grads[11], all_grads[12]], axis=1),
            jnp.concatenate([all_grads[11 + SET_PIECES], all_grads[12 + SET_PIECES]], axis=1),
        ],
        axis=0,
    )
    norm_grads = lax.psum(norm_part, ("dp", "row"))
    padding = jnp.zeros((TOTAL_ROWS * 128 - PARAMS,), jnp.float32)
    flat_grad = jnp.concatenate([g.reshape(-1) for g in all_grads] + [padding]).reshape(
        TOTAL_ROWS, 128
    )
    targets, live = target_rows(owner, segment_rows, held_rows)
    by_owner = jnp.where(live[:, None], jnp.take(flat_grad, targets, axis=0), 0.0)
    everywhere = lax.psum(by_owner.astype(jnp.bfloat16), "row")
    owned_grad = lax.psum_scatter(everywhere, "dp", scatter_dimension=0, tiled=True).astype(
        jnp.float32
    )
    my_start = lax.axis_index("dp") * held_rows
    my_rows = lax.dynamic_slice_in_dim(targets, my_start, held_rows)
    my_live = lax.dynamic_slice_in_dim(live, my_start, held_rows)[:, None]
    positions = my_rows[:, None] * 128 + jnp.arange(128, dtype=jnp.int32)[None, :]
    entry_rates = rate_table(positions)
    step_value = step_count[0].astype(jnp.float32)
    first_new = BETA_ONE * first_moment + (1.0 - BETA_ONE) * owned_grad
    second_new = BETA_TWO * second_moment + (1.0 - BETA_TWO) * owned_grad * owned_grad
    first_hat = first_new / (1.0 - jnp.power(jnp.float32(BETA_ONE), step_value))
    second_hat = second_new / (1.0 - jnp.power(jnp.float32(BETA_TWO), step_value))
    master_new = master - entry_rates * (
        first_hat / (jnp.sqrt(second_hat) + ADAM_EPS) + WEIGHT_DECAY * master
    )
    master_new = jnp.where(my_live, master_new, master)
    first_new = jnp.where(my_live, first_new, first_moment)
    second_new = jnp.where(my_live, second_new, second_moment)
    return (
        small_second[0],
        small_second[1],
        big_node_out,
        big_edge_out,
        small_node_grad,
        small_edge_grad,
        big_node_grad,
        big_edge_grad,
        master_new,
        first_new,
        second_new,
        norm_grads,
    )


def solution(mesh):
    in_specs = (
        P(("dp", "row"), None, None),
        P(("dp", "row"), None, None),
        P(("dp", "row")),
        P("dp", "row", None),
        P("dp", "row", None),
        P("dp"),
        P(("dp", "row"), None, None),
        P(("dp", "row"), None, None),
        P("dp", "row", None),
        P("dp", "row", None),
        P("dp", None),
        P("dp", None),
        P("dp", None),
        P(),
        P(),
        P(),
    )
    out_specs = (
        P(("dp", "row"), None, None),
        P(("dp", "row"), None, None),
        P("dp", "row", None),
        P("dp", "row", None),
        P(("dp", "row"), None, None),
        P(("dp", "row"), None, None),
        P("dp", "row", None),
        P("dp", "row", None),
        P("dp", None),
        P("dp", None),
        P("dp", None),
        P(),
    )
    return jax.shard_map(
        per_device, mesh=mesh, in_specs=in_specs, out_specs=out_specs, check_vma=False
    )
```

profile of v0, /device:TPU:0, one launch (start us, length us, event | category | flops | bytes accessed | tf_op | source)
XLA Modules:
  0.0 1523.3 jit_solution(10799876672571047208)
XLA Ops:
  10.6 6.5 all-to-all-start.4
  27.9 5.3 copy.717
  50.1 4.8 mul.1562
  57.6 5.2 sub.371
  72.3 5.0 all-to-all-start.5
  79.8 23.4 %all-to-all-done.5 = bf16[8,16,4096]{2,1,0:T(8,128)(2,1)S(1)} async-done(((bf16[8,16,4096]{2,1,0:T(8,128)(2,1)}), bf16[8,16,4096]{2,1,0:T(8,128)(2,1)S(1)}, u32[]{:S(2)}, u32[]{:S(2)}) %all-to-all-start.5) | async-done | bytes 1048608 | tf_op jit(solution)/shard_map/all_to_all | solution.py:377
  116.1 17.9 %reshape.1500 = bf16[66320,128]{1,0:T(8,128)(2,1)} reshape(bf16[8,8290,128]{2,1,0:T(8,128)(2,1)} %all-gather.3.cloned.1.call-done) | data formatting | bytes 33955840
  134.0 69.8 %gather_fusion = bf16[33156,128]{1,0:T(8,128)(2,1)} fusion(bf16[66320,128]{1,0:T(8,128)(2,1)} %reshape.1500, s32[33792]{0:T(1024)S(1)} %pad_clamp_fusion.1), kind=kCustom, calls=%fused_computation | custom fusion | bytes 17108496 | tf_op jit(solution)/shard_map/jit(_take)/gather | solution.py:359
  203.9 18.6 %broadcast_select_fusion = bf16[33156,128]{1,0:T(8,128)(2,1)S(1)} fusion(bf16[33156,128]{1,0:T(8,128)(2,1)} %gather_fusion, pred[33156]{0:T(1024)(128)(4,1)S(1)} %compare_and_fusion.1), kind=kLoop, calls=%fused_computation.7 | loop fusion | flops 4243968 | bytes 17009028 | tf_op jit(solution)/shard_map/jit(_take)/select_n | solution.py:359
  240.7 5.1 fusion.311
  262.8 4.5 fusion.379
  355.7 4.8 fusion.160
  387.4 6.6 add_convert_fusion.14
  451.4 5.7 add_convert_fusion.12
  468.2 16.2 %all_gather.11 = bf16[8,64,512]{2,1,0:T(8,128)(2,1)S(1)} all-gather(bf16[8,16,512]{2,1,0:T(8,128)(2,1)S(1)} %copy-done.299), channel_id=1, replica_groups=mesh['dp'=8,'row'=4] {'row'}, dimensions={1}, use_global_device_ids=true | all-gather | bytes 655360 | tf_op jit(solution)/shard_map/all_gather | solution.py:190
  484.4 15.1 all_gather.10
  575.0 5.2 all-to-all-start.1
  586.1 13.2 all-to-all-done.1
  607.3 5.6 copy.737
  627.0 4.8 sub.385
  669.6 4.4 fusion.119
  696.4 5.6 copy.789
  702.1 6.1 multiply_reduce_fusion
  719.2 6.7 add_convert_fusion.8
  748.7 5.9 add_convert_fusion.4
  792.9 4.8 reshape.1587
  802.3 5.2 all-to-all-start.7
  826.2 5.8 fusion.1
  832.1 8.9 reduce-scatter.7.cloned.1.call-done
  856.2 6.0 fusion.93
  862.2 4.5 fusion.392
  866.7 5.5 copy.812
  872.3 6.0 multiply_reduce_fusion.2
  885.8 4.5 fusion.116
  910.1 5.1 multiply_reduce_fusion.4
  919.7 8.1 add_convert_fusion.1
  965.1 18.1 %dynamic-update-slice.17 = f32[4243968]{0:T(1024)} dynamic-update-slice(f32[4243968]{0:T(1024)} %constant_dynamic-update-slice_fusion.7, f32[524288]{0:T(1024)S(1)} %bitcast.971, s32[]{} %constant.318) | dynamic-update-slice | bytes 4194308
  983.3 19.2 %dynamic-update-slice.18 = f32[4243968]{0:T(1024)} dynamic-update-slice(f32[4243968]{0:T(1024)} %dynamic-update-slice.17, f32[524288]{0:T(1024)} %bitcast.972, s32[]{} %constant.319) | dynamic-update-slice | bytes 4194308
  1011.8 128.0 %gather_fusion.1 = bf16[66320,128]{1,0:T(8,128)(2,1)} fusion(f32[33156,128]{1,0:T(8,128)} %bitcast.955, s32[66560]{0:T(1024)S(1)} %copy-done.242), kind=kCustom, calls=%fused_computation.1 | custom fusion | bytes 34221120 | tf_op jit(solution)/shard_map/jit(_take)/gather | solution.py:407
  1139.8 45.1 %select_convert_fusion = bf16[66320,128]{1,0:T(8,128)(2,1)} fusion(bf16[66320,128]{1,0:T(8,128)(2,1)} %gather_fusion.1, pred[66320]{0:T(1024)(128)(4,1)S(1)} %copy-done.327, pred[66320]{0:T(1024)(128)(4,1)S(1)} %copy-done.323), kind=kLoop, calls=%fused_computation.6 | loop fusion | flops 16977920 | bytes 34088480 | tf_op jit(solution)/shard_map/convert_element_type | solution.py:408
  1185.0 167.8 %fusion = bf16[8304,128]{1,0:T(8,128)(2,1)S(1)} fusion(bf16[66320,128]{1,0:T(8,128)(2,1)} %select_convert_fusion), kind=kCustom, calls=%all-reduce-scatter | all-reduce-scatter fusion | flops 8503297 | bytes 19104256
  1363.9 4.6 reshape.1586
  1368.6 9.3 concatenate.16
  1381.4 5.2 all-to-all-start.3
  1391.9 6.2 add_convert_fusion.11
  1405.1 33.6 %all-to-all-done.3 = bf16[2,64,4096]{2,0,1:T(2,128)(2,1)} async-done(((bf16[2,64,4096]{2,0,1:T(2,128)(2,1)}), bf16[2,64,4096]{2,0,1:T(2,128)(2,1)}, u32[]{:S(2)}, u32[]{:S(2)}) %all-to-all-start.3) | async-done | bytes 1048608 | tf_op jit(solution)/shard_map/all_to_all | solution.py:386
  1448.4 39.9 %psum.15 = f32[8,576]{1,0:T(8,128)} all-reduce(f32[8,576]{1,0:T(8,128)S(1)} %maximum_maximum_fusion), channel_id=1, replica_groups=mesh['dp'=8,'row'=4] {'dp','row'}, use_global_device_ids=true, to_apply=%region_119.120 | all-reduce | flops 4608 | bytes 36864 | tf_op jit(solution)/shard_map/psum | solution.py:401
  1492.1 24.5 %fusion.7 = (f32[8290,128]{1,0:T(8,128)}, f32[8290,128]{1,0:T(8,128)}, f32[8290,128]{1,0:T(8,128)}) fusion(f32[8290,128]{1,0:T(8,128)} %param.28, bf16[8290,128]{1,0:T(8,128)(2,1)} %all-reduce.4.cloned.1.call-done, pred[8290]{0:T(1024)(128)(4,1)S(1)} %copy-done.397, f32[8290,128]{1,0:T(8,128)} %param.26, f32[]{:T(128)} %bitcast.240, f32[]{:T(128)} %bitcast.239, ...), kind=kLoop, calls=%fused_computation.21 | loop fusion | flops 131578880 | bytes 27630578 | tf_op jit(solution)/shard_map/jit(_where)/select_n | solution.py:427
  (1552 shorter events, 663.5 us)
Async XLA Ops:
  7.2 109.0 %all-gather.3.cloned.1.call-start = ((), (), s32[]{:S(2)}) async-start(), calls=%async_computation.13 | async-start | bytes 19113984 | tf_op jit(solution)/shard_map/all_gather | solution.py:358
  10.6 61.7 %all-to-all-start.4 = ((bf16[8,16,512]{2,1,0:T(8,128)(2,1)}), bf16[8,16,512]{2,1,0:T(8,128)(2,1)}, u32[]{:S(2)}, u32[]{:S(2)}) async-start(bf16[8,16,512]{2,1,0:T(8,128)(2,1)} %param.24), calls=%async_computation.4 | async-start | bytes 262144 | tf_op jit(solution)/shard_map/all_to_all | solution.py:376
  24.0 40.2 %copy-start.322 = (pred[66320]{0:T(1024)(128)(4,1)}, pred[66320]{0:T(1024)(128)(4,1)S(1)}, u32[]{:S(2)}) copy-start(pred[66320]{0:T(1024)(128)(4,1)S(1)} %lt.256) | copy-start | bytes 198964
  24.7 531.4 %copy-start.7 = (f32[3,32,32,64]{3,2,1,0:T(8,128)}, f32[3,32,32,64]{3,2,1,0:T(8,128)S(1)}, u32[]{:S(2)}) copy-start(f32[3,32,32,64]{3,2,1,0:T(8,128)S(1)} %reshape.1389) | copy-start | bytes 2359300
  67.6 186.5 %copy-start.370 = (f32[3,32]{1,0:T(4,128)}, f32[3,32]{1,0:T(4,128)S(1)}, u32[]{:S(2)}) copy-start(f32[3,32]{1,0:T(4,128)S(1)} %broadcast_multiply_fusion.15) | copy-start | bytes 1156
  67.8 186.4 %copy-start.344 = (f32[8,16]{1,0:T(8,128)}, f32[8,16]{1,0:T(8,128)S(1)}, u32[]{:S(2)}) copy-start(f32[8,16]{1,0:T(8,128)S(1)} %broadcast_multiply_fusion.11) | copy-start | bytes 1540
  70.0 184.1 %copy-start.403 = (f32[3,32]{1,0:T(4,128)}, f32[3,32]{1,0:T(4,128)S(1)}, u32[]{:S(2)}) copy-start(f32[3,32]{1,0:T(4,128)S(1)} %fusion.344) | copy-start | bytes 1156
  70.0 184.2 %copy-start.374 = (f32[8,16]{1,0:T(8,128)}, f32[8,16]{1,0:T(8,128)S(1)}, u32[]{:S(2)}) copy-start(f32[8,16]{1,0:T(8,128)S(1)} %fusion.342) | copy-start | bytes 1540
  72.3 221.2 %copy-start.443 = (pred[3,32]{1,0:T(4,128)(4,1)}, pred[3,32]{1,0:T(4,128)(4,1)S(1)}, u32[]{:S(2)}) copy-start(pred[3,32]{1,0:T(4,128)(4,1)S(1)} %iota_compare_fusion.6) | copy-start | bytes 292
  72.3 30.9 %all-to-all-start.5 = ((bf16[8,16,4096]{2,1,0:T(8,128)(2,1)}), bf16[8,16,4096]{2,1,0:T(8,128)(2,1)S(1)}, u32[]{:S(2)}, u32[]{:S(2)}) async-start(bf16[8,16,4096]{2,1,0:T(8,128)(2,1)} %param.25), calls=%async_computation.5 | async-start | bytes 2097152 | tf_op jit(solution)/shard_map/all_to_all | solution.py:377
  203.9 24.9 %copy-start.184 = (f32[3,32,2048]{2,1,0:T(8,128)S(1)}, f32[3,32,2048]{2,1,0:T(8,128)}, u32[]{:S(2)}) copy-start(f32[3,32,2048]{2,1,0:T(8,128)} %mul.1490) | copy-start | bytes 2359300
  227.1 72.2 %copy-start.417 = (f32[64]{0:T(128)}, f32[64]{0:T(128)S(1)}, u32[]{:S(2)}) copy-start(f32[64]{0:T(128)S(1)} %get-tuple-element.134) | copy-start | bytes 772
  254.1 73.5 %copy-start.359 = (f32[512]{0:T(512)}, f32[512]{0:T(512)S(1)}, u32[]{:S(2)}) copy-start(f32[512]{0:T(512)S(1)} %get-tuple-element.124) | copy-start | bytes 6148
  254.1 73.5 %copy-start.428 = (f32[512]{0:T(512)}, f32[512]{0:T(512)S(1)}, u32[]{:S(2)}) copy-start(f32[512]{0:T(512)S(1)} %get-tuple-element.125) | copy-start | bytes 6148
  268.0 42.4 %copy-start.378 = (f32[64]{0:T(128)}, f32[64]{0:T(128)S(1)}, u32[]{:S(2)}) copy-start(f32[64]{0:T(128)S(1)} %get-tuple-element.133) | copy-start | bytes 772
  268.8 28.8 %copy-start.328 = (bf16[32,64,1,1]{1,0,2,3:T(8,128)(2,1)}, bf16[32,64,1,1]{1,0,2,3:T(8,128)(2,1)S(1)}, u32[]{:S(2)}) copy-start(bf16[32,64,1,1]{1,0,2,3:T(8,128)(2,1)S(1)} %reshape.1512) | copy-start | bytes 12292
  269.5 40.9 %copy-start.315 = (bf16[64,32]{1,0:T(8,128)(2,1)}, bf16[64,32]{1,0:T(8,128)(2,1)S(1)}, u32[]{:S(2)}) copy-start(bf16[64,32]{1,0:T(8,128)(2,1)S(1)} %reshape.1404) | copy-start | bytes 12292
  296.6 111.9 %copy-start.69 = (f32[3,32,512]{2,1,0:T(8,128)}, f32[3,32,512]{2,1,0:T(8,128)S(1)}, u32[]{:S(2)}) copy-start(f32[3,32,512]{2,1,0:T(8,128)S(1)} %get-tuple-element.143) | copy-start | bytes 589828
  296.6 31.0 %copy-start.363 = (f32[3,32]{1,0:T(4,128)}, f32[3,32]{1,0:T(4,128)S(1)}, u32[]{:S(2)}) copy-start(f32[3,32]{1,0:T(4,128)S(1)} %broadcast_multiply_fusion.14) | copy-start | bytes 1156
  297.6 30.0 %copy-start.382 = (f32[3,32]{1,0:T(4,128)}, f32[3,32]{1,0:T(4,128)S(1)}, u32[]{:S(2)}) copy-start(f32[3,32]{1,0:T(4,128)S(1)} %fusion.345) | copy-start | bytes 1156
  298.3 143.3 %copy-start.12 = (f32[3,32,32,64]{3,2,1,0:T(8,128)}, f32[3,32,32,64]{3,2,1,0:T(8,128)S(1)}, u32[]{:S(2)}) copy-start(f32[3,32,32,64]{3,2,1,0:T(8,128)S(1)} %get-tuple-element.147) | copy-start | bytes 2359300
  468.2 33.1 %copy-start.174 = (bf16[3,32,16,32]{3,2,1,0:T(8,128)(2,1)S(1)}, bf16[3,32,16,32]{3,2,1,0:T(8,128)(2,1)}, u32[]{:S(2)}) copy-start(bf16[3,32,16,32]{3,2,1,0:T(8,128)(2,1)} %copy-done.173) | copy-start | bytes 294916
  519.7 55.3 %all-to-all-start = ((bf16[8,16,512]{2,1,0:T(8,128)(2,1)}), bf16[8,16,512]{2,1,0:T(8,128)(2,1)S(1)}, u32[]{:S(2)}, u32[]{:S(2)}) async-start(bf16[8,16,512]{2,1,0:T(8,128)(2,1)} %fusion.185), calls=%async_computation | async-start | bytes 262144 | tf_op jit(solution)/shard_map/all_to_all | solution.py:374
  575.0 24.3 %all-to-all-start.1 = ((bf16[8,16,4096]{2,1,0:T(8,128)(2,1)}), bf16[8,16,4096]{2,1,0:T(8,128)(2,1)}, u32[]{:S(2)}, u32[]{:S(2)}) async-start(bf16[8,16,4096]{2,1,0:T(8,128)(2,1)} %reshape.1421), calls=%async_computation.1 | async-start | bytes 2097152 | tf_op jit(solution)/shard_map/all_to_all | solution.py:375
  773.8 28.4 %all-to-all-start.6 = ((bf16[2,64,512]{2,0,1:T(2,128)(2,1)}), bf16[2,64,512]{2,0,1:T(2,128)(2,1)S(1)}, u32[]{:S(2)}, u32[]{:S(2)}) async-start(bf16[2,64,512]{2,0,1:T(2,128)(2,1)} %copy.798), calls=%async_computation.6 | async-start | bytes 262144 | tf_op jit(solution)/shard_map/all_to_all | solution.py:387
  802.3 41.7 %all-to-all-start.7 = ((bf16[2,64,4096]{2,0,1:T(2,128)(2,1)}), bf16[2,64,4096]{2,0,1:T(2,128)(2,1)}, u32[]{:S(2)}, u32[]{:S(2)}) async-start(bf16[2,64,4096]{2,0,1:T(2,128)(2,1)} %reshape.1587), calls=%async_computation.7 | async-start | bytes 2097152 | tf_op jit(solution)/shard_map/all_to_all | solution.py:388
  807.5 33.4 %reduce-scatter.7.cloned.1.call-start = ((), (), s32[]{:S(2)}) async-start(), calls=%async_computation.11 | async-start | bytes 655360 | tf_op jit(solution)/shard_map/reduce_scatter | solution.py:291
  817.7 119.8 %reduce-scatter.5.cloned.1.call-start = ((), (), s32[]{:S(2)}) async-start(), calls=%async_computation.10 | async-start | bytes 655360 | tf_op jit(solution)/shard_map/reduce_scatter | solution.py:288
  983.3 26.0 %copy-start.413 = (f32[1,4,4,128]{3,1,2,0:T(4,128)S(1)}, f32[1,4,4,128]{3,1,2,0:T(4,128)}, u32[]{:S(2)}) copy-start(f32[1,4,4,128]{3,1,2,0:T(4,128)} %copy.1009) | copy-start | bytes 24580
  983.3 27.3 %copy-start.485 = (f32[256]{0:T(256)S(1)}, f32[256]{0:T(256)}, u32[]{:S(2)}) copy-start(f32[256]{0:T(256)} %add.1012) | copy-start | bytes 3076
  983.3 28.5 %copy-start.242 = (s32[66560]{0:T(1024)S(1)}, s32[66560]{0:T(1024)}, u32[]{:S(2)}) copy-start(s32[66560]{0:T(1024)} %pad_clamp_fusion) | copy-start | bytes 798724
  1011.8 128.0 %copy-start.323 = (pred[66320]{0:T(1024)(128)(4,1)S(1)}, pred[66320]{0:T(1024)(128)(4,1)}, u32[]{:S(2)}) copy-start(pred[66320]{0:T(1024)(128)(4,1)} %copy-done.322) | copy-start | bytes 198964
  1011.8 128.0 %copy-start.327 = (pred[66320]{0:T(1024)(128)(4,1)S(1)}, pred[66320]{0:T(1024)(128)(4,1)}, u32[]{:S(2)}) copy-start(pred[66320]{0:T(1024)(128)(4,1)} %compare_and_fusion) | copy-start | bytes 198964
  1184.9 169.1 %copy-start.78 = (f32[2,64,512]{2,1,0:T(8,128)S(1)}, f32[2,64,512]{2,1,0:T(8,128)}, u32[]{:S(2)}) copy-start(f32[2,64,512]{2,1,0:T(8,128)} %copy-done.77) | copy-start | bytes 786436
  1184.9 169.1 %copy-start.253 = (bf16[2,64,1024]{2,1,0:T(8,128)(2,1)S(1)}, bf16[2,64,1024]{2,1,0:T(8,128)(2,1)}, u32[]{:S(2)}) copy-start(bf16[2,64,1024]{2,1,0:T(8,128)(2,1)} %get-tuple-element.173) | copy-start | bytes 786436
  1352.8 15.8 %collective-permute-start = (bf16[98,128]{1,0:T(8,128)(2,1)S(1)}, bf16[98,128]{1,0:T(8,128)(2,1)S(1)}, u32[]{:S(2)}, u32[]{:S(2)}) collective-permute-start(bf16[98,128]{1,0:T(8,128)(2,1)S(1)} %slice.256), channel_id=1, source_target_pairs={{0,4},{4,8},{8,12},{12,16},{16,20},{20,24},{24,28},{1,5},{5,9},{9,... | collective-permute-start | bytes 75272
  1356.4 24.3 %all-to-all-start.2 = ((bf16[2,64,512]{2,0,1:T(2,128)(2,1)}), bf16[2,64,512]{2,0,1:T(2,128)(2,1)S(1)}, u32[]{:S(2)}, u32[]{:S(2)}) async-start(bf16[2,64,512]{2,0,1:T(2,128)(2,1)} %copy.747), calls=%async_computation.2 | async-start | bytes 262144 | tf_op jit(solution)/shard_map/all_to_all | solution.py:385
  1359.8 132.3 %all-reduce.4.cloned.1.call-start = ((), (), s32[]{:S(2)}) async-start(), calls=%async_computation.12 | async-start | bytes 4247552 | tf_op jit(solution)/shard_map/psum | solution.py:408
  1381.4 57.3 %all-to-all-start.3 = ((bf16[2,64,4096]{2,0,1:T(2,128)(2,1)}), bf16[2,64,4096]{2,0,1:T(2,128)(2,1)}, u32[]{:S(2)}, u32[]{:S(2)}) async-start(bf16[2,64,4096]{2,0,1:T(2,128)(2,1)} %reshape.1586), calls=%async_computation.3 | async-start | bytes 2097152 | tf_op jit(solution)/shard_map/all_to_all | solution.py:386
  1405.1 36.5 %copy-start.90 = (bf16[8,16,64,64]{2,3,1,0:T(8,128)(2,1)S(1)}, bf16[8,16,64,64]{2,3,1,0:T(8,128)(2,1)}, u32[]{:S(2)}) copy-start(bf16[8,16,64,64]{2,3,1,0:T(8,128)(2,1)} %get-tuple-element.111) | copy-start | bytes 3145732
  1444.1 44.2 %copy-start.454 = (f32[8,16]{1,0:T(8,128)S(1)}, f32[8,16]{1,0:T(8,128)}, u32[]{:S(2)}) copy-start(f32[8,16]{1,0:T(8,128)} %get-tuple-element.39) | copy-start | bytes 1540
  1444.1 44.2 %copy-start.192 = (f32[8,16,512]{2,1,0:T(8,128)S(1)}, f32[8,16,512]{2,1,0:T(8,128)}, u32[]{:S(2)}) copy-start(f32[8,16,512]{2,1,0:T(8,128)} %copy-done.191) | copy-start | bytes 786436
  1444.1 44.2 %copy-start.194 = (f32[8,16,512]{2,1,0:T(8,128)S(1)}, f32[8,16,512]{2,1,0:T(8,128)}, u32[]{:S(2)}) copy-start(f32[8,16,512]{2,1,0:T(8,128)} %copy-done.193) | copy-start | bytes 786436
  1444.1 44.2 %copy-start.209 = (bf16[2,4,16,512]{3,2,0,1:T(8,128)(2,1)S(1)}, bf16[2,4,16,512]{3,2,0,1:T(8,128)(2,1)}, u32[]{:S(2)}) copy-start(bf16[2,4,16,512]{3,2,0,1:T(8,128)(2,1)} %copy-done.208) | copy-start | bytes 393220
  1444.1 44.2 %copy-start.392 = (f32[8,16]{1,0:T(8,128)S(1)}, f32[8,16]{1,0:T(8,128)}, u32[]{:S(2)}) copy-start(f32[8,16]{1,0:T(8,128)} %copy-done.391) | copy-start | bytes 1540
  1444.2 44.2 %copy-start.394 = (f32[8,16]{1,0:T(8,128)S(1)}, f32[8,16]{1,0:T(8,128)}, u32[]{:S(2)}) copy-start(f32[8,16]{1,0:T(8,128)} %copy-done.393) | copy-start | bytes 1540
  1444.2 47.9 %copy-start.346 = (s32[8290]{0:T(1024)S(1)}, s32[8290]{0:T(1024)}, u32[]{:S(2)}) copy-start(s32[8290]{0:T(1024)} %dynamic-slice_multiply_fusion) | copy-start | bytes 99484
  1444.2 47.9 %copy-start.397 = (pred[8290]{0:T(1024)(128)(4,1)S(1)}, pred[8290]{0:T(1024)(128)(4,1)}, u32[]{:S(2)}) copy-start(pred[8290]{0:T(1024)(128)(4,1)} %dynamic_slice.10) | copy-start | bytes 24874
  (476 other events, 1844.4 us)
Sparse Core Ops, SparseCore 0:
  10.7 93.4 all-gather.2
  817.8 23.1 reduce-scatter.6
  910.2 20.2 reduce-scatter.4
  1380.9 111.1 all-reduce.3
where the time goes:
time: 1540 us; the launch traced here: 1520 us
  local copies, waits for them, and re-layouts  643 us (42%)
  matrix products  294 us (19%)
  blocking collectives  239 us (16%)
  other arithmetic  204 us (13%)
  waiting for transfers between devices  82 us (5%)
  starting transfers between devices  39.4 us (3%)
  between operations  21.7 us (1%)
    unnamed x1, blocking collectives  168 us
    unnamed x1065, local copies, waits for them, and re-layouts  154 us
    gather x1, local copies, waits for them, and re-layouts, per_device(): jnp.take(flat_grad, targets, axis=0)  128 us
    dot_general x44, matrix products, forward_dot(): return jnp.dot(values, weight, preferred_element_type=jnp.float32)  79.4 us
    dot_general x44, matrix products, back_through(): lax.dot_general(grad_rows, weight, (((grad_rows.ndim - 1,), (1,)), ((), (...  75.1 us
    gather x1, local copies, waits for them, and re-layouts, per_device(): jnp.take(gathered, source_rows(owner, segment_rows, held_rows), axis=0)  69.8 us
    dot_general x44, matrix products, weight_grad(): lax.dot_general(flat_in, flat_back, (((0,), (0,)), ((), ())), preferred_e...  57 us
    convert_element_type x1, other arithmetic, per_device(): everywhere = lax.psum(by_owner.astype(jnp.bfloat16), 'row')  45.1 us
  transfers between devices with their start and end apart: 13, of which 5 were waited for; matrix products, arithmetic and copies ran while one was open for 16% of the time, Pallas kernels for 0%

commit v1 on v0

v1 whole, which is shorter than its diff:
```python
import functools

import jax
import jax.numpy as jnp
from jax import lax
from jax.experimental import pallas as pl
from jax.experimental.pallas import tpu as pltpu
from jax.sharding import PartitionSpec as P

D = 512
H = 32
DE = 64
FF = 1024
FFE = 128
NS = 32
NB = 64
SET_ROWS = 16578
TOTAL_ROWS = 33156
NORM_EPS = 1e-05
BETA_ONE = 0.9
BETA_TWO = 0.95
WEIGHT_DECAY = 0.1
ADAM_EPS = 1e-08
MASK_FILL = -1e30
BF = jnp.bfloat16
F32 = jnp.float32
VMEM_LIMIT = 58 * 1024 * 1024
ROW_QKV, ROW_O, ROW_UP, ROW_DOWN = 0, 6144, 8192, 12288
ROW_BIAS, ROW_GATE, ROW_EDGE, ROW_EUP, ROW_EDOWN = 16384, 16400, 16416, 16432, 16496
ROW_NN, ROW_EN = 16560, 16576
GELU_C = 0.7978845608028654


def nn(a, b):
    return lax.dot_general(a, b, (((1,), (0,)), ((), ())), preferred_element_type=F32)


def nt(a, b):
    return lax.dot_general(a, b, (((1,), (1,)), ((), ())), preferred_element_type=F32)


def tn(a, b):
    return lax.dot_general(a, b, (((0,), (0,)), ((), ())), preferred_element_type=F32)


def iota(shape, axis):
    return lax.broadcasted_iota(jnp.int32, shape, axis)


def gelu_parts(u):
    u2 = u * u
    t = jnp.tanh(u * (GELU_C + (GELU_C * 0.044715) * u2))
    half = 0.5 + 0.5 * t
    value = u * half
    slope = half + value * (1.0 - t) * (GELU_C + (3.0 * GELU_C * 0.044715) * u2)
    return value, slope


def gelu_value(u):
    return u * (0.5 + 0.5 * jnp.tanh(u * (GELU_C + (GELU_C * 0.044715) * (u * u))))


def sigmoid(v):
    return 0.5 + 0.5 * jnp.tanh(0.5 * v)


def group_sum(v):
    v = v + pltpu.roll(v, 32, 1)
    return v + pltpu.roll(v, 64, 1)


def group_max(v):
    v = jnp.maximum(v, pltpu.roll(v, 32, 1))
    return jnp.maximum(v, pltpu.roll(v, 64, 1))


def fold8(v):
    return jnp.sum(v.reshape(v.shape[0] // 8, 8, v.shape[1]), axis=0)


class Bucket:
    def __init__(self, graphs, slots, node0, edge0, count0):
        self.graphs, self.slots = graphs, slots
        self.node0, self.edge0, self.count0 = node0, edge0, count0
        self.rows = graphs * slots
        self.chunks = slots // 4
        self.blocks = slots // 16
        self.edges = self.rows * self.chunks
        self.edge_lanes = slots * DE


class Dims:
    def __init__(self, small_graphs, big_graphs):
        self.small = Bucket(small_graphs, NS, 0, 0, 0)
        self.big = Bucket(
            big_graphs, NB, self.small.rows, self.small.edges, small_graphs
        )
        self.buckets = (self.small, self.big)
        self.nodes = self.small.rows + self.big.rows
        self.edges = self.small.edges + self.big.edges
        self.step = next(s for s in (256, 128, 64, 32) if self.edges % s == 0)
        self.blocks = sum(b.graphs * b.blocks for b in self.buckets)


def make_masks(mean_ref, head_ref, pick_ref):
    shape = (256, 256)
    same = (iota(shape, 0) >> 6) == (iota(shape, 1) >> 6)
    mean_ref[...] = jnp.where(same, 1.0 / DE, 0.0).astype(BF)
    shape = (512, 512)
    head_ref[...] = jnp.where((iota(shape, 0) >> 4) == (iota(shape, 1) & 31), 1.0, 0.0).astype(BF)
    shape = (16, 512)
    pick_ref[...] = jnp.where(iota(shape, 0) == (iota(shape, 1) >> 5), 1.0, 0.0).astype(BF)


def node_norm(v):
    centred = v - jnp.mean(v, axis=1, keepdims=True)
    r = lax.rsqrt(jnp.mean(centred * centred, axis=1, keepdims=True) + NORM_EPS)
    return centred * r, r


def node_norm_back(gdy, n, r):
    return r * (gdy - jnp.mean(gdy, axis=1, keepdims=True) - n * jnp.mean(gdy * n, axis=1, keepdims=True))


def aligned(value, by):
    return pl.multiple_of(value, by)


def block_of(bucket, t):
    g = t // bucket.blocks
    b = t % bucket.blocks
    rows = pl.ds(aligned(bucket.node0 + g * bucket.slots, 16), bucket.slots)
    keys = pl.ds(aligned(bucket.node0 + t * 16, 16), 16)
    chunk_rows = [
        pl.ds(
            aligned(bucket.edge0 + (4 * b + c) * bucket.rows + g * bucket.slots, 16),
            bucket.slots,
        )
        for c in range(4)
    ]
    return g, rows, keys, chunk_rows


def forward(dm, counts, w, io, res, scr):
    step = dm.step
    x = io.nodes[...].astype(F32)
    n, r = node_norm(x)
    res.node_n1[...] = n.astype(BF)
    res.node_r1[...] = jnp.broadcast_to(r, (dm.nodes, 128))
    hn = (n * w.nn[0:1, :] + w.nn[1:2, :]).astype(BF)
    res.qkv[...] = nn(hn, w.qkv[...]).astype(BF)

    @pl.loop(0, dm.edges // step)
    def _(i):
        rows = pl.ds(aligned(i * step, step), step)
        x = io.edges[rows, :]
        centred = x.astype(F32) - nn(x, scr.mean[...])
        r = lax.rsqrt(nn((centred * centred).astype(BF), scr.mean[...]) + NORM_EPS)
        n = centred * r
        res.edge_n1[rows, :] = n.astype(BF)
        res.edge_r1[rows, :] = r.astype(BF)
        xn = (n * w.en[0:1, :] + w.en[1:2, :]).astype(BF)
        both = nn(xn, w.eg[...])
        scr.scores[rows, :] = both[:, :128]
        res.gate[rows, :] = both[:, 128:]

    t0 = 0
    for bucket in dm.buckets:
        @pl.loop(0, bucket.graphs * bucket.blocks)
        def _(t, bucket=bucket, t0=t0):
            g, rows, keys, chunk_rows = block_of(bucket, t)
            kb = tn(res.qkv[keys, 512:1024], scr.pick[...]).astype(BF) * scr.head[...]
            scr.vbig[t0 + t] = tn(res.qkv[keys, 1024:1536], scr.pick[...]).astype(BF) * scr.head[...]
            s = nn(res.qkv[rows, 0:512], kb) * 0.25
            for c in range(4):
                scr.scores[chunk_rows[c], :] += s[:, 128 * c : 128 * (c + 1)]

        @pl.loop(0, bucket.rows // 32)
        def _(i, bucket=bucket):
            count = counts[bucket.count0 + i * 32 // bucket.slots]
            lane_key = iota((32, 128), 1) >> 5
            row = [
                pl.ds(aligned(bucket.edge0 + c * bucket.rows + i * 32, 32), 32)
                for c in range(bucket.chunks)
            ]
            top = jnp.full((32, 128), MASK_FILL, F32)
            for c in range(bucket.chunks):
                s = scr.scores[row[c], :]
                res.low[row[c], :] = s.astype(BF)
                top = jnp.maximum(top, jnp.where(lane_key < count - 4 * c, s, MASK_FILL))
            top = group_max(top)
            total = jnp.zeros((32, 128), F32)
            for c in range(bucket.chunks):
                s = jnp.where(lane_key < count - 4 * c, scr.scores[row[c], :], MASK_FILL)
                e = jnp.exp(s - top)
                total = total + e
                scr.scores[row[c], :] = e
            inv = 1.0 / group_sum(total)
            for c in range(bucket.chunks):
                p = scr.scores[row[c], :] * inv
                res.prob[row[c], :] = p.astype(BF)
                scr.attn[row[c], :] = (p * sigmoid(res.gate[row[c], :])).astype(BF)

        @pl.loop(0, bucket.graphs)
        def _(g, bucket=bucket, t0=t0):
            total = None
            for b in range(bucket.blocks):
                _, rows, _, chunk_rows = block_of(bucket, g * bucket.blocks + b)
                a = jnp.concatenate([scr.attn[chunk_rows[c], :] for c in range(4)], axis=1)
                part = nt(a, scr.vbig[t0 + g * bucket.blocks + b])
                total = part if total is None else total + part
            res.mixed[rows, :] = total.astype(BF)

        t0 += bucket.graphs * bucket.blocks

    y = io.nodes[...].astype(F32) + nn(res.mixed[...], w.o[...])
    n, r = node_norm(y)
    res.node_n2[...] = n.astype(BF)
    res.node_r2[...] = jnp.broadcast_to(r, (dm.nodes, 128))
    z = (n * w.nn[2:3, :] + w.nn[3:4, :]).astype(BF)
    u = nn(z, w.up[...])
    res.node_u[...] = u
    io.nodes_out[...] = (y + nn(gelu_value(u).astype(BF), w.down[...])).astype(BF)

    @pl.loop(0, dm.edges // step)
    def _(i):
        rows = pl.ds(aligned(i * step, step), step)
        m = io.edges[rows, :].astype(F32) + nn(res.low[rows, :], w.x[...])
        high = m.astype(BF)
        rest = (m - high.astype(F32)).astype(BF)
        centred = m - nn(high, scr.mean[...]) - nn(rest, scr.mean[...])
        r = lax.rsqrt(nn((centred * centred).astype(BF), scr.mean[...]) + NORM_EPS)
        n = centred * r
        res.edge_n2[rows, :] = n.astype(BF)
        res.edge_r2[rows, :] = r.astype(BF)
        mn = (n * w.en[2:3, :] + w.en[3:4, :]).astype(BF)
        ua = nn(mn, w.a[...])
        res.edge_u[rows, :] = ua.astype(BF)
        io.edges_out[rows, :] = (m + nn(gelu_value(ua).astype(BF), w.b[...])).astype(BF)


def put_strided(flat, first, value, parts):
    for q in range(parts):
        flat[pl.ds(first + q, value.shape[0], stride=parts), :] = value[:, 128 * q : 128 * (q + 1)]


def backward(dm, off, w, io, res, scr):
    step = dm.step
    flat = scr.flat
    gy = io.nodes_cot[...]
    act, slope = gelu_parts(res.node_u[...])
    du = (nt(gy, w.down[...]) * slope).astype(BF)
    put_strided(flat, off + ROW_DOWN, tn(act.astype(BF), gy), 4)
    n = res.node_n2[...].astype(F32)
    z = (n * w.nn[2:3, :] + w.nn[3:4, :]).astype(BF)
    put_strided(flat, off + ROW_UP, tn(z, du), 8)
    dz = nt(du, w.up[...])
    io.norms[2:3, 0:512] = jnp.sum(dz * n, axis=0, keepdims=True)
    io.norms[3:4, 0:512] = jnp.sum(dz, axis=0, keepdims=True)
    dy = gy.astype(F32) + node_norm_back(dz * w.nn[2:3, :], n, res.node_r2[:, 0:1])
    scr.dy[...] = dy
    dyl = dy.astype(BF)
    put_strided(flat, off + ROW_O, tn(res.mixed[...], dyl), 4)
    scr.do[...] = nt(dyl, w.o[...]).astype(BF)

    scr.gb[...] = jnp.zeros((512, 256), F32)
    scr.ga[...] = jnp.zeros((256, 512), F32)
    scr.gx[...] = jnp.zeros((128, 256), F32)
    scr.geg[...] = jnp.zeros((256, 256), F32)
    scr.en[...] = jnp.zeros((4, 8, 256), F32)

    @pl.loop(0, dm.edges // step)
    def _(i):
        rows = pl.ds(aligned(i * step, step), step)
        gx = io.edges_cot[rows, :]
        act, slope = gelu_parts(res.edge_u[rows, :].astype(F32))
        dua = (nt(gx, w.b[...]) * slope).astype(BF)
        scr.gb[...] += tn(act.astype(BF), gx)
        n = res.edge_n2[rows, :].astype(F32)
        mn = (n * w.en[2:3, :] + w.en[3:4, :]).astype(BF)
        scr.ga[...] += tn(mn, dua)
        dmn = nt(dua, w.a[...])
        scr.en[2] += fold8(dmn * n)
        scr.en[3] += fold8(dmn)
        gdy = dmn * w.en[2:3, :]
        m1 = nn(gdy.astype(BF), scr.mean[...])
        m2 = nn((gdy * n).astype(BF), scr.mean[...])
        dmid = gx.astype(F32) + res.edge_r2[rows, :].astype(F32) * (gdy - m1 - n * m2)
        scr.dmid[rows, :] = dmid
        dml = dmid.astype(BF)
        scr.gx[...] += tn(res.low[rows, :], dml)
        scr.scores[rows, :] = nt(dml, w.x[...])

    t0 = 0
    for bucket in dm.buckets:
        @pl.loop(0, bucket.graphs * bucket.blocks)
        def _(t, bucket=bucket, t0=t0):
            g, rows, keys, chunk_rows = block_of(bucket, t)
            scr.vbig[t0 + t] = tn(res.qkv[keys, 512:1024], scr.pick[...]).astype(BF) * scr.head[...]
            vb = tn(res.qkv[keys, 1024:1536], scr.pick[...]).astype(BF) * scr.head[...]
            da = nn(scr.do[rows, :], vb)
            for c in range(4):
                scr.da[chunk_rows[c], :] = da[:, 128 * c : 128 * (c + 1)]

        @pl.loop(0, bucket.rows // 32)
        def _(i, bucket=bucket):
            row = [
                pl.ds(aligned(bucket.edge0 + c * bucket.rows + i * 32, 32), 32)
                for c in range(bucket.chunks)
            ]
            total = jnp.zeros((32, 128), F32)
            for c in range(bucket.chunks):
                p = res.prob[row[c], :].astype(F32)
                s = sigmoid(res.gate[row[c], :])
                scr.attn[row[c], :] = (p * s).astype(BF)
                pt = p * scr.da[row[c], :] * s
                scr.da[row[c], :] = pt
                total = total + pt
                scr.dsg[row[c], 128:] = (pt * (1.0 - s)).astype(BF)
            total = group_sum(total)
            for c in range(bucket.chunks):
                p = res.prob[row[c], :].astype(F32)
                ds = scr.da[row[c], :] - p * total + scr.scores[row[c], :]
                scr.dsg[row[c], :128] = ds.astype(BF)

        @pl.loop(0, bucket.graphs)
        def _(g, bucket=bucket, t0=t0):
            total = None
            for b in range(bucket.blocks):
                t = g * bucket.blocks + b
                _, rows, keys, chunk_rows = block_of(bucket, t)
                ds = jnp.concatenate([scr.dsg[chunk_rows[c], :128] for c in range(4)], axis=1)
                part = nt(ds, scr.vbig[t0 + t])
                total = part if total is None else total + part
                gk = tn(res.qkv[rows, 0:512], ds).astype(BF) * scr.head[...]
                scr.dqkv[keys, 512:1024] = (nt(scr.pick[...], gk) * 0.25).astype(BF)
                a = jnp.concatenate([scr.attn[chunk_rows[c], :] for c in range(4)], axis=1)
                gv = tn(scr.do[rows, :], a).astype(BF) * scr.head[...]
                scr.dqkv[keys, 1024:1536] = nt(scr.pick[...], gv).astype(BF)
            scr.dqkv[rows, 0:512] = (total * 0.25).astype(BF)

        t0 += bucket.graphs * bucket.blocks

    n = res.node_n1[...].astype(F32)
    hn = (n * w.nn[0:1, :] + w.nn[1:2, :]).astype(BF)
    for m in range(3):
        put_strided(flat, off + ROW_QKV + 2048 * m, tn(hn, scr.dqkv[:, 512 * m : 512 * (m + 1)]), 4)
    dhn = nt(scr.dqkv[...], w.qkv[...])
    io.norms[0:1, 0:512] = jnp.sum(dhn * n, axis=0, keepdims=True)
    io.norms[1:2, 0:512] = jnp.sum(dhn, axis=0, keepdims=True)
    dx = scr.dy[...] + node_norm_back(dhn * w.nn[0:1, :], n, res.node_r1[:, 0:1])
    io.nodes_grad[...] = dx.astype(BF)

    @pl.loop(0, dm.edges // step)
    def _(i):
        rows = pl.ds(aligned(i * step, step), step)
        dsg = scr.dsg[rows, :]
        n = res.edge_n1[rows, :].astype(F32)
        xn = (n * w.en[0:1, :] + w.en[1:2, :]).astype(BF)
        scr.geg[...] += tn(xn, dsg)
        dxn = nt(dsg, w.eg[...])
        scr.en[0] += fold8(dxn * n)
        scr.en[1] += fold8(dxn)
        gdy = dxn * w.en[0:1, :]
        m1 = nn(gdy.astype(BF), scr.mean[...])
        m2 = nn((gdy * n).astype(BF), scr.mean[...])
        dx = scr.dmid[rows, :] + res.edge_r1[rows, :].astype(F32) * (gdy - m1 - n * m2)
        io.edges_grad[rows, :] = dx.astype(BF)

    small_grads(off, io, scr)
    io.grads[...] = scr.flat[...].astype(BF)


def small_grads(off, io, scr):
    flat, tmp = scr.flat, scr.tmp
    lane64 = lambda rows: iota((rows, 128), 1) >> 6
    lane32 = lambda rows: iota((rows, 128), 1) >> 5
    up = scr.ga[0:64, 0:128]
    for k in range(1, 4):
        up = up + scr.ga[64 * k : 64 * (k + 1), 128 * k : 128 * (k + 1)]
    flat[pl.ds(off + ROW_EUP, 64), :] = up

    def halves(ref, rows, first, out_rows):
        total = jnp.zeros((rows, 128), F32)
        for k in range(4):
            part = ref[rows * k : rows * (k + 1), 128 * (k // 2) : 128 * (k // 2 + 1)]
            total = total + jnp.where(lane64(rows) == k % 2, part, 0.0)
        tmp[0:rows, :] = total + pltpu.roll(total, 64, 1)
        even = tmp[pl.ds(0, out_rows, stride=2), :]
        odd = tmp[pl.ds(1, out_rows, stride=2), :]
        flat[pl.ds(off + first, out_rows), :] = jnp.where(lane64(out_rows) == 0, even, odd)

    halves(scr.gb, 128, ROW_EDOWN, 64)
    halves(scr.gx, 32, ROW_EDGE, 16)
    for half, first in ((0, ROW_BIAS), (1, ROW_GATE)):
        total = jnp.zeros((64, 128), F32)
        for k in range(4):
            part = scr.geg[64 * k : 64 * (k + 1), 128 * half : 128 * (half + 1)]
            total = total + jnp.where(lane32(64) == k, part, 0.0)
        tmp[0:64, :] = group_sum(total)
        rows = jnp.zeros((16, 128), F32)
        for b in range(4):
            rows = jnp.where(lane32(16) == b, tmp[pl.ds(b, 16, stride=4), :], rows)
        flat[pl.ds(off + first, 16), :] = rows
    sums = []
    for t in range(4):
        both = jnp.sum(scr.en[t], axis=0, keepdims=True)
        one = both[:, :128] + both[:, 128:]
        one = one + pltpu.roll(one, 64, 1)
        io.norms[t : t + 1, 512:576] = one[:, 0:64]
        sums.append(one)
    for t in range(2):
        flat[pl.ds(off + ROW_EN + t, 1), :] = jnp.where(lane64(1) == 0, sums[2 * t], sums[2 * t + 1])
    for t in range(4):
        for q in range(4):
            flat[pl.ds(off + ROW_NN + 4 * t + q, 1), :] = io.norms[t : t + 1, 128 * q : 128 * (q + 1)]
    if off:
        flat[pl.ds(0, off), :] = jnp.zeros((off, 128), F32)
    end = off + SET_ROWS
    flat[pl.ds(end, flat.shape[0] - end), :] = jnp.zeros((flat.shape[0] - end, 128), F32)


def assemble_set(off, flat, tmp, w):
    def strided(first, rows, parts, out, lane0=0):
        for q in range(parts):
            out[:, lane0 + 128 * q : lane0 + 128 * (q + 1)] = flat[
                pl.ds(off + first + q, rows, stride=parts), :
            ].astype(BF)

    for m in range(3):
        strided(ROW_QKV + 2048 * m, 512, 4, w.qkv, 512 * m)
    strided(ROW_O, 512, 4, w.o)
    strided(ROW_UP, 512, 8, w.up)
    strided(ROW_DOWN, 1024, 4, w.down)
    lane64 = lambda rows: iota((rows, 128), 1) >> 6
    lane32 = lambda rows: iota((rows, 128), 1) >> 5
    w.eg[...] = jnp.zeros((256, 256), BF)
    w.x[...] = jnp.zeros((128, 256), BF)
    w.a[...] = jnp.zeros((256, 512), BF)
    w.b[...] = jnp.zeros((512, 256), BF)
    up = flat[pl.ds(off + ROW_EUP, 64), :].astype(BF)
    for k in range(4):
        w.a[64 * k : 64 * (k + 1), 128 * k : 128 * (k + 1)] = up

    def halves(first, in_rows, out):
        rows = 2 * in_rows
        v = flat[pl.ds(off + first, in_rows), :]
        other = pltpu.roll(v, 64, 1)
        tmp[pl.ds(0, in_rows, stride=2), :] = jnp.where(lane64(in_rows) == 0, v, other)
        tmp[pl.ds(1, in_rows, stride=2), :] = jnp.where(lane64(in_rows) == 0, other, v)
        both = tmp[0:rows, :]
        for k in range(4):
            out[rows * k : rows * (k + 1), 128 * (k // 2) : 128 * (k // 2 + 1)] = jnp.where(
                lane64(rows) == k % 2, both, 0.0
            ).astype(BF)

    halves(ROW_EDOWN, 64, w.b)
    halves(ROW_EDGE, 16, w.x)
    for half, first in ((0, ROW_BIAS), (1, ROW_GATE)):
        v = flat[pl.ds(off + first, 16), :]
        for b in range(4):
            tmp[pl.ds(b, 16, stride=4), :] = group_sum(jnp.where(lane32(16) == b, v, 0.0))
        both = tmp[0:64, :]
        for k in range(4):
            w.eg[64 * k : 64 * (k + 1), 128 * half : 128 * (half + 1)] = jnp.where(
                lane32(64) == k, both, 0.0
            ).astype(BF)
    for t in range(4):
        for q in range(4):
            w.nn[t : t + 1, 128 * q : 128 * (q + 1)] = flat[pl.ds(off + ROW_NN + 4 * t + q, 1), :]
    for t in range(2):
        v = flat[pl.ds(off + ROW_EN + t, 1), :]
        other = pltpu.roll(v, 64, 1)
        gain = jnp.where(lane64(1) == 0, v, other)
        bias = jnp.where(lane64(1) == 0, other, v)
        for half in range(2):
            w.en[2 * t : 2 * t + 1, 128 * half : 128 * (half + 1)] = gain
            w.en[2 * t + 1 : 2 * t + 2, 128 * half : 128 * (half + 1)] = bias


class Group:
    def __init__(self, names, refs):
        for name, ref in zip(names, refs):
            setattr(self, name, ref)


WEIGHTS = {
    "qkv": ((D, 3 * D), BF),
    "o": ((D, D), BF),
    "up": ((D, FF), BF),
    "down": ((FF, D), BF),
    "eg": ((256, 256), BF),
    "x": ((128, 256), BF),
    "a": ((256, 512), BF),
    "b": ((512, 256), BF),
    "nn": ((4, D), F32),
    "en": ((4, 256), F32),
}


def residual_shapes(dm):
    return {
        "node_n1": ((dm.nodes, D), BF),
        "node_r1": ((dm.nodes, 128), F32),
        "qkv": ((dm.nodes, 3 * D), BF),
        "mixed": ((dm.nodes, D), BF),
        "node_n2": ((dm.nodes, D), BF),
        "node_r2": ((dm.nodes, 128), F32),
        "node_u": ((dm.nodes, FF), F32),
        "edge_n1": ((dm.edges, 256), BF),
        "edge_r1": ((dm.edges, 256), BF),
        "gate": ((dm.edges, 128), F32),
        "low": ((dm.edges, 128), BF),
        "prob": ((dm.edges, 128), BF),
        "edge_n2": ((dm.edges, 256), BF),
        "edge_r2": ((dm.edges, 256), BF),
        "edge_u": ((dm.edges, 512), BF),
    }


def mask_shapes():
    return {"mean": ((256, 256), BF), "head": ((512, 512), BF), "pick": ((16, 512), BF)}


def forward_scratch(dm):
    return {
        "scores": ((dm.edges, 128), F32),
        "attn": ((dm.edges, 128), BF),
        "vbig": ((dm.blocks, 512, 512), BF),
    }


def backward_scratch(dm, set_pad):
    return {
        "scores": ((dm.edges, 128), F32),
        "attn": ((dm.edges, 128), BF),
        "vbig": ((dm.blocks, 512, 512), BF),
        "da": ((dm.edges, 128), F32),
        "dsg": ((dm.edges, 256), BF),
        "dmid": ((dm.edges, 256), F32),
        "dy": ((dm.nodes, D), F32),
        "do": ((dm.nodes, D), BF),
        "dqkv": ((dm.nodes, 3 * D), BF),
        "gb": ((512, 256), F32),
        "ga": ((256, 512), F32),
        "gx": ((128, 256), F32),
        "geg": ((256, 256), F32),
        "en": ((4, 8, 256), F32),
        "tmp": ((128, 128), F32),
        "flat": ((set_pad, 128), F32),
    }


def structs(shapes):
    return [jax.ShapeDtypeStruct(s, t) for s, t in shapes.values()]


def vmem(shapes):
    return [pltpu.VMEM(s, t) for s, t in shapes.values()]


def whole(n):
    return [pl.BlockSpec(memory_space=pltpu.VMEM)] * n


def split(refs, *groups):
    out, at = [], 0
    for names in groups:
        out.append(Group(names, refs[at : at + len(names)]))
        at += len(names)
    assert at == len(refs)
    return out


def edge_copies(dm, whole_refs, stacked, sems, out):
    copies = []
    for bucket, ref in zip(dm.buckets, whole_refs):
        for c in range(bucket.chunks):
            a = ref.at[:, pl.ds(256 * c, 256)]
            b = stacked.at[pl.ds(bucket.edge0 + c * bucket.rows, bucket.rows), :]
            src, dst = (b, a) if out else (a, b)
            copies.append(pltpu.make_async_copy(src, dst, sems.at[len(copies)]))
    return copies


def copy_count(dm):
    return dm.small.chunks + dm.big.chunks


HBM = pl.BlockSpec(memory_space=pl.ANY)
SMEM = pl.BlockSpec(memory_space=pltpu.SMEM)


def compiler_params():
    return pltpu.CompilerParams(vmem_limit_bytes=VMEM_LIMIT)


def join_nodes(dm, small, big, out):
    out[0 : dm.small.rows, :] = small[...]
    out[dm.small.rows :, :] = big[...]


def part_nodes(dm, value, small, big):
    small[...] = value[0 : dm.small.rows, :]
    big[...] = value[dm.small.rows :, :]


def first_forward(dm, counts, weights, nodes, edges):
    res, masks = residual_shapes(dm), mask_shapes()
    out = {"nodes_out": ((dm.nodes, D), BF), "edges_out": ((dm.edges, 256), BF), **res}
    scr = {**masks, **forward_scratch(dm), "nodes": ((dm.nodes, D), BF), "edges": ((dm.edges, 256), BF)}

    def body(*refs):
        counts_ref, refs, sems = refs[0], refs[1:-1], refs[-1]
        w, src, dst, s = split(refs, WEIGHTS, ("sn", "bn", "se", "be"), out, scr)
        copies = edge_copies(dm, (src.se, src.be), s.edges, sems, False)
        for c in copies:
            c.start()
        make_masks(s.mean, s.head, s.pick)
        join_nodes(dm, src.sn, src.bn, s.nodes)
        io = Group(
            ("nodes", "edges", "nodes_out", "edges_out"),
            (s.nodes, s.edges, dst.nodes_out, dst.edges_out),
        )
        for c in copies:
            c.wait()
        forward(dm, counts_ref, w, io, dst, s)

    got = pl.pallas_call(
        body,
        out_shape=structs(out),
        in_specs=[SMEM] + whole(len(WEIGHTS) + 2) + [HBM] * 2,
        out_specs=whole(len(out)),
        scratch_shapes=vmem(scr) + [pltpu.SemaphoreType.DMA((copy_count(dm),))],
        compiler_params=compiler_params(),
    )(counts, *weights, *nodes, *edges)
    return got[0], got[1], got[2:]


def second_layer(dm, set_pad, off, counts, weights, nodes, edges, node_cots, edge_cots):
    out = {
        "sno": ((dm.small.rows, D), BF),
        "bno": ((dm.big.rows, D), BF),
        "seo": ((dm.small.rows, dm.small.edge_lanes), BF),
        "beo": ((dm.big.rows, dm.big.edge_lanes), BF),
        "nodes_grad": ((dm.nodes, D), BF),
        "edges_grad": ((dm.edges, 256), BF),
        "grads": ((set_pad, 128), BF),
        "norms": ((4, 576), F32),
    }
    res = residual_shapes(dm)
    scr = {
        **mask_shapes(),
        **forward_scratch(dm),
        **backward_scratch(dm, set_pad),
        **{"res_" + k: v for k, v in res.items()},
        "nodes_out": ((dm.nodes, D), BF),
        "edges_out": ((dm.edges, 256), BF),
        "node_cot": ((dm.nodes, D), BF),
        "edge_cot": ((dm.edges, 256), BF),
    }

    def body(*refs):
        counts_ref, refs, in_sems, out_sems = refs[0], refs[1:-2], refs[-2], refs[-1]
        w, src, dst, s = split(
            refs, WEIGHTS, ("nodes", "edges", "snc", "bnc", "sec", "bec"), out, scr
        )
        copies = edge_copies(dm, (src.sec, src.bec), s.edge_cot, in_sems, False)
        for c in copies:
            c.start()
        make_masks(s.mean, s.head, s.pick)
        join_nodes(dm, src.snc, src.bnc, s.node_cot)
        kept = Group(res, [getattr(s, "res_" + k) for k in res])
        io = Group(
            ("nodes", "edges", "nodes_out", "edges_out"),
            (src.nodes, src.edges, s.nodes_out, s.edges_out),
        )
        forward(dm, counts_ref, w, io, kept, s)
        outgoing = edge_copies(dm, (dst.seo, dst.beo), s.edges_out, out_sems, True)
        for c in outgoing:
            c.start()
        part_nodes(dm, s.nodes_out[...], dst.sno, dst.bno)
        for c in copies:
            c.wait()
        io = Group(
            ("nodes_cot", "edges_cot", "nodes_grad", "edges_grad", "grads", "norms"),
            (s.node_cot, s.edge_cot, dst.nodes_grad, dst.edges_grad, dst.grads, dst.norms),
        )
        backward(dm, off, w, io, kept, s)
        for c in outgoing:
            c.wait()

    count = copy_count(dm)
    return pl.pallas_call(
        body,
        out_shape=structs(out),
        in_specs=[SMEM] + whole(len(WEIGHTS) + 4) + [HBM] * 2,
        out_specs=whole(2) + [HBM] * 2 + whole(4),
        scratch_shapes=vmem(scr) + [pltpu.SemaphoreType.DMA((count,))] * 2,
        compiler_params=compiler_params(),
    )(counts, *weights, nodes, edges, *node_cots, *edge_cots)


def first_backward(dm, set_pad, off, weights, kept, nodes_cot, edges_cot):
    out = {
        "sng": ((dm.small.rows, D), BF),
        "bng": ((dm.big.rows, D), BF),
        "seg": ((dm.small.rows, dm.small.edge_lanes), BF),
        "beg": ((dm.big.rows, dm.big.edge_lanes), BF),
        "grads": ((set_pad, 128), BF),
        "norms": ((4, 576), F32),
    }
    res = residual_shapes(dm)
    scr = {
        **mask_shapes(),
        **backward_scratch(dm, set_pad),
        "nodes_grad": ((dm.nodes, D), BF),
        "edges_grad": ((dm.edges, 256), BF),
    }

    def body(*refs):
        refs, out_sems = refs[:-1], refs[-1]
        w, kept_refs, src, dst, s = split(refs, WEIGHTS, res, ("nodes_cot", "edges_cot"), out, scr)
        make_masks(s.mean, s.head, s.pick)
        io = Group(
            ("nodes_cot", "edges_cot", "nodes_grad", "edges_grad", "grads", "norms"),
            (src.nodes_cot, src.edges_cot, s.nodes_grad, s.edges_grad, dst.grads, dst.norms),
        )
        backward(dm, off, w, io, kept_refs, s)
        outgoing = edge_copies(dm, (dst.seg, dst.beg), s.edges_grad, out_sems, True)
        for c in outgoing:
            c.start()
        part_nodes(dm, s.nodes_grad[...], dst.sng, dst.bng)
        for c in outgoing:
            c.wait()

    return pl.pallas_call(
        body,
        out_shape=structs(out),
        in_specs=whole(len(WEIGHTS) + len(res) + 2),
        out_specs=whole(2) + [HBM] * 2 + whole(2),
        scratch_shapes=vmem(scr) + [pltpu.SemaphoreType.DMA((copy_count(dm),))],
        compiler_params=compiler_params(),
    )(*weights, *kept, nodes_cot, edges_cot)


def round_up(value, by):
    return -(-value // by) * by


def shifted_segment(master, shift, length):
    held = master.shape[0]
    padded = round_up(held + 15, 16)
    step = 1024

    def body(info, src, dst, window):
        i = pl.program_id(0)

        @pl.when(i == 0)
        def _():
            window[0:16, :] = jnp.zeros((16, 128), F32)

        window[16:, :] = src[...]
        moved = window[pl.ds(16 - info[0], step), :]
        index = i * step - info[0] + iota((step, 128), 0)
        live = (index >= 0) & (index < info[1])
        dst[...] = jnp.where(live, moved, 0.0).astype(BF)
        window[0:16, :] = window[step : step + 16, :]

    return pl.pallas_call(
        body,
        grid=(pl.cdiv(padded, step),),
        out_shape=jax.ShapeDtypeStruct((padded, 128), BF),
        in_specs=[
            SMEM,
            pl.BlockSpec((step, 128), lambda i: (jnp.minimum(i, (held - 1) // step), 0)),
        ],
        out_specs=pl.BlockSpec((step, 128), lambda i: (i, 0)),
        scratch_shapes=[pltpu.VMEM((step + 16, 128), F32)],
        compiler_params=compiler_params(),
    )(jnp.stack([shift, length]), master)


def assemble(first, last, parts):
    count = len(parts)
    padded = parts[0].shape[0]
    bits = (padded // 16).bit_length()
    tiles = -(-TOTAL_ROWS // 16)
    set_tiles = -(-(SET_ROWS + 2) // 16)
    out = {**{"one_" + k: v for k, v in WEIGHTS.items()}, **{"two_" + k: v for k, v in WEIGHTS.items()}}

    def body(first_ref, last_ref, *refs):
        srcs, refs = refs[:count], refs[count:]
        dsts, (rows, flat, tmp, edge, sems, edge_sems) = refs[: len(out)], refs[len(out) :]

        def each(act):
            for i in range(count):
                a, b = first_ref[i], last_ref[i]
                inner = b - a - 1
                for bit in range(bits):
                    size = 16 << bit
                    if size > padded:
                        continue
                    done = (inner >> (bit + 1)) << (bit + 1)

                    @pl.when((inner > 0) & (((inner >> bit) & 1) == 1))
                    def _(i=i, a=a, done=done, size=size, bit=bit):
                        act(
                            pltpu.make_async_copy(
                                srcs[i].at[pl.ds(aligned(16 * (1 + done), 16), size), :],
                                rows.at[pl.ds(aligned(16 * (a + 1 + done), 16), size), :],
                                sems.at[i, bit],
                            )
                        )

                act(pltpu.make_async_copy(srcs[i].at[pl.ds(0, 16), :], edge.at[2 * i], edge_sems.at[2 * i]))
                act(
                    pltpu.make_async_copy(
                        srcs[i].at[pl.ds(aligned(16 * (b - a), 16), 16), :],
                        edge.at[2 * i + 1],
                        edge_sems.at[2 * i + 1],
                    )
                )

        each(lambda c: c.start())
        each(lambda c: c.wait())
        tile = lambda t: pl.ds(aligned(16 * t, 16), 16)
        for i in range(count):
            rows[tile(first_ref[i]), :] = jnp.zeros((16, 128), BF)
            rows[tile(last_ref[i]), :] = jnp.zeros((16, 128), BF)
        for i in range(count):
            rows[tile(first_ref[i]), :] += edge[2 * i]

            @pl.when(last_ref[i] != first_ref[i])
            def _(i=i):
                rows[tile(last_ref[i]), :] += edge[2 * i + 1]

        for which in range(2):
            base = which * (SET_ROWS // 16) * 16
            flat[...] = rows[pl.ds(base, 16 * set_tiles), :].astype(F32)
            w = Group(WEIGHTS, dsts[which * len(WEIGHTS) : (which + 1) * len(WEIGHTS)])
            assemble_set(which * (SET_ROWS % 16), flat, tmp, w)

    got = pl.pallas_call(
        body,
        out_shape=structs(out),
        in_specs=[SMEM] * 2 + [HBM] * count,
        out_specs=whole(len(out)),
        scratch_shapes=[
            pltpu.VMEM((16 * tiles, 128), BF),
            pltpu.VMEM((16 * set_tiles, 128), F32),
            pltpu.VMEM((128, 128), F32),
            pltpu.VMEM((2 * count, 16, 128), BF),
            pltpu.SemaphoreType.DMA((count, bits)),
            pltpu.SemaphoreType.DMA((2 * count,)),
        ],
        compiler_params=compiler_params(),
    )(first, last, *parts)
    return got[: len(WEIGHTS)], got[len(WEIGHTS) :]


def adam(info, scales, places, grads, master, first, second):
    held = master.shape[0]
    step = 1040
    count = len(grads)
    each = count // 2
    block = grads[0].shape[0]
    base = (SET_ROWS // 16) * 16
    total = round_up(base + each * block + round_up(held + 16, step) + 16, 16)

    def body(info_ref, scale_ref, place_ref, *refs):
        srcs, refs = refs[:count], refs[count:]
        master_ref, first_ref, second_ref, o_master, o_first, o_second, rows, window, sems = refs
        i = pl.program_id(0)

        @pl.when(i == 0)
        def _():
            def copies(which):
                return [
                    pltpu.make_async_copy(
                        srcs[which * each + k],
                        rows.at[pl.ds(aligned(which * base + place_ref[which * each + k], 16), block), :],
                        sems.at[which * each + k],
                    )
                    for k in range(each)
                ]

            for c in copies(0):
                c.start()
            for c in copies(0):
                c.wait()
            kept = rows[base : base + 16, :]
            for c in copies(1):
                c.start()
            for c in copies(1):
                c.wait()
            rows[base : base + 16, :] += kept

        start, length = info_ref[0], info_ref[1]
        shift = start % 16
        from_row = aligned(start - shift + i * step, 16)
        window[...] = rows[pl.ds(from_row, step + 16), :].astype(F32)
        g = window[pl.ds(shift, step), :]
        index = i * step + iota((step, 128), 0)
        live = index < length
        at = start + index
        at = jnp.where(at >= SET_ROWS, at - SET_ROWS, at)
        rate = jnp.full((step, 128), 0.25, F32)
        for end, value in reversed(RATES):
            rate = jnp.where(at < end, value, rate)
        p, m, v = master_ref[...], first_ref[...], second_ref[...]
        m_new = BETA_ONE * m + (1.0 - BETA_ONE) * g
        v_new = BETA_TWO * v + (1.0 - BETA_TWO) * g * g
        move = (m_new * scale_ref[0]) / (jnp.sqrt(v_new * scale_ref[1]) + ADAM_EPS)
        o_master[...] = jnp.where(live, p - rate * (move + WEIGHT_DECAY * p), p)
        o_first[...] = jnp.where(live, m_new, m)
        o_second[...] = jnp.where(live, v_new, v)

    spec = pl.BlockSpec((step, 128), lambda i: (i, 0))
    shape = jax.ShapeDtypeStruct((held, 128), F32)
    return pl.pallas_call(
        body,
        grid=(pl.cdiv(held, step),),
        out_shape=[shape] * 3,
        in_specs=[SMEM] * 3 + [HBM] * count + [spec] * 3,
        out_specs=[spec] * 3,
        scratch_shapes=[
            pltpu.VMEM((total, 128), BF),
            pltpu.VMEM((step + 16, 128), F32),
            pltpu.SemaphoreType.DMA((count,)),
        ],
        compiler_params=compiler_params(),
    )(info, scales, places, *grads, master, first, second)


RATES = [
    (ROW_O, 0.5 * D ** (-0.5)),
    (ROW_UP, 2.0 * D ** (-0.5)),
    (ROW_DOWN, 0.5 * D ** (-0.5)),
    (ROW_BIAS, 0.5 * FF ** (-0.5)),
    (ROW_EDGE, 0.5 * DE ** (-0.5)),
    (ROW_EUP, 0.5 * H ** (-0.5)),
    (ROW_EDOWN, 0.5 * DE ** (-0.5)),
    (ROW_NN, 0.5 * FFE ** (-0.5)),
]


class Cube:
    def __init__(self, size):
        self.size = size
        self.bits = size.bit_length() - 1
        assert size == 1 << self.bits
        up = list(range(1, self.bits))
        self.order = (up, up[::-1])

    def pairs(self, step):
        return [(i, i ^ (1 << self.order[i & 1][step])) for i in range(self.size)]

    def core_pairs(self):
        return [(i, i ^ 1) for i in range(self.size)]

    def gather(self, value, backward=False):
        me = lax.axis_index("dp")
        core = me & 1
        held = [((), value)]
        steps = range(self.bits - 1)
        for step in reversed(steps) if backward else steps:
            held += [(used + (step,), lax.ppermute(v, "dp", self.pairs(step))) for used, v in held]
        out = []
        for other in (0, 1):
            for used, v in held:
                masks = [sum(1 << self.order[c][s] for s in used) for c in (0, 1)]
                if other:
                    v = lax.ppermute(v, "dp", self.core_pairs())
                    source = (me ^ 1) ^ jnp.where(core == 0, masks[1], masks[0])
                else:
                    source = me ^ jnp.where(core == 0, masks[0], masks[1])
                out.append((v, source))
        return [v for v, _ in out], jnp.stack([s for _, s in out])

    def place(self, index, rows):
        core = index & 1
        at, size = core * (rows // 2), rows // 2
        for step in range(self.bits - 1):
            size //= 2
            low, high = self.order[0][step], self.order[1][step]
            at = at + jnp.where(core == 0, (index >> low) & 1, (index >> high) & 1) * size
        return at

    def reduce(self, value):
        me = lax.axis_index("dp")
        core = me & 1
        value = exchange_half(value, "dp", core, self.core_pairs())
        for step in range(self.bits - 1):
            low, high = self.order[0][step], self.order[1][step]
            bit = jnp.where(core == 0, (me >> low) & 1, (me >> high) & 1)
            value = exchange_half(value, "dp", bit, self.pairs(step))
        return value


def exchange_half(value, axis, bit, pairs):
    halves = value.reshape((2, value.shape[0] // 2) + value.shape[1:])
    keep = lax.dynamic_index_in_dim(halves, bit, 0, keepdims=False)
    send = lax.dynamic_index_in_dim(halves, 1 - bit, 0, keepdims=False)
    got = lax.ppermute(send, axis, pairs)
    return (keep.astype(F32) + got.astype(F32)).astype(BF)


def sum_over_row(value):
    size = lax.axis_size("row")
    me = lax.axis_index("row")
    bits = size.bit_length() - 1
    assert size == 1 << bits
    for b in range(bits):
        value = exchange_half(value, "row", (me >> b) & 1, [(i, i ^ (1 << b)) for i in range(size)])
    for b in reversed(range(bits)):
        got = lax.ppermute(value, "row", [(i, i ^ (1 << b)) for i in range(size)])
        mine = ((me >> b) & 1) == 0
        value = jnp.concatenate([jnp.where(mine, value, got), jnp.where(mine, got, value)])
    return value


def pick_from(table, index):
    slots = jnp.arange(table.shape[0], dtype=jnp.int32)
    return jnp.sum(jnp.where(index[:, None] == slots[None, :], table[None, :], 0), axis=1)


def per_device(
    small_nodes,
    small_edges,
    small_counts,
    big_nodes,
    big_edges,
    big_counts,
    small_node_cot,
    small_edge_cot,
    big_node_cot,
    big_edge_cot,
    master,
    first_moment,
    second_moment,
    owner,
    segment_rows,
    step_count,
):
    n_dp, n_row = lax.axis_size("dp"), lax.axis_size("row")
    cube = Cube(n_dp)
    share = big_nodes.shape[0] // n_row
    dm = Dims(small_nodes.shape[0], share)
    set_pad = round_up(SET_ROWS + 2, 16 * n_dp)
    me = lax.axis_index("dp")

    ends = jnp.cumsum(segment_rows)
    start_of = pick_from(ends - segment_rows, owner)
    length_of = pick_from(segment_rows, owner)
    my_start = lax.dynamic_index_in_dim(start_of, me, keepdims=False)
    my_length = lax.dynamic_index_in_dim(length_of, me, keepdims=False)
    parts, sources = cube.gather(shifted_segment(master, my_start % 16, my_length))
    part_start = pick_from(start_of, sources)
    part_end = part_start + pick_from(length_of, sources) - 1
    one, two = assemble(part_start // 16, part_end // 16, parts)

    def to_whole(v):
        return lax.all_to_all(v, "row", split_axis=0, concat_axis=1, tiled=True)

    def to_rows(v, lanes):
        v = v.reshape(share, NB, lanes)
        return lax.all_to_all(v, "row", split_axis=1, concat_axis=0, tiled=True)

    def flat2(v):
        return v.reshape(-1, v.shape[-1])

    whole_edges, whole_nodes = to_whole(big_edges), to_whole(big_nodes)
    whole_edge_cot, whole_node_cot = to_whole(big_edge_cot), to_whole(big_node_cot)
    own_counts = lax.dynamic_slice_in_dim(big_counts, lax.axis_index("row") * share, share)
    counts = jnp.concatenate([small_counts, own_counts])

    mid_nodes, mid_edges, kept = first_forward(
        dm,
        counts,
        one,
        (flat2(small_nodes), flat2(whole_nodes)),
        (flat2(small_edges), flat2(whole_edges)),
    )
    sno, bno, seo, beo, node_grad, edge_grad, grads_two, norms_two = second_layer(
        dm,
        set_pad,
        SET_ROWS % 16,
        counts,
        two,
        mid_nodes,
        mid_edges,
        (flat2(small_node_cot), flat2(whole_node_cot)),
        (flat2(small_edge_cot), flat2(whole_edge_cot)),
    )
    sng, bng, seg, beg, grads_one, norms_one = first_backward(
        dm, set_pad, 0, one, kept, node_grad, edge_grad
    )
    norm_grads = lax.psum(jnp.concatenate([norms_one, norms_two]), ("dp", "row"))
    blocks, places = [], []
    for value in (grads_one, grads_two):
        got, sources = cube.gather(sum_over_row(cube.reduce(value)), backward=True)
        blocks += got
        places.append(cube.place(sources, set_pad))
    step_value = step_count[0].astype(F32)
    scales = jnp.stack(
        [
            1.0 / (1.0 - jnp.power(F32(BETA_ONE), step_value)),
            1.0 / (1.0 - jnp.power(F32(BETA_TWO), step_value)),
        ]
    )
    new_master, new_first, new_second = adam(
        jnp.stack([my_start, my_length]),
        scales,
        jnp.concatenate(places).astype(jnp.int32),
        blocks,
        master,
        first_moment,
        second_moment,
    )
    return (
        sno.reshape(small_nodes.shape),
        seo.reshape(small_edges.shape),
        to_rows(bno, D),
        to_rows(beo, NB * DE),
        sng.reshape(small_nodes.shape),
        seg.reshape(small_edges.shape),
        to_rows(bng, D),
        to_rows(beg, NB * DE),
        new_master,
        new_first,
        new_second,
        norm_grads,
    )


def solution(mesh):
    both = P(("dp", "row"), None, None)
    rows = P("dp", "row", None)
    held = P("dp", None)
    in_specs = (
        both, both, P(("dp", "row")), rows, rows, P("dp"), both, both, rows, rows,
        held, held, held, P(), P(), P(),
    )
    out_specs = (both, both, rows, rows, both, both, rows, rows, held, held, held, P())
    return jax.shard_map(
        per_device, mesh=mesh, in_specs=in_specs, out_specs=out_specs, check_vma=False
    )
```

time: 1540 us -> 537 us (0.35)
  local copies, waits for them, and re-layouts: 643 us -> 22 us
  matrix products: 294 us -> 0 us
  Pallas kernels: 0 us -> 203 us
  other arithmetic: 204 us -> 14.6 us
  blocking collectives: 239 us -> 59.7 us
  waiting for transfers between devices: 82 us -> 172 us
  between operations: 21.7 us -> 4.14 us
    dot_general x156 -> x0, matrix products: 269 us -> none  [the longest x44 79.4 us: forward_dot(): return jnp.dot(values, weight, preferred_element_type=jnp.float32)]
    pallas_call x0 -> x6, Pallas kernels: none -> 203 us  [the longest x1 75.3 us: second_layer(): pl.pallas_call(body, out_shape=structs(out), in_specs=[SMEM] + whole(len(...]
    gather x2 -> x0, local copies, waits for them, and re-layouts: 198 us -> none  [the longest x1 128 us: per_device(): jnp.take(flat_grad, targets, axis=0)]
    unnamed x1 -> x0, blocking collectives: 168 us -> none
    unnamed x1065 -> x32, local copies, waits for them, and re-layouts: 154 us -> 0.07 us
    ppermute x0 -> x35, waiting for transfers between devices: none -> 112 us  [the longest x9 60.5 us: gather(): lax.ppermute(v, 'dp', self.pairs(step))]
    convert_element_type x35 -> x10, other arithmetic: 89.4 us -> 5.21 us  [exchange_half(): return (keep.astype(F32) + got.astype(F32)).astype(BF)]
    reshape x46 -> x4, local copies, waits for them, and re-layouts: 87.8 us -> 5.71 us  [to_rows(): v = v.reshape(share, NB, lanes)]
  transfers between devices with their start and end apart: 13 -> 41, of which waited for: 5 -> 16; matrix products, arithmetic and copies ran while one was open for 16% -> 6% of each run, Pallas kernels for 0% -> 10%
where the time goes in v1:
time: 537 us; the launch traced here: 530 us
  Pallas kernels  203 us (38%)
  waiting for transfers between devices  172 us (32%)
  blocking collectives  59.7 us (11%)
  starting transfers between devices  54.4 us (10%)
  local copies, waits for them, and re-layouts  22 us (4%)
  other arithmetic  14.6 us (3%)
    pallas_call x1, Pallas kernels, second_layer(): pl.pallas_call(body, out_shape=structs(out), in_specs=[SMEM] + whole(len(...  75.3 us
    ppermute x9, waiting for transfers between devices, gather(): lax.ppermute(v, 'dp', self.pairs(step))  60.5 us
    pallas_call x1, Pallas kernels, first_backward(): pl.pallas_call(body, out_shape=structs(out), in_specs=whole(len(WEIGHTS)...  50.8 us
    ppermute x10, waiting for transfers between devices, exchange_half(): got = lax.ppermute(send, axis, pairs)  44.7 us
    psum x1, blocking collectives, per_device(): lax.psum(jnp.concatenate([norms_one, norms_two]), ('dp', 'row'))  40.5 us
    all_to_all x2, waiting for transfers between devices, to_whole(): return lax.all_to_all(v, 'row', split_axis=0, concat_axis=1, tiled=True)  37.9 us
    pallas_call x1, Pallas kernels, first_forward(): pl.pallas_call(body, out_shape=structs(out), in_specs=[SMEM] + whole(len(...  37.7 us
    all_to_all x4, waiting for transfers between devices, to_rows(): return lax.all_to_all(v, 'row', split_axis=1, concat_axis=0, tiled=True)  22.2 us
  transfers between devices with their start and end apart: 41, of which 16 were waited for; matrix products, arithmetic and copies ran while one was open for 6% of the time, Pallas kernels for 10%

profile of v1, /device:TPU:0, one launch (start us, length us, event | category | flops | bytes accessed | tf_op | source)
XLA Modules:
  0.0 529.9 jit_solution(7202588032146245773)
XLA Ops:
  7.3 7.2 %shard_map.247.refs_0_ = bf16[8320,128]{1,0:T(8,128)(2,1)} custom-call(s32[2]{0:T(128)} %pad_add_fusion.1.info, f32[8290,128]{1,0:T(8,128)} %refs_16_.1), custom_call_target="tpu_custom_call" | custom-call | tf_op jit(solution)/shard_map/pallas_call | solution.py:770
  14.5 2.9 collective-permute-start
  19.0 45.5 %collective-permute-done.refs_1_ = bf16[8320,128]{1,0:T(8,128)(2,1)} collective-permute-done((bf16[8320,128]{1,0:T(8,128)(2,1)}, bf16[8320,128]{1,0:T(8,128)(2,1)}, u32[]{:S(2)}, u32[]{:S(2)}) %collective-permute-start) | collective-permute-done | bytes 2129952 | tf_op jit(solution)/shard_map/ppermute | solution.py:968
  65.9 10.8 %all_to_all.132 = bf16[8,16,512]{2,1,0:T(8,128)(2,1)S(1)} all-to-all(bf16[8,16,512]{2,1,0:T(8,128)(2,1)S(1)} %copy-done.6), channel_id=1, replica_groups=mesh['dp'=8,'row'=4] {'row'}, dimensions={0} | all-to-all | bytes 262144 | tf_op jit(solution)/shard_map/all_to_all | solution.py:1064
  76.7 8.4 %all_to_all.133 = bf16[8,16,512]{2,1,0:T(8,128)(2,1)S(1)} all-to-all(bf16[8,16,512]{2,1,0:T(8,128)(2,1)S(1)} %copy-done.7), channel_id=1, replica_groups=mesh['dp'=8,'row'=4] {'row'}, dimensions={0} | all-to-all | bytes 262144 | tf_op jit(solution)/shard_map/all_to_all | solution.py:1064
  85.1 3.6 all-to-all-start.1
  89.4 1.8 collective-permute-done.2.refs_3_
  91.2 18.8 %all-to-all-done.1 = bf16[8,16,4096]{2,1,0:T(8,128)(2,1)S(1)} async-done(((bf16[8,16,4096]{2,1,0:T(8,128)(2,1)}), bf16[8,16,4096]{2,1,0:T(8,128)(2,1)S(1)}, u32[]{:S(2)}, u32[]{:S(2)}) %all-to-all-start.1) | async-done | bytes 1048608 | tf_op jit(solution)/shard_map/all_to_all | solution.py:1064
  110.1 4.2 all-to-all-start.3
  118.3 19.1 %all-to-all-done.3 = bf16[8,16,4096]{2,1,0:T(8,128)(2,1)} async-done(((bf16[8,16,4096]{2,1,0:T(8,128)(2,1)}), bf16[8,16,4096]{2,1,0:T(8,128)(2,1)}, u32[]{:S(2)}, u32[]{:S(2)}) %all-to-all-start.3) | async-done | bytes 1048608 | tf_op jit(solution)/shard_map/all_to_all | solution.py:1064
  137.3 2.3 copy.51
  139.7 10.1 %shard_map.248 = (bf16[512,1536]{1,0:T(8,128)(2,1)}, bf16[512,512]{1,0:T(8,128)(2,1)}, bf16[512,1024]{1,0:T(8,128)(2,1)}, bf16[1024,512]{1,0:T(8,128)(2,1)}, bf1...) custom-call(s32[8]{0:T(128)} %get-tuple-element.133.first_ref, ...), custom_call_target="tpu_custom_call" | custom-call | tf_op jit(solution)/shard_map/pallas_call | solution.py:844
  149.8 37.7 %shard_map.249 = (bf16[224,512]{1,0:T(8,128)(2,1)}, bf16[2816,256]{1,0:T(8,128)(2,1)}, bf16[224,512]{1,0:T(8,128)(2,1)}, f32[224,128]{1,0:T(8,128)}, bf16[224,15...) custom-call(s32[5]{0:T(128)} %pad_add_fusion.refs_0_, ...), custom_call_target="tpu_custom_call" | custom-call | tf_op jit(solution)/shard_map/pallas_call | solution.py:629
  187.4 75.3 %shard_map.250 = (bf16[96,512]{1,0:T(8,128)(2,1)}, bf16[128,512]{1,0:T(8,128)(2,1)}, bf16[96,2048]{1,0:T(8,128)(2,1)}, bf16[128,4096]{1,0:T(8,128)(2,1)}, bf16[2...) custom-call(s32[5]{0:T(128)} %pad_add_fusion.refs_0_, ...), custom_call_target="tpu_custom_call" | custom-call | tf_op jit(solution)/shard_map/pallas_call | solution.py:694
  262.7 2.6 dynamic-slice_bitcast_fusion
  265.4 50.8 %shard_map.251 = (bf16[96,512]{1,0:T(8,128)(2,1)}, bf16[128,512]{1,0:T(8,128)(2,1)}, bf16[96,2048]{1,0:T(8,128)(2,1)}, bf16[128,4096]{1,0:T(8,128)(2,1)}, bf16[16640,128]{1,0:T(8,128)(2,1)}, /*index=5*/f32[4,576]{1,0:T(4,128)}) custom-call(bf16[512,1536]{1,0:T(8,128)(2,1)} %get-tuple-element.76.refs_1_.refs_0_, ...), custom_call_target="tpu_custom_call" | custom-call | tf_op jit(solution)/shard_map/pallas_call | solution.py:737
  316.2 2.7 dynamic-slice_bitcast_fusion.1
  319.4 2.1 copy.58
  322.3 3.3 all-to-all-start.6
  326.4 2.3 fusion
  328.9 1.9 fusion.1
  330.9 2.1 collective-permute-start.8
  333.0 10.9 %collective-permute-done.22 = bf16[4160,128]{1,0:T(8,128)(2,1)S(1)} collective-permute-done((bf16[4160,128]{1,0:T(8,128)(2,1)S(1)}, bf16[4160,128]{1,0:T(8,128)(2,1)S(1)}, u32[]{:S(2)}, u32[]{:S(2)}) %collective-permute-start.22) | collective-permute-done | bytes 1064992 | tf_op jit(solution)/shard_map/ppermute | solution.py:1005
  344.2 1.9 collective-permute-start.23
  346.1 14.9 %collective-permute-done.8 = bf16[4160,128]{1,0:T(8,128)(2,1)S(1)} collective-permute-done((bf16[4160,128]{1,0:T(8,128)(2,1)S(1)}, bf16[4160,128]{1,0:T(8,128)(2,1)S(1)}, u32[]{:S(2)}, u32[]{:S(2)}) %collective-permute-start.8) | collective-permute-done | bytes 1064992 | tf_op jit(solution)/shard_map/ppermute | solution.py:1005
  361.3 1.9 collective-permute-start.9
  363.4 2.0 collective-permute-start.24
  365.4 5.2 collective-permute-done.9
  370.8 2.0 collective-permute-start.10
  373.0 2.4 collective-permute-start.25
  375.4 5.1 collective-permute-done.10
  383.7 8.6 %collective-permute-done.11 = bf16[520,128]{1,0:T(8,128)(2,1)S(1)} collective-permute-done((bf16[520,128]{1,0:T(8,128)(2,1)S(1)}, bf16[520,128]{1,0:T(8,128)(2,1)S(1)}, u32[]{:S(2)}, u32[]{:S(2)}) %collective-permute-start.11) | collective-permute-done | bytes 133152 | tf_op jit(solution)/shard_map/ppermute | solution.py:1005
  392.4 2.7 collective-permute-done.26
  396.0 4.4 collective-permute-done.12
  400.5 3.3 all-to-all-start.4
  403.8 2.0 collective-permute-start.13
  405.9 4.2 all-to-all-done.4
  410.1 3.5 all-to-all-start.7
  417.4 2.1 copy.54
  419.5 17.9 %all-to-all-done.7 = bf16[2,64,4096]{2,0,1:T(2,128)(2,1)S(1)} async-done(((bf16[2,64,4096]{2,0,1:T(2,128)(2,1)}), bf16[2,64,4096]{2,0,1:T(2,128)(2,1)S(1)}, u32[]{:S(2)}, u32[]{:S(2)}) %all-to-all-start.7) | async-done | bytes 1048608 | tf_op jit(solution)/shard_map/all_to_all | solution.py:1068
  437.4 3.5 all-to-all-start.5
  443.1 1.8 collective-permute-start.16
  445.9 1.8 pad_add_fusion.2.info_ref
  447.7 2.7 collective-permute-done.15.refs_2_
  450.9 5.2 collective-permute-done.30.refs_11_
  456.6 5.2 collective-permute-done.16.refs_3_
  463.1 40.5 %psum.7 = f32[8,576]{1,0:T(8,128)} all-reduce(f32[8,576]{1,0:T(8,128)S(1)} %pad_maximum_fusion.4), channel_id=1, replica_groups=mesh['dp'=8,'row'=4] {'dp','row'}, use_global_device_ids=true, to_apply=%region_5.6 | all-reduce | flops 4608 | bytes 36864 | tf_op jit(solution)/shard_map/psum | solution.py:1099
  508.1 21.6 %shard_map.252 = (f32[8290,128]{1,0:T(8,128)}, f32[8290,128]{1,0:T(8,128)}, f32[8290,128]{1,0:T(8,128)}) custom-call(s32[2]{0:T(128)} %pad_add_fusion.2.info_ref, f32[2]{0:T(128)} %pad_maximum_fusion.5.scale_ref, s32[16]{0:T(128)} %pad_add_fusion.3.place_ref, bf16[2080,128]{1,0:T(8,128)(2,1)} %copy-done.2, ...), custom_call_target="tpu_custom_call" | custom-call | tf_op jit(solution)/shard_map/pallas_call | solution.py:921
  (133 shorter events, 32.5 us)
Async XLA Ops:
  7.3 58.6 %copy-start.6 = (bf16[8,16,512]{2,1,0:T(8,128)(2,1)S(1)}, bf16[8,16,512]{2,1,0:T(8,128)(2,1)}, u32[]{:S(2)}) copy-start(bf16[8,16,512]{2,1,0:T(8,128)(2,1)} %param.19) | copy-start | bytes 393220
  7.3 69.4 %copy-start.7 = (bf16[8,16,512]{2,1,0:T(8,128)(2,1)S(1)}, bf16[8,16,512]{2,1,0:T(8,128)(2,1)}, u32[]{:S(2)}) copy-start(bf16[8,16,512]{2,1,0:T(8,128)(2,1)} %param.24) | copy-start | bytes 393220
  14.5 74.2 %copy-start = (bf16[8320,128]{1,0:T(8,128)(2,1)S(1)}, bf16[8320,128]{1,0:T(8,128)(2,1)}, u32[]{:S(2)}) copy-start(bf16[8320,128]{1,0:T(8,128)(2,1)} %shard_map.247.refs_0_) | copy-start | bytes 6389764
  14.5 50.0 %collective-permute-start = (bf16[8320,128]{1,0:T(8,128)(2,1)}, bf16[8320,128]{1,0:T(8,128)(2,1)}, u32[]{:S(2)}, u32[]{:S(2)}) collective-permute-start(bf16[8320,128]{1,0:T(8,128)(2,1)} %shard_map.247.refs_0_), channel_id=1, source_target_pairs={{0,8},{4,20},{8,0},{12,28},{16,24},{20,4},{24,16},{28,12},{1,9},{5... | collective-permute-start | bytes 6389768 | tf_op jit(solution)/shard_map/ppermute | solution.py:968
  17.5 71.9 %collective-permute-start.1 = (bf16[8320,128]{1,0:T(8,128)(2,1)}, bf16[8320,128]{1,0:T(8,128)(2,1)}, u32[]{:S(2)}, u32[]{:S(2)}) collective-permute-start(bf16[8320,128]{1,0:T(8,128)(2,1)} %shard_map.247.refs_0_), channel_id=1, source_target_pairs={{0,16},{4,12},{8,24},{12,4},{16,0},{20,28},{24,8},{28,20},{1,17},{... | collective-permute-start | bytes 6389768 | tf_op jit(solution)/shard_map/ppermute | solution.py:968
  64.5 26.7 %collective-permute-start.2 = (bf16[8320,128]{1,0:T(8,128)(2,1)}, bf16[8320,128]{1,0:T(8,128)(2,1)}, u32[]{:S(2)}, u32[]{:S(2)}) collective-permute-start(bf16[8320,128]{1,0:T(8,128)(2,1)} %collective-permute-done.refs_1_), channel_id=1, source_target_pairs={{0,16},{4,12},{8,24},{12,4},{16,0},{20,28},{24,8},{28,20},{1,17},{... | collective-permute-start | bytes 6389768 | tf_op jit(solution)/shard_map/ppermute | solution.py:968
  85.1 25.0 %all-to-all-start.1 = ((bf16[8,16,4096]{2,1,0:T(8,128)(2,1)}), bf16[8,16,4096]{2,1,0:T(8,128)(2,1)S(1)}, u32[]{:S(2)}, u32[]{:S(2)}) async-start(bf16[8,16,4096]{2,1,0:T(8,128)(2,1)} %param.20), calls=%async_computation.1 | async-start | bytes 2097152 | tf_op jit(solution)/shard_map/all_to_all | solution.py:1064
  88.8 50.9 %collective-permute-start.3 = (bf16[8320,128]{1,0:T(8,128)(2,1)S(1)}, bf16[8320,128]{1,0:T(8,128)(2,1)}, u32[]{:S(2)}, u32[]{:S(2)}) collective-permute-start(bf16[8320,128]{1,0:T(8,128)(2,1)S(1)} %copy-done), channel_id=1, source_target_pairs={{0,4},{4,0},{8,12},{12,8},{16,20},{20,16},{24,28},{28,24},{1,5},{5... | collective-permute-start | bytes 6389768 | tf_op jit(solution)/shard_map/ppermute | solution.py:974
  88.8 50.8 %collective-permute-start.4 = (bf16[8320,128]{1,0:T(8,128)(2,1)}, bf16[8320,128]{1,0:T(8,128)(2,1)}, u32[]{:S(2)}, u32[]{:S(2)}) collective-permute-start(bf16[8320,128]{1,0:T(8,128)(2,1)} %collective-permute-done.refs_1_), channel_id=1, source_target_pairs={{0,4},{4,0},{8,12},{12,8},{16,20},{20,16},{24,28},{28,24},{1,5},{5... | collective-permute-start | bytes 6389768 | tf_op jit(solution)/shard_map/ppermute | solution.py:974
  89.3 50.3 %collective-permute-start.5 = (bf16[8320,128]{1,0:T(8,128)(2,1)}, bf16[8320,128]{1,0:T(8,128)(2,1)}, u32[]{:S(2)}, u32[]{:S(2)}) collective-permute-start(bf16[8320,128]{1,0:T(8,128)(2,1)} %collective-permute-done.1.refs_2_), channel_id=1, source_target_pairs={{0,4},{4,0},{8,12},{12,8},{16,20},{20,16},{24,28},{28,24},{1,5},{5... | collective-permute-start | bytes 6389768 | tf_op jit(solution)/shard_map/ppermute | solution.py:974
  91.2 48.4 %collective-permute-start.6 = (bf16[8320,128]{1,0:T(8,128)(2,1)}, bf16[8320,128]{1,0:T(8,128)(2,1)}, u32[]{:S(2)}, u32[]{:S(2)}) collective-permute-start(bf16[8320,128]{1,0:T(8,128)(2,1)} %collective-permute-done.2.refs_3_), channel_id=1, source_target_pairs={{0,4},{4,0},{8,12},{12,8},{16,20},{20,16},{24,28},{28,24},{1,5},{5... | collective-permute-start | bytes 6389768 | tf_op jit(solution)/shard_map/ppermute | solution.py:974
  110.1 27.3 %all-to-all-start.3 = ((bf16[8,16,4096]{2,1,0:T(8,128)(2,1)}), bf16[8,16,4096]{2,1,0:T(8,128)(2,1)}, u32[]{:S(2)}, u32[]{:S(2)}) async-start(bf16[8,16,4096]{2,1,0:T(8,128)(2,1)} %param.25), calls=%async_computation.3 | async-start | bytes 2097152 | tf_op jit(solution)/shard_map/all_to_all | solution.py:1064
  265.4 61.1 %collective-permute-start.21 = (bf16[8320,128]{1,0:T(8,128)(2,1)}, bf16[8320,128]{1,0:T(8,128)(2,1)S(1)}, u32[]{:S(2)}, u32[]{:S(2)}) collective-permute-start(bf16[8320,128]{1,0:T(8,128)(2,1)} %dynamic-slice_bitcast_fusion), channel_id=1, source_target_pairs={{0,4},{4,0},{8,12},{12,8},{16,20},{20,16},{24,28},{28,24},{1,5},{5... | collective-permute-start | bytes 6389768 | tf_op jit(solution)/shard_map/ppermute | solution.py:1005
  318.9 10.0 %collective-permute-start.7 = (bf16[8320,128]{1,0:T(8,128)(2,1)}, bf16[8320,128]{1,0:T(8,128)(2,1)}, u32[]{:S(2)}, u32[]{:S(2)}) collective-permute-start(bf16[8320,128]{1,0:T(8,128)(2,1)} %dynamic-slice_bitcast_fusion.1), channel_id=1, source_target_pairs={{0,4},{4,0},{8,12},{12,8},{16,20},{20,16},{24,28},{28,24},{1,5},{5... | collective-permute-start | bytes 6389768 | tf_op jit(solution)/shard_map/ppermute | solution.py:1005
  322.3 78.2 %all-to-all-start.6 = ((bf16[2,64,512]{2,0,1:T(2,128)(2,1)}), bf16[2,64,512]{2,0,1:T(2,128)(2,1)S(1)}, u32[]{:S(2)}, u32[]{:S(2)}) async-start(bf16[2,64,512]{2,0,1:T(2,128)(2,1)} %copy.56), calls=%async_computation.6 | async-start | bytes 262144 | tf_op jit(solution)/shard_map/all_to_all | solution.py:1068
  328.8 15.0 %collective-permute-start.22 = (bf16[4160,128]{1,0:T(8,128)(2,1)S(1)}, bf16[4160,128]{1,0:T(8,128)(2,1)S(1)}, u32[]{:S(2)}, u32[]{:S(2)}) collective-permute-start(bf16[4160,128]{1,0:T(8,128)(2,1)S(1)} %dynamic-slice_bitcast_fusion.2), channel_id=1, source_target_pairs={{0,8},{4,20},{8,0},{12,28},{16,24},{20,4},{24,16},{28,12},{1,9},{5... | collective-permute-start | bytes 3194888 | tf_op jit(solution)/shard_map/ppermute | solution.py:1005
  330.9 30.1 %collective-permute-start.8 = (bf16[4160,128]{1,0:T(8,128)(2,1)S(1)}, bf16[4160,128]{1,0:T(8,128)(2,1)S(1)}, u32[]{:S(2)}, u32[]{:S(2)}) collective-permute-start(bf16[4160,128]{1,0:T(8,128)(2,1)S(1)} %dynamic-slice_bitcast_fusion.3), channel_id=1, source_target_pairs={{0,8},{4,20},{8,0},{12,28},{16,24},{20,4},{24,16},{28,12},{1,9},{5... | collective-permute-start | bytes 3194888 | tf_op jit(solution)/shard_map/ppermute | solution.py:1005
  344.2 19.0 %collective-permute-start.23 = (bf16[2080,128]{1,0:T(8,128)(2,1)S(1)}, bf16[2080,128]{1,0:T(8,128)(2,1)S(1)}, u32[]{:S(2)}, u32[]{:S(2)}) collective-permute-start(bf16[2080,128]{1,0:T(8,128)(2,1)S(1)} %dynamic-slice_bitcast_fusion.4), channel_id=1, source_target_pairs={{0,16},{4,12},{8,24},{12,4},{16,0},{20,28},{24,8},{28,20},{1,17},{... | collective-permute-start | bytes 1597448 | tf_op jit(solution)/shard_map/ppermute | solution.py:1005
  361.3 9.3 %collective-permute-start.9 = (bf16[2080,128]{1,0:T(8,128)(2,1)S(1)}, bf16[2080,128]{1,0:T(8,128)(2,1)S(1)}, u32[]{:S(2)}, u32[]{:S(2)}) collective-permute-start(bf16[2080,128]{1,0:T(8,128)(2,1)S(1)} %dynamic-slice_bitcast_fusion.5), channel_id=1, source_target_pairs={{0,16},{4,12},{8,24},{12,4},{16,0},{20,28},{24,8},{28,20},{1,17},{... | collective-permute-start | bytes 1597448 | tf_op jit(solution)/shard_map/ppermute | solution.py:1005
  363.4 9.5 %collective-permute-start.24 = (bf16[1040,128]{1,0:T(8,128)(2,1)S(1)}, bf16[1040,128]{1,0:T(8,128)(2,1)S(1)}, u32[]{:S(2)}, u32[]{:S(2)}) collective-permute-start(bf16[1040,128]{1,0:T(8,128)(2,1)S(1)} %dynamic-slice_bitcast_fusion.6), channel_id=1, source_target_pairs={{0,1},{1,0},{2,3},{3,2},{4,5},{5,4},{6,7},{7,6},{8,9},{9,8},{10,11... | collective-permute-start | bytes 798728 | tf_op jit(solution)/shard_map/ppermute | solution.py:1005
  370.8 9.6 %collective-permute-start.10 = (bf16[1040,128]{1,0:T(8,128)(2,1)S(1)}, bf16[1040,128]{1,0:T(8,128)(2,1)S(1)}, u32[]{:S(2)}, u32[]{:S(2)}) collective-permute-start(bf16[1040,128]{1,0:T(8,128)(2,1)S(1)} %dynamic-slice_bitcast_fusion.7), channel_id=1, source_target_pairs={{0,1},{1,0},{2,3},{3,2},{4,5},{5,4},{6,7},{7,6},{8,9},{9,8},{10,11... | collective-permute-start | bytes 798728 | tf_op jit(solution)/shard_map/ppermute | solution.py:1005
  373.0 9.2 %collective-permute-start.25 = (bf16[520,128]{1,0:T(8,128)(2,1)S(1)}, bf16[520,128]{1,0:T(8,128)(2,1)S(1)}, u32[]{:S(2)}, u32[]{:S(2)}) collective-permute-start(bf16[520,128]{1,0:T(8,128)(2,1)S(1)} %dynamic-slice_bitcast_fusion.8), channel_id=1, source_target_pairs={{0,2},{1,3},{2,0},{3,1},{4,6},{5,7},{6,4},{7,5},{8,10},{9,11},{10,... | collective-permute-start | bytes 399368 | tf_op jit(solution)/shard_map/ppermute | solution.py:1005
  380.6 11.7 %collective-permute-start.11 = (bf16[520,128]{1,0:T(8,128)(2,1)S(1)}, bf16[520,128]{1,0:T(8,128)(2,1)S(1)}, u32[]{:S(2)}, u32[]{:S(2)}) collective-permute-start(bf16[520,128]{1,0:T(8,128)(2,1)S(1)} %dynamic-slice_bitcast_fusion.9), channel_id=1, source_target_pairs={{0,2},{1,3},{2,0},{3,1},{4,6},{5,7},{6,4},{7,5},{8,10},{9,11},{10,... | collective-permute-start | bytes 399368 | tf_op jit(solution)/shard_map/ppermute | solution.py:1005
  382.3 12.9 %collective-permute-start.26 = (bf16[520,128]{1,0:T(8,128)(2,1)S(1)}, bf16[520,128]{1,0:T(8,128)(2,1)S(1)}, u32[]{:S(2)}, u32[]{:S(2)}) collective-permute-start(bf16[520,128]{1,0:T(8,128)(2,1)S(1)} %fusion.8), channel_id=1, source_target_pairs={{0,2},{1,3},{2,0},{3,1},{4,6},{5,7},{6,4},{7,5},{8,10},{9,11},{10,... | collective-permute-start | bytes 399368 | tf_op jit(solution)/shard_map/ppermute | solution.py:1017
  392.3 8.1 %collective-permute-start.12 = (bf16[520,128]{1,0:T(8,128)(2,1)S(1)}, bf16[520,128]{1,0:T(8,128)(2,1)S(1)}, u32[]{:S(2)}, u32[]{:S(2)}) collective-permute-start(bf16[520,128]{1,0:T(8,128)(2,1)S(1)} %fusion.9), channel_id=1, source_target_pairs={{0,2},{1,3},{2,0},{3,1},{4,6},{5,7},{6,4},{7,5},{8,10},{9,11},{10,... | collective-permute-start | bytes 399368 | tf_op jit(solution)/shard_map/ppermute | solution.py:1017
  395.2 18.4 %collective-permute-start.27 = (bf16[1040,128]{1,0:T(8,128)(2,1)S(1)}, bf16[1040,128]{1,0:T(8,128)(2,1)S(1)}, u32[]{:S(2)}, u32[]{:S(2)}) collective-permute-start(bf16[1040,128]{1,0:T(8,128)(2,1)S(1)} %pad_maximum_fusion.3), channel_id=1, source_target_pairs={{0,1},{1,0},{2,3},{3,2},{4,5},{5,4},{6,7},{7,6},{8,9},{9,8},{10,11... | collective-permute-start | bytes 798728 | tf_op jit(solution)/shard_map/ppermute | solution.py:1017
  400.5 9.6 %all-to-all-start.4 = ((bf16[2,64,512]{2,0,1:T(2,128)(2,1)}), bf16[2,64,512]{2,0,1:T(2,128)(2,1)S(1)}, u32[]{:S(2)}, u32[]{:S(2)}) async-start(bf16[2,64,512]{2,0,1:T(2,128)(2,1)} %copy.52), calls=%async_computation.4 | async-start | bytes 262144 | tf_op jit(solution)/shard_map/all_to_all | solution.py:1068
  403.8 11.7 %collective-permute-start.13 = (bf16[1040,128]{1,0:T(8,128)(2,1)S(1)}, bf16[1040,128]{1,0:T(8,128)(2,1)}, u32[]{:S(2)}, u32[]{:S(2)}) collective-permute-start(bf16[1040,128]{1,0:T(8,128)(2,1)S(1)} %pad_maximum_fusion.2), channel_id=1, source_target_pairs={{0,1},{1,0},{2,3},{3,2},{4,5},{5,4},{6,7},{7,6},{8,9},{9,8},{10,11... | collective-permute-start | bytes 798728 | tf_op jit(solution)/shard_map/ppermute | solution.py:1017
  410.1 27.3 %all-to-all-start.7 = ((bf16[2,64,4096]{2,0,1:T(2,128)(2,1)}), bf16[2,64,4096]{2,0,1:T(2,128)(2,1)S(1)}, u32[]{:S(2)}, u32[]{:S(2)}) async-start(bf16[2,64,4096]{2,0,1:T(2,128)(2,1)} %copy.58), calls=%async_computation.7 | async-start | bytes 2097152 | tf_op jit(solution)/shard_map/all_to_all | solution.py:1068
  413.8 27.5 %collective-permute-start.28 = (bf16[2080,128]{1,0:T(8,128)(2,1)S(1)}, bf16[2080,128]{1,0:T(8,128)(2,1)}, u32[]{:S(2)}, u32[]{:S(2)}) collective-permute-start(bf16[2080,128]{1,0:T(8,128)(2,1)S(1)} %pad_maximum_fusion.1.refs_8_), channel_id=1, source_target_pairs={{0,16},{4,12},{8,24},{12,4},{16,0},{20,28},{24,8},{28,20},{1,17},{... | collective-permute-start | bytes 1597448 | tf_op jit(solution)/shard_map/ppermute | solution.py:968
  415.6 25.9 %collective-permute-start.29 = (bf16[2080,128]{1,0:T(8,128)(2,1)S(1)}, bf16[2080,128]{1,0:T(8,128)(2,1)}, u32[]{:S(2)}, u32[]{:S(2)}) collective-permute-start(bf16[2080,128]{1,0:T(8,128)(2,1)S(1)} %pad_maximum_fusion.1.refs_8_), channel_id=1, source_target_pairs={{0,8},{4,20},{8,0},{12,28},{16,24},{20,4},{24,16},{28,12},{1,9},{5... | collective-permute-start | bytes 1597448 | tf_op jit(solution)/shard_map/ppermute | solution.py:968
  415.6 27.6 %collective-permute-start.31 = (bf16[2080,128]{1,0:T(8,128)(2,1)S(1)}, bf16[2080,128]{1,0:T(8,128)(2,1)}, u32[]{:S(2)}, u32[]{:S(2)}) collective-permute-start(bf16[2080,128]{1,0:T(8,128)(2,1)S(1)} %pad_maximum_fusion.1.refs_8_), channel_id=1, source_target_pairs={{0,4},{4,0},{8,12},{12,8},{16,20},{20,16},{24,28},{28,24},{1,5},{5... | collective-permute-start | bytes 1597448 | tf_op jit(solution)/shard_map/ppermute | solution.py:974
  416.7 46.4 %copy-start.2 = (bf16[2080,128]{1,0:T(8,128)(2,1)}, bf16[2080,128]{1,0:T(8,128)(2,1)S(1)}, u32[]{:S(2)}) copy-start(bf16[2080,128]{1,0:T(8,128)(2,1)S(1)} %pad_maximum_fusion.refs_0_) | copy-start | bytes 1597444
  416.7 46.4 %copy-start.10 = (f32[4,576]{1,0:T(4,128)S(1)}, f32[4,576]{1,0:T(4,128)}, u32[]{:S(2)}) copy-start(f32[4,576]{1,0:T(4,128)} %get-tuple-element.119) | copy-start | bytes 27652
  416.7 46.4 %copy-start.11 = (f32[4,576]{1,0:T(4,128)S(1)}, f32[4,576]{1,0:T(4,128)}, u32[]{:S(2)}) copy-start(f32[4,576]{1,0:T(4,128)} %get-tuple-element.118) | copy-start | bytes 27652
  416.7 26.4 %collective-permute-start.14 = (bf16[2080,128]{1,0:T(8,128)(2,1)S(1)}, bf16[2080,128]{1,0:T(8,128)(2,1)}, u32[]{:S(2)}, u32[]{:S(2)}) collective-permute-start(bf16[2080,128]{1,0:T(8,128)(2,1)S(1)} %pad_maximum_fusion.refs_0_), channel_id=1, source_target_pairs={{0,16},{4,12},{8,24},{12,4},{16,0},{20,28},{24,8},{28,20},{1,17},{... | collective-permute-start | bytes 1597448 | tf_op jit(solution)/shard_map/ppermute | solution.py:968
  437.4 69.1 %all-to-all-start.5 = ((bf16[2,64,4096]{2,0,1:T(2,128)(2,1)}), bf16[2,64,4096]{2,0,1:T(2,128)(2,1)S(1)}, u32[]{:S(2)}, u32[]{:S(2)}) async-start(bf16[2,64,4096]{2,0,1:T(2,128)(2,1)} %copy.54), calls=%async_computation.5 | async-start | bytes 2097152 | tf_op jit(solution)/shard_map/all_to_all | solution.py:1068
  441.0 9.4 %collective-permute-start.15 = (bf16[2080,128]{1,0:T(8,128)(2,1)S(1)}, bf16[2080,128]{1,0:T(8,128)(2,1)}, u32[]{:S(2)}, u32[]{:S(2)}) collective-permute-start(bf16[2080,128]{1,0:T(8,128)(2,1)S(1)} %pad_maximum_fusion.refs_0_), channel_id=1, source_target_pairs={{0,8},{4,20},{8,0},{12,28},{16,24},{20,4},{24,16},{28,12},{1,9},{5... | collective-permute-start | bytes 1597448 | tf_op jit(solution)/shard_map/ppermute | solution.py:968
  441.3 9.1 %collective-permute-start.17 = (bf16[2080,128]{1,0:T(8,128)(2,1)S(1)}, bf16[2080,128]{1,0:T(8,128)(2,1)}, u32[]{:S(2)}, u32[]{:S(2)}) collective-permute-start(bf16[2080,128]{1,0:T(8,128)(2,1)S(1)} %pad_maximum_fusion.refs_0_), channel_id=1, source_target_pairs={{0,4},{4,0},{8,12},{12,8},{16,20},{20,16},{24,28},{28,24},{1,5},{5... | collective-permute-start | bytes 1597448 | tf_op jit(solution)/shard_map/ppermute | solution.py:974
  441.5 14.6 %collective-permute-start.30 = (bf16[2080,128]{1,0:T(8,128)(2,1)}, bf16[2080,128]{1,0:T(8,128)(2,1)}, u32[]{:S(2)}, u32[]{:S(2)}) collective-permute-start(bf16[2080,128]{1,0:T(8,128)(2,1)} %collective-permute-done.28.refs_9_), channel_id=1, source_target_pairs={{0,8},{4,20},{8,0},{12,28},{16,24},{20,4},{24,16},{28,12},{1,9},{5... | collective-permute-start | bytes 1597448 | tf_op jit(solution)/shard_map/ppermute | solution.py:968
  443.1 13.0 %collective-permute-start.32 = (bf16[2080,128]{1,0:T(8,128)(2,1)}, bf16[2080,128]{1,0:T(8,128)(2,1)S(1)}, u32[]{:S(2)}, u32[]{:S(2)}) collective-permute-start(bf16[2080,128]{1,0:T(8,128)(2,1)} %collective-permute-done.28.refs_9_), channel_id=1, source_target_pairs={{0,4},{4,0},{8,12},{12,8},{16,20},{20,16},{24,28},{28,24},{1,5},{5... | collective-permute-start | bytes 1597448 | tf_op jit(solution)/shard_map/ppermute | solution.py:974
  443.1 18.7 %collective-permute-start.16 = (bf16[2080,128]{1,0:T(8,128)(2,1)}, bf16[2080,128]{1,0:T(8,128)(2,1)}, u32[]{:S(2)}, u32[]{:S(2)}) collective-permute-start(bf16[2080,128]{1,0:T(8,128)(2,1)} %collective-permute-done.14.refs_1_), channel_id=1, source_target_pairs={{0,8},{4,20},{8,0},{12,28},{16,24},{20,4},{24,16},{28,12},{1,9},{5... | collective-permute-start | bytes 1597448 | tf_op jit(solution)/shard_map/ppermute | solution.py:968
  450.4 57.7 %collective-permute-start.18 = (bf16[2080,128]{1,0:T(8,128)(2,1)}, bf16[2080,128]{1,0:T(8,128)(2,1)}, u32[]{:S(2)}, u32[]{:S(2)}) collective-permute-start(bf16[2080,128]{1,0:T(8,128)(2,1)} %collective-permute-done.14.refs_1_), channel_id=1, source_target_pairs={{0,4},{4,0},{8,12},{12,8},{16,20},{20,16},{24,28},{28,24},{1,5},{5... | collective-permute-start | bytes 1597448 | tf_op jit(solution)/shard_map/ppermute | solution.py:974
  450.4 57.6 %collective-permute-start.33 = (bf16[2080,128]{1,0:T(8,128)(2,1)}, bf16[2080,128]{1,0:T(8,128)(2,1)}, u32[]{:S(2)}, u32[]{:S(2)}) collective-permute-start(bf16[2080,128]{1,0:T(8,128)(2,1)} %collective-permute-done.29.refs_10_), channel_id=1, source_target_pairs={{0,4},{4,0},{8,12},{12,8},{16,20},{20,16},{24,28},{28,24},{1,5},{5... | collective-permute-start | bytes 1597448 | tf_op jit(solution)/shard_map/ppermute | solution.py:974
  456.1 52.0 %collective-permute-start.19 = (bf16[2080,128]{1,0:T(8,128)(2,1)}, bf16[2080,128]{1,0:T(8,128)(2,1)}, u32[]{:S(2)}, u32[]{:S(2)}) collective-permute-start(bf16[2080,128]{1,0:T(8,128)(2,1)} %collective-permute-done.15.refs_2_), channel_id=1, source_target_pairs={{0,4},{4,0},{8,12},{12,8},{16,20},{20,16},{24,28},{28,24},{1,5},{5... | collective-permute-start | bytes 1597448 | tf_op jit(solution)/shard_map/ppermute | solution.py:974
  456.1 51.9 %copy-start.5 = (bf16[2080,128]{1,0:T(8,128)(2,1)}, bf16[2080,128]{1,0:T(8,128)(2,1)S(1)}, u32[]{:S(2)}) copy-start(bf16[2080,128]{1,0:T(8,128)(2,1)S(1)} %collective-permute-done.32.refs_13_) | copy-start | bytes 1597444
  456.1 52.0 %collective-permute-start.34 = (bf16[2080,128]{1,0:T(8,128)(2,1)}, bf16[2080,128]{1,0:T(8,128)(2,1)}, u32[]{:S(2)}, u32[]{:S(2)}) collective-permute-start(bf16[2080,128]{1,0:T(8,128)(2,1)} %collective-permute-done.30.refs_11_), channel_id=1, source_target_pairs={{0,4},{4,0},{8,12},{12,8},{16,20},{20,16},{24,28},{28,24},{1,5},{5... | collective-permute-start | bytes 1597448 | tf_op jit(solution)/shard_map/ppermute | solution.py:974
  461.8 46.3 %collective-permute-start.20 = (bf16[2080,128]{1,0:T(8,128)(2,1)}, bf16[2080,128]{1,0:T(8,128)(2,1)}, u32[]{:S(2)}, u32[]{:S(2)}) collective-permute-start(bf16[2080,128]{1,0:T(8,128)(2,1)} %collective-permute-done.16.refs_3_), channel_id=1, source_target_pairs={{0,4},{4,0},{8,12},{12,8},{16,20},{20,16},{24,28},{28,24},{1,5},{5... | collective-permute-start | bytes 1597448 | tf_op jit(solution)/shard_map/ppermute | solution.py:974
  (9 other events, 107.1 us)

commit v2 on v1

v2 whole, which is shorter than its diff:
```python
import functools

import jax
import jax.numpy as jnp
from jax import lax
from jax.experimental import pallas as pl
from jax.experimental.pallas import tpu as pltpu
from jax.sharding import PartitionSpec as P

D = 512
H = 32
DE = 64
FF = 1024
FFE = 128
NS = 32
NB = 64
SET_ROWS = 16578
TOTAL_ROWS = 33156
NORM_EPS = 1e-05
BETA_ONE = 0.9
BETA_TWO = 0.95
WEIGHT_DECAY = 0.1
ADAM_EPS = 1e-08
MASK_FILL = -1e30
BF = jnp.bfloat16
F32 = jnp.float32
VMEM_LIMIT = 58 * 1024 * 1024
ROW_QKV, ROW_O, ROW_UP, ROW_DOWN = 0, 6144, 8192, 12288
ROW_BIAS, ROW_GATE, ROW_EDGE, ROW_EUP, ROW_EDOWN = 16384, 16400, 16416, 16432, 16496
ROW_NN, ROW_EN = 16560, 16576
SMALL_USED, SMALL_ROWS = SET_ROWS - ROW_BIAS, 256
BIAS, GATE, EDGE, EUP, EDOWN = 0, 16, 32, 48, 112
NN, EN = ROW_NN - ROW_BIAS, ROW_EN - ROW_BIAS
UPPER_ROWS = ROW_BIAS - ROW_O
GELU_C = 0.7978845608028654


def nn(a, b):
    return lax.dot_general(a, b, (((1,), (0,)), ((), ())), preferred_element_type=F32)


def nt(a, b):
    return lax.dot_general(a, b, (((1,), (1,)), ((), ())), preferred_element_type=F32)


def tn(a, b):
    return lax.dot_general(a, b, (((0,), (0,)), ((), ())), preferred_element_type=F32)


def iota(shape, axis):
    return lax.broadcasted_iota(jnp.int32, shape, axis)


def gelu_parts(u):
    u2 = u * u
    t = jnp.tanh(u * (GELU_C + (GELU_C * 0.044715) * u2))
    half = 0.5 + 0.5 * t
    value = u * half
    slope = half + value * (1.0 - t) * (GELU_C + (3.0 * GELU_C * 0.044715) * u2)
    return value, slope


def gelu_value(u):
    return u * (0.5 + 0.5 * jnp.tanh(u * (GELU_C + (GELU_C * 0.044715) * (u * u))))


def sigmoid(v):
    return 0.5 + 0.5 * jnp.tanh(0.5 * v)


def group_sum(v, first=16):
    while first < 128:
        v = v + pltpu.roll(v, first, 1)
        first *= 2
    return v


def group_max(v):
    for shift in (16, 32, 64):
        v = jnp.maximum(v, pltpu.roll(v, shift, 1))
    return v


def fold8(v):
    return jnp.sum(v.reshape(v.shape[0] // 8, 8, v.shape[1]), axis=0)


class Bucket:
    def __init__(self, graphs, slots, node0, edge0, count0):
        self.graphs, self.slots = graphs, slots
        self.node0, self.edge0, self.count0 = node0, edge0, count0
        self.rows = graphs * slots
        self.chunks = slots // 4
        self.pairs = slots // 8
        self.blocks = slots // 16
        self.edges = self.rows * self.chunks
        self.edge_lanes = slots * DE


class Dims:
    def __init__(self, small_graphs, big_graphs, parts):
        self.lower = round_up(ROW_O + SMALL_ROWS, 16 * parts)
        self.small = Bucket(small_graphs, NS, 0, 0, 0)
        self.big = Bucket(big_graphs, NB, self.small.rows, self.small.edges, small_graphs)
        self.buckets = (self.small, self.big)
        self.nodes = self.small.rows + self.big.rows
        self.edges = self.small.edges + self.big.edges
        self.scores = self.edges // 2
        self.blocks = sum(b.graphs * b.blocks for b in self.buckets)

    def each_pair(self, body):
        for bucket in self.buckets:
            two = 2 * bucket.rows

            @pl.loop(0, bucket.pairs, unroll=4)
            def _(i, bucket=bucket, two=two):
                body(
                    pl.ds(aligned(bucket.edge0 + i * two, 32), two),
                    pl.ds(aligned(bucket.edge0 // 2 + i * bucket.rows, 16), bucket.rows),
                )


def beside(v):
    half = v.shape[0] // 2
    return jnp.concatenate([v[:half], v[half:]], axis=1)


def below(v):
    return jnp.concatenate([v[:, :256], v[:, 256:]], axis=0)


def make_masks(scr):
    make_mean(scr)
    make_heads(scr)


def make_mean(scr):
    shape = (256, 256)
    same = (iota(shape, 0) >> 6) == (iota(shape, 1) >> 6)
    scr.mean[...] = jnp.where(same, 1.0 / DE, 0.0).astype(BF)


def make_heads(scr):
    shape = (256, 256)
    scr.head[...] = jnp.where((iota(shape, 0) >> 4) == (iota(shape, 1) & 15), 1.0, 0.0).astype(BF)
    shape = (16, 256)
    scr.pick[...] = jnp.where(iota(shape, 0) == (iota(shape, 1) >> 4), 1.0, 0.0).astype(BF)


def node_norm(v):
    centred = v - jnp.mean(v, axis=1, keepdims=True)
    r = lax.rsqrt(jnp.mean(centred * centred, axis=1, keepdims=True) + NORM_EPS)
    return centred * r, r


def node_norm_back(gdy, n, r):
    return r * (gdy - jnp.mean(gdy, axis=1, keepdims=True) - n * jnp.mean(gdy * n, axis=1, keepdims=True))


def aligned(value, by):
    return pl.multiple_of(value, by)


def block_of(bucket, t):
    g = t // bucket.blocks
    b = t % bucket.blocks
    rows = pl.ds(aligned(bucket.node0 + g * bucket.slots, 16), bucket.slots)
    keys = pl.ds(aligned(bucket.node0 + t * 16, 16), 16)
    pair_rows = [
        pl.ds(
            aligned(bucket.edge0 // 2 + (2 * b + c) * bucket.rows + g * bucket.slots, 16),
            bucket.slots,
        )
        for c in range(2)
    ]
    return rows, keys, pair_rows


def side(first, half):
    return slice(first + 256 * half, first + 256 * (half + 1))


def lanes(half):
    return slice(128 * half, 128 * (half + 1))


def expand(values, scr):
    return tn(values, scr.pick[...]).astype(BF) * scr.head[...]


def joined(ref, pair_rows, half):
    return jnp.concatenate([ref[r, lanes(half)] for r in pair_rows], axis=1)


def forward(dm, counts, w, io, res, scr):
    x = io.nodes[...].astype(F32)
    n, r = node_norm(x)
    res.node_n1[...] = n.astype(BF)
    res.node_r1[...] = jnp.broadcast_to(r, (dm.nodes, 128))
    hn = (n * w.nn[0:1, :] + w.nn[1:2, :]).astype(BF)
    res.qkv[...] = nn(hn, w.qkv[...]).astype(BF)

    @dm.each_pair
    def _(rows, pair):
        x = io.edges[rows, :]
        centred = x.astype(F32) - nn(x, scr.mean[...])
        r = lax.rsqrt(nn((centred * centred).astype(BF), scr.mean[...]) + NORM_EPS)
        n = centred * r
        res.edge_n1[rows, :] = n.astype(BF)
        res.edge_r1[rows, :] = r.astype(BF)
        xn = (n * w.en[0:1, :] + w.en[1:2, :]).astype(BF)
        both = nn(beside(xn), w.eg[...])
        scr.scores[pair, :] = both[:, :256]
        res.gate[pair, :] = both[:, 256:]

    t0 = 0
    for bucket in dm.buckets:
        @pl.loop(0, bucket.graphs * bucket.blocks, unroll=True)
        def _(t, bucket=bucket, t0=t0):
            rows, keys, pair_rows = block_of(bucket, t)
            for half in range(2):
                kb = expand(res.qkv[keys, side(512, half)], scr)
                scr.vbig[t0 + t, half] = expand(res.qkv[keys, side(1024, half)], scr)
                s = nn(res.qkv[rows, side(0, half)], kb) * 0.25
                for c in range(2):
                    scr.scores[pair_rows[c], lanes(half)] += s[:, lanes(c)]

        @pl.loop(0, bucket.rows // 32, unroll=True)
        def _(i, bucket=bucket):
            count = counts[bucket.count0 + i * 32 // bucket.slots]
            lane_key = iota((32, 128), 1) >> 4
            row = [
                pl.ds(aligned(bucket.edge0 // 2 + c * bucket.rows + i * 32, 32), 32)
                for c in range(bucket.pairs)
            ]
            for half in range(2):
                at = lanes(half)
                top = jnp.full((32, 128), MASK_FILL, F32)
                for c in range(bucket.pairs):
                    s = scr.scores[row[c], at]
                    res.low[row[c], at] = s.astype(BF)
                    top = jnp.maximum(top, jnp.where(lane_key < count - 8 * c, s, MASK_FILL))
                top = group_max(top)
                sums = jnp.zeros((32, 128), F32)
                for c in range(bucket.pairs):
                    s = jnp.where(lane_key < count - 8 * c, scr.scores[row[c], at], MASK_FILL)
                    e = jnp.exp(s - top)
                    sums = sums + e
                    scr.scores[row[c], at] = e
                inv = 1.0 / group_sum(sums)
                for c in range(bucket.pairs):
                    p = scr.scores[row[c], at] * inv
                    res.prob[row[c], at] = p.astype(BF)
                    scr.attn[row[c], at] = (p * sigmoid(res.gate[row[c], at])).astype(BF)

        @pl.loop(0, bucket.graphs, unroll=True)
        def _(g, bucket=bucket, t0=t0):
            for half in range(2):
                sums = None
                for b in range(bucket.blocks):
                    t = g * bucket.blocks + b
                    rows, _, pair_rows = block_of(bucket, t)
                    part = nt(joined(scr.attn, pair_rows, half), scr.vbig[t0 + t, half])
                    sums = part if sums is None else sums + part
                res.mixed[rows, side(0, half)] = sums.astype(BF)

        t0 += bucket.graphs * bucket.blocks

    y = io.nodes[...].astype(F32) + nn(res.mixed[...], w.o[...])
    n, r = node_norm(y)
    res.node_n2[...] = n.astype(BF)
    res.node_r2[...] = jnp.broadcast_to(r, (dm.nodes, 128))
    z = (n * w.nn[2:3, :] + w.nn[3:4, :]).astype(BF)
    u = nn(z, w.up[...])
    res.node_u[...] = u
    io.nodes_out[...] = (y + nn(gelu_value(u).astype(BF), w.down[...])).astype(BF)

    @dm.each_pair
    def _(rows, pair):
        m = io.edges[rows, :].astype(F32) + below(nn(res.low[pair, :], w.x[...]))
        high = m.astype(BF)
        rest = (m - high.astype(F32)).astype(BF)
        centred = m - nn(high, scr.mean[...]) - nn(rest, scr.mean[...])
        r = lax.rsqrt(nn((centred * centred).astype(BF), scr.mean[...]) + NORM_EPS)
        n = centred * r
        res.edge_n2[rows, :] = n.astype(BF)
        res.edge_r2[rows, :] = r.astype(BF)
        mn = (n * w.en[2:3, :] + w.en[3:4, :]).astype(BF)
        ua = nn(mn, w.a[...])
        io.edges_out[rows, :] = (m + nn(gelu_value(ua).astype(BF), w.b[...])).astype(BF)


def put_strided(flat, first, value, parts):
    for q in range(parts):
        flat[pl.ds(first + q, value.shape[0], stride=parts), :] = value[:, 128 * q : 128 * (q + 1)]


def back_ffn(dm, w, io, res, scr):
    flat = scr.upper
    gy = io.nodes_cot[...]
    act, slope = gelu_parts(res.node_u[...])
    du = (nt(gy, w.down[...]) * slope).astype(BF)
    put_strided(flat, ROW_DOWN - ROW_O, tn(act.astype(BF), gy), 4)
    n = res.node_n2[...].astype(F32)
    z = (n * w.nn[2:3, :] + w.nn[3:4, :]).astype(BF)
    put_strided(flat, ROW_UP - ROW_O, tn(z, du), 8)
    dz = nt(du, w.up[...])
    gain = jnp.sum(dz * n, axis=0, keepdims=True)
    bias = jnp.sum(dz, axis=0, keepdims=True)
    dy = gy.astype(F32) + node_norm_back(dz * w.nn[2:3, :], n, res.node_r2[:, 0:1])
    io.dy[...] = dy
    dyl = dy.astype(BF)
    put_strided(flat, 0, tn(res.mixed[...], dyl), 4)
    io.do[...] = nt(dyl, w.o[...]).astype(BF)
    for q in range(4):
        io.sums[q : q + 1, :] = gain[:, 128 * q : 128 * (q + 1)]
        io.sums[4 + q : 5 + q, :] = bias[:, 128 * q : 128 * (q + 1)]
    if hasattr(io, "upper"):
        io.upper[...] = flat[...].astype(BF)
    else:
        put_halves(flat, io.keep, io.send)


def put_halves(flat, keep, send):
    half = keep.shape[0]
    core = lax.axis_index("dp") & 1
    keep[...] = flat[pl.ds(aligned(core * half, 16), half), :].astype(BF)
    send[...] = flat[pl.ds(aligned((1 - core) * half, 16), half), :].astype(BF)


def back_edges(dm, w, io, res, scr):
    io.small[NN + 8 : NN + 16, :] = io.sums[...]
    scr.gb[...] = jnp.zeros((512, 256), F32)
    scr.ga[...] = jnp.zeros((256, 512), F32)
    scr.gx[...] = jnp.zeros((256, 512), F32)
    scr.en[...] = jnp.zeros((2, 8, 256), F32)

    @dm.each_pair
    def _(rows, pair):
        gx = io.edges_cot[rows, :]
        n = res.edge_n2[rows, :].astype(F32)
        mn = (n * w.en[2:3, :] + w.en[3:4, :]).astype(BF)
        act, slope = gelu_parts(nn(mn, w.a[...]))
        dua = (nt(gx, w.b[...]) * slope).astype(BF)
        scr.gb[...] += tn(act.astype(BF), gx)
        scr.ga[...] += tn(mn, dua)
        dmn = nt(dua, w.a[...])
        scr.en[0] += fold8(dmn * n)
        scr.en[1] += fold8(dmn)
        gdy = dmn * w.en[2:3, :]
        m1 = nn(gdy.astype(BF), scr.mean[...])
        m2 = nn((gdy * n).astype(BF), scr.mean[...])
        dmid = gx.astype(F32) + res.edge_r2[rows, :].astype(F32) * (gdy - m1 - n * m2)
        dml = dmid.astype(BF)
        io.dmid[rows, :] = dml
        dml = beside(dml)
        scr.gx[...] += tn(res.low[pair, :], dml)
        io.scores[pair, :] = nt(dml, w.x[...])

    up = scr.ga[0:64, 0:128]
    for k in range(1, 4):
        up = up + scr.ga[64 * k : 64 * (k + 1), 128 * k : 128 * (k + 1)]
    io.small[EUP : EUP + 64, :] = up
    sums = jnp.zeros((128, 128), F32)
    for k in range(4):
        part = scr.gb[128 * k : 128 * (k + 1), 128 * (k // 2) : 128 * (k // 2 + 1)]
        sums = sums + jnp.where(lane_group(128, 6) == k % 2, part, 0.0)
    fold_halves(sums, scr.tmp, io.small, EDOWN)
    sides = []
    for half in range(2):
        sums = jnp.zeros((16, 128), F32)
        for k in range(8):
            at = 128 * half + 16 * k
            part = scr.gx[at : at + 16, 128 * (k // 2) : 128 * (k // 2 + 1)]
            sums = sums + jnp.where(lane_group(16, 6) == k % 2, part, 0.0)
        sides.append(sums)
    fold_halves(jnp.concatenate(sides), scr.tmp, io.small, EDGE)
    put_edge_norm(scr.en, io.small, EN + 1)
    io.small[SMALL_USED:, :] = jnp.zeros((SMALL_ROWS - SMALL_USED, 128), F32)


def back_attention(dm, io, res, scr):
    t0 = 0
    for bucket in dm.buckets:
        @pl.loop(0, bucket.graphs * bucket.blocks, unroll=True)
        def _(t, bucket=bucket, t0=t0):
            rows, keys, pair_rows = block_of(bucket, t)
            for half in range(2):
                scr.vbig[t0 + t, half] = expand(res.qkv[keys, side(512, half)], scr)
                vb = expand(res.qkv[keys, side(1024, half)], scr)
                da = nn(io.do[rows, side(0, half)], vb)
                for c in range(2):
                    scr.da[pair_rows[c], lanes(half)] = da[:, lanes(c)]

        @pl.loop(0, bucket.rows // 32, unroll=True)
        def _(i, bucket=bucket):
            row = [
                pl.ds(aligned(bucket.edge0 // 2 + c * bucket.rows + i * 32, 32), 32)
                for c in range(bucket.pairs)
            ]
            for half in range(2):
                at = lanes(half)
                sums = jnp.zeros((32, 128), F32)
                for c in range(bucket.pairs):
                    p = res.prob[row[c], at].astype(F32)
                    s = sigmoid(res.gate[row[c], at])
                    scr.attn[row[c], at] = (p * s).astype(BF)
                    pt = p * scr.da[row[c], at] * s
                    scr.da[row[c], at] = pt
                    sums = sums + pt
                    io.dsg[row[c], lanes(2 + half)] = (pt * (1.0 - s)).astype(BF)
                sums = group_sum(sums)
                for c in range(bucket.pairs):
                    p = res.prob[row[c], at].astype(F32)
                    ds = scr.da[row[c], at] - p * sums + io.scores[row[c], at]
                    io.dsg[row[c], at] = ds.astype(BF)

        @pl.loop(0, bucket.graphs, unroll=True)
        def _(g, bucket=bucket, t0=t0):
            for half in range(2):
                sums = None
                for b in range(bucket.blocks):
                    t = g * bucket.blocks + b
                    rows, keys, pair_rows = block_of(bucket, t)
                    ds = joined(io.dsg, pair_rows, half)
                    part = nt(ds, scr.vbig[t0 + t, half])
                    sums = part if sums is None else sums + part
                    gk = tn(res.qkv[rows, side(0, half)], ds).astype(BF) * scr.head[...]
                    io.dqkv[keys, side(512, half)] = (nt(scr.pick[...], gk) * 0.25).astype(BF)
                    gv = tn(io.do[rows, side(0, half)], joined(scr.attn, pair_rows, half))
                    gv = gv.astype(BF) * scr.head[...]
                    io.dqkv[keys, side(1024, half)] = nt(scr.pick[...], gv).astype(BF)
                io.dqkv[rows, side(0, half)] = (sums * 0.25).astype(BF)

        t0 += bucket.graphs * bucket.blocks


def back_last(dm, w, io, res, scr):
    flat = scr.lower
    n = res.node_n1[...].astype(F32)
    hn = (n * w.nn[0:1, :] + w.nn[1:2, :]).astype(BF)
    for m in range(3):
        put_strided(flat, 2048 * m, tn(hn, io.dqkv[:, 512 * m : 512 * (m + 1)]), 4)
    dhn = nt(io.dqkv[...], w.qkv[...])
    gain = jnp.sum(dhn * n, axis=0, keepdims=True)
    bias = jnp.sum(dhn, axis=0, keepdims=True)
    small = flat.at[pl.ds(ROW_O, SMALL_ROWS), :]
    small[...] = io.small[...]
    for q in range(4):
        small[NN + q : NN + 1 + q, :] = gain[:, 128 * q : 128 * (q + 1)]
        small[NN + 4 + q : NN + 5 + q, :] = bias[:, 128 * q : 128 * (q + 1)]
    dx = io.dy[...] + node_norm_back(dhn * w.nn[0:1, :], n, res.node_r1[:, 0:1])
    io.nodes_grad[...] = dx.astype(BF)

    scr.geg[...] = jnp.zeros((512, 512), F32)
    scr.en[...] = jnp.zeros((2, 8, 256), F32)

    @dm.each_pair
    def _(rows, pair):
        dsg = io.dsg[pair, :]
        n = res.edge_n1[rows, :].astype(F32)
        xn = (n * w.en[0:1, :] + w.en[1:2, :]).astype(BF)
        scr.geg[...] += tn(beside(xn), dsg)
        dxn = below(nt(dsg, w.eg[...]))
        scr.en[0] += fold8(dxn * n)
        scr.en[1] += fold8(dxn)
        gdy = dxn * w.en[0:1, :]
        m1 = nn(gdy.astype(BF), scr.mean[...])
        m2 = nn((gdy * n).astype(BF), scr.mean[...])
        dx = io.dmid[rows, :].astype(F32) + res.edge_r1[rows, :].astype(F32) * (gdy - m1 - n * m2)
        io.edges_grad[rows, :] = dx.astype(BF)

    for which, first in ((0, BIAS), (1, GATE)):
        sides = []
        for half in range(2):
            sums = jnp.zeros((64, 128), F32)
            for k in range(8):
                part = scr.geg[64 * k : 64 * (k + 1), lanes(2 * which + half)]
                sums = sums + jnp.where(lane_group(64, 4) == k, part, 0.0)
            sides.append(group_sum(sums))
        scr.tmp[0:64, :] = jnp.where(lane_group(64, 4) % 2 == 0, sides[0], sides[1])
        rows = jnp.zeros((16, 128), F32)
        for b in range(4):
            rows = jnp.where(lane_group(16, 5) == b, scr.tmp[pl.ds(b, 16, stride=4), :], rows)
        small[first : first + 16, :] = rows
    put_edge_norm(scr.en, small, EN)
    end = ROW_O + SMALL_ROWS
    if dm.lower > end:
        flat[end:, :] = jnp.zeros((dm.lower - end, 128), F32)
    put_halves(flat, io.keep, io.send)


def lane_group(rows, bits):
    return iota((rows, 128), 1) >> bits


def fold_halves(sums, tmp, out, first):
    rows, half = sums.shape[0], sums.shape[0] // 2
    tmp[0:rows, :] = sums + pltpu.roll(sums, 64, 1)
    even = tmp[pl.ds(0, half, stride=2), :]
    odd = tmp[pl.ds(1, half, stride=2), :]
    out[first : first + half, :] = jnp.where(lane_group(half, 6) == 0, even, odd)


def put_edge_norm(sums, out, at):
    ones = []
    for t in range(2):
        both = jnp.sum(sums[t], axis=0, keepdims=True)
        one = both[:, :128] + both[:, 128:]
        ones.append(one + pltpu.roll(one, 64, 1))
    out[at : at + 1, :] = jnp.where(lane_group(1, 6) == 0, ones[0], ones[1])


def assemble_set(off, flat, tmp, w):
    def strided(first, rows, parts, out, lane0=0):
        for q in range(parts):
            out[:, lane0 + 128 * q : lane0 + 128 * (q + 1)] = flat[
                pl.ds(off + first + q, rows, stride=parts), :
            ].astype(BF)

    for m in range(3):
        strided(ROW_QKV + 2048 * m, 512, 4, w.qkv, 512 * m)
    strided(ROW_O, 512, 4, w.o)
    strided(ROW_UP, 512, 8, w.up)
    strided(ROW_DOWN, 1024, 4, w.down)
    w.eg[...] = jnp.zeros((512, 512), BF)
    w.x[...] = jnp.zeros((256, 512), BF)
    w.a[...] = jnp.zeros((256, 512), BF)
    w.b[...] = jnp.zeros((512, 256), BF)
    up = flat[pl.ds(off + ROW_EUP, 64), :].astype(BF)
    for k in range(4):
        w.a[64 * k : 64 * (k + 1), 128 * k : 128 * (k + 1)] = up

    def doubled(first, in_rows):
        v = flat[pl.ds(off + first, in_rows), :]
        other = pltpu.roll(v, 64, 1)
        low = lane_group(in_rows, 6) == 0
        tmp[pl.ds(0, in_rows, stride=2), :] = jnp.where(low, v, other)
        tmp[pl.ds(1, in_rows, stride=2), :] = jnp.where(low, other, v)
        return tmp[0 : 2 * in_rows, :]

    both = doubled(ROW_EDOWN, 64)
    for k in range(4):
        w.b[128 * k : 128 * (k + 1), 128 * (k // 2) : 128 * (k // 2 + 1)] = jnp.where(
            lane_group(128, 6) == k % 2, both, 0.0
        ).astype(BF)
    both = doubled(ROW_EDGE, 16)
    for half in range(2):
        for k in range(8):
            at = 128 * half + 16 * k
            w.x[at : at + 16, 128 * (k // 2) : 128 * (k // 2 + 1)] = jnp.where(
                lane_group(16, 6) == k % 2, both[16 * half : 16 * (half + 1)], 0.0
            ).astype(BF)
    for which, first in ((0, ROW_BIAS), (1, ROW_GATE)):
        v = flat[pl.ds(off + first, 16), :]
        for b in range(4):
            tmp[pl.ds(b, 16, stride=4), :] = group_sum(jnp.where(lane_group(16, 5) == b, v, 0.0), 32)
        both = tmp[0:64, :]
        even = lane_group(64, 4) % 2 == 0
        sides = (
            jnp.where(even, both, pltpu.roll(both, 16, 1)),
            jnp.where(even, pltpu.roll(both, 112, 1), both),
        )
        for half in range(2):
            for k in range(8):
                w.eg[64 * k : 64 * (k + 1), lanes(2 * which + half)] = jnp.where(
                    lane_group(64, 4) == k, sides[half], 0.0
                ).astype(BF)
    for t in range(4):
        for q in range(4):
            w.nn[t : t + 1, 128 * q : 128 * (q + 1)] = flat[pl.ds(off + ROW_NN + 4 * t + q, 1), :]
    for t in range(2):
        v = flat[pl.ds(off + ROW_EN + t, 1), :]
        other = pltpu.roll(v, 64, 1)
        gain = jnp.where(lane_group(1, 6) == 0, v, other)
        bias = jnp.where(lane_group(1, 6) == 0, other, v)
        for half in range(2):
            w.en[2 * t : 2 * t + 1, 128 * half : 128 * (half + 1)] = gain
            w.en[2 * t + 1 : 2 * t + 2, 128 * half : 128 * (half + 1)] = bias


class Group:
    def __init__(self, names, refs):
        for name, ref in zip(names, refs):
            setattr(self, name, ref)


WEIGHTS = {
    "qkv": ((D, 3 * D), BF),
    "o": ((D, D), BF),
    "up": ((D, FF), BF),
    "down": ((FF, D), BF),
    "eg": ((512, 512), BF),
    "x": ((256, 512), BF),
    "a": ((256, 512), BF),
    "b": ((512, 256), BF),
    "nn": ((4, D), F32),
    "en": ((4, 256), F32),
}


def residual_shapes(dm):
    return {
        "node_n1": ((dm.nodes, D), BF),
        "node_r1": ((dm.nodes, 128), F32),
        "qkv": ((dm.nodes, 3 * D), BF),
        "mixed": ((dm.nodes, D), BF),
        "node_n2": ((dm.nodes, D), BF),
        "node_r2": ((dm.nodes, 128), F32),
        "node_u": ((dm.nodes, FF), F32),
        "edge_n1": ((dm.edges, 256), BF),
        "edge_r1": ((dm.edges, 256), BF),
        "gate": ((dm.scores, 256), F32),
        "low": ((dm.scores, 256), BF),
        "prob": ((dm.scores, 256), BF),
        "edge_n2": ((dm.edges, 256), BF),
        "edge_r2": ((dm.edges, 256), BF),
    }


def mean_shapes():
    return {"mean": ((256, 256), BF)}


def head_shapes():
    return {"head": ((256, 256), BF), "pick": ((16, 256), BF)}


def mask_shapes():
    return {**mean_shapes(), **head_shapes()}


def forward_scratch(dm):
    return {
        "scores": ((dm.scores, 256), F32),
        "attn": ((dm.scores, 256), BF),
        "vbig": ((dm.blocks, 2, 256, 256), BF),
    }


def ffn_shapes(dm, halves):
    half = ((UPPER_ROWS // 2, 128), BF)
    grads = {"keep": half, "send": half} if halves else {"upper": ((UPPER_ROWS, 128), BF)}
    return {
        "dy": ((dm.nodes, D), F32),
        "do": ((dm.nodes, D), BF),
        "sums": ((8, 128), F32),
        **grads,
    }


def edge_shapes(dm):
    return {
        "dmid": ((dm.edges, 256), BF),
        "scores": ((dm.scores, 256), F32),
        "small": ((SMALL_ROWS, 128), F32),
    }


def attention_shapes(dm):
    return {"dsg": ((dm.scores, 512), BF), "dqkv": ((dm.nodes, 3 * D), BF)}


def ffn_scratch():
    return {"upper": ((UPPER_ROWS, 128), F32)}


def edge_scratch():
    return {
        "gb": ((512, 256), F32),
        "ga": ((256, 512), F32),
        "gx": ((256, 512), F32),
        "en": ((2, 8, 256), F32),
        "tmp": ((128, 128), F32),
    }


def attention_scratch(dm):
    return {
        "attn": ((dm.scores, 256), BF),
        "vbig": ((dm.blocks, 2, 256, 256), BF),
        "da": ((dm.scores, 256), F32),
    }


def last_scratch(dm):
    return {
        "geg": ((512, 512), F32),
        "en": ((2, 8, 256), F32),
        "tmp": ((128, 128), F32),
        "lower": ((dm.lower, 128), F32),
    }


def structs(shapes):
    return [jax.ShapeDtypeStruct(s, t) for s, t in shapes.values()]


def vmem(shapes):
    return [pltpu.VMEM(s, t) for s, t in shapes.values()]


def whole(n):
    return [pl.BlockSpec(memory_space=pltpu.VMEM)] * n


def split(refs, *groups):
    out, at = [], 0
    for names in groups:
        out.append(Group(names, refs[at : at + len(names)]))
        at += len(names)
    assert at == len(refs)
    return out


def edge_copies(dm, small, big, big_lane, stacked, sems, out):
    copies = []
    for bucket, ref, lane in ((dm.small, small, 0), (dm.big, big, big_lane)):
        for c in range(bucket.chunks):
            a = ref.at[:, pl.ds(lane + 256 * c, 256)]
            b = stacked.at[pl.ds(bucket.edge0 + c * bucket.rows, bucket.rows), :]
            src, dst = (b, a) if out else (a, b)
            copies.append(pltpu.make_async_copy(src, dst, sems.at[len(copies)]))
    return copies


def node_copies(dm, small, big, big_lane, nodes, sems, at, out):
    copies = []
    for bucket, ref in ((dm.small, small), (dm.big, big.at[:, pl.ds(big_lane, D)])):
        b = nodes.at[pl.ds(bucket.node0, bucket.rows), :]
        src, dst = (b, ref) if out else (ref, b)
        copies.append(pltpu.make_async_copy(src, dst, sems.at[at + len(copies)]))
    return copies


def copy_sems(dm):
    return pltpu.SemaphoreType.DMA((dm.small.chunks + dm.big.chunks + 2,))


def all_copies(dm, small_nodes, small_edges, big, edge_lane, node_lane, nodes, edges, sems, out):
    copies = edge_copies(dm, small_edges, big, edge_lane, edges, sems, out)
    return node_copies(dm, small_nodes, big, node_lane, nodes, sems, len(copies), out) + copies


def start(copies):
    for c in copies:
        c.start()


def wait(copies):
    for c in copies:
        c.wait()


HBM = pl.BlockSpec(memory_space=pl.ANY)
SMEM = pl.BlockSpec(memory_space=pltpu.SMEM)
EDGE_LANES = NB * DE
IN_LANES = 2 * EDGE_LANES + 2 * D
OUT_LANES = EDGE_LANES + D


def compiler_params():
    return pltpu.CompilerParams(vmem_limit_bytes=VMEM_LIMIT)


def cost(us):
    return pl.CostEstimate(flops=0, bytes_accessed=int(us * 3.4e6), transcendentals=0)


def take(group, names):
    return [getattr(group, k) for k in names]


NODE_BACK = ("node_n2", "node_r2", "node_u", "mixed")
EDGE_BACK = ("edge_n2", "edge_r2", "low")
ATTENTION_BACK = ("qkv", "prob", "gate")
LAST_BACK = ("node_n1", "node_r1", "edge_n1", "edge_r1")
W_NODE = ("o", "up", "down", "nn")
W_EDGE = ("x", "a", "b", "en")
W_LAST = ("qkv", "eg", "nn", "en")


def kernel(body, inputs, out, scr, us, counts=None, hbm_in=0, hbm_out=(), sems=()):
    smem = [] if counts is None else [counts]
    return Group(
        out,
        pl.pallas_call(
            body,
            out_shape=structs(out),
            in_specs=[SMEM] * len(smem) + whole(len(inputs) - hbm_in) + [HBM] * hbm_in,
            out_specs=[HBM if k in hbm_out else pl.BlockSpec(memory_space=pltpu.VMEM) for k in out],
            scratch_shapes=vmem(scr) + list(sems),
            compiler_params=compiler_params(),
            cost_estimate=cost(us),
        )(*smem, *inputs),
    )


def first_forward(dm, counts, weights, small_nodes, small_edges, big):
    res = residual_shapes(dm)
    out = {"nodes_out": ((dm.nodes, D), BF), "edges_out": ((dm.edges, 256), BF), **res}
    scr = {
        **mask_shapes(),
        **forward_scratch(dm),
        "nodes": ((dm.nodes, D), BF),
        "edges": ((dm.edges, 256), BF),
    }

    def body(*refs):
        counts_ref, refs, sems = refs[0], refs[1:-1], refs[-1]
        w, src, dst, s = split(refs, WEIGHTS, ("sn", "se", "big"), out, scr)
        copies = all_copies(
            dm, src.sn, src.se, src.big, 0, 2 * EDGE_LANES, s.nodes, s.edges, sems, False
        )
        start(copies)
        make_masks(s)
        io = Group(
            ("nodes", "edges", "nodes_out", "edges_out"),
            (s.nodes, s.edges, dst.nodes_out, dst.edges_out),
        )
        wait(copies)
        forward(dm, counts_ref, w, io, dst, s)

    inputs = take(weights, WEIGHTS) + [small_nodes, small_edges, big]
    got = kernel(body, inputs, out, scr, 38, counts, 3, (), [copy_sems(dm)])
    return got.nodes_out, got.edges_out, got


def second_forward(dm, counts, weights, nodes, edges, small_node_cot, small_edge_cot, big):
    res, ffn = residual_shapes(dm), ffn_shapes(dm, False)
    whole_outs = {
        "sno": ((dm.small.rows, D), BF),
        "seo": ((dm.small.rows, dm.small.edge_lanes), BF),
        "bout": ((dm.big.rows, OUT_LANES), BF),
    }
    node_res = [k for k in res if k in NODE_BACK]
    kept = {k: v for k, v in res.items() if k not in NODE_BACK}
    out = {**whole_outs, "edge_cot": ((dm.edges, 256), BF), **kept, **ffn}
    scr = {
        **mask_shapes(),
        **forward_scratch(dm),
        **ffn_scratch(),
        **{k: res[k] for k in node_res},
        "nodes_out": ((dm.nodes, D), BF),
        "edges_out": ((dm.edges, 256), BF),
        "node_cot": ((dm.nodes, D), BF),
    }

    def body(*refs):
        counts_ref, refs, in_sems, out_sems = refs[0], refs[1:-2], refs[-2], refs[-1]
        w, src, dst, s = split(refs, WEIGHTS, ("nodes", "edges", "snc", "sec", "big"), out, scr)
        copies = all_copies(
            dm, src.snc, src.sec, src.big, EDGE_LANES, 2 * EDGE_LANES + D, s.node_cot, dst.edge_cot, in_sems, False
        )
        start(copies)
        make_masks(s)
        every = Group(
            [*kept, *node_res], [getattr(dst, k) for k in kept] + [getattr(s, k) for k in node_res]
        )
        io = Group(
            ("nodes", "edges", "nodes_out", "edges_out"),
            (src.nodes, src.edges, s.nodes_out, s.edges_out),
        )
        forward(dm, counts_ref, w, io, every, s)
        outgoing = all_copies(
            dm, dst.sno, dst.seo, dst.bout, 0, EDGE_LANES, s.nodes_out, s.edges_out, out_sems, True
        )
        start(outgoing)
        wait(copies)
        back_ffn(dm, w, Group(("nodes_cot", *ffn), (s.node_cot, *take(dst, ffn))), every, s)
        wait(outgoing)

    inputs = take(weights, WEIGHTS) + [nodes, edges, small_node_cot, small_edge_cot, big]
    got = kernel(body, inputs, out, scr, 46, counts, 3, tuple(whole_outs), [copy_sems(dm)] * 2)
    return got.sno, got.seo, got.bout, None, got.edge_cot, got, got


def between(dm, weights_two, weights_one, kept_two, kept_one, ffn_two, edges_cot):
    half = {k: ((dm.lower // 2, 128), BF) for k in ("keep", "send")}
    ffn = ffn_shapes(dm, True)
    out = {
        "edges_grad": ((dm.edges, 256), BF),
        **{"two_" + k: v for k, v in half.items()},
        **ffn,
    }
    edge, att = edge_shapes(dm), attention_shapes(dm)
    scr = {
        **mask_shapes(),
        **edge_scratch(),
        **attention_scratch(dm),
        **last_scratch(dm),
        **ffn_scratch(),
        **edge,
        **att,
        "nodes_grad": ((dm.nodes, D), BF),
    }
    w_two = ("qkv", *W_EDGE, "eg", "nn")
    res_two = EDGE_BACK + ATTENTION_BACK + LAST_BACK

    def body(*refs):
        w, w_one, res, res_one, src, dst, s = split(
            refs, w_two, W_NODE, res_two, NODE_BACK, ("edges_cot", "sums", "do", "dy"), out, scr
        )
        make_masks(s)
        io = Group(
            ("edges_cot", "sums", "do", "dy", *edge, *att, "nodes_grad", "edges_grad", "keep", "send"),
            (src.edges_cot, src.sums, src.do, src.dy, *take(s, edge), *take(s, att))
            + (s.nodes_grad, dst.edges_grad, dst.two_keep, dst.two_send),
        )
        back_edges(dm, w, io, res, s)
        back_attention(dm, io, res, s)
        back_last(dm, w, io, res, s)
        back_ffn(dm, w_one, Group(("nodes_cot", *ffn), (s.nodes_grad, *take(dst, ffn))), res_one, s)

    inputs = take(weights_two, w_two) + take(weights_one, W_NODE)
    inputs += take(kept_two, res_two) + take(kept_one, NODE_BACK)
    inputs += [edges_cot, ffn_two.sums, ffn_two.do, ffn_two.dy]
    return kernel(body, inputs, out, scr, 45)


def call_edges(dm, weights, kept, ffn, edges_cot):
    out, scr = edge_shapes(dm), {**mean_shapes(), **edge_scratch()}

    def body(*refs):
        w, res, src, dst, s = split(refs, W_EDGE, EDGE_BACK, ("edges_cot", "sums"), out, scr)
        make_mean(s)
        io = Group(("edges_cot", "sums", *out), (src.edges_cot, src.sums, *take(dst, out)))
        back_edges(dm, w, io, res, s)

    inputs = take(weights, W_EDGE) + take(kept, EDGE_BACK) + [edges_cot, ffn.sums]
    return kernel(body, inputs, out, scr, 16)


def call_attention(dm, kept, ffn, edge):
    out, scr = attention_shapes(dm), {**head_shapes(), **attention_scratch(dm)}

    def body(*refs):
        res, src, dst, s = split(refs, ATTENTION_BACK, ("do", "scores"), out, scr)
        make_heads(s)
        back_attention(dm, Group(("do", "scores", *out), (src.do, src.scores, *take(dst, out))), res, s)

    return kernel(body, take(kept, ATTENTION_BACK) + [ffn.do, edge.scores], out, scr, 14)


def call_last(dm, weights, kept, ffn, edge, att):
    half = {k: ((dm.lower // 2, 128), BF) for k in ("keep", "send")}
    outs = {
        "sng": ((dm.small.rows, D), BF),
        "seg": ((dm.small.rows, dm.small.edge_lanes), BF),
        "bgrad": ((dm.big.rows, OUT_LANES), BF),
    }
    out = {**outs, **half}
    scr = {
        **mean_shapes(),
        **last_scratch(dm),
        "nodes_grad": ((dm.nodes, D), BF),
        "edges_grad": ((dm.edges, 256), BF),
    }
    given = ("dy", "dmid", "small", "dsg", "dqkv")

    def body(*refs):
        refs, sems = refs[:-1], refs[-1]
        w, res, src, dst, s = split(refs, W_LAST, LAST_BACK, given, out, scr)
        make_mean(s)
        io = Group(
            (*given, "nodes_grad", "edges_grad", "keep", "send"),
            (*take(src, given), s.nodes_grad, s.edges_grad, dst.keep, dst.send),
        )
        back_last(dm, w, io, res, s)
        outgoing = all_copies(
            dm, dst.sng, dst.seg, dst.bgrad, 0, EDGE_LANES, s.nodes_grad, s.edges_grad, sems, True
        )
        start(outgoing)
        wait(outgoing)

    inputs = take(weights, W_LAST) + take(kept, LAST_BACK)
    inputs += [ffn.dy, edge.dmid, edge.small, att.dsg, att.dqkv]
    got = kernel(body, inputs, out, scr, 13, hbm_out=tuple(outs), sems=[copy_sems(dm)])
    return take(got, out)


def round_up(value, by):
    return -(-value // by) * by


def segment_of(owner, rows, index, count):
    name = owner[index]
    first = jnp.int32(0)
    for t in range(count):
        first = first + jnp.where(t < name, rows[t], 0)
    return first, rows[name]


def shifted_segment(owner, segment_rows, master):
    held = master.shape[0]
    count = owner.shape[0]
    padded = round_up(held + 15, 16)
    step = 1664

    def body(owner_ref, rows_ref, src, dst, window):
        i = pl.program_id(0)
        first, length = segment_of(owner_ref, rows_ref, lax.axis_index("dp"), count)
        shift = first % 16

        @pl.when(i == 0)
        def _():
            window[0:16, :] = jnp.zeros((16, 128), F32)

        window[16:, :] = src[...]
        moved = window[pl.ds(16 - shift, step), :]
        index = i * step - shift + iota((step, 128), 0)
        live = (index >= 0) & (index < length)
        dst[...] = jnp.where(live, moved, 0.0).astype(BF)
        window[0:16, :] = window[step : step + 16, :]

    return pl.pallas_call(
        body,
        grid=(pl.cdiv(padded, step),),
        out_shape=jax.ShapeDtypeStruct((padded, 128), BF),
        in_specs=[
            SMEM,
            SMEM,
            pl.BlockSpec((step, 128), lambda i: (jnp.minimum(i, (held - 1) // step), 0)),
        ],
        out_specs=pl.BlockSpec((step, 128), lambda i: (i, 0)),
        scratch_shapes=[pltpu.VMEM((step + 16, 128), F32)],
        compiler_params=compiler_params(),
    )(owner, segment_rows, master)


def assemble(cube, owner, segment_rows, parts, sources):
    count = len(parts)
    padded = parts[0].shape[0]
    bits = (padded // 16).bit_length()
    tiles = -(-TOTAL_ROWS // 16)
    set_tiles = -(-(SET_ROWS + 2) // 16)
    out = {**{"one_" + k: v for k, v in WEIGHTS.items()}, **{"two_" + k: v for k, v in WEIGHTS.items()}}

    def body(owner_ref, rows_ref, *refs):
        srcs, refs = refs[:count], refs[count:]
        dsts, (rows, flat, tmp, edge, sems, edge_sems) = refs[: len(out)], refs[len(out) :]
        me = lax.axis_index("dp")
        spans = []
        for i in range(count):
            first, length = segment_of(owner_ref, rows_ref, cube.source(me, sources[i]), count)
            spans.append((first // 16, (first + length - 1) // 16))

        def each(act):
            for i, (a, b) in enumerate(spans):
                inner = b - a - 1
                for bit in range(bits):
                    size = 16 << bit
                    if size > padded:
                        continue
                    done = (inner >> (bit + 1)) << (bit + 1)

                    @pl.when((inner > 0) & (((inner >> bit) & 1) == 1))
                    def _(i=i, a=a, done=done, size=size, bit=bit):
                        act(
                            pltpu.make_async_copy(
                                srcs[i].at[pl.ds(aligned(16 * (1 + done), 16), size), :],
                                rows.at[pl.ds(aligned(16 * (a + 1 + done), 16), size), :],
                                sems.at[i, bit],
                            )
                        )

                act(pltpu.make_async_copy(srcs[i].at[pl.ds(0, 16), :], edge.at[2 * i], edge_sems.at[2 * i]))
                act(
                    pltpu.make_async_copy(
                        srcs[i].at[pl.ds(aligned(16 * (b - a), 16), 16), :],
                        edge.at[2 * i + 1],
                        edge_sems.at[2 * i + 1],
                    )
                )

        each(lambda c: c.start())
        each(lambda c: c.wait())
        tile = lambda t: pl.ds(aligned(16 * t, 16), 16)
        for a, b in spans:
            rows[tile(a), :] = jnp.zeros((16, 128), BF)
            rows[tile(b), :] = jnp.zeros((16, 128), BF)
        for i, (a, b) in enumerate(spans):
            rows[tile(a), :] += edge[2 * i]

            @pl.when(b != a)
            def _(i=i, b=b):
                rows[tile(b), :] += edge[2 * i + 1]

        for which in range(2):
            base = which * (SET_ROWS // 16) * 16
            flat[...] = rows[pl.ds(base, 16 * set_tiles), :].astype(F32)
            w = Group(WEIGHTS, dsts[which * len(WEIGHTS) : (which + 1) * len(WEIGHTS)])
            assemble_set(which * (SET_ROWS % 16), flat, tmp, w)

    got = pl.pallas_call(
        body,
        out_shape=structs(out),
        in_specs=[SMEM] * 2 + [HBM] * count,
        out_specs=whole(len(out)),
        scratch_shapes=[
            pltpu.VMEM((16 * tiles, 128), BF),
            pltpu.VMEM((16 * set_tiles, 128), F32),
            pltpu.VMEM((128, 128), F32),
            pltpu.VMEM((2 * count, 16, 128), BF),
            pltpu.SemaphoreType.DMA((count, bits)),
            pltpu.SemaphoreType.DMA((2 * count,)),
        ],
        compiler_params=compiler_params(),
        cost_estimate=cost(10),
    )(owner, segment_rows, *parts)
    return Group(WEIGHTS, got[: len(WEIGHTS)]), Group(WEIGHTS, got[len(WEIGHTS) :])


def adam(n_row, lower, owner, segment_rows, scales, whole_upper, blocks, master, first, second):
    held = master.shape[0]
    step = 1040
    front = step + 16
    count = len(blocks)
    n_dp = owner.shape[0]
    set_rows = ROW_BIAS - ROW_O + lower
    total_rows = front + set_rows + step + 32
    ways = 3 * n_row
    arrivals = sum(len(keys) for _, _, keys, _ in blocks)

    def body(owner_ref, rows_ref, scale_ref, *refs):
        upper, srcs, refs = refs[0], refs[1 : 1 + count], refs[1 + count :]
        master_ref, first_ref, second_ref, o_master, o_first, o_second, o_norms, rows, window, grad, rate, sems, upper_sem = refs
        i = pl.program_id(0)
        me, row = lax.axis_index("dp"), lax.axis_index("row")
        begin, length = segment_of(owner_ref, rows_ref, me, n_dp)

        @pl.when(i == 0)
        def _():
            def each(act):
                copy = pltpu.make_async_copy(
                    upper, rows.at[1, pl.ds(front + ROW_O, UPPER_ROWS), :], upper_sem
                )
                pl.when(begin + length > SET_ROWS + ROW_O)(functools.partial(act, copy))
                every = [
                    (k, core, key, n, sections)
                    for k, (_, core, keys, sections) in enumerate(blocks)
                    for n, key in enumerate(keys)
                ]
                for at_sem, (k, core, key, n, sections) in enumerate(every):
                    mine = (me ^ core) & 1
                    source = me ^ core ^ jnp.where(mine == 0, key[0], key[1])
                    stride = sum(size for _, _, size in sections)
                    offset = n * stride * n_row
                    for number, (which, part, size) in enumerate(sections):
                        block = ((source & 1) * (n_dp // 2) + (source >> 1)) * size * n_row
                        for z in range(n_row):
                            at = block + (row ^ z) * size
                            dest = at + ROW_O if part else jnp.where(at >= ROW_O, at - ROW_O + ROW_BIAS, at)
                            wanted = (dest + which * SET_ROWS < begin + length) & (
                                dest + size + which * SET_ROWS > begin
                            )
                            wanted = wanted | (dest + size > ROW_NN)
                            lies = z * stride + offset

                            def move(frm, extent, to, way, k=k, which=which, at_sem=at_sem):
                                act(
                                    pltpu.make_async_copy(
                                        srcs[k].at[pl.ds(frm, extent), :],
                                        rows.at[which, pl.ds(aligned(front + to, 16), extent), :],
                                        sems.at[at_sem, way],
                                    )
                                )

                            cut = 0 if part else ROW_O % size
                            way = number * n_row + z
                            if not cut:
                                pl.when(wanted)(functools.partial(move, lies, size, dest, way))
                                continue
                            split_here = (at < ROW_O) & (at + size > ROW_O)
                            pl.when(wanted & jnp.logical_not(split_here))(
                                functools.partial(move, lies, size, dest, way)
                            )

                            @pl.when(split_here)
                            def _(move=move, lies=lies, size=size, at=at, cut=cut, way=way, z=z):
                                move(lies, cut, at, way)
                                move(lies + cut, size - cut, ROW_BIAS, 2 * n_row + z)

                        offset += size

            each(lambda c: c.start())
            each(lambda c: c.wait())
            for which in range(2):
                v = rows[which, front + ROW_NN : front + ROW_NN + 32, :].astype(F32)
                for t in range(4):
                    for q in range(4):
                        o_norms[4 * which + t : 4 * which + t + 1, 128 * q : 128 * (q + 1)] = v[
                            4 * t + q : 4 * t + q + 1, :
                        ]
                for t in range(2):
                    both = v[16 + t : 17 + t, :]
                    at = 4 * which + 2 * t
                    o_norms[at : at + 1, 512:576] = both[:, 0:64]
                    o_norms[at + 1 : at + 2, 512:576] = pltpu.roll(both, 64, 1)[:, 0:64]

        low = begin + i * step
        high = low + step
        some = i * step < length

        @pl.when(jnp.logical_not(some))
        def _():
            o_master[...] = master_ref[...]
            o_first[...] = first_ref[...]
            o_second[...] = second_ref[...]

        @pl.when(some)
        def _():
            def shifted(which):
                local = low - which * SET_ROWS + front
                shift = local % 16
                window[...] = rows[which, pl.ds(aligned(local - shift, 16), step + 16), :].astype(F32)
                return window[pl.ds(shift, step), :]

            index = iota((step, 128), 0)

            @pl.when(low < SET_ROWS)
            def _():
                grad[...] = shifted(0)

            @pl.when(low >= SET_ROWS)
            def _():
                grad[...] = shifted(1)

            @pl.when((low < SET_ROWS) & (high > SET_ROWS))
            def _():
                grad[...] = jnp.where(index + low >= SET_ROWS, shifted(1), grad[...])

            at = index + low
            at = jnp.where(at >= SET_ROWS, at - SET_ROWS, at)
            a, b, c = RATES[0][1], RATES[1][1], RATES[3][1]
            far = jnp.where(at < ROW_DOWN, a, c)
            rate[...] = jnp.where(at < ROW_O, a, jnp.where(at < ROW_UP, b, far))
            near = (low < SET_ROWS) & (high > ROW_BIAS)

            @pl.when(near | (high > SET_ROWS + ROW_BIAS))
            def _():
                value = jnp.full((step, 128), 0.25, F32)
                for end, one in reversed(RATES[4:]):
                    value = jnp.where(at < end, one, value)
                rate[...] = jnp.where(at < ROW_BIAS, rate[...], value)

            g = grad[...]
            p, m, v = master_ref[...], first_ref[...], second_ref[...]
            m_new = BETA_ONE * m + (1.0 - BETA_ONE) * g
            v_new = BETA_TWO * v + (1.0 - BETA_TWO) * g * g
            move = (m_new * scale_ref[0]) / (jnp.sqrt(v_new * scale_ref[1]) + ADAM_EPS)
            live = index < length - i * step
            o_master[...] = jnp.where(live, p - rate[...] * (move + WEIGHT_DECAY * p), p)
            o_first[...] = jnp.where(live, m_new, m)
            o_second[...] = jnp.where(live, v_new, v)

    spec = pl.BlockSpec((step, 128), lambda i: (i, 0))
    shape = jax.ShapeDtypeStruct((held, 128), F32)
    return pl.pallas_call(
        body,
        grid=(pl.cdiv(held, step),),
        out_shape=[shape] * 3 + [jax.ShapeDtypeStruct((8, D + DE), F32)],
        in_specs=[SMEM] * 3 + [HBM] * (count + 1) + [spec] * 3,
        out_specs=[spec] * 3 + [pl.BlockSpec((8, D + DE), lambda i: (0, 0))],
        scratch_shapes=[
            pltpu.VMEM((2, total_rows, 128), BF),
            pltpu.VMEM((step + 16, 128), F32),
            pltpu.VMEM((step, 128), F32),
            pltpu.VMEM((step, 128), F32),
            pltpu.SemaphoreType.DMA((arrivals, ways)),
            pltpu.SemaphoreType.DMA(()),
        ],
        compiler_params=compiler_params(),
        cost_estimate=cost(10),
    )(owner, segment_rows, scales, whole_upper, *[b[0] for b in blocks], master, first, second)


RATES = [
    (ROW_O, 0.5 * D ** (-0.5)),
    (ROW_UP, 2.0 * D ** (-0.5)),
    (ROW_DOWN, 0.5 * D ** (-0.5)),
    (ROW_BIAS, 0.5 * FF ** (-0.5)),
    (ROW_EDGE, 0.5 * DE ** (-0.5)),
    (ROW_EUP, 0.5 * H ** (-0.5)),
    (ROW_EDOWN, 0.5 * DE ** (-0.5)),
    (ROW_NN, 0.5 * FFE ** (-0.5)),
]


class Cube:
    def __init__(self, size):
        self.size = size
        self.bits = size.bit_length() - 1
        assert size == 1 << self.bits
        up = list(range(1, self.bits))
        self.order = (up, up[::-1])

    def pairs(self, step):
        return [(i, i ^ (1 << self.order[i & 1][step])) for i in range(self.size)]

    def core_pairs(self):
        return [(i, i ^ 1) for i in range(self.size)]

    def source(self, me, key):
        other, used = key
        even, odd = [sum(1 << self.order[c][s] for s in used) for c in (0, 1)]
        if other:
            even, odd = odd, even
        return me ^ jnp.where(me & 1 == 0, even, odd) ^ other

    def gather(self, value, also):
        steps = range(self.bits - 1)
        new, done = [((), value)], []
        while new:
            sent = []
            for used, v in new:
                done.append(((0, used), v))
                for step in steps:
                    if not used or step > used[-1]:
                        sent.append((0, used + (step,), lax.ppermute(v, "dp", self.pairs(step))))
            for used, v in new:
                sent.append((1, used, lax.ppermute(v, "dp", self.core_pairs())))
            moved, also = lax.optimization_barrier(([v for _, _, v in sent], also))
            new = []
            for (other, used, _), v in zip(sent, moved):
                if other:
                    done.append(((1, used), v))
                else:
                    new.append((used, v))
        return done, also


def total(values):
    out = values[0].astype(F32)
    for v in values[1:]:
        out = out + v.astype(F32)
    return out.astype(BF)


class Chain:
    def __init__(self, cube, direct, *halves):
        self.cube, self.direct = cube, direct
        self.kept = [k for k, _ in halves]
        self.value = [s for _, s in halves]
        self.step, self.done = 0, False
        self.sides = lax.axis_size("dp") // 2
        self.rows = lax.axis_size("row")

    def swap(self, value):
        return lax.ppermute(value, "dp", [(i, i ^ 1) for i in range(2 * self.sides)])

    def to_chip(self, value, k):
        return lax.ppermute(value, "dp", [(i, i ^ (k << 1)) for i in range(2 * self.sides)])

    def to_row(self, value, k):
        return lax.ppermute(value, "row", [(i, i ^ k) for i in range(self.rows)])

    def scatter(self, index, count, send):
        def at(k):
            parts = [v.reshape(count, v.shape[0] // count, 128) for v in self.value]
            parts = [lax.dynamic_index_in_dim(v, index ^ k, 0, keepdims=False) for v in parts]
            return jnp.concatenate(parts) if len(parts) > 1 else parts[0]

        self.sizes = [v.shape[0] // count for v in self.value]
        self.kept = at(0)
        return [send(at(k), k) for k in range(1, count)]

    def launch(self):
        self.step += 1
        if self.step == 1:
            return [self.swap(v) for v in self.value]
        if self.step == 2:
            return self.scatter(lax.axis_index("dp") >> 1, self.sides, self.to_chip)
        if self.step == 3:
            return self.scatter(lax.axis_index("row"), self.rows, self.to_row)
        if self.step == 4:
            return [self.to_row(self.value, k) for k in range(1, self.rows)]
        if not self.spread():
            return [self.swap(self.value)]
        if self.direct:
            return [self.to_chip(self.value, k) for k in range(1, self.sides)]
        return [lax.ppermute(self.value, "dp", self.cube.pairs(self.step - 5))]

    def spread(self):
        return self.step < 6 if self.direct else self.step < 5 + self.cube.bits - 1

    def land(self, got):
        if self.step == 1:
            self.value = [total(pair) for pair in zip(self.kept, got)]
        elif self.step <= 3:
            value = total([self.kept, *got])
            if self.step == 3:
                self.value = value
            else:
                self.value, at = [], 0
                for size in self.sizes:
                    self.value.append(value[at : at + size])
                    at += size
        elif self.step == 4:
            self.value = jnp.concatenate([self.value, *got])
            self.size = self.value.shape[0]
        elif self.spread():
            self.value = jnp.concatenate([self.value, *got])
            if self.direct:
                self.keys = [(k << 1, k << 1) for k in range(self.sides)]
            else:
                bit = [1 << order[self.step - 5] for order in self.cube.order]
                keys = self.keys if self.step > 5 else [(0, 0)]
                self.keys = keys + [(a ^ bit[0], b ^ bit[1]) for a, b in keys]
        else:
            self.value, self.done = [self.value, *got], True

    def blocks(self, *names):
        sections = [(which, part, size) for (which, part), size in zip(names, self.sizes)]
        return [(v, core, self.keys, sections) for core, v in enumerate(self.value)]


def phase(chains, *ready):
    chains = [c for c in chains if not c.done]
    sent = [c.launch() for c in chains]
    got, ready = lax.optimization_barrier((sent, ready))
    for c, g in zip(chains, got):
        c.land(g)
    return ready


def per_device(
    small_nodes,
    small_edges,
    small_counts,
    big_nodes,
    big_edges,
    big_counts,
    small_node_cot,
    small_edge_cot,
    big_node_cot,
    big_edge_cot,
    master,
    first_moment,
    second_moment,
    owner,
    segment_rows,
    step_count,
):
    n_dp, n_row = lax.axis_size("dp"), lax.axis_size("row")
    cube = Cube(n_dp)
    share = big_nodes.shape[0] // n_row
    dm = Dims(small_nodes.shape[0], share, n_dp * n_row)

    def flat2(v):
        return v.reshape(-1, v.shape[-1])

    def to_rows(v):
        v = v.reshape(share, NB, OUT_LANES)
        v = lax.all_to_all(v, "row", split_axis=1, concat_axis=0, tiled=True)
        return v[..., EDGE_LANES:], v[..., :EDGE_LANES]

    own = shifted_segment(owner, segment_rows, master)
    own, big = lax.optimization_barrier((own, (big_edges, big_edge_cot, big_nodes, big_node_cot)))
    big = jnp.concatenate(big, axis=2)
    big = flat2(lax.all_to_all(big, "row", split_axis=0, concat_axis=1, tiled=True))
    held, big = cube.gather(own, big)
    one, two = assemble(cube, owner, segment_rows, [v for _, v in held], [k for k, _ in held])

    own_counts = lax.dynamic_slice_in_dim(big_counts, lax.axis_index("row") * share, share)
    counts = jnp.concatenate([small_counts, own_counts])

    mid_nodes, mid_edges, kept = first_forward(
        dm, counts, one, flat2(small_nodes), flat2(small_edges), big
    )
    sno, seo, bout, node_cot, edge_cot, kept_two, ffn_two = second_forward(
        dm, counts, two, mid_nodes, mid_edges, flat2(small_node_cot), flat2(small_edge_cot), big
    )
    spread = lax.psum_scatter(ffn_two.upper, "dp", scatter_dimension=0, tiled=True)
    got = between(dm, two, one, kept_two, kept, ffn_two, edge_cot)
    outs = to_rows(bout)
    names = tuple(k for k in vars(got))
    *values, bno, beo = phase([], *take(got, names), *outs)
    got = Group(names, values)
    middle = Chain(cube, False, (got.keep, got.send), (got.two_keep, got.two_send))
    names = tuple(edge_shapes(dm))
    edge_one = call_edges(dm, one, kept, got, got.edges_grad)
    spread, *edge = phase([middle], spread, *take(edge_one, names))
    edge_one = Group(names, edge)
    spread = lax.psum(spread, "row")
    names = tuple(attention_shapes(dm))
    att_one = Group(names, phase([middle], *take(call_attention(dm, kept, got, edge_one), names)))
    sng, seg, bgrad, keep, send = call_last(dm, one, kept, got, edge_one, att_one)
    spread, sng, seg, bgrad, keep, send = phase([middle], spread, sng, seg, bgrad, keep, send)
    upper_two = lax.all_gather(spread, "dp", axis=0, tiled=True)
    last = Chain(cube, True, (keep, send))
    for _ in range(4):
        phase([last, middle])
    bgrad, upper_two = phase([last, middle], bgrad, upper_two)
    bng, beg = to_rows(bgrad)
    while not (last.done and middle.done):
        phase([last, middle])
    blocks = last.blocks((0, 0)) + middle.blocks((0, 1), (1, 0))
    step_value = step_count[0].astype(F32)
    scales = jnp.stack(
        [
            1.0 / (1.0 - jnp.power(F32(BETA_ONE), step_value)),
            1.0 / (1.0 - jnp.power(F32(BETA_TWO), step_value)),
        ]
    )
    new_master, new_first, new_second, norm_grads = adam(
        n_row, dm.lower, owner, segment_rows, scales, upper_two, blocks, master, first_moment, second_moment
    )
    return (
        sno.reshape(small_nodes.shape),
        seo.reshape(small_edges.shape),
        bno,
        beo,
        sng.reshape(small_nodes.shape),
        seg.reshape(small_edges.shape),
        bng,
        beg,
        new_master,
        new_first,
        new_second,
        norm_grads,
    )


def solution(mesh):
    both = P(("dp", "row"), None, None)
    rows = P("dp", "row", None)
    held = P("dp", None)
    in_specs = (
        both, both, P(("dp", "row")), rows, rows, P("dp"), both, both, rows, rows,
        held, held, held, P(), P(), P(),
    )
    out_specs = (both, both, rows, rows, both, both, rows, rows, held, held, held, P())
    return jax.shard_map(
        per_device, mesh=mesh, in_specs=in_specs, out_specs=out_specs, check_vma=False
    )
```

time: 537 us -> 438 us (0.82)
  blocking collectives: 59.7 us -> 0 us
  waiting for transfers between devices: 172 us -> 146 us
  Pallas kernels: 203 us -> 188 us
  between operations: 4.14 us -> 15.3 us
  other arithmetic: 14.6 us -> 8.63 us
    psum x1 -> x0, blocking collectives: 40.5 us -> none  [per_device(): lax.psum(jnp.concatenate([norms_one, norms_two]), ('dp', 'row'))]
    ppermute x35, waiting for transfers between devices: 112 us -> 89.4 us  [the longest x9 36.2 us: to_chip(): lax.ppermute(value, 'dp', [(i, i ^ k << 1) for i in range(2 * self.sides)])]
    all_to_all x2 -> x0, blocking collectives: 19.2 us -> none  [to_whole(): return lax.all_to_all(v, 'row', split_axis=0, concat_axis=1, tiled=True)]
    pallas_call x4 -> x7, Pallas kernels: 185 us -> 172 us  [the longest x6 154 us: kernel(): pl.pallas_call(body, out_shape=structs(out), in_specs=[SMEM] * len(smem)...]
    all_to_all x6 -> x3, starting transfers between devices: 21.6 us -> 13.5 us  [the longest x2 7.21 us: to_rows(): v = lax.all_to_all(v, 'row', split_axis=1, concat_axis=0, tiled=True)]
    ppermute x35, starting transfers between devices: 32.8 us -> 40.8 us  [the longest x12 22.6 us: to_row(): return lax.ppermute(value, 'row', [(i, i ^ k) for i in range(self.rows)])]
    all_to_all x8 -> x3, local copies, waits for them, and re-layouts: 9.1 us -> 1.86 us  [the longest x1 1.62 us: per_device(): lax.all_to_all(big, 'row', split_axis=0, concat_axis=1, tiled=True)]
    unnamed x32 -> x58, local copies, waits for them, and re-layouts: 0.07 us -> 7.08 us
  transfers between devices with their start and end apart: 41 -> 41, of which waited for: 16 -> 19; matrix products, arithmetic and copies ran while one was open for 6% -> 3% of each run, Pallas kernels for 10% -> 26%
where the time goes in v2:
time: 438 us; the launch traced here: 431 us
  Pallas kernels  188 us (43%)
  waiting for transfers between devices  146 us (33%)
  starting transfers between devices  54.6 us (12%)
  local copies, waits for them, and re-layouts  18.5 us (4%)
  between operations  15.3 us (3%)
  other arithmetic  8.63 us (2%)
    pallas_call x6, Pallas kernels, kernel(): pl.pallas_call(body, out_shape=structs(out), in_specs=[SMEM] * len(smem)...  154 us
    all_to_all x1, waiting for transfers between devices, per_device(): lax.all_to_all(big, 'row', split_axis=0, concat_axis=1, tiled=True)  50.8 us
    ppermute x9, waiting for transfers between devices, to_chip(): lax.ppermute(value, 'dp', [(i, i ^ k << 1) for i in range(2 * self.sides)])  36.2 us
    ppermute x3, waiting for transfers between devices, gather(): sent.append((0, used + (step,), lax.ppermute(v, 'dp', self.pairs(step))))  24.6 us
    ppermute x12, starting transfers between devices, to_row(): return lax.ppermute(value, 'row', [(i, i ^ k) for i in range(self.rows)])  22.6 us
    ppermute x12, waiting for transfers between devices, to_row(): return lax.ppermute(value, 'row', [(i, i ^ k) for i in range(self.rows)])  19.6 us
    pallas_call x1, Pallas kernels, adam(): pl.pallas_call(body, grid=(pl.cdiv(held, step),), out_shape=[shape] * 3 +...  17.2 us
    ppermute x9, starting transfers between devices, to_chip(): lax.ppermute(value, 'dp', [(i, i ^ k << 1) for i in range(2 * self.sides)])  10.7 us
  transfers between devices with their start and end apart: 41, of which 19 were waited for; matrix products, arithmetic and copies ran while one was open for 3% of the time, Pallas kernels for 26%

profile of v2, /device:TPU:0, one launch (start us, length us, event | category | flops | bytes accessed | tf_op | source)
XLA Modules:
  0.0 430.8 jit_solution(3290424072099927507)
XLA Ops:
  7.2 5.9 %shard_map.247.refs_0_ = bf16[8320,128]{1,0:T(8,128)(2,1)} custom-call(s32[8]{0:T(128)} %owner_ref.5, s32[8]{0:T(128)} %rows_ref.5, f32[8290,128]{1,0:T(8,128)} %refs_5_.1), custom_call_target="tpu_custom_call" | custom-call | tf_op jit(solution)/shard_map/pallas_call | solution.py:1016
  13.1 1.5 pad_maximum_fusion
  14.6 6.3 %all-to-all-start = ((bf16[8,16,9216]{2,1,0:T(8,128)(2,1)}), bf16[8,16,9216]{2,1,0:T(8,128)(2,1)S(1)}, u32[]{:S(2)}, u32[]{:S(2)}) async-start(bf16[8,16,9216]{2,1,0:T(8,128)(2,1)} %pad_maximum_fusion), calls=%async_computation | async-start | bytes 4718592 | tf_op jit(solution)/shard_map/all_to_all | solution.py:1461
  21.0 1.5 collective-permute-start
  22.5 1.5 collective-permute-start.1
  24.0 50.8 %all-to-all-done = bf16[8,16,9216]{2,1,0:T(8,128)(2,1)S(1)} async-done(((bf16[8,16,9216]{2,1,0:T(8,128)(2,1)}), bf16[8,16,9216]{2,1,0:T(8,128)(2,1)S(1)}, u32[]{:S(2)}, u32[]{:S(2)}) %all-to-all-start) | async-done | bytes 2359328 | tf_op jit(solution)/shard_map/all_to_all | solution.py:1461
  74.8 1.6 copy.31
  76.4 1.6 collective-permute-start.3
  78.5 24.6 %collective-permute-done.3.refs_6_ = bf16[8320,128]{1,0:T(8,128)(2,1)S(1)} collective-permute-done((bf16[8320,128]{1,0:T(8,128)(2,1)}, bf16[8320,128]{1,0:T(8,128)(2,1)S(1)}, u32[]{:S(2)}, u32[]{:S(2)}) %collective-permute-start.3) | collective-permute-done | bytes 2129952 | tf_op jit(solution)/shard_map/ppermute | solution.py:1320
  104.4 1.4 copy-done.3
  106.5 3.7 collective-permute-done.6.refs_7_
  110.2 10.4 %shard_map.248 = (bf16[512,1536]{1,0:T(8,128)(2,1)}, bf16[512,512]{1,0:T(8,128)(2,1)}, bf16[512,1024]{1,0:T(8,128)(2,1)}, bf16[1024,512]{1,0:T(8,128)(2,1)}, bf1...) custom-call(s32[8]{0:T(128)} %owner_ref.5, ...), custom_call_target="tpu_custom_call" | custom-call | bytes 34000000 | tf_op jit(solution)/shard_map/pallas_call | solution.py:1095
  120.6 28.7 %shard_map.249 = (bf16[224,512]{1,0:T(8,128)(2,1)}, bf16[2816,256]{1,0:T(8,128)(2,1)}, bf16[224,512]{1,0:T(8,128)(2,1)}, f32[224,128]{1,0:T(8,128)}, bf16[224,15...) custom-call(s32[5]{0:T(128)} %pad_add_fusion.refs_0_, ...), custom_call_target="tpu_custom_call" | custom-call | bytes 129200000 | tf_op jit(solution)/shard_map/pallas_call | solution.py:787
  149.3 32.5 %shard_map.250 = (bf16[96,512]{1,0:T(8,128)(2,1)}, bf16[96,2048]{1,0:T(8,128)(2,1)}, bf16[128,4608]{1,0:T(8,128)(2,1)}, bf16[2816,256]{1,0:T(8,128)(2,1)}, bf16[...) custom-call(s32[5]{0:T(128)} %pad_add_fusion.refs_0_, ...), custom_call_target="tpu_custom_call" | custom-call | bytes 156400000 | tf_op jit(solution)/shard_map/pallas_call | solution.py:787
  183.1 2.2 copy.32
  185.3 3.5 all-to-all-start.1
  188.9 46.0 %shard_map.251 = (bf16[2816,256]{1,0:T(8,128)(2,1)}, bf16[3328,128]{1,0:T(8,128)(2,1)}, bf16[3328,128]{1,0:T(8,128)(2,1)}, f32[224,512]{1,0:T(8,128)}, bf16[224,...) custom-call(bf16[512,1536]{1,0:T(8,128)(2,1)} %get-tuple-element.168.refs_1_.refs_0_,, ...), custom_call_target="tpu_custom_call" | custom-call | bytes 153000000 | tf_op jit(solution)/shard_map/pallas_call | solution.py:787
  237.4 16.7 %shard_map.252 = (bf16[2816,256]{1,0:T(8,128)(2,1)}, f32[1408,256]{1,0:T(8,128)}, f32[256,128]{1,0:T(8,128)}) custom-call(bf16[256,512]{1,0:T(8,128)(2,1)} %get-tuple-element.183.refs_6_.refs_0_, bf16[256,512]{1,0:T(8,128)(2,1)} %get-tuple-element.184.refs_7_.refs_1_, bf16[512,256]{1,0:T(8,128)(2,1)} %get-tuple-element.185.refs_8_.refs_2_, ...), custom_call_target="tpu_custom_call" | custom-call | bytes 54400000 | tf_op jit(solution)/shard_map/pallas_call | solution.py:787
  255.7 2.5 collective-permute-start.11
  259.8 17.2 %shard_map.253 = (bf16[1408,512]{1,0:T(8,128)(2,1)}, bf16[224,1536]{1,0:T(8,128)(2,1)}) custom-call(bf16[224,1536]{1,0:T(8,128)(2,1)} %get-tuple-element.237.refs_0_, bf16[1408,256]{1,0:T(8,128)(2,1)} %get-tuple-element.238.refs_1_, f32[1408,256]{1,0:T(8,128)} %get-tuple-element.239.refs_2_, bf16[224,512]{1,0:T(8,128)(2,1)} %get-tuple-element.240.refs_3_, ...), custom_call_target="tpu_custom_call" | custom-call | bytes 47600000 | tf_op jit(solution)/shard_map/pallas_call | solution.py:787
  277.0 5.7 %collective-permute-done.10 = bf16[2112,128]{1,0:T(8,128)(2,1)S(1)} collective-permute-done((bf16[2112,128]{1,0:T(8,128)(2,1)S(1)}, bf16[2112,128]{1,0:T(8,128)(2,1)S(1)}, u32[]{:S(2)}, u32[]{:S(2)}) %collective-permute-start.10) | collective-permute-done | bytes 540704 | tf_op jit(solution)/shard_map/ppermute | solution.py:1353
  284.4 3.5 collective-permute-start.14
  289.0 13.3 %shard_map.254 = (bf16[96,512]{1,0:T(8,128)(2,1)}, bf16[96,2048]{1,0:T(8,128)(2,1)}, bf16[128,4608]{1,0:T(8,128)(2,1)}, bf16[3328,128]{1,0:T(8,128)(2,1)}, bf16[3328,128]{1,0:T(8,128)(2,1)}) custom-call(bf16[512,1536]{1,0:T(8,128)(2,1)} %get-tuple-element.178.refs_1_.refs_0_, bf16[512,512]{1,0:T(8,128)(2,1)} %get-tuple-element.182.refs_5_.refs_1_, ...), custom_call_target="tpu_custom_call" | custom-call | bytes 44200000 | tf_op jit(solution)/shard_map/pallas_call | solution.py:787
  302.4 2.3 collective-permute-done.13
  305.8 2.1 collective-permute-start.17
  307.8 2.3 collective-permute-start.18
  310.2 3.3 collective-permute-done.16
  313.5 5.4 %collective-permute-done.17 = bf16[528,128]{1,0:T(8,128)(2,1)S(1)} collective-permute-done((bf16[528,128]{1,0:T(8,128)(2,1)S(1)}, bf16[528,128]{1,0:T(8,128)(2,1)S(1)}, u32[]{:S(2)}, u32[]{:S(2)}) %collective-permute-start.17) | collective-permute-done | bytes 135200 | tf_op jit(solution)/shard_map/ppermute | solution.py:1356
  319.0 1.6 collective-permute-start.22
  320.6 1.4 add_convert_fusion.1
  322.6 1.4 collective-permute-start.20
  324.1 1.6 collective-permute-start.21
  325.7 15.6 %collective-permute-done.19 = bf16[832,128]{1,0:T(8,128)(2,1)S(1)} collective-permute-done((bf16[832,128]{1,0:T(8,128)(2,1)S(1)}, bf16[832,128]{1,0:T(8,128)(2,1)S(1)}, u32[]{:S(2)}, u32[]{:S(2)}) %collective-permute-start.19) | collective-permute-done | bytes 213024 | tf_op jit(solution)/shard_map/ppermute | solution.py:1353
  341.4 5.9 %collective-permute-done.21 = bf16[832,128]{1,0:T(8,128)(2,1)S(1)} collective-permute-done((bf16[832,128]{1,0:T(8,128)(2,1)S(1)}, bf16[832,128]{1,0:T(8,128)(2,1)S(1)}, u32[]{:S(2)}, u32[]{:S(2)}) %collective-permute-start.21) | collective-permute-done | bytes 213024 | tf_op jit(solution)/shard_map/ppermute | solution.py:1353
  347.7 4.6 %collective-permute-start.23 = (bf16[208,128]{1,0:T(8,128)(2,1)S(1)}, bf16[208,128]{1,0:T(8,128)(2,1)S(1)}, u32[]{:S(2)}, u32[]{:S(2)}) collective-permute-start(bf16[208,128]{1,0:T(8,128)(2,1)S(1)} %get-tuple-element.319), channel_id=1, source_target_pairs={{0,1},{1,0},{2,3},{3,2},{4,5},{5,4},{6,7},{7,6},{8,9},{9,8},{10,11... | collective-permute-start | bytes 159752 | tf_op jit(solution)/shard_map/ppermute | solution.py:1356
  352.3 2.4 collective-permute-start.25
  354.7 2.7 collective-permute-done.24
  358.3 4.3 %collective-permute-done.26 = bf16[4224,128]{1,0:T(8,128)(2,1)S(1)} collective-permute-done((bf16[4224,128]{1,0:T(8,128)(2,1)S(1)}, bf16[4224,128]{1,0:T(8,128)(2,1)S(1)}, u32[]{:S(2)}, u32[]{:S(2)}) %collective-permute-start.26) | collective-permute-done | bytes 1081376 | tf_op jit(solution)/shard_map/ppermute | solution.py:1382
  363.5 4.2 collective-permute-start.27
  367.8 2.2 collective-permute-start.29
  370.2 4.8 %collective-permute-done.28 = bf16[208,128]{1,0:T(8,128)(2,1)S(1)} collective-permute-done((bf16[208,128]{1,0:T(8,128)(2,1)S(1)}, bf16[208,128]{1,0:T(8,128)(2,1)S(1)}, u32[]{:S(2)}, u32[]{:S(2)}) %collective-permute-start.28) | collective-permute-done | bytes 53280 | tf_op jit(solution)/shard_map/ppermute | solution.py:1356
  376.5 1.5 collective-permute-start.32
  379.2 4.9 %collective-permute-done.31 = bf16[832,128]{1,0:T(8,128)(2,1)S(1)} collective-permute-done((bf16[832,128]{1,0:T(8,128)(2,1)}, bf16[832,128]{1,0:T(8,128)(2,1)S(1)}, u32[]{:S(2)}, u32[]{:S(2)}) %collective-permute-start.31) | collective-permute-done | bytes 213024 | tf_op jit(solution)/shard_map/ppermute | solution.py:1353
  384.1 3.9 collective-permute-done.32
  388.0 2.3 copy.34
  390.4 3.7 all-to-all-start.2
  399.5 17.2 %shard_map.255 = (f32[8290,128]{1,0:T(8,128)}, f32[8290,128]{1,0:T(8,128)}, f32[8290,128]{1,0:T(8,128)}, f32[8,576]{1,0:T(8,128)}) custom-call(s32[8]{0:T(128)} %owner_ref.5, s32[8]{0:T(128)} %rows_ref.5, f32[2]{0:T(128)} %pad_maximum_fusion.9.scale_ref, bf16[10240,128]{1,0:T(8,128)(2,1)} %all-gather.2.cloned.1.call-done.refs_0_, ...), custom_call_target="tpu_custom_call" | custom-call | bytes 34000000 | tf_op jit(solution)/shard_map/pallas_call | solution.py:1259
  416.7 5.4 %all-to-all-done.2 = bf16[2,64,4608]{2,0,1:T(2,128)(2,1)S(1)} async-done(((bf16[2,64,4608]{2,0,1:T(2,128)(2,1)}), bf16[2,64,4608]{2,0,1:T(2,128)(2,1)S(1)}, u32[]{:S(2)}, u32[]{:S(2)}) %all-to-all-start.2) | async-done | bytes 1179680 | tf_op jit(solution)/shard_map/all_to_all | solution.py:1455
  (142 shorter events, 25.5 us)
Async XLA Ops:
  14.6 60.1 %all-to-all-start = ((bf16[8,16,9216]{2,1,0:T(8,128)(2,1)}), bf16[8,16,9216]{2,1,0:T(8,128)(2,1)S(1)}, u32[]{:S(2)}, u32[]{:S(2)}) async-start(bf16[8,16,9216]{2,1,0:T(8,128)(2,1)} %pad_maximum_fusion), calls=%async_computation | async-start | bytes 4718592 | tf_op jit(solution)/shard_map/all_to_all | solution.py:1461
  21.0 233.2 %reduce-scatter.2.cloned.1.call-start = ((), (), s32[]{:S(2)}) async-start(), calls=%async_computation.4 | async-start | bytes 2949120 | tf_op jit(solution)/shard_map/reduce_scatter | solution.py:1474
  21.0 55.4 %collective-permute-start = (bf16[8320,128]{1,0:T(8,128)(2,1)}, bf16[8320,128]{1,0:T(8,128)(2,1)}, u32[]{:S(2)}, u32[]{:S(2)}) collective-permute-start(bf16[8320,128]{1,0:T(8,128)(2,1)} %shard_map.247.refs_0_), channel_id=1, source_target_pairs={{0,8},{4,20},{8,0},{12,28},{16,24},{20,4},{24,16},{28,12},{1,9},{5... | collective-permute-start | bytes 6389768 | tf_op jit(solution)/shard_map/ppermute | solution.py:1320
  22.5 54.0 %collective-permute-start.1 = (bf16[8320,128]{1,0:T(8,128)(2,1)}, bf16[8320,128]{1,0:T(8,128)(2,1)}, u32[]{:S(2)}, u32[]{:S(2)}) collective-permute-start(bf16[8320,128]{1,0:T(8,128)(2,1)} %shard_map.247.refs_0_), channel_id=1, source_target_pairs={{0,16},{4,12},{8,24},{12,4},{16,0},{20,28},{24,8},{28,20},{1,17},{... | collective-permute-start | bytes 6389768 | tf_op jit(solution)/shard_map/ppermute | solution.py:1320
  24.0 52.4 %collective-permute-start.2 = (bf16[8320,128]{1,0:T(8,128)(2,1)}, bf16[8320,128]{1,0:T(8,128)(2,1)}, u32[]{:S(2)}, u32[]{:S(2)}) collective-permute-start(bf16[8320,128]{1,0:T(8,128)(2,1)} %shard_map.247.refs_0_), channel_id=1, source_target_pairs={{0,4},{4,0},{8,12},{12,8},{16,20},{20,16},{24,28},{28,24},{1,5},{5... | collective-permute-start | bytes 6389768 | tf_op jit(solution)/shard_map/ppermute | solution.py:1322
  74.8 31.1 %copy-start.22 = (s32[8]{0:T(128)S(1)}, s32[8]{0:T(128)}, u32[]{:S(2)}) copy-start(s32[8]{0:T(128)} %param.21) | copy-start | bytes 100
  74.8 31.1 %copy-start.23 = (s32[3]{0:T(128)S(1)}, s32[3]{0:T(128)}, u32[]{:S(2)}) copy-start(s32[3]{0:T(128)} %param.18) | copy-start | bytes 40
  76.4 26.7 %collective-permute-start.3 = (bf16[8320,128]{1,0:T(8,128)(2,1)}, bf16[8320,128]{1,0:T(8,128)(2,1)S(1)}, u32[]{:S(2)}, u32[]{:S(2)}) collective-permute-start(bf16[8320,128]{1,0:T(8,128)(2,1)} %collective-permute-done.refs_2_), channel_id=1, source_target_pairs={{0,16},{4,12},{8,24},{12,4},{16,0},{20,28},{24,8},{28,20},{1,17},{... | collective-permute-start | bytes 6389768 | tf_op jit(solution)/shard_map/ppermute | solution.py:1320
  78.0 25.1 %collective-permute-start.4 = (bf16[8320,128]{1,0:T(8,128)(2,1)}, bf16[8320,128]{1,0:T(8,128)(2,1)S(1)}, u32[]{:S(2)}, u32[]{:S(2)}) collective-permute-start(bf16[8320,128]{1,0:T(8,128)(2,1)} %collective-permute-done.refs_2_), channel_id=1, source_target_pairs={{0,4},{4,0},{8,12},{12,8},{16,20},{20,16},{24,28},{28,24},{1,5},{5... | collective-permute-start | bytes 6389768 | tf_op jit(solution)/shard_map/ppermute | solution.py:1322
  78.0 26.4 %collective-permute-start.5 = (bf16[8320,128]{1,0:T(8,128)(2,1)}, bf16[8320,128]{1,0:T(8,128)(2,1)S(1)}, u32[]{:S(2)}, u32[]{:S(2)}) collective-permute-start(bf16[8320,128]{1,0:T(8,128)(2,1)} %collective-permute-done.1.refs_3_), channel_id=1, source_target_pairs={{0,4},{4,0},{8,12},{12,8},{16,20},{20,16},{24,28},{28,24},{1,5},{5... | collective-permute-start | bytes 6389768 | tf_op jit(solution)/shard_map/ppermute | solution.py:1322
  103.1 7.1 %copy-start.1 = (bf16[8320,128]{1,0:T(8,128)(2,1)}, bf16[8320,128]{1,0:T(8,128)(2,1)S(1)}, u32[]{:S(2)}) copy-start(bf16[8320,128]{1,0:T(8,128)(2,1)S(1)} %collective-permute-done.3.refs_6_) | copy-start | bytes 6389764
  105.8 4.3 %collective-permute-start.6 = (bf16[8320,128]{1,0:T(8,128)(2,1)S(1)}, bf16[8320,128]{1,0:T(8,128)(2,1)}, u32[]{:S(2)}, u32[]{:S(2)}) collective-permute-start(bf16[8320,128]{1,0:T(8,128)(2,1)S(1)} %collective-permute-done.3.refs_6_), channel_id=1, source_target_pairs={{0,4},{4,0},{8,12},{12,8},{16,20},{20,16},{24,28},{28,24},{1,5},{5... | collective-permute-start | bytes 6389768 | tf_op jit(solution)/shard_map/ppermute | solution.py:1322
  185.3 49.6 %all-to-all-start.1 = ((bf16[2,64,4608]{2,0,1:T(2,128)(2,1)}), bf16[2,64,4608]{2,0,1:T(2,128)(2,1)S(1)}, u32[]{:S(2)}, u32[]{:S(2)}) async-start(bf16[2,64,4608]{2,0,1:T(2,128)(2,1)} %copy.32), calls=%async_computation.1 | async-start | bytes 2359296 | tf_op jit(solution)/shard_map/all_to_all | solution.py:1455
  188.9 113.5 %all-reduce.2.cloned.1.call-start = ((), (), s32[]{:S(2)}) async-start(), calls=%async_computation.5 | async-start | bytes 655360 | tf_op jit(solution)/shard_map/psum | solution.py:1485
  236.8 17.3 %collective-permute-start.7 = (bf16[5120,128]{1,0:T(8,128)(2,1)}, bf16[5120,128]{1,0:T(8,128)(2,1)S(1)}, u32[]{:S(2)}, u32[]{:S(2)}) collective-permute-start(bf16[5120,128]{1,0:T(8,128)(2,1)} %get-tuple-element.223), channel_id=1, source_target_pairs={{0,4},{4,0},{8,12},{12,8},{16,20},{20,16},{24,28},{28,24},{1,5},{5... | collective-permute-start | bytes 3932168 | tf_op jit(solution)/shard_map/ppermute | solution.py:1350
  237.0 17.1 %collective-permute-start.8 = (bf16[3328,128]{1,0:T(8,128)(2,1)}, bf16[3328,128]{1,0:T(8,128)(2,1)S(1)}, u32[]{:S(2)}, u32[]{:S(2)}) collective-permute-start(bf16[3328,128]{1,0:T(8,128)(2,1)} %get-tuple-element.224), channel_id=1, source_target_pairs={{0,4},{4,0},{8,12},{12,8},{16,20},{20,16},{24,28},{28,24},{1,5},{5... | collective-permute-start | bytes 2555912 | tf_op jit(solution)/shard_map/ppermute | solution.py:1350
  237.3 16.8 %copy-start.4 = (bf16[5120,128]{1,0:T(8,128)(2,1)S(1)}, bf16[5120,128]{1,0:T(8,128)(2,1)}, u32[]{:S(2)}) copy-start(bf16[5120,128]{1,0:T(8,128)(2,1)} %get-tuple-element.222) | copy-start | bytes 3932164
  255.7 21.2 %collective-permute-start.11 = (bf16[2112,128]{1,0:T(8,128)(2,1)S(1)}, bf16[2112,128]{1,0:T(8,128)(2,1)S(1)}, u32[]{:S(2)}, u32[]{:S(2)}) collective-permute-start(bf16[2112,128]{1,0:T(8,128)(2,1)S(1)} %pad_maximum_fusion.3), channel_id=1, source_target_pairs={{0,24},{4,28},{8,16},{12,20},{16,8},{20,12},{24,0},{28,4},{1,25},{... | collective-permute-start | bytes 1622024 | tf_op jit(solution)/shard_map/ppermute | solution.py:1353
  258.3 24.3 %collective-permute-start.10 = (bf16[2112,128]{1,0:T(8,128)(2,1)S(1)}, bf16[2112,128]{1,0:T(8,128)(2,1)S(1)}, u32[]{:S(2)}, u32[]{:S(2)}) collective-permute-start(bf16[2112,128]{1,0:T(8,128)(2,1)S(1)} %pad_maximum_fusion.2), channel_id=1, source_target_pairs={{0,16},{4,20},{8,24},{12,28},{16,0},{20,4},{24,8},{28,12},{1,17},{... | collective-permute-start | bytes 1622024 | tf_op jit(solution)/shard_map/ppermute | solution.py:1353
  258.9 24.0 %collective-permute-start.9 = (bf16[2112,128]{1,0:T(8,128)(2,1)S(1)}, bf16[2112,128]{1,0:T(8,128)(2,1)}, u32[]{:S(2)}, u32[]{:S(2)}) collective-permute-start(bf16[2112,128]{1,0:T(8,128)(2,1)S(1)} %pad_maximum_fusion.1), channel_id=1, source_target_pairs={{0,8},{4,12},{8,0},{12,4},{16,24},{20,28},{24,16},{28,20},{1,9},{5... | collective-permute-start | bytes 1622024 | tf_op jit(solution)/shard_map/ppermute | solution.py:1353
  259.5 119.7 %all-gather.2.cloned.1.call-start = ((), (), s32[]{:S(2)}) async-start(), calls=%async_computation.6 | async-start | bytes 2949120 | tf_op jit(solution)/shard_map/all_gather | solution.py:1490
  284.4 18.0 %collective-permute-start.14 = (bf16[528,128]{1,0:T(8,128)(2,1)S(1)}, bf16[528,128]{1,0:T(8,128)(2,1)S(1)}, u32[]{:S(2)}, u32[]{:S(2)}) collective-permute-start(bf16[528,128]{1,0:T(8,128)(2,1)S(1)} %pad_maximum_fusion.8), channel_id=1, source_target_pairs={{0,3},{1,2},{2,1},{3,0},{4,7},{5,6},{6,5},{7,4},{8,11},{9,10},{10,... | collective-permute-start | bytes 405512 | tf_op jit(solution)/shard_map/ppermute | solution.py:1356
  288.0 16.7 %collective-permute-start.13 = (bf16[528,128]{1,0:T(8,128)(2,1)S(1)}, bf16[528,128]{1,0:T(8,128)(2,1)S(1)}, u32[]{:S(2)}, u32[]{:S(2)}) collective-permute-start(bf16[528,128]{1,0:T(8,128)(2,1)S(1)} %pad_maximum_fusion.7), channel_id=1, source_target_pairs={{0,2},{1,3},{2,0},{3,1},{4,6},{5,7},{6,4},{7,5},{8,10},{9,11},{10,... | collective-permute-start | bytes 405512 | tf_op jit(solution)/shard_map/ppermute | solution.py:1356
  288.1 16.6 %collective-permute-start.12 = (bf16[528,128]{1,0:T(8,128)(2,1)S(1)}, bf16[528,128]{1,0:T(8,128)(2,1)}, u32[]{:S(2)}, u32[]{:S(2)}) collective-permute-start(bf16[528,128]{1,0:T(8,128)(2,1)S(1)} %pad_maximum_fusion.6), channel_id=1, source_target_pairs={{0,1},{1,0},{2,3},{3,2},{4,5},{5,4},{6,7},{7,6},{8,9},{9,8},{10,11... | collective-permute-start | bytes 405512 | tf_op jit(solution)/shard_map/ppermute | solution.py:1356
  302.3 18.3 %copy-start.12 = (bf16[3328,128]{1,0:T(8,128)(2,1)S(1)}, bf16[3328,128]{1,0:T(8,128)(2,1)}, u32[]{:S(2)}) copy-start(bf16[3328,128]{1,0:T(8,128)(2,1)} %get-tuple-element.264) | copy-start | bytes 2555908
  304.7 14.3 %collective-permute-start.15 = (bf16[3328,128]{1,0:T(8,128)(2,1)}, bf16[3328,128]{1,0:T(8,128)(2,1)}, u32[]{:S(2)}, u32[]{:S(2)}) collective-permute-start(bf16[3328,128]{1,0:T(8,128)(2,1)} %get-tuple-element.265), channel_id=1, source_target_pairs={{0,4},{4,0},{8,12},{12,8},{16,20},{20,16},{24,28},{28,24},{1,5},{5... | collective-permute-start | bytes 2555912 | tf_op jit(solution)/shard_map/ppermute | solution.py:1350
  305.7 7.8 %collective-permute-start.16 = (bf16[528,128]{1,0:T(8,128)(2,1)S(1)}, bf16[528,128]{1,0:T(8,128)(2,1)S(1)}, u32[]{:S(2)}, u32[]{:S(2)}) collective-permute-start(bf16[528,128]{1,0:T(8,128)(2,1)S(1)} %get-tuple-element.299), channel_id=1, source_target_pairs={{0,1},{1,0},{2,3},{3,2},{4,5},{5,4},{6,7},{7,6},{8,9},{9,8},{10,11... | collective-permute-start | bytes 405512 | tf_op jit(solution)/shard_map/ppermute | solution.py:1356
  305.8 13.2 %collective-permute-start.17 = (bf16[528,128]{1,0:T(8,128)(2,1)S(1)}, bf16[528,128]{1,0:T(8,128)(2,1)S(1)}, u32[]{:S(2)}, u32[]{:S(2)}) collective-permute-start(bf16[528,128]{1,0:T(8,128)(2,1)S(1)} %get-tuple-element.299), channel_id=1, source_target_pairs={{0,2},{1,3},{2,0},{3,1},{4,6},{5,7},{6,4},{7,5},{8,10},{9,11},{10,... | collective-permute-start | bytes 405512 | tf_op jit(solution)/shard_map/ppermute | solution.py:1356
  307.8 11.1 %collective-permute-start.18 = (bf16[528,128]{1,0:T(8,128)(2,1)S(1)}, bf16[528,128]{1,0:T(8,128)(2,1)S(1)}, u32[]{:S(2)}, u32[]{:S(2)}) collective-permute-start(bf16[528,128]{1,0:T(8,128)(2,1)S(1)} %get-tuple-element.299), channel_id=1, source_target_pairs={{0,3},{1,2},{2,1},{3,0},{4,7},{5,6},{6,5},{7,4},{8,11},{9,10},{10,... | collective-permute-start | bytes 405512 | tf_op jit(solution)/shard_map/ppermute | solution.py:1356
  319.0 28.3 %collective-permute-start.22 = (bf16[2112,128]{1,0:T(8,128)(2,1)S(1)}, bf16[2112,128]{1,0:T(8,128)(2,1)S(1)}, u32[]{:S(2)}, u32[]{:S(2)}) collective-permute-start(bf16[2112,128]{1,0:T(8,128)(2,1)S(1)} %pad_maximum_fusion.4), channel_id=1, source_target_pairs={{0,8},{4,20},{8,0},{12,28},{16,24},{20,4},{24,16},{28,12},{1,9},{5... | collective-permute-start | bytes 1622024 | tf_op jit(solution)/shard_map/ppermute | solution.py:1382
  322.1 19.3 %collective-permute-start.19 = (bf16[832,128]{1,0:T(8,128)(2,1)S(1)}, bf16[832,128]{1,0:T(8,128)(2,1)S(1)}, u32[]{:S(2)}, u32[]{:S(2)}) collective-permute-start(bf16[832,128]{1,0:T(8,128)(2,1)S(1)} %get-tuple-element.306), channel_id=1, source_target_pairs={{0,8},{4,12},{8,0},{12,4},{16,24},{20,28},{24,16},{28,20},{1,9},{5... | collective-permute-start | bytes 638984 | tf_op jit(solution)/shard_map/ppermute | solution.py:1353
  322.6 18.8 %collective-permute-start.20 = (bf16[832,128]{1,0:T(8,128)(2,1)S(1)}, bf16[832,128]{1,0:T(8,128)(2,1)S(1)}, u32[]{:S(2)}, u32[]{:S(2)}) collective-permute-start(bf16[832,128]{1,0:T(8,128)(2,1)S(1)} %get-tuple-element.305), channel_id=1, source_target_pairs={{0,16},{4,20},{8,24},{12,28},{16,0},{20,4},{24,8},{28,12},{1,17},{... | collective-permute-start | bytes 638984 | tf_op jit(solution)/shard_map/ppermute | solution.py:1353
  324.1 23.2 %collective-permute-start.21 = (bf16[832,128]{1,0:T(8,128)(2,1)S(1)}, bf16[832,128]{1,0:T(8,128)(2,1)S(1)}, u32[]{:S(2)}, u32[]{:S(2)}) collective-permute-start(bf16[832,128]{1,0:T(8,128)(2,1)S(1)} %get-tuple-element.304), channel_id=1, source_target_pairs={{0,24},{4,28},{8,16},{12,20},{16,8},{20,12},{24,0},{28,4},{1,25},{... | collective-permute-start | bytes 638984 | tf_op jit(solution)/shard_map/ppermute | solution.py:1353
  347.4 15.2 %collective-permute-start.26 = (bf16[4224,128]{1,0:T(8,128)(2,1)S(1)}, bf16[4224,128]{1,0:T(8,128)(2,1)S(1)}, u32[]{:S(2)}, u32[]{:S(2)}) collective-permute-start(bf16[4224,128]{1,0:T(8,128)(2,1)S(1)} %get-tuple-element.312), channel_id=1, source_target_pairs={{0,16},{4,12},{8,24},{12,4},{16,0},{20,28},{24,8},{28,20},{1,17},{... | collective-permute-start | bytes 3244040 | tf_op jit(solution)/shard_map/ppermute | solution.py:1382
  347.7 7.1 %collective-permute-start.23 = (bf16[208,128]{1,0:T(8,128)(2,1)S(1)}, bf16[208,128]{1,0:T(8,128)(2,1)S(1)}, u32[]{:S(2)}, u32[]{:S(2)}) collective-permute-start(bf16[208,128]{1,0:T(8,128)(2,1)S(1)} %get-tuple-element.319), channel_id=1, source_target_pairs={{0,1},{1,0},{2,3},{3,2},{4,5},{5,4},{6,7},{7,6},{8,9},{9,8},{10,11... | collective-permute-start | bytes 159752 | tf_op jit(solution)/shard_map/ppermute | solution.py:1356
  352.3 5.1 %collective-permute-start.24 = (bf16[208,128]{1,0:T(8,128)(2,1)S(1)}, bf16[208,128]{1,0:T(8,128)(2,1)S(1)}, u32[]{:S(2)}, u32[]{:S(2)}) collective-permute-start(bf16[208,128]{1,0:T(8,128)(2,1)S(1)} %get-tuple-element.318), channel_id=1, source_target_pairs={{0,2},{1,3},{2,0},{3,1},{4,6},{5,7},{6,4},{7,5},{8,10},{9,11},{10,... | collective-permute-start | bytes 159752 | tf_op jit(solution)/shard_map/ppermute | solution.py:1356
  352.3 6.0 %collective-permute-start.25 = (bf16[208,128]{1,0:T(8,128)(2,1)S(1)}, bf16[208,128]{1,0:T(8,128)(2,1)S(1)}, u32[]{:S(2)}, u32[]{:S(2)}) collective-permute-start(bf16[208,128]{1,0:T(8,128)(2,1)S(1)} %get-tuple-element.317), channel_id=1, source_target_pairs={{0,3},{1,2},{2,1},{3,0},{4,7},{5,6},{6,5},{7,4},{8,11},{9,10},{10,... | collective-permute-start | bytes 159752 | tf_op jit(solution)/shard_map/ppermute | solution.py:1356
  362.6 25.4 %copy-start.5 = (bf16[128,4608]{1,0:T(8,128)(2,1)S(1)}, bf16[128,4608]{1,0:T(8,128)(2,1)}, u32[]{:S(2)}) copy-start(bf16[128,4608]{1,0:T(8,128)(2,1)} %get-tuple-element.286) | copy-start | bytes 3538948
  362.8 27.6 %copy-start = (bf16[8448,128]{1,0:T(8,128)(2,1)}, bf16[8448,128]{1,0:T(8,128)(2,1)S(1)}, u32[]{:S(2)}) copy-start(bf16[8448,128]{1,0:T(8,128)(2,1)S(1)} %constant_dynamic-update-slice_fusion.5.refs_3_) | copy-start | bytes 6488068
  362.8 12.2 %collective-permute-start.30 = (bf16[8448,128]{1,0:T(8,128)(2,1)S(1)}, bf16[8448,128]{1,0:T(8,128)(2,1)}, u32[]{:S(2)}, u32[]{:S(2)}) collective-permute-start(bf16[8448,128]{1,0:T(8,128)(2,1)S(1)} %constant_dynamic-update-slice_fusion.5.refs_3_), channel_id=1, source_target_pairs={{0,4},{4,0},{8,12},{12,8},{16,20},{20,16},{24,28},{28,24},{1,5},{5... | collective-permute-start | bytes 6488072 | tf_op jit(solution)/shard_map/ppermute | solution.py:1350
  363.5 6.7 %collective-permute-start.27 = (bf16[208,128]{1,0:T(8,128)(2,1)S(1)}, bf16[208,128]{1,0:T(8,128)(2,1)S(1)}, u32[]{:S(2)}, u32[]{:S(2)}) collective-permute-start(bf16[208,128]{1,0:T(8,128)(2,1)S(1)} %get-tuple-element.297), channel_id=1, source_target_pairs={{0,1},{1,0},{2,3},{3,2},{4,5},{5,4},{6,7},{7,6},{8,9},{9,8},{10,11... | collective-permute-start | bytes 159752 | tf_op jit(solution)/shard_map/ppermute | solution.py:1356
  367.7 7.3 %collective-permute-start.28 = (bf16[208,128]{1,0:T(8,128)(2,1)S(1)}, bf16[208,128]{1,0:T(8,128)(2,1)S(1)}, u32[]{:S(2)}, u32[]{:S(2)}) collective-permute-start(bf16[208,128]{1,0:T(8,128)(2,1)S(1)} %get-tuple-element.297), channel_id=1, source_target_pairs={{0,2},{1,3},{2,0},{3,1},{4,6},{5,7},{6,4},{7,5},{8,10},{9,11},{10,... | collective-permute-start | bytes 159752 | tf_op jit(solution)/shard_map/ppermute | solution.py:1356
  367.8 7.2 %collective-permute-start.29 = (bf16[208,128]{1,0:T(8,128)(2,1)S(1)}, bf16[208,128]{1,0:T(8,128)(2,1)S(1)}, u32[]{:S(2)}, u32[]{:S(2)}) collective-permute-start(bf16[208,128]{1,0:T(8,128)(2,1)S(1)} %get-tuple-element.297), channel_id=1, source_target_pairs={{0,3},{1,2},{2,1},{3,0},{4,7},{5,6},{6,5},{7,4},{8,11},{9,10},{10,... | collective-permute-start | bytes 159752 | tf_op jit(solution)/shard_map/ppermute | solution.py:1356
  375.7 8.4 %collective-permute-start.31 = (bf16[832,128]{1,0:T(8,128)(2,1)}, bf16[832,128]{1,0:T(8,128)(2,1)S(1)}, u32[]{:S(2)}, u32[]{:S(2)}) collective-permute-start(bf16[832,128]{1,0:T(8,128)(2,1)} %pad_maximum_fusion.5), channel_id=1, source_target_pairs={{0,8},{4,12},{8,0},{12,4},{16,24},{20,28},{24,16},{28,20},{1,9},{5... | collective-permute-start | bytes 638984 | tf_op jit(solution)/shard_map/ppermute | solution.py:1353
  376.5 11.5 %collective-permute-start.32 = (bf16[832,128]{1,0:T(8,128)(2,1)}, bf16[832,128]{1,0:T(8,128)(2,1)}, u32[]{:S(2)}, u32[]{:S(2)}) collective-permute-start(bf16[832,128]{1,0:T(8,128)(2,1)} %pad_maximum_fusion.5), channel_id=1, source_target_pairs={{0,16},{4,20},{8,24},{12,28},{16,0},{20,4},{24,8},{28,12},{1,17},{... | collective-permute-start | bytes 638984 | tf_op jit(solution)/shard_map/ppermute | solution.py:1353
  378.0 10.0 %collective-permute-start.33 = (bf16[832,128]{1,0:T(8,128)(2,1)}, bf16[832,128]{1,0:T(8,128)(2,1)}, u32[]{:S(2)}, u32[]{:S(2)}) collective-permute-start(bf16[832,128]{1,0:T(8,128)(2,1)} %pad_maximum_fusion.5), channel_id=1, source_target_pairs={{0,24},{4,28},{8,16},{12,20},{16,8},{20,12},{24,0},{28,4},{1,25},{... | collective-permute-start | bytes 638984 | tf_op jit(solution)/shard_map/ppermute | solution.py:1353
  390.4 31.8 %all-to-all-start.2 = ((bf16[2,64,4608]{2,0,1:T(2,128)(2,1)}), bf16[2,64,4608]{2,0,1:T(2,128)(2,1)S(1)}, u32[]{:S(2)}, u32[]{:S(2)}) async-start(bf16[2,64,4608]{2,0,1:T(2,128)(2,1)} %copy.34), calls=%async_computation.3 | async-start | bytes 2359296 | tf_op jit(solution)/shard_map/all_to_all | solution.py:1455
  396.1 2.4 collective-permute-start.34
  (17 other events, 57.1 us)
Sparse Core Ops, SparseCore 0:
  182.0 42.7 reduce-scatter.1
  259.7 41.9 all-reduce.1
  310.3 34.4 all-gather.1

commit v3 on v2

--- a/solution.py
+++ b/solution.py
@@ -141,10 +141,8 @@
 
 
 def make_heads(scr):
-    shape = (256, 256)
-    scr.head[...] = jnp.where((iota(shape, 0) >> 4) == (iota(shape, 1) & 15), 1.0, 0.0).astype(BF)
     shape = (16, 256)
-    scr.pick[...] = jnp.where(iota(shape, 0) == (iota(shape, 1) >> 4), 1.0, 0.0).astype(BF)
+    scr.head[...] = jnp.where(iota(shape, 0) == (iota(shape, 1) >> 4), 1.0, 0.0)
 
 
 def node_norm(v):
@@ -185,7 +183,12 @@
 
 
 def expand(values, scr):
-    return tn(values, scr.pick[...]).astype(BF) * scr.head[...]
+    spread = values.astype(F32)[:, None, :] * scr.head[...][None]
+    return spread.reshape(256, 256).astype(BF)
+
+
+def collect(values, scr):
+    return jnp.sum(values.reshape(16, 16, 256) * scr.head[...][None], axis=1)
 
 
 def joined(ref, pair_rows, half):
@@ -221,7 +224,7 @@
             for half in range(2):
                 kb = expand(res.qkv[keys, side(512, half)], scr)
                 scr.vbig[t0 + t, half] = expand(res.qkv[keys, side(1024, half)], scr)
-                s = nn(res.qkv[rows, side(0, half)], kb) * 0.25
+                s = nt(res.qkv[rows, side(0, half)], kb) * 0.25
                 for c in range(2):
                     scr.scores[pair_rows[c], lanes(half)] += s[:, lanes(c)]
 
@@ -260,7 +263,7 @@
                 for b in range(bucket.blocks):
                     t = g * bucket.blocks + b
                     rows, _, pair_rows = block_of(bucket, t)
-                    part = nt(joined(scr.attn, pair_rows, half), scr.vbig[t0 + t, half])
+                    part = nn(joined(scr.attn, pair_rows, half), scr.vbig[t0 + t, half])
                     sums = part if sums is None else sums + part
                 res.mixed[rows, side(0, half)] = sums.astype(BF)
 
@@ -388,7 +391,7 @@
             for half in range(2):
                 scr.vbig[t0 + t, half] = expand(res.qkv[keys, side(512, half)], scr)
                 vb = expand(res.qkv[keys, side(1024, half)], scr)
-                da = nn(io.do[rows, side(0, half)], vb)
+                da = nt(io.do[rows, side(0, half)], vb)
                 for c in range(2):
                     scr.da[pair_rows[c], lanes(half)] = da[:, lanes(c)]
 
@@ -423,13 +426,12 @@
                     t = g * bucket.blocks + b
                     rows, keys, pair_rows = block_of(bucket, t)
                     ds = joined(io.dsg, pair_rows, half)
-                    part = nt(ds, scr.vbig[t0 + t, half])
+                    part = nn(ds, scr.vbig[t0 + t, half])
                     sums = part if sums is None else sums + part
-                    gk = tn(res.qkv[rows, side(0, half)], ds).astype(BF) * scr.head[...]
-                    io.dqkv[keys, side(512, half)] = (nt(scr.pick[...], gk) * 0.25).astype(BF)
-                    gv = tn(io.do[rows, side(0, half)], joined(scr.attn, pair_rows, half))
-                    gv = gv.astype(BF) * scr.head[...]
-                    io.dqkv[keys, side(1024, half)] = nt(scr.pick[...], gv).astype(BF)
+                    gk = collect(tn(ds, res.qkv[rows, side(0, half)]), scr)
+                    io.dqkv[keys, side(512, half)] = (gk * 0.25).astype(BF)
+                    gv = tn(joined(scr.attn, pair_rows, half), io.do[rows, side(0, half)])
+                    io.dqkv[keys, side(1024, half)] = collect(gv, scr).astype(BF)
                 io.dqkv[rows, side(0, half)] = (sums * 0.25).astype(BF)
 
         t0 += bucket.graphs * bucket.blocks
@@ -623,7 +625,7 @@
 
 
 def head_shapes():
-    return {"head": ((256, 256), BF), "pick": ((16, 256), BF)}
+    return {"head": ((16, 256), F32)}
 
 
 def mask_shapes():
@@ -1113,7 +1115,7 @@
 
 def adam(n_row, lower, owner, segment_rows, scales, whole_upper, blocks, master, first, second):
     held = master.shape[0]
-    step = 1040
+    step = 2080
     front = step + 16
     count = len(blocks)
     n_dp = owner.shape[0]
@@ -1308,9 +1310,9 @@
             even, odd = odd, even
         return me ^ jnp.where(me & 1 == 0, even, odd) ^ other
 
-    def gather(self, value, also):
+    def gather(self, value, meanwhile):
         steps = range(self.bits - 1)
-        new, done = [((), value)], []
+        new, done, also = [((), value)], [], None
         while new:
             sent = []
             for used, v in new:
@@ -1320,7 +1322,13 @@
                         sent.append((0, used + (step,), lax.ppermute(v, "dp", self.pairs(step))))
             for used, v in new:
                 sent.append((1, used, lax.ppermute(v, "dp", self.core_pairs())))
-            moved, also = lax.optimization_barrier(([v for _, _, v in sent], also))
+            beside = None
+            if also is None:
+                also = meanwhile(lax.ppermute(value[:16], "dp", self.core_pairs()))
+            else:
+                beside = also
+            moved, beside = lax.optimization_barrier(([v for _, _, v in sent], beside))
+            also = also if beside is None else beside
             new = []
             for (other, used, _), v in zip(sent, moved):
                 if other:
@@ -1455,11 +1463,13 @@
         v = lax.all_to_all(v, "row", split_axis=1, concat_axis=0, tiled=True)
         return v[..., EDGE_LANES:], v[..., :EDGE_LANES]
 
-    own = shifted_segment(owner, segment_rows, master)
-    own, big = lax.optimization_barrier((own, (big_edges, big_edge_cot, big_nodes, big_node_cot)))
-    big = jnp.concatenate(big, axis=2)
-    big = flat2(lax.all_to_all(big, "row", split_axis=0, concat_axis=1, tiled=True))
-    held, big = cube.gather(own, big)
+    def to_whole(first):
+        big = (big_edges, big_edge_cot, big_nodes, big_node_cot)
+        _, big = lax.optimization_barrier((first, big))
+        big = jnp.concatenate(big, axis=2)
+        return flat2(lax.all_to_all(big, "row", split_axis=0, concat_axis=1, tiled=True))
+
+    held, big = cube.gather(shifted_segment(owner, segment_rows, master), to_whole)
     one, two = assemble(cube, owner, segment_rows, [v for _, v in held], [k for k, _ in held])
 
     own_counts = lax.dynamic_slice_in_dim(big_counts, lax.axis_index("row") * share, share)
@@ -1475,24 +1485,26 @@
     got = between(dm, two, one, kept_two, kept, ffn_two, edge_cot)
     outs = to_rows(bout)
     names = tuple(k for k in vars(got))
-    *values, bno, beo = phase([], *take(got, names), *outs)
+    spread, *values, bno, beo = phase([], spread, *take(got, names), *outs)
+    spread = lax.psum(spread, "row")
     got = Group(names, values)
     middle = Chain(cube, False, (got.keep, got.send), (got.two_keep, got.two_send))
     names = tuple(edge_shapes(dm))
     edge_one = call_edges(dm, one, kept, got, got.edges_grad)
-    spread, *edge = phase([middle], spread, *take(edge_one, names))
-    edge_one = Group(names, edge)
-    spread = lax.psum(spread, "row")
+    edge_one = Group(names, phase([middle], *take(edge_one, names)))
     names = tuple(attention_shapes(dm))
     att_one = Group(names, phase([middle], *take(call_attention(dm, kept, got, edge_one), names)))
     sng, seg, bgrad, keep, send = call_last(dm, one, kept, got, edge_one, att_one)
     spread, sng, seg, bgrad, keep, send = phase([middle], spread, sng, seg, bgrad, keep, send)
     upper_two = lax.all_gather(spread, "dp", axis=0, tiled=True)
     last = Chain(cube, True, (keep, send))
-    for _ in range(4):
-        phase([last, middle])
-    bgrad, upper_two = phase([last, middle], bgrad, upper_two)
-    bng, beg = to_rows(bgrad)
+    bgrad, = phase([last, middle], bgrad)
+    outs = to_rows(bgrad)
+    phase([last, middle])
+    sent = middle.launch()
+    phase([last])
+    sent, bng, beg, upper_two = phase([last], sent, *outs, upper_two)
+    middle.land(sent)
     while not (last.done and middle.done):
         phase([last, middle])
     blocks = last.blocks((0, 0)) + middle.blocks((0, 1), (1, 0))

time: 438 us -> 391 us (0.89)
  Pallas kernels: 188 us -> 163 us
  waiting for transfers between devices: 146 us -> 123 us
    all_to_all x1, waiting for transfers between devices: 50.8 us -> 13.1 us  [to_whole(): lax.all_to_all(big, 'row', split_axis=0, concat_axis=1, tiled=True)]
    ppermute x3, waiting for transfers between devices: 24.6 us -> 48.6 us  [gather(): sent.append((0, used + (step,), lax.ppermute(v, 'dp', self.pairs(step))))]
    pallas_call x6, Pallas kernels: 154 us -> 131 us  [kernel(): pl.pallas_call(body, out_shape=structs(out), in_specs=[SMEM] * len(smem)...]
    all_to_all x2, waiting for transfers between devices: 5.44 us -> 0.01 us  [to_rows(): v = lax.all_to_all(v, 'row', split_axis=1, concat_axis=0, tiled=True)]
    unnamed x58 -> x48, local copies, waits for them, and re-layouts: 7.08 us -> 9.42 us
  transfers between devices with their start and end apart: 41 -> 41, of which waited for: 19 -> 18; matrix products, arithmetic and copies ran while one was open for 3% -> 6% of each run, Pallas kernels for 26% -> 20%
where the time goes in v3:
time: 391 us; the launch traced here: 384 us
  Pallas kernels  163 us (42%)
  waiting for transfers between devices  123 us (31%)
  starting transfers between devices  54.4 us (14%)
  local copies, waits for them, and re-layouts  20.7 us (5%)
  between operations  15.5 us (4%)
  other arithmetic  7.71 us (2%)
    pallas_call x6, Pallas kernels, kernel(): pl.pallas_call(body, out_shape=structs(out), in_specs=[SMEM] * len(smem)...  131 us
    ppermute x3, waiting for transfers between devices, gather(): sent.append((0, used + (step,), lax.ppermute(v, 'dp', self.pairs(step))))  48.6 us
    ppermute x9, waiting for transfers between devices, to_chip(): lax.ppermute(value, 'dp', [(i, i ^ k << 1) for i in range(2 * self.sides)])  35.5 us
    ppermute x12, waiting for transfers between devices, to_row(): return lax.ppermute(value, 'row', [(i, i ^ k) for i in range(self.rows)])  21.5 us
    ppermute x12, starting transfers between devices, to_row(): return lax.ppermute(value, 'row', [(i, i ^ k) for i in range(self.rows)])  18.9 us
    pallas_call x1, Pallas kernels, adam(): pl.pallas_call(body, grid=(pl.cdiv(held, step),), out_shape=[shape] * 3 +...  15.6 us
    all_to_all x1, waiting for transfers between devices, to_whole(): lax.all_to_all(big, 'row', split_axis=0, concat_axis=1, tiled=True)  13.1 us
    ppermute x9, starting transfers between devices, to_chip(): lax.ppermute(value, 'dp', [(i, i ^ k << 1) for i in range(2 * self.sides)])  10.7 us
  transfers between devices with their start and end apart: 41, of which 18 were waited for; matrix products, arithmetic and copies ran while one was open for 6% of the time, Pallas kernels for 20%

profile of v3, /device:TPU:0, one launch (start us, length us, event | category | flops | bytes accessed | tf_op | source)
XLA Modules:
  0.0 384.4 jit_solution(13589685188152276344)
XLA Ops:
  7.2 5.9 %shard_map.247.refs_0_ = bf16[8320,128]{1,0:T(8,128)(2,1)} custom-call(s32[8]{0:T(128)} %owner_ref.5, s32[8]{0:T(128)} %rows_ref.5, f32[8290,128]{1,0:T(8,128)} %refs_5_.1), custom_call_target="tpu_custom_call" | custom-call | tf_op jit(solution)/shard_map/pallas_call | solution.py:1018
  13.1 2.9 collective-permute-start
  16.1 1.5 collective-permute-start.1
  17.6 1.5 pad_maximum_fusion
  19.1 4.9 %all-to-all-start = ((bf16[8,16,9216]{2,1,0:T(8,128)(2,1)}), bf16[8,16,9216]{2,1,0:T(8,128)(2,1)S(1)}, u32[]{:S(2)}, u32[]{:S(2)}) async-start(bf16[8,16,9216]{2,1,0:T(8,128)(2,1)} %pad_maximum_fusion), calls=%async_computation | async-start | bytes 4718592 | tf_op jit(solution)/shard_map/all_to_all | solution.py:1470
  24.0 39.0 %collective-permute-done.refs_2_ = bf16[8320,128]{1,0:T(8,128)(2,1)} collective-permute-done((bf16[8320,128]{1,0:T(8,128)(2,1)}, bf16[8320,128]{1,0:T(8,128)(2,1)}, u32[]{:S(2)}, u32[]{:S(2)}) %collective-permute-start) | collective-permute-done | bytes 2129952 | tf_op jit(solution)/shard_map/ppermute | solution.py:1322
  63.0 1.5 collective-permute-start.3
  65.3 13.1 %all-to-all-done = bf16[8,16,9216]{2,1,0:T(8,128)(2,1)S(1)} async-done(((bf16[8,16,9216]{2,1,0:T(8,128)(2,1)}), bf16[8,16,9216]{2,1,0:T(8,128)(2,1)S(1)}, u32[]{:S(2)}, u32[]{:S(2)}) %all-to-all-start) | async-done | bytes 2359328 | tf_op jit(solution)/shard_map/all_to_all | solution.py:1470
  78.5 1.6 copy.31
  80.1 9.6 %collective-permute-done.3.refs_6_ = bf16[8320,128]{1,0:T(8,128)(2,1)} collective-permute-done((bf16[8320,128]{1,0:T(8,128)(2,1)}, bf16[8320,128]{1,0:T(8,128)(2,1)}, u32[]{:S(2)}, u32[]{:S(2)}) %collective-permute-start.3) | collective-permute-done | bytes 2129952 | tf_op jit(solution)/shard_map/ppermute | solution.py:1322
  90.4 3.7 collective-permute-done.6.refs_7_
  94.1 1.3 copy-done.3
  95.5 10.5 %shard_map.248 = (bf16[512,1536]{1,0:T(8,128)(2,1)}, bf16[512,512]{1,0:T(8,128)(2,1)}, bf16[512,1024]{1,0:T(8,128)(2,1)}, bf16[1024,512]{1,0:T(8,128)(2,1)}, bf1...) custom-call(s32[8]{0:T(128)} %owner_ref.5, ...), custom_call_target="tpu_custom_call" | custom-call | bytes 34000000 | tf_op jit(solution)/shard_map/pallas_call | solution.py:1097
  106.0 25.3 %shard_map.249 = (bf16[224,512]{1,0:T(8,128)(2,1)}, bf16[2816,256]{1,0:T(8,128)(2,1)}, bf16[224,512]{1,0:T(8,128)(2,1)}, f32[224,128]{1,0:T(8,128)}, bf16[224,15...) custom-call(s32[5]{0:T(128)} %pad_add_fusion.refs_0_, ...), custom_call_target="tpu_custom_call" | custom-call | bytes 129200000 | tf_op jit(solution)/shard_map/pallas_call | solution.py:789
  131.3 28.8 %shard_map.250 = (bf16[96,512]{1,0:T(8,128)(2,1)}, bf16[96,2048]{1,0:T(8,128)(2,1)}, bf16[128,4608]{1,0:T(8,128)(2,1)}, bf16[2816,256]{1,0:T(8,128)(2,1)}, bf16[...) custom-call(s32[5]{0:T(128)} %pad_add_fusion.refs_0_, ...), custom_call_target="tpu_custom_call" | custom-call | bytes 156400000 | tf_op jit(solution)/shard_map/pallas_call | solution.py:789
  161.3 2.3 copy.32
  163.6 5.9 %all-to-all-start.1 = ((bf16[2,64,4608]{2,0,1:T(2,128)(2,1)}), bf16[2,64,4608]{2,0,1:T(2,128)(2,1)S(1)}, u32[]{:S(2)}, u32[]{:S(2)}) async-start(bf16[2,64,4608]{2,0,1:T(2,128)(2,1)} %copy.32), calls=%async_computation.2 | async-start | bytes 2359296 | tf_op jit(solution)/shard_map/all_to_all | solution.py:1463
  169.5 37.6 %shard_map.251 = (bf16[2816,256]{1,0:T(8,128)(2,1)}, bf16[3328,128]{1,0:T(8,128)(2,1)}, bf16[3328,128]{1,0:T(8,128)(2,1)}, f32[224,512]{1,0:T(8,128)}, bf16[224,...) custom-call(bf16[512,1536]{1,0:T(8,128)(2,1)} %get-tuple-element.166.refs_1_.refs_0_,, ...), custom_call_target="tpu_custom_call" | custom-call | bytes 153000000 | tf_op jit(solution)/shard_map/pallas_call | solution.py:789
  209.5 16.7 %shard_map.252 = (bf16[2816,256]{1,0:T(8,128)(2,1)}, f32[1408,256]{1,0:T(8,128)}, f32[256,128]{1,0:T(8,128)}) custom-call(bf16[256,512]{1,0:T(8,128)(2,1)} %get-tuple-element.181.refs_6_.refs_0_, bf16[256,512]{1,0:T(8,128)(2,1)} %get-tuple-element.182.refs_7_.refs_1_, bf16[512,256]{1,0:T(8,128)(2,1)} %get-tuple-element.183.refs_8_.refs_2_, ...), custom_call_target="tpu_custom_call" | custom-call | bytes 54400000 | tf_op jit(solution)/shard_map/pallas_call | solution.py:789
  227.8 1.7 collective-permute-start.11
  231.6 8.9 %shard_map.253 = (bf16[1408,512]{1,0:T(8,128)(2,1)}, bf16[224,1536]{1,0:T(8,128)(2,1)}) custom-call(bf16[224,1536]{1,0:T(8,128)(2,1)} %get-tuple-element.235.refs_0_, bf16[1408,256]{1,0:T(8,128)(2,1)} %get-tuple-element.236.refs_1_, f32[1408,256]{1,0:T(8,128)} %get-tuple-element.237.refs_2_, bf16[224,512]{1,0:T(8,128)(2,1)} %get-tuple-element.238.refs_3_, ...), custom_call_target="tpu_custom_call" | custom-call | bytes 47600000 | tf_op jit(solution)/shard_map/pallas_call | solution.py:789
  240.6 3.4 collective-permute-done.11
  243.9 10.7 %collective-permute-done.10 = bf16[2112,128]{1,0:T(8,128)(2,1)S(1)} collective-permute-done((bf16[2112,128]{1,0:T(8,128)(2,1)S(1)}, bf16[2112,128]{1,0:T(8,128)(2,1)S(1)}, u32[]{:S(2)}, u32[]{:S(2)}) %collective-permute-start.10) | collective-permute-done | bytes 540704 | tf_op jit(solution)/shard_map/ppermute | solution.py:1361
  254.6 1.3 add_convert_fusion.3
  256.1 3.9 %collective-permute-start.14 = (bf16[528,128]{1,0:T(8,128)(2,1)S(1)}, bf16[528,128]{1,0:T(8,128)(2,1)S(1)}, u32[]{:S(2)}, u32[]{:S(2)}) collective-permute-start(bf16[528,128]{1,0:T(8,128)(2,1)S(1)} %pad_maximum_fusion.8), channel_id=1, source_target_pairs={{0,3},{1,2},{2,1},{3,0},{4,7},{5,6},{6,5},{7,4},{8,11},{9,10},{10,... | collective-permute-start | bytes 405512 | tf_op jit(solution)/shard_map/ppermute | solution.py:1364
  260.7 13.4 %shard_map.254 = (bf16[96,512]{1,0:T(8,128)(2,1)}, bf16[96,2048]{1,0:T(8,128)(2,1)}, bf16[128,4608]{1,0:T(8,128)(2,1)}, bf16[3328,128]{1,0:T(8,128)(2,1)}, bf16[3328,128]{1,0:T(8,128)(2,1)}) custom-call(bf16[512,1536]{1,0:T(8,128)(2,1)} %get-tuple-element.176.refs_1_.refs_0_, bf16[512,512]{1,0:T(8,128)(2,1)} %get-tuple-element.180.refs_5_.refs_1_, ...), custom_call_target="tpu_custom_call" | custom-call | bytes 44200000 | tf_op jit(solution)/shard_map/pallas_call | solution.py:789
  274.1 2.3 collective-permute-done.13
  277.2 2.1 collective-permute-start.17
  279.3 2.3 collective-permute-start.18
  282.3 2.8 collective-permute-done.16
  285.1 5.3 %collective-permute-done.17 = bf16[528,128]{1,0:T(8,128)(2,1)S(1)} collective-permute-done((bf16[528,128]{1,0:T(8,128)(2,1)S(1)}, bf16[528,128]{1,0:T(8,128)(2,1)S(1)}, u32[]{:S(2)}, u32[]{:S(2)}) %collective-permute-start.17) | collective-permute-done | bytes 135200 | tf_op jit(solution)/shard_map/ppermute | solution.py:1364
  290.4 1.3 collective-permute-start.22
  294.8 1.5 collective-permute-start.21
  296.3 2.2 copy.34
  298.5 4.4 %all-to-all-start.2 = ((bf16[2,64,4608]{2,0,1:T(2,128)(2,1)}), bf16[2,64,4608]{2,0,1:T(2,128)(2,1)S(1)}, u32[]{:S(2)}, u32[]{:S(2)}) async-start(bf16[2,64,4608]{2,0,1:T(2,128)(2,1)} %copy.34), calls=%async_computation.3 | async-start | bytes 2359296 | tf_op jit(solution)/shard_map/all_to_all | solution.py:1463
  305.1 8.7 %collective-permute-done.19 = bf16[832,128]{1,0:T(8,128)(2,1)} collective-permute-done((bf16[832,128]{1,0:T(8,128)(2,1)}, bf16[832,128]{1,0:T(8,128)(2,1)}, u32[]{:S(2)}, u32[]{:S(2)}) %collective-permute-start.19) | collective-permute-done | bytes 213024 | tf_op jit(solution)/shard_map/ppermute | solution.py:1361
  313.8 3.0 collective-permute-done.21
  319.9 3.1 collective-permute-start.23
  323.0 1.7 collective-permute-start.24
  325.6 8.6 %collective-permute-done.24 = bf16[208,128]{1,0:T(8,128)(2,1)S(1)} collective-permute-done((bf16[208,128]{1,0:T(8,128)(2,1)S(1)}, bf16[208,128]{1,0:T(8,128)(2,1)S(1)}, u32[]{:S(2)}, u32[]{:S(2)}) %collective-permute-start.24) | collective-permute-done | bytes 53280 | tf_op jit(solution)/shard_map/ppermute | solution.py:1364
  336.0 1.6 collective-permute-start.27
  337.6 1.7 collective-permute-start.28
  341.6 1.9 collective-permute-done.28
  343.8 1.5 collective-permute-start.30
  345.9 1.4 collective-permute-start.32
  347.4 4.5 %collective-permute-done.30 = bf16[832,128]{1,0:T(8,128)(2,1)S(1)} collective-permute-done((bf16[832,128]{1,0:T(8,128)(2,1)S(1)}, bf16[832,128]{1,0:T(8,128)(2,1)S(1)}, u32[]{:S(2)}, u32[]{:S(2)}) %collective-permute-start.30) | collective-permute-done | bytes 213024 | tf_op jit(solution)/shard_map/ppermute | solution.py:1361
  351.9 5.3 %collective-permute-done.31 = bf16[832,128]{1,0:T(8,128)(2,1)S(1)} collective-permute-done((bf16[832,128]{1,0:T(8,128)(2,1)S(1)}, bf16[832,128]{1,0:T(8,128)(2,1)S(1)}, u32[]{:S(2)}, u32[]{:S(2)}) %collective-permute-start.31) | collective-permute-done | bytes 213024 | tf_op jit(solution)/shard_map/ppermute | solution.py:1361
  361.8 15.6 %shard_map.255 = (f32[8290,128]{1,0:T(8,128)}, f32[8290,128]{1,0:T(8,128)}, f32[8290,128]{1,0:T(8,128)}, f32[8,576]{1,0:T(8,128)}) custom-call(s32[8]{0:T(128)} %owner_ref.5, s32[8]{0:T(128)} %rows_ref.5, f32[2]{0:T(128)} %pad_maximum_fusion.9.scale_ref, bf16[10240,128]{1,0:T(8,128)(2,1)} %all-gather.2.cloned.1.call-done.refs_0_, ...), custom_call_target="tpu_custom_call" | custom-call | bytes 34000000 | tf_op jit(solution)/shard_map/pallas_call | solution.py:1261
  (132 shorter events, 29.2 us)
Async XLA Ops:
  7.2 10.4 %copy-start.15 = (bf16[8,16,512]{2,1,0:T(8,128)(2,1)S(1)}, bf16[8,16,512]{2,1,0:T(8,128)(2,1)}, u32[]{:S(2)}) copy-start(bf16[8,16,512]{2,1,0:T(8,128)(2,1)} %param.19) | copy-start | bytes 393220
  7.2 10.4 %copy-start.8 = (bf16[8,16,4096]{2,1,0:T(8,128)(2,1)S(1)}, bf16[8,16,4096]{2,1,0:T(8,128)(2,1)}, u32[]{:S(2)}) copy-start(bf16[8,16,4096]{2,1,0:T(8,128)(2,1)} %param.20) | copy-start | bytes 3145732
  13.1 49.9 %collective-permute-start = (bf16[8320,128]{1,0:T(8,128)(2,1)}, bf16[8320,128]{1,0:T(8,128)(2,1)}, u32[]{:S(2)}, u32[]{:S(2)}) collective-permute-start(bf16[8320,128]{1,0:T(8,128)(2,1)} %shard_map.247.refs_0_), channel_id=1, source_target_pairs={{0,8},{4,20},{8,0},{12,28},{16,24},{20,4},{24,16},{28,12},{1,9},{5... | collective-permute-start | bytes 6389768 | tf_op jit(solution)/shard_map/ppermute | solution.py:1322
  16.1 46.9 %collective-permute-start.1 = (bf16[8320,128]{1,0:T(8,128)(2,1)}, bf16[8320,128]{1,0:T(8,128)(2,1)}, u32[]{:S(2)}, u32[]{:S(2)}) collective-permute-start(bf16[8320,128]{1,0:T(8,128)(2,1)} %shard_map.247.refs_0_), channel_id=1, source_target_pairs={{0,16},{4,12},{8,24},{12,4},{16,0},{20,28},{24,8},{28,20},{1,17},{... | collective-permute-start | bytes 6389768 | tf_op jit(solution)/shard_map/ppermute | solution.py:1322
  17.6 45.4 %collective-permute-start.2 = (bf16[8320,128]{1,0:T(8,128)(2,1)}, bf16[8320,128]{1,0:T(8,128)(2,1)}, u32[]{:S(2)}, u32[]{:S(2)}) collective-permute-start(bf16[8320,128]{1,0:T(8,128)(2,1)} %shard_map.247.refs_0_), channel_id=1, source_target_pairs={{0,4},{4,0},{8,12},{12,8},{16,20},{20,16},{24,28},{28,24},{1,5},{5... | collective-permute-start | bytes 6389768 | tf_op jit(solution)/shard_map/ppermute | solution.py:1324
  19.1 59.3 %all-to-all-start = ((bf16[8,16,9216]{2,1,0:T(8,128)(2,1)}), bf16[8,16,9216]{2,1,0:T(8,128)(2,1)S(1)}, u32[]{:S(2)}, u32[]{:S(2)}) async-start(bf16[8,16,9216]{2,1,0:T(8,128)(2,1)} %pad_maximum_fusion), calls=%async_computation | async-start | bytes 4718592 | tf_op jit(solution)/shard_map/all_to_all | solution.py:1470
  24.0 185.0 %reduce-scatter.2.cloned.1.call-start = ((), (), s32[]{:S(2)}) async-start(), calls=%async_computation.4 | async-start | bytes 2949120 | tf_op jit(solution)/shard_map/reduce_scatter | solution.py:1484
  63.0 26.7 %collective-permute-start.3 = (bf16[8320,128]{1,0:T(8,128)(2,1)}, bf16[8320,128]{1,0:T(8,128)(2,1)}, u32[]{:S(2)}, u32[]{:S(2)}) collective-permute-start(bf16[8320,128]{1,0:T(8,128)(2,1)} %collective-permute-done.refs_2_), channel_id=1, source_target_pairs={{0,16},{4,12},{8,24},{12,4},{16,0},{20,28},{24,8},{28,20},{1,17},{... | collective-permute-start | bytes 6389768 | tf_op jit(solution)/shard_map/ppermute | solution.py:1322
  64.5 25.2 %collective-permute-start.4 = (bf16[8320,128]{1,0:T(8,128)(2,1)}, bf16[8320,128]{1,0:T(8,128)(2,1)}, u32[]{:S(2)}, u32[]{:S(2)}) collective-permute-start(bf16[8320,128]{1,0:T(8,128)(2,1)} %collective-permute-done.refs_2_), channel_id=1, source_target_pairs={{0,4},{4,0},{8,12},{12,8},{16,20},{20,16},{24,28},{28,24},{1,5},{5... | collective-permute-start | bytes 6389768 | tf_op jit(solution)/shard_map/ppermute | solution.py:1324
  65.3 24.4 %collective-permute-start.5 = (bf16[8320,128]{1,0:T(8,128)(2,1)}, bf16[8320,128]{1,0:T(8,128)(2,1)}, u32[]{:S(2)}, u32[]{:S(2)}) collective-permute-start(bf16[8320,128]{1,0:T(8,128)(2,1)} %collective-permute-done.1.refs_3_), channel_id=1, source_target_pairs={{0,4},{4,0},{8,12},{12,8},{16,20},{20,16},{24,28},{28,24},{1,5},{5... | collective-permute-start | bytes 6389768 | tf_op jit(solution)/shard_map/ppermute | solution.py:1324
  78.5 11.3 %copy-start.17 = (s32[8]{0:T(128)S(1)}, s32[8]{0:T(128)}, u32[]{:S(2)}) copy-start(s32[8]{0:T(128)} %param.21) | copy-start | bytes 100
  78.5 11.3 %copy-start.18 = (s32[3]{0:T(128)S(1)}, s32[3]{0:T(128)}, u32[]{:S(2)}) copy-start(s32[3]{0:T(128)} %param.18) | copy-start | bytes 40
  89.7 4.4 %collective-permute-start.6 = (bf16[8320,128]{1,0:T(8,128)(2,1)}, bf16[8320,128]{1,0:T(8,128)(2,1)S(1)}, u32[]{:S(2)}, u32[]{:S(2)}) collective-permute-start(bf16[8320,128]{1,0:T(8,128)(2,1)} %collective-permute-done.3.refs_6_), channel_id=1, source_target_pairs={{0,4},{4,0},{8,12},{12,8},{16,20},{20,16},{24,28},{28,24},{1,5},{5... | collective-permute-start | bytes 6389768 | tf_op jit(solution)/shard_map/ppermute | solution.py:1324
  163.6 43.4 %all-to-all-start.1 = ((bf16[2,64,4608]{2,0,1:T(2,128)(2,1)}), bf16[2,64,4608]{2,0,1:T(2,128)(2,1)S(1)}, u32[]{:S(2)}, u32[]{:S(2)}) async-start(bf16[2,64,4608]{2,0,1:T(2,128)(2,1)} %copy.32), calls=%async_computation.2 | async-start | bytes 2359296 | tf_op jit(solution)/shard_map/all_to_all | solution.py:1463
  169.5 104.6 %all-reduce.2.cloned.1.call-start = ((), (), s32[]{:S(2)}) async-start(), calls=%async_computation.5 | async-start | bytes 655360 | tf_op jit(solution)/shard_map/psum | solution.py:1489
  209.0 17.2 %collective-permute-start.7 = (bf16[5120,128]{1,0:T(8,128)(2,1)S(1)}, bf16[5120,128]{1,0:T(8,128)(2,1)S(1)}, u32[]{:S(2)}, u32[]{:S(2)}) collective-permute-start(bf16[5120,128]{1,0:T(8,128)(2,1)S(1)} %copy-done.16), channel_id=1, source_target_pairs={{0,4},{4,0},{8,12},{12,8},{16,20},{20,16},{24,28},{28,24},{1,5},{5... | collective-permute-start | bytes 3932168 | tf_op jit(solution)/shard_map/ppermute | solution.py:1358
  209.0 17.2 %collective-permute-start.8 = (bf16[3328,128]{1,0:T(8,128)(2,1)}, bf16[3328,128]{1,0:T(8,128)(2,1)S(1)}, u32[]{:S(2)}, u32[]{:S(2)}) collective-permute-start(bf16[3328,128]{1,0:T(8,128)(2,1)} %get-tuple-element.223), channel_id=1, source_target_pairs={{0,4},{4,0},{8,12},{12,8},{16,20},{20,16},{24,28},{28,24},{1,5},{5... | collective-permute-start | bytes 2555912 | tf_op jit(solution)/shard_map/ppermute | solution.py:1358
  209.5 16.7 %copy-start.4 = (bf16[5120,128]{1,0:T(8,128)(2,1)S(1)}, bf16[5120,128]{1,0:T(8,128)(2,1)}, u32[]{:S(2)}) copy-start(bf16[5120,128]{1,0:T(8,128)(2,1)} %get-tuple-element.221) | copy-start | bytes 3932164
  227.8 16.1 %collective-permute-start.11 = (bf16[2112,128]{1,0:T(8,128)(2,1)S(1)}, bf16[2112,128]{1,0:T(8,128)(2,1)S(1)}, u32[]{:S(2)}, u32[]{:S(2)}) collective-permute-start(bf16[2112,128]{1,0:T(8,128)(2,1)S(1)} %pad_maximum_fusion.3), channel_id=1, source_target_pairs={{0,24},{4,28},{8,16},{12,20},{16,8},{20,12},{24,0},{28,4},{1,25},{... | collective-permute-start | bytes 1622024 | tf_op jit(solution)/shard_map/ppermute | solution.py:1361
  229.6 25.0 %collective-permute-start.10 = (bf16[2112,128]{1,0:T(8,128)(2,1)S(1)}, bf16[2112,128]{1,0:T(8,128)(2,1)S(1)}, u32[]{:S(2)}, u32[]{:S(2)}) collective-permute-start(bf16[2112,128]{1,0:T(8,128)(2,1)S(1)} %pad_maximum_fusion.2), channel_id=1, source_target_pairs={{0,16},{4,20},{8,24},{12,28},{16,0},{20,4},{24,8},{28,12},{1,17},{... | collective-permute-start | bytes 1622024 | tf_op jit(solution)/shard_map/ppermute | solution.py:1361
  230.9 23.7 %collective-permute-start.9 = (bf16[2112,128]{1,0:T(8,128)(2,1)S(1)}, bf16[2112,128]{1,0:T(8,128)(2,1)}, u32[]{:S(2)}, u32[]{:S(2)}) collective-permute-start(bf16[2112,128]{1,0:T(8,128)(2,1)S(1)} %pad_maximum_fusion.1), channel_id=1, source_target_pairs={{0,8},{4,12},{8,0},{12,4},{16,24},{20,28},{24,16},{28,20},{1,9},{5... | collective-permute-start | bytes 1622024 | tf_op jit(solution)/shard_map/ppermute | solution.py:1361
  231.6 111.9 %all-gather.2.cloned.1.call-start = ((), (), s32[]{:S(2)}) async-start(), calls=%async_computation.6 | async-start | bytes 2949120 | tf_op jit(solution)/shard_map/all_gather | solution.py:1499
  256.1 18.0 %collective-permute-start.14 = (bf16[528,128]{1,0:T(8,128)(2,1)S(1)}, bf16[528,128]{1,0:T(8,128)(2,1)S(1)}, u32[]{:S(2)}, u32[]{:S(2)}) collective-permute-start(bf16[528,128]{1,0:T(8,128)(2,1)S(1)} %pad_maximum_fusion.8), channel_id=1, source_target_pairs={{0,3},{1,2},{2,1},{3,0},{4,7},{5,6},{6,5},{7,4},{8,11},{9,10},{10,... | collective-permute-start | bytes 405512 | tf_op jit(solution)/shard_map/ppermute | solution.py:1364
  260.0 16.4 %collective-permute-start.13 = (bf16[528,128]{1,0:T(8,128)(2,1)S(1)}, bf16[528,128]{1,0:T(8,128)(2,1)S(1)}, u32[]{:S(2)}, u32[]{:S(2)}) collective-permute-start(bf16[528,128]{1,0:T(8,128)(2,1)S(1)} %pad_maximum_fusion.7), channel_id=1, source_target_pairs={{0,2},{1,3},{2,0},{3,1},{4,6},{5,7},{6,4},{7,5},{8,10},{9,11},{10,... | collective-permute-start | bytes 405512 | tf_op jit(solution)/shard_map/ppermute | solution.py:1364
  260.1 16.3 %collective-permute-start.12 = (bf16[528,128]{1,0:T(8,128)(2,1)S(1)}, bf16[528,128]{1,0:T(8,128)(2,1)S(1)}, u32[]{:S(2)}, u32[]{:S(2)}) collective-permute-start(bf16[528,128]{1,0:T(8,128)(2,1)S(1)} %pad_maximum_fusion.6), channel_id=1, source_target_pairs={{0,1},{1,0},{2,3},{3,2},{4,5},{5,4},{6,7},{7,6},{8,9},{9,8},{10,11... | collective-permute-start | bytes 405512 | tf_op jit(solution)/shard_map/ppermute | solution.py:1364
  274.1 17.7 %copy-start.12 = (bf16[3328,128]{1,0:T(8,128)(2,1)S(1)}, bf16[3328,128]{1,0:T(8,128)(2,1)}, u32[]{:S(2)}) copy-start(bf16[3328,128]{1,0:T(8,128)(2,1)} %get-tuple-element.262) | copy-start | bytes 2555908
  276.4 13.9 %collective-permute-start.15 = (bf16[3328,128]{1,0:T(8,128)(2,1)}, bf16[3328,128]{1,0:T(8,128)(2,1)S(1)}, u32[]{:S(2)}, u32[]{:S(2)}) collective-permute-start(bf16[3328,128]{1,0:T(8,128)(2,1)} %get-tuple-element.263), channel_id=1, source_target_pairs={{0,4},{4,0},{8,12},{12,8},{16,20},{20,16},{24,28},{28,24},{1,5},{5... | collective-permute-start | bytes 2555912 | tf_op jit(solution)/shard_map/ppermute | solution.py:1358
  277.2 7.8 %collective-permute-start.16 = (bf16[528,128]{1,0:T(8,128)(2,1)S(1)}, bf16[528,128]{1,0:T(8,128)(2,1)S(1)}, u32[]{:S(2)}, u32[]{:S(2)}) collective-permute-start(bf16[528,128]{1,0:T(8,128)(2,1)S(1)} %get-tuple-element.297), channel_id=1, source_target_pairs={{0,1},{1,0},{2,3},{3,2},{4,5},{5,4},{6,7},{7,6},{8,9},{9,8},{10,11... | collective-permute-start | bytes 405512 | tf_op jit(solution)/shard_map/ppermute | solution.py:1364
  277.2 13.1 %collective-permute-start.17 = (bf16[528,128]{1,0:T(8,128)(2,1)S(1)}, bf16[528,128]{1,0:T(8,128)(2,1)S(1)}, u32[]{:S(2)}, u32[]{:S(2)}) collective-permute-start(bf16[528,128]{1,0:T(8,128)(2,1)S(1)} %get-tuple-element.297), channel_id=1, source_target_pairs={{0,2},{1,3},{2,0},{3,1},{4,6},{5,7},{6,4},{7,5},{8,10},{9,11},{10,... | collective-permute-start | bytes 405512 | tf_op jit(solution)/shard_map/ppermute | solution.py:1364
  279.3 11.0 %collective-permute-start.18 = (bf16[528,128]{1,0:T(8,128)(2,1)S(1)}, bf16[528,128]{1,0:T(8,128)(2,1)S(1)}, u32[]{:S(2)}, u32[]{:S(2)}) collective-permute-start(bf16[528,128]{1,0:T(8,128)(2,1)S(1)} %get-tuple-element.297), channel_id=1, source_target_pairs={{0,3},{1,2},{2,1},{3,0},{4,7},{5,6},{6,5},{7,4},{8,11},{9,10},{10,... | collective-permute-start | bytes 405512 | tf_op jit(solution)/shard_map/ppermute | solution.py:1364
  290.4 26.4 %collective-permute-start.22 = (bf16[2112,128]{1,0:T(8,128)(2,1)S(1)}, bf16[2112,128]{1,0:T(8,128)(2,1)S(1)}, u32[]{:S(2)}, u32[]{:S(2)}) collective-permute-start(bf16[2112,128]{1,0:T(8,128)(2,1)S(1)} %pad_maximum_fusion.4), channel_id=1, source_target_pairs={{0,8},{4,20},{8,0},{12,28},{16,24},{20,4},{24,16},{28,12},{1,9},{5... | collective-permute-start | bytes 1622024 | tf_op jit(solution)/shard_map/ppermute | solution.py:1390
  292.8 21.0 %collective-permute-start.19 = (bf16[832,128]{1,0:T(8,128)(2,1)}, bf16[832,128]{1,0:T(8,128)(2,1)}, u32[]{:S(2)}, u32[]{:S(2)}) collective-permute-start(bf16[832,128]{1,0:T(8,128)(2,1)} %get-tuple-element.306), channel_id=1, source_target_pairs={{0,8},{4,12},{8,0},{12,4},{16,24},{20,28},{24,16},{28,20},{1,9},{5... | collective-permute-start | bytes 638984 | tf_op jit(solution)/shard_map/ppermute | solution.py:1361
  293.6 20.2 %collective-permute-start.20 = (bf16[832,128]{1,0:T(8,128)(2,1)}, bf16[832,128]{1,0:T(8,128)(2,1)}, u32[]{:S(2)}, u32[]{:S(2)}) collective-permute-start(bf16[832,128]{1,0:T(8,128)(2,1)} %get-tuple-element.305), channel_id=1, source_target_pairs={{0,16},{4,20},{8,24},{12,28},{16,0},{20,4},{24,8},{28,12},{1,17},{... | collective-permute-start | bytes 638984 | tf_op jit(solution)/shard_map/ppermute | solution.py:1361
  294.8 21.9 %collective-permute-start.21 = (bf16[832,128]{1,0:T(8,128)(2,1)}, bf16[832,128]{1,0:T(8,128)(2,1)}, u32[]{:S(2)}, u32[]{:S(2)}) collective-permute-start(bf16[832,128]{1,0:T(8,128)(2,1)} %get-tuple-element.304), channel_id=1, source_target_pairs={{0,24},{4,28},{8,16},{12,20},{16,8},{20,12},{24,0},{28,4},{1,25},{... | collective-permute-start | bytes 638984 | tf_op jit(solution)/shard_map/ppermute | solution.py:1361
  298.5 40.7 %all-to-all-start.2 = ((bf16[2,64,4608]{2,0,1:T(2,128)(2,1)}), bf16[2,64,4608]{2,0,1:T(2,128)(2,1)S(1)}, u32[]{:S(2)}, u32[]{:S(2)}) async-start(bf16[2,64,4608]{2,0,1:T(2,128)(2,1)} %copy.34), calls=%async_computation.3 | async-start | bytes 2359296 | tf_op jit(solution)/shard_map/all_to_all | solution.py:1463
  317.8 25.7 %collective-permute-start.29 = (bf16[4224,128]{1,0:T(8,128)(2,1)}, bf16[4224,128]{1,0:T(8,128)(2,1)S(1)}, u32[]{:S(2)}, u32[]{:S(2)}) collective-permute-start(bf16[4224,128]{1,0:T(8,128)(2,1)} %get-tuple-element.312), channel_id=1, source_target_pairs={{0,16},{4,12},{8,24},{12,4},{16,0},{20,28},{24,8},{28,20},{1,17},{... | collective-permute-start | bytes 3244040 | tf_op jit(solution)/shard_map/ppermute | solution.py:1390
  319.9 5.7 %collective-permute-start.23 = (bf16[208,128]{1,0:T(8,128)(2,1)S(1)}, bf16[208,128]{1,0:T(8,128)(2,1)S(1)}, u32[]{:S(2)}, u32[]{:S(2)}) collective-permute-start(bf16[208,128]{1,0:T(8,128)(2,1)S(1)} %get-tuple-element.319), channel_id=1, source_target_pairs={{0,1},{1,0},{2,3},{3,2},{4,5},{5,4},{6,7},{7,6},{8,9},{9,8},{10,11... | collective-permute-start | bytes 159752 | tf_op jit(solution)/shard_map/ppermute | solution.py:1364
  323.0 11.2 %collective-permute-start.24 = (bf16[208,128]{1,0:T(8,128)(2,1)S(1)}, bf16[208,128]{1,0:T(8,128)(2,1)S(1)}, u32[]{:S(2)}, u32[]{:S(2)}) collective-permute-start(bf16[208,128]{1,0:T(8,128)(2,1)S(1)} %get-tuple-element.318), channel_id=1, source_target_pairs={{0,2},{1,3},{2,0},{3,1},{4,6},{5,7},{6,4},{7,5},{8,10},{9,11},{10,... | collective-permute-start | bytes 159752 | tf_op jit(solution)/shard_map/ppermute | solution.py:1364
  324.7 9.5 %collective-permute-start.25 = (bf16[208,128]{1,0:T(8,128)(2,1)S(1)}, bf16[208,128]{1,0:T(8,128)(2,1)S(1)}, u32[]{:S(2)}, u32[]{:S(2)}) collective-permute-start(bf16[208,128]{1,0:T(8,128)(2,1)S(1)} %get-tuple-element.317), channel_id=1, source_target_pairs={{0,3},{1,2},{2,1},{3,0},{4,7},{5,6},{6,5},{7,4},{8,11},{9,10},{10,... | collective-permute-start | bytes 159752 | tf_op jit(solution)/shard_map/ppermute | solution.py:1364
  334.9 6.3 %collective-permute-start.26 = (bf16[208,128]{1,0:T(8,128)(2,1)S(1)}, bf16[208,128]{1,0:T(8,128)(2,1)S(1)}, u32[]{:S(2)}, u32[]{:S(2)}) collective-permute-start(bf16[208,128]{1,0:T(8,128)(2,1)S(1)} %get-tuple-element.299), channel_id=1, source_target_pairs={{0,1},{1,0},{2,3},{3,2},{4,5},{5,4},{6,7},{7,6},{8,9},{9,8},{10,11... | collective-permute-start | bytes 159752 | tf_op jit(solution)/shard_map/ppermute | solution.py:1364
  336.0 5.6 %collective-permute-start.27 = (bf16[208,128]{1,0:T(8,128)(2,1)S(1)}, bf16[208,128]{1,0:T(8,128)(2,1)S(1)}, u32[]{:S(2)}, u32[]{:S(2)}) collective-permute-start(bf16[208,128]{1,0:T(8,128)(2,1)S(1)} %get-tuple-element.299), channel_id=1, source_target_pairs={{0,2},{1,3},{2,0},{3,1},{4,6},{5,7},{6,4},{7,5},{8,10},{9,11},{10,... | collective-permute-start | bytes 159752 | tf_op jit(solution)/shard_map/ppermute | solution.py:1364
  337.6 5.9 %collective-permute-start.28 = (bf16[208,128]{1,0:T(8,128)(2,1)S(1)}, bf16[208,128]{1,0:T(8,128)(2,1)S(1)}, u32[]{:S(2)}, u32[]{:S(2)}) collective-permute-start(bf16[208,128]{1,0:T(8,128)(2,1)S(1)} %get-tuple-element.299), channel_id=1, source_target_pairs={{0,3},{1,2},{2,1},{3,0},{4,7},{5,6},{6,5},{7,4},{8,11},{9,10},{10,... | collective-permute-start | bytes 159752 | tf_op jit(solution)/shard_map/ppermute | solution.py:1364
  343.7 17.2 %copy-start.1 = (bf16[8448,128]{1,0:T(8,128)(2,1)}, bf16[8448,128]{1,0:T(8,128)(2,1)S(1)}, u32[]{:S(2)}) copy-start(bf16[8448,128]{1,0:T(8,128)(2,1)S(1)} %constant_dynamic-update-slice_fusion.5.refs_3_) | copy-start | bytes 6488068
  343.7 13.6 %collective-permute-start.33 = (bf16[8448,128]{1,0:T(8,128)(2,1)S(1)}, bf16[8448,128]{1,0:T(8,128)(2,1)S(1)}, u32[]{:S(2)}, u32[]{:S(2)}) collective-permute-start(bf16[8448,128]{1,0:T(8,128)(2,1)S(1)} %constant_dynamic-update-slice_fusion.5.refs_3_), channel_id=1, source_target_pairs={{0,4},{4,0},{8,12},{12,8},{16,20},{20,16},{24,28},{28,24},{1,5},{5... | collective-permute-start | bytes 6488072 | tf_op jit(solution)/shard_map/ppermute | solution.py:1358
  343.8 8.1 %collective-permute-start.30 = (bf16[832,128]{1,0:T(8,128)(2,1)S(1)}, bf16[832,128]{1,0:T(8,128)(2,1)S(1)}, u32[]{:S(2)}, u32[]{:S(2)}) collective-permute-start(bf16[832,128]{1,0:T(8,128)(2,1)S(1)} %pad_maximum_fusion.5), channel_id=1, source_target_pairs={{0,8},{4,12},{8,0},{12,4},{16,24},{20,28},{24,16},{28,20},{1,9},{5... | collective-permute-start | bytes 638984 | tf_op jit(solution)/shard_map/ppermute | solution.py:1361
  345.3 11.9 %collective-permute-start.31 = (bf16[832,128]{1,0:T(8,128)(2,1)S(1)}, bf16[832,128]{1,0:T(8,128)(2,1)S(1)}, u32[]{:S(2)}, u32[]{:S(2)}) collective-permute-start(bf16[832,128]{1,0:T(8,128)(2,1)S(1)} %pad_maximum_fusion.5), channel_id=1, source_target_pairs={{0,16},{4,20},{8,24},{12,28},{16,0},{20,4},{24,8},{28,12},{1,17},{... | collective-permute-start | bytes 638984 | tf_op jit(solution)/shard_map/ppermute | solution.py:1361
  345.9 11.3 %collective-permute-start.32 = (bf16[832,128]{1,0:T(8,128)(2,1)S(1)}, bf16[832,128]{1,0:T(8,128)(2,1)S(1)}, u32[]{:S(2)}, u32[]{:S(2)}) collective-permute-start(bf16[832,128]{1,0:T(8,128)(2,1)S(1)} %pad_maximum_fusion.5), channel_id=1, source_target_pairs={{0,24},{4,28},{8,16},{12,20},{16,8},{20,12},{24,0},{28,4},{1,25},{... | collective-permute-start | bytes 638984 | tf_op jit(solution)/shard_map/ppermute | solution.py:1361
  358.5 2.4 collective-permute-start.34
  (12 other events, 45.9 us)
Sparse Core Ops, SparseCore 0:
  160.2 44.9 reduce-scatter.1
  231.7 41.4 all-reduce.1
  276.5 37.1 all-gather.1

commit v4 on v3

--- a/solution.py
+++ b/solution.py
@@ -33,6 +33,7 @@
 NN, EN = ROW_NN - ROW_BIAS, ROW_EN - ROW_BIAS
 UPPER_ROWS = ROW_BIAS - ROW_O
 GELU_C = 0.7978845608028654
+PAIRS = 4
 
 
 def nn(a, b):
@@ -110,23 +111,27 @@
 
     def each_pair(self, body):
         for bucket in self.buckets:
-            two = 2 * bucket.rows
-
-            @pl.loop(0, bucket.pairs, unroll=4)
+            two = 2 * PAIRS * bucket.rows
+
+            @pl.loop(0, bucket.pairs // PAIRS, unroll=True)
             def _(i, bucket=bucket, two=two):
                 body(
                     pl.ds(aligned(bucket.edge0 + i * two, 32), two),
-                    pl.ds(aligned(bucket.edge0 // 2 + i * bucket.rows, 16), bucket.rows),
+                    pl.ds(aligned((bucket.edge0 + i * two) // 2, 16), two // 2),
                 )
 
 
 def beside(v):
-    half = v.shape[0] // 2
-    return jnp.concatenate([v[:half], v[half:]], axis=1)
+    one = v.shape[0] // (2 * PAIRS)
+    at = lambda c: v[c * one : (c + 1) * one]
+    sides = [[at(2 * p + c) for p in range(PAIRS)] for c in range(2)]
+    return jnp.concatenate([jnp.concatenate(s) for s in sides], axis=1)
 
 
 def below(v):
-    return jnp.concatenate([v[:, :256], v[:, 256:]], axis=0)
+    one = v.shape[0] // PAIRS
+    at = lambda p, c: v[p * one : (p + 1) * one, 256 * c : 256 * (c + 1)]
+    return jnp.concatenate([at(p, c) for p in range(PAIRS) for c in range(2)])
 
 
 def make_masks(scr):
@@ -331,10 +336,14 @@
     send[...] = flat[pl.ds(aligned((1 - core) * half, 16), half), :].astype(BF)
 
 
+def stacked(v, width):
+    return jnp.concatenate([v[:, i : i + width] for i in range(0, v.shape[1], width)])
+
+
 def back_edges(dm, w, io, res, scr):
     io.small[NN + 8 : NN + 16, :] = io.sums[...]
-    scr.gb[...] = jnp.zeros((512, 256), F32)
-    scr.ga[...] = jnp.zeros((256, 512), F32)
+    scr.gb[...] = jnp.zeros((256, 128), F32)
+    scr.ga[...] = jnp.zeros((128, 256), F32)
     scr.gx[...] = jnp.zeros((256, 512), F32)
     scr.en[...] = jnp.zeros((2, 8, 256), F32)
 
@@ -345,8 +354,9 @@
         mn = (n * w.en[2:3, :] + w.en[3:4, :]).astype(BF)
         act, slope = gelu_parts(nn(mn, w.a[...]))
         dua = (nt(gx, w.b[...]) * slope).astype(BF)
-        scr.gb[...] += tn(act.astype(BF), gx)
-        scr.ga[...] += tn(mn, dua)
+        act = act.astype(BF)
+        scr.gb[...] += tn(stacked(act, 256), stacked(gx, 128))
+        scr.ga[...] += tn(stacked(mn, 128), stacked(dua, 256))
         dmn = nt(dua, w.a[...])
         scr.en[0] += fold8(dmn * n)
         scr.en[1] += fold8(dmn)
@@ -360,14 +370,8 @@
         scr.gx[...] += tn(res.low[pair, :], dml)
         io.scores[pair, :] = nt(dml, w.x[...])
 
-    up = scr.ga[0:64, 0:128]
-    for k in range(1, 4):
-        up = up + scr.ga[64 * k : 64 * (k + 1), 128 * k : 128 * (k + 1)]
-    io.small[EUP : EUP + 64, :] = up
-    sums = jnp.zeros((128, 128), F32)
-    for k in range(4):
-        part = scr.gb[128 * k : 128 * (k + 1), 128 * (k // 2) : 128 * (k // 2 + 1)]
-        sums = sums + jnp.where(lane_group(128, 6) == k % 2, part, 0.0)
+    io.small[EUP : EUP + 64, :] = scr.ga[0:64, 0:128] + scr.ga[64:128, 128:256]
+    sums = jnp.where(lane_group(128, 6) == 0, scr.gb[0:128, :], scr.gb[128:256, :])
     fold_halves(sums, scr.tmp, io.small, EDOWN)
     sides = []
     for half in range(2):
@@ -437,22 +441,27 @@
         t0 += bucket.graphs * bucket.blocks
 
 
+def back_nodes(dm, w, io, res, scr):
+    n = res.node_n1[...].astype(F32)
+    dhn = nt(io.dqkv[...], w.qkv[...])
+    gain = jnp.sum(dhn * n, axis=0, keepdims=True)
+    bias = jnp.sum(dhn, axis=0, keepdims=True)
+    for q in range(4):
+        io.sums_one[q : q + 1, :] = gain[:, 128 * q : 128 * (q + 1)]
+        io.sums_one[4 + q : 5 + q, :] = bias[:, 128 * q : 128 * (q + 1)]
+    dx = io.dy[...] + node_norm_back(dhn * w.nn[0:1, :], n, res.node_r1[:, 0:1])
+    io.nodes_grad[...] = dx.astype(BF)
+
+
 def back_last(dm, w, io, res, scr):
     flat = scr.lower
     n = res.node_n1[...].astype(F32)
     hn = (n * w.nn[0:1, :] + w.nn[1:2, :]).astype(BF)
     for m in range(3):
         put_strided(flat, 2048 * m, tn(hn, io.dqkv[:, 512 * m : 512 * (m + 1)]), 4)
-    dhn = nt(io.dqkv[...], w.qkv[...])
-    gain = jnp.sum(dhn * n, axis=0, keepdims=True)
-    bias = jnp.sum(dhn, axis=0, keepdims=True)
     small = flat.at[pl.ds(ROW_O, SMALL_ROWS), :]
     small[...] = io.small[...]
-    for q in range(4):
-        small[NN + q : NN + 1 + q, :] = gain[:, 128 * q : 128 * (q + 1)]
-        small[NN + 4 + q : NN + 5 + q, :] = bias[:, 128 * q : 128 * (q + 1)]
-    dx = io.dy[...] + node_norm_back(dhn * w.nn[0:1, :], n, res.node_r1[:, 0:1])
-    io.nodes_grad[...] = dx.astype(BF)
+    small[NN : NN + 8, :] = io.sums_one[...]
 
     scr.geg[...] = jnp.zeros((512, 512), F32)
     scr.en[...] = jnp.zeros((2, 8, 256), F32)
@@ -669,8 +678,8 @@
 
 def edge_scratch():
     return {
-        "gb": ((512, 256), F32),
-        "ga": ((256, 512), F32),
+        "gb": ((256, 128), F32),
+        "ga": ((128, 256), F32),
         "gx": ((256, 512), F32),
         "en": ((2, 8, 256), F32),
         "tmp": ((128, 128), F32),
@@ -878,26 +887,19 @@
 
 
 def between(dm, weights_two, weights_one, kept_two, kept_one, ffn_two, edges_cot):
-    half = {k: ((dm.lower // 2, 128), BF) for k in ("keep", "send")}
-    ffn = ffn_shapes(dm, True)
-    out = {
-        "edges_grad": ((dm.edges, 256), BF),
-        **{"two_" + k: v for k, v in half.items()},
-        **ffn,
-    }
-    edge, att = edge_shapes(dm), attention_shapes(dm)
+    ffn, edge, att = ffn_shapes(dm, True), edge_shapes(dm), attention_shapes(dm)
+    handed = {"dmid": edge["dmid"], "small": edge["small"], **att, "sums_one": ((8, 128), F32)}
+    out = {**{"two_" + k: v for k, v in handed.items()}, **ffn}
     scr = {
         **mask_shapes(),
         **edge_scratch(),
         **attention_scratch(dm),
-        **last_scratch(dm),
         **ffn_scratch(),
-        **edge,
-        **att,
+        "scores": edge["scores"],
         "nodes_grad": ((dm.nodes, D), BF),
     }
-    w_two = ("qkv", *W_EDGE, "eg", "nn")
-    res_two = EDGE_BACK + ATTENTION_BACK + LAST_BACK
+    w_two = ("qkv", *W_EDGE, "nn")
+    res_two = EDGE_BACK + ATTENTION_BACK + ("node_n1", "node_r1")
 
     def body(*refs):
         w, w_one, res, res_one, src, dst, s = split(
@@ -905,19 +907,37 @@
         )
         make_masks(s)
         io = Group(
-            ("edges_cot", "sums", "do", "dy", *edge, *att, "nodes_grad", "edges_grad", "keep", "send"),
-            (src.edges_cot, src.sums, src.do, src.dy, *take(s, edge), *take(s, att))
-            + (s.nodes_grad, dst.edges_grad, dst.two_keep, dst.two_send),
+            ("edges_cot", "sums", "do", "dy", "scores", "nodes_grad", *handed),
+            (src.edges_cot, src.sums, src.do, src.dy, s.scores, s.nodes_grad)
+            + tuple(getattr(dst, "two_" + k) for k in handed),
         )
         back_edges(dm, w, io, res, s)
         back_attention(dm, io, res, s)
-        back_last(dm, w, io, res, s)
+        back_nodes(dm, w, io, res, s)
         back_ffn(dm, w_one, Group(("nodes_cot", *ffn), (s.nodes_grad, *take(dst, ffn))), res_one, s)
 
     inputs = take(weights_two, w_two) + take(weights_one, W_NODE)
     inputs += take(kept_two, res_two) + take(kept_one, NODE_BACK)
     inputs += [edges_cot, ffn_two.sums, ffn_two.do, ffn_two.dy]
-    return kernel(body, inputs, out, scr, 45)
+    return kernel(body, inputs, out, scr, 25)
+
+
+def second_last(dm, weights, kept, got):
+    half = {k: ((dm.lower // 2, 128), BF) for k in ("keep", "send")}
+    out = {"edges_grad": ((dm.edges, 256), BF), **half}
+    scr = {**mean_shapes(), **last_scratch(dm)}
+    given = ("dmid", "small", "dsg", "dqkv", "sums_one")
+    w_last = ("eg", "nn", "en")
+    last_res = ("node_n1", "edge_n1", "edge_r1")
+
+    def body(*refs):
+        w, res, src, dst, s = split(refs, w_last, last_res, given, out, scr)
+        make_mean(s)
+        back_last(dm, w, Group((*given, *out), (*take(src, given), *take(dst, out))), res, s)
+
+    inputs = take(weights, w_last) + take(kept, last_res)
+    inputs += [getattr(got, "two_" + k) for k in given]
+    return kernel(body, inputs, out, scr, 9)
 
 
 def call_edges(dm, weights, kept, ffn, edges_cot):
@@ -957,6 +977,7 @@
         **last_scratch(dm),
         "nodes_grad": ((dm.nodes, D), BF),
         "edges_grad": ((dm.edges, 256), BF),
+        "sums_one": ((8, 128), F32),
     }
     given = ("dy", "dmid", "small", "dsg", "dqkv")
 
@@ -965,9 +986,10 @@
         w, res, src, dst, s = split(refs, W_LAST, LAST_BACK, given, out, scr)
         make_mean(s)
         io = Group(
-            (*given, "nodes_grad", "edges_grad", "keep", "send"),
-            (*take(src, given), s.nodes_grad, s.edges_grad, dst.keep, dst.send),
+            (*given, "nodes_grad", "edges_grad", "keep", "send", "sums_one"),
+            (*take(src, given), s.nodes_grad, s.edges_grad, dst.keep, dst.send, s.sums_one),
         )
+        back_nodes(dm, w, io, res, s)
         back_last(dm, w, io, res, s)
         outgoing = all_copies(
             dm, dst.sng, dst.seg, dst.bgrad, 0, EDGE_LANES, s.nodes_grad, s.edges_grad, sems, True
@@ -1121,7 +1143,7 @@
     n_dp = owner.shape[0]
     set_rows = ROW_BIAS - ROW_O + lower
     total_rows = front + set_rows + step + 32
-    ways = 3 * n_row
+    ways = 3
     arrivals = sum(len(keys) for _, _, keys, _ in blocks)
 
     def body(owner_ref, rows_ref, scale_ref, *refs):
@@ -1146,43 +1168,37 @@
                 for at_sem, (k, core, key, n, sections) in enumerate(every):
                     mine = (me ^ core) & 1
                     source = me ^ core ^ jnp.where(mine == 0, key[0], key[1])
-                    stride = sum(size for _, _, size in sections)
-                    offset = n * stride * n_row
+                    offset = n * n_row * sum(size for _, _, size in sections)
+                    place = (source & 1) * (n_dp // 2) + (source >> 1)
                     for number, (which, part, size) in enumerate(sections):
-                        block = ((source & 1) * (n_dp // 2) + (source >> 1)) * size * n_row
-                        for z in range(n_row):
-                            at = block + (row ^ z) * size
-                            dest = at + ROW_O if part else jnp.where(at >= ROW_O, at - ROW_O + ROW_BIAS, at)
-                            wanted = (dest + which * SET_ROWS < begin + length) & (
-                                dest + size + which * SET_ROWS > begin
+                        size = size * n_row
+                        at = place * size
+                        dest = at + ROW_O if part else jnp.where(at >= ROW_O, at - ROW_O + ROW_BIAS, at)
+                        wanted = (dest + which * SET_ROWS < begin + length) & (
+                            dest + size + which * SET_ROWS > begin
+                        )
+                        wanted = wanted | (dest + size > ROW_NN)
+
+                        def move(frm, extent, to, way, k=k, which=which, at_sem=at_sem):
+                            act(
+                                pltpu.make_async_copy(
+                                    srcs[k].at[pl.ds(frm, extent), :],
+                                    rows.at[which, pl.ds(aligned(front + to, 16), extent), :],
+                                    sems.at[at_sem, way],
+                                )
                             )
-                            wanted = wanted | (dest + size > ROW_NN)
-                            lies = z * stride + offset
-
-                            def move(frm, extent, to, way, k=k, which=which, at_sem=at_sem):
-                                act(
-                                    pltpu.make_async_copy(
-                                        srcs[k].at[pl.ds(frm, extent), :],
-                                        rows.at[which, pl.ds(aligned(front + to, 16), extent), :],
-                                        sems.at[at_sem, way],
-                                    )
-                                )
-
-                            cut = 0 if part else ROW_O % size
-                            way = number * n_row + z
-                            if not cut:
-                                pl.when(wanted)(functools.partial(move, lies, size, dest, way))
-                                continue
+
+                        cut = 0 if part else ROW_O % size
+                        if cut:
                             split_here = (at < ROW_O) & (at + size > ROW_O)
-                            pl.when(wanted & jnp.logical_not(split_here))(
-                                functools.partial(move, lies, size, dest, way)
-                            )
+                            wanted = wanted & jnp.logical_not(split_here)
 
                             @pl.when(split_here)
-                            def _(move=move, lies=lies, size=size, at=at, cut=cut, way=way, z=z):
-                                move(lies, cut, at, way)
-                                move(lies + cut, size - cut, ROW_BIAS, 2 * n_row + z)
-
+                            def _(move=move, offset=offset, size=size, at=at, cut=cut, number=number):
+                                move(offset, cut, at, number)
+                                move(offset + cut, size - cut, ROW_BIAS, 2)
+
+                        pl.when(wanted)(functools.partial(move, offset, size, dest, number))
                         offset += size
 
             each(lambda c: c.start())
@@ -1345,6 +1361,42 @@
     return out.astype(BF)
 
 
+def side_by_side(parts, sections, row_order):
+    count, total_rows = len(parts), len(parts) * parts[0].shape[0]
+
+    def body(*refs):
+        srcs, dst, sems = refs[:count], refs[count], refs[count + 1]
+        row = lax.axis_index("row")
+        copies = []
+        for k in range(count):
+            inside = 0
+            for number, size in enumerate(sections):
+                if row_order:
+                    to = aligned(count * inside + (row ^ k) * size, 16)
+                else:
+                    to = k * parts[0].shape[0] + inside
+                copies.append(
+                    pltpu.make_async_copy(
+                        srcs[k].at[pl.ds(inside, size), :],
+                        dst.at[pl.ds(to, size), :],
+                        sems.at[k, number],
+                    )
+                )
+                inside += size
+        start(copies)
+        wait(copies)
+
+    return pl.pallas_call(
+        body,
+        out_shape=jax.ShapeDtypeStruct((total_rows, 128), BF),
+        in_specs=[HBM] * count,
+        out_specs=HBM,
+        scratch_shapes=[pltpu.SemaphoreType.DMA((count, len(sections)))],
+        compiler_params=pltpu.CompilerParams(vmem_limit_bytes=4 * 1024 * 1024),
+        cost_estimate=cost(1),
+    )(*parts)
+
+
 class Chain:
     def __init__(self, cube, direct, *halves):
         self.cube, self.direct = cube, direct
@@ -1372,6 +1424,10 @@
         self.sizes = [v.shape[0] // count for v in self.value]
         self.kept = at(0)
         return [send(at(k), k) for k in range(1, count)]
+
+    def join(self, other):
+        assert self.step == other.step == 2
+        self.value = self.value + other.value
 
     def launch(self):
         self.step += 1
@@ -1405,10 +1461,9 @@
                     self.value.append(value[at : at + size])
                     at += size
         elif self.step == 4:
-            self.value = jnp.concatenate([self.value, *got])
-            self.size = self.value.shape[0]
+            self.value = side_by_side([self.value, *got], self.sizes, True)
         elif self.spread():
-            self.value = jnp.concatenate([self.value, *got])
+            self.value = side_by_side([self.value, *got], [self.value.shape[0]], False)
             if self.direct:
                 self.keys = [(k << 1, k << 1) for k in range(self.sides)]
             else:
@@ -1483,27 +1538,34 @@
     )
     spread = lax.psum_scatter(ffn_two.upper, "dp", scatter_dimension=0, tiled=True)
     got = between(dm, two, one, kept_two, kept, ffn_two, edge_cot)
+    names = tuple(vars(got))
     outs = to_rows(bout)
-    names = tuple(k for k in vars(got))
-    spread, *values, bno, beo = phase([], spread, *take(got, names), *outs)
+    *values, bno, beo = phase([], *take(got, names), *outs)
+    got = Group(names, values)
+    middle = Chain(cube, False, (got.keep, got.send))
+    rest = second_last(dm, two, kept_two, got)
+    spread, edge_grad, keep, send = phase([middle], spread, rest.edges_grad, rest.keep, rest.send)
     spread = lax.psum(spread, "row")
-    got = Group(names, values)
-    middle = Chain(cube, False, (got.keep, got.send), (got.two_keep, got.two_send))
+    lower_two = Chain(cube, False, (keep, send))
     names = tuple(edge_shapes(dm))
-    edge_one = call_edges(dm, one, kept, got, got.edges_grad)
-    edge_one = Group(names, phase([middle], *take(edge_one, names)))
+    edge_one = call_edges(dm, one, kept, got, edge_grad)
+    edge_one = Group(names, phase([middle, lower_two], *take(edge_one, names)))
     names = tuple(attention_shapes(dm))
-    att_one = Group(names, phase([middle], *take(call_attention(dm, kept, got, edge_one), names)))
+    att_one = Group(names, phase([lower_two], *take(call_attention(dm, kept, got, edge_one), names)))
+    middle.join(lower_two)
     sng, seg, bgrad, keep, send = call_last(dm, one, kept, got, edge_one, att_one)
     spread, sng, seg, bgrad, keep, send = phase([middle], spread, sng, seg, bgrad, keep, send)
     upper_two = lax.all_gather(spread, "dp", axis=0, tiled=True)
     last = Chain(cube, True, (keep, send))
-    bgrad, = phase([last, middle], bgrad)
+    sent = middle.launch()
+    bgrad, = phase([last], bgrad)
     outs = to_rows(bgrad)
+    sent, = phase([last], sent)
+    middle.land(sent)
     phase([last, middle])
     sent = middle.launch()
-    phase([last])
-    sent, bng, beg, upper_two = phase([last], sent, *outs, upper_two)
+    bng, beg, upper_two = phase([last], *outs, upper_two)
+    sent, = phase([last], sent)
     middle.land(sent)
     while not (last.done and middle.done):
         phase([last, middle])

time: 391 us -> 358 us (0.916)
  Pallas kernels: 163 us -> 139 us
  waiting for transfers between devices: 123 us -> 116 us
  starting transfers between devices: 54.4 us -> 59.9 us
    ppermute x9 -> x12, waiting for transfers between devices: 35.5 us -> 3.91 us  [to_chip(): lax.ppermute(value, 'dp', [(i, i ^ k << 1) for i in range(2 * self.sides)])]
    pallas_call x6 -> x7, Pallas kernels: 131 us -> 106 us  [kernel(): pl.pallas_call(body, out_shape=structs(out), in_specs=[SMEM] * len(smem)...]
    ppermute x2, waiting for transfers between devices: 0.01 us -> 9.37 us  [launch(): return [lax.ppermute(self.value, 'dp', self.cube.pairs(self.step - 5))]]
    ppermute x12, waiting for transfers between devices: 21.5 us -> 30.5 us  [to_row(): return lax.ppermute(value, 'row', [(i, i ^ k) for i in range(self.rows)])]
    unnamed x48 -> x32, local copies, waits for them, and re-layouts: 9.42 us -> 5.91 us
    ppermute x9 -> x12, starting transfers between devices: 10.7 us -> 14.1 us  [to_chip(): lax.ppermute(value, 'dp', [(i, i ^ k << 1) for i in range(2 * self.sides)])]
  transfers between devices with their start and end apart: 41 -> 44, of which waited for: 18 -> 15; matrix products, arithmetic and copies ran while one was open for 6% -> 5% of each run, Pallas kernels for 20% -> 20%
where the time goes in v4:
time: 358 us; the launch traced here: 355 us
  Pallas kernels  139 us (39%)
  waiting for transfers between devices  116 us (32%)
  starting transfers between devices  59.9 us (17%)
  local copies, waits for them, and re-layouts  18.2 us (5%)
  between operations  15.3 us (4%)
  other arithmetic  5.37 us (2%)
    pallas_call x7, Pallas kernels, kernel(): pl.pallas_call(body, out_shape=structs(out), in_specs=[SMEM] * len(smem)...  106 us
    ppermute x3, waiting for transfers between devices, gather(): sent.append((0, used + (step,), lax.ppermute(v, 'dp', self.pairs(step))))  50.5 us
    ppermute x12, waiting for transfers between devices, to_row(): return lax.ppermute(value, 'row', [(i, i ^ k) for i in range(self.rows)])  30.5 us
    ppermute x12, starting transfers between devices, to_row(): return lax.ppermute(value, 'row', [(i, i ^ k) for i in range(self.rows)])  19.6 us
    pallas_call x1, Pallas kernels, adam(): pl.pallas_call(body, grid=(pl.cdiv(held, step),), out_shape=[shape] * 3 +...  14.7 us
    ppermute x12, starting transfers between devices, to_chip(): lax.ppermute(value, 'dp', [(i, i ^ k << 1) for i in range(2 * self.sides)])  14.1 us
    all_to_all x1, waiting for transfers between devices, to_whole(): lax.all_to_all(big, 'row', split_axis=0, concat_axis=1, tiled=True)  12.2 us
    pallas_call x1, Pallas kernels, assemble(): pl.pallas_call(body, out_shape=structs(out), in_specs=[SMEM] * 2 + [HBM]...  10.6 us
  transfers between devices with their start and end apart: 44, of which 15 were waited for; matrix products, arithmetic and copies ran while one was open for 5% of the time, Pallas kernels for 20%

profile of v4, /device:TPU:0, one launch (start us, length us, event | category | flops | bytes accessed | tf_op | source)
XLA Modules:
  0.0 354.6 jit_solution(9522956887165755849)
XLA Ops:
  7.2 5.9 %shard_map.247.refs_0_ = bf16[8320,128]{1,0:T(8,128)(2,1)} custom-call(s32[8]{0:T(128)} %owner_ref.5, s32[8]{0:T(128)} %rows_ref.5, f32[8290,128]{1,0:T(8,128)} %refs_5_.1), custom_call_target="tpu_custom_call" | custom-call | tf_op jit(solution)/shard_map/pallas_call | solution.py:1040
  13.6 2.5 collective-permute-start.1
  16.1 1.5 collective-permute-start
  17.6 1.5 pad_maximum_fusion
  19.1 4.9 %all-to-all-start = ((bf16[8,16,9216]{2,1,0:T(8,128)(2,1)}), bf16[8,16,9216]{2,1,0:T(8,128)(2,1)S(1)}, u32[]{:S(2)}, u32[]{:S(2)}) async-start(bf16[8,16,9216]{2,1,0:T(8,128)(2,1)} %pad_maximum_fusion), calls=%async_computation | async-start | bytes 4718592 | tf_op jit(solution)/shard_map/all_to_all | solution.py:1525
  24.0 38.4 %collective-permute-done.1.refs_3_ = bf16[8320,128]{1,0:T(8,128)(2,1)} collective-permute-done((bf16[8320,128]{1,0:T(8,128)(2,1)}, bf16[8320,128]{1,0:T(8,128)(2,1)}, u32[]{:S(2)}, u32[]{:S(2)}) %collective-permute-start.1) | collective-permute-done | bytes 2129952 | tf_op jit(solution)/shard_map/ppermute | solution.py:1338
  63.9 1.8 collective-permute-start.3
  65.7 12.2 %all-to-all-done = bf16[8,16,9216]{2,1,0:T(8,128)(2,1)S(1)} async-done(((bf16[8,16,9216]{2,1,0:T(8,128)(2,1)}), bf16[8,16,9216]{2,1,0:T(8,128)(2,1)S(1)}, u32[]{:S(2)}, u32[]{:S(2)}) %all-to-all-start) | async-done | bytes 2359328 | tf_op jit(solution)/shard_map/all_to_all | solution.py:1525
  77.9 1.6 copy.31
  79.5 11.1 %collective-permute-done.3.refs_6_ = bf16[8320,128]{1,0:T(8,128)(2,1)} collective-permute-done((bf16[8320,128]{1,0:T(8,128)(2,1)}, bf16[8320,128]{1,0:T(8,128)(2,1)}, u32[]{:S(2)}, u32[]{:S(2)}) %collective-permute-start.3) | collective-permute-done | bytes 2129952 | tf_op jit(solution)/shard_map/ppermute | solution.py:1338
  91.3 3.7 %collective-permute-done.6.refs_7_ = bf16[8320,128]{1,0:T(8,128)(2,1)S(1)} collective-permute-done((bf16[8320,128]{1,0:T(8,128)(2,1)}, bf16[8320,128]{1,0:T(8,128)(2,1)S(1)}, u32[]{:S(2)}, u32[]{:S(2)}) %collective-permute-start.6) | collective-permute-done | bytes 2129952 | tf_op jit(solution)/shard_map/ppermute | solution.py:1340
  96.3 10.6 %shard_map.248 = (bf16[512,1536]{1,0:T(8,128)(2,1)}, bf16[512,512]{1,0:T(8,128)(2,1)}, bf16[512,1024]{1,0:T(8,128)(2,1)}, bf16[1024,512]{1,0:T(8,128)(2,1)}, bf1...) custom-call(s32[8]{0:T(128)} %owner_ref.5, ...), custom_call_target="tpu_custom_call" | custom-call | bytes 34000000 | tf_op jit(solution)/shard_map/pallas_call | solution.py:1119
  107.0 16.2 %shard_map.249 = (bf16[224,512]{1,0:T(8,128)(2,1)}, bf16[2816,256]{1,0:T(8,128)(2,1)}, bf16[224,512]{1,0:T(8,128)(2,1)}, f32[224,128]{1,0:T(8,128)}, bf16[224,15...) custom-call(s32[5]{0:T(128)} %pad_add_fusion.refs_0_, ...), custom_call_target="tpu_custom_call" | custom-call | bytes 129200000 | tf_op jit(solution)/shard_map/pallas_call | solution.py:798
  123.2 22.6 %shard_map.250 = (bf16[96,512]{1,0:T(8,128)(2,1)}, bf16[96,2048]{1,0:T(8,128)(2,1)}, bf16[128,4608]{1,0:T(8,128)(2,1)}, bf16[2816,256]{1,0:T(8,128)(2,1)}, bf16[...) custom-call(s32[5]{0:T(128)} %pad_add_fusion.refs_0_, ...), custom_call_target="tpu_custom_call" | custom-call | bytes 156400000 | tf_op jit(solution)/shard_map/pallas_call | solution.py:798
  147.1 2.3 copy.32
  149.4 5.1 %all-to-all-start.1 = ((bf16[2,64,4608]{2,0,1:T(2,128)(2,1)}), bf16[2,64,4608]{2,0,1:T(2,128)(2,1)S(1)}, u32[]{:S(2)}, u32[]{:S(2)}) async-start(bf16[2,64,4608]{2,0,1:T(2,128)(2,1)} %copy.32), calls=%async_computation.1 | async-start | bytes 2359296 | tf_op jit(solution)/shard_map/all_to_all | solution.py:1518
  154.5 26.0 %shard_map.251 = (bf16[2816,256]{1,0:T(8,128)(2,1)}, f32[256,128]{1,0:T(8,128)}, bf16[1408,512]{1,0:T(8,128)(2,1)}, bf16[224,1536]{1,0:T(8,128)(2,1)}, f32[8,128...) custom-call(bf16[512,1536]{1,0:T(8,128)(2,1)} %get-tuple-element.180, ...), custom_call_target="tpu_custom_call" | custom-call | bytes 85000000 | tf_op jit(solution)/shard_map/pallas_call | solution.py:798
  180.5 2.9 all-to-all-done.1
  185.3 8.7 %shard_map.252 = (bf16[2816,256]{1,0:T(8,128)(2,1)}, bf16[3328,128]{1,0:T(8,128)(2,1)}, bf16[3328,128]{1,0:T(8,128)(2,1)}) custom-call(bf16[512,512]{1,0:T(8,128)(2,1)} %get-tuple-element.184.refs_5_.refs_0_, f32[4,512]{1,0:T(4,128)} %get-tuple-element.188.refs_9_.refs_5_.refs_1_, f32[4,256]{1,0:T(4,128)} %get-tuple-element.189.refs_10_.refs_4_.refs_2_, ...), custom_call_target="tpu_custom_call" | custom-call | bytes 30600000 | tf_op jit(solution)/shard_map/pallas_call | solution.py:798
  195.7 1.7 add_convert_fusion
  198.2 2.6 collective-permute-start.10
  202.0 12.4 %shard_map.253 = (bf16[2816,256]{1,0:T(8,128)(2,1)}, f32[1408,256]{1,0:T(8,128)}, f32[256,128]{1,0:T(8,128)}) custom-call(bf16[256,512]{1,0:T(8,128)(2,1)} %get-tuple-element.195.refs_6_.refs_0_, bf16[256,512]{1,0:T(8,128)(2,1)} %get-tuple-element.196.refs_7_.refs_1_, bf16[512,256]{1,0:T(8,128)(2,1)} %get-tuple-element.197.refs_8_.refs_2_, ...), custom_call_target="tpu_custom_call" | custom-call | bytes 54400000 | tf_op jit(solution)/shard_map/pallas_call | solution.py:798
  214.4 1.6 collective-permute-done.9
  216.3 1.8 collective-permute-start.14
  218.1 1.5 collective-permute-start.13
  220.0 9.2 %shard_map.254 = (bf16[1408,512]{1,0:T(8,128)(2,1)}, bf16[224,1536]{1,0:T(8,128)(2,1)}) custom-call(bf16[224,1536]{1,0:T(8,128)(2,1)} %get-tuple-element.262.refs_0_, bf16[1408,256]{1,0:T(8,128)(2,1)} %get-tuple-element.263.refs_1_, f32[1408,256]{1,0:T(8,128)} %get-tuple-element.264.refs_2_, bf16[224,512]{1,0:T(8,128)(2,1)} %get-tuple-element.265.refs_3_, ...), custom_call_target="tpu_custom_call" | custom-call | bytes 47600000 | tf_op jit(solution)/shard_map/pallas_call | solution.py:798
  229.5 2.3 collective-permute-start.16
  231.8 2.2 collective-permute-start.17
  234.0 10.5 %shard_map.255 = (bf16[96,512]{1,0:T(8,128)(2,1)}, bf16[96,2048]{1,0:T(8,128)(2,1)}, bf16[128,4608]{1,0:T(8,128)(2,1)}, bf16[3328,128]{1,0:T(8,128)(2,1)}, bf16[3328,128]{1,0:T(8,128)(2,1)}) custom-call(bf16[512,1536]{1,0:T(8,128)(2,1)} %get-tuple-element.190.refs_1_.refs_0_, bf16[512,512]{1,0:T(8,128)(2,1)} %get-tuple-element.194.refs_5_.refs_1_, ...), custom_call_target="tpu_custom_call" | custom-call | bytes 44200000 | tf_op jit(solution)/shard_map/pallas_call | solution.py:798
  244.8 1.7 collective-permute-start.24
  247.3 3.5 copy.34
  250.8 4.9 %all-to-all-start.2 = ((bf16[2,64,4608]{2,0,1:T(2,128)(2,1)}), bf16[2,64,4608]{2,0,1:T(2,128)(2,1)S(1)}, u32[]{:S(2)}, u32[]{:S(2)}) async-start(bf16[2,64,4608]{2,0,1:T(2,128)(2,1)} %copy.34), calls=%async_computation.3 | async-start | bytes 2359296 | tf_op jit(solution)/shard_map/all_to_all | solution.py:1518
  256.0 1.8 collective-permute-start.21
  259.5 2.9 collective-permute-start.23
  262.4 1.5 collective-permute-start.22
  263.9 26.4 %collective-permute-done.23.refs_2_ = bf16[528,128]{1,0:T(8,128)(2,1)S(1)} collective-permute-done((bf16[528,128]{1,0:T(8,128)(2,1)S(1)}, bf16[528,128]{1,0:T(8,128)(2,1)S(1)}, u32[]{:S(2)}, u32[]{:S(2)}) %collective-permute-start.23) | collective-permute-done | bytes 135200 | tf_op jit(solution)/shard_map/ppermute | solution.py:1416
  291.1 1.7 collective-permute-start.28
  292.9 2.0 collective-permute-start.27
  294.9 2.4 collective-permute-start.25
  297.4 2.0 collective-permute-done.27
  300.7 1.5 collective-permute-start.35
  302.2 2.1 collective-permute-start.31
  304.2 2.4 collective-permute-start.29
  309.8 1.6 collective-permute-start.34
  313.3 9.4 %collective-permute-done.35.refs_1_ = bf16[4224,128]{1,0:T(8,128)(2,1)S(1)} collective-permute-done((bf16[4224,128]{1,0:T(8,128)(2,1)S(1)}, bf16[4224,128]{1,0:T(8,128)(2,1)S(1)}, u32[]{:S(2)}, u32[]{:S(2)}) %collective-permute-start.35) | collective-permute-done | bytes 1081376 | tf_op jit(solution)/shard_map/ppermute | solution.py:1446
  322.7 2.3 collective-permute-done.33.refs_2_
  328.5 2.3 collective-permute-done.36.refs_2_
  333.1 14.7 %shard_map.261 = (f32[8290,128]{1,0:T(8,128)}, f32[8290,128]{1,0:T(8,128)}, f32[8290,128]{1,0:T(8,128)}, f32[8,576]{1,0:T(8,128)}) custom-call(s32[8]{0:T(128)} %owner_ref.5, s32[8]{0:T(128)} %rows_ref.5, f32[2]{0:T(128)} %pad_maximum_fusion.4.scale_ref, bf16[10240,128]{1,0:T(8,128)(2,1)} %all-gather.2.cloned.1.call-done.refs_0_, ...), custom_call_target="tpu_custom_call" | custom-call | bytes 34000000 | tf_op jit(solution)/shard_map/pallas_call | solution.py:1277
  (120 shorter events, 27.0 us)
Async XLA Ops:
  7.2 10.4 %copy-start.7 = (bf16[8,16,4096]{2,1,0:T(8,128)(2,1)S(1)}, bf16[8,16,4096]{2,1,0:T(8,128)(2,1)}, u32[]{:S(2)}) copy-start(bf16[8,16,4096]{2,1,0:T(8,128)(2,1)} %param.25) | copy-start | bytes 3145732
  13.1 10.9 %collective-permute-start.2 = (bf16[8320,128]{1,0:T(8,128)(2,1)}, bf16[8320,128]{1,0:T(8,128)(2,1)}, u32[]{:S(2)}, u32[]{:S(2)}) collective-permute-start(bf16[8320,128]{1,0:T(8,128)(2,1)} %shard_map.247.refs_0_), channel_id=1, source_target_pairs={{0,4},{4,0},{8,12},{12,8},{16,20},{20,16},{24,28},{28,24},{1,5},{5... | collective-permute-start | bytes 6389768 | tf_op jit(solution)/shard_map/ppermute | solution.py:1340
  13.6 48.8 %collective-permute-start.1 = (bf16[8320,128]{1,0:T(8,128)(2,1)}, bf16[8320,128]{1,0:T(8,128)(2,1)}, u32[]{:S(2)}, u32[]{:S(2)}) collective-permute-start(bf16[8320,128]{1,0:T(8,128)(2,1)} %shard_map.247.refs_0_), channel_id=1, source_target_pairs={{0,16},{4,12},{8,24},{12,4},{16,0},{20,28},{24,8},{28,20},{1,17},{... | collective-permute-start | bytes 6389768 | tf_op jit(solution)/shard_map/ppermute | solution.py:1338
  16.1 47.3 %collective-permute-start = (bf16[8320,128]{1,0:T(8,128)(2,1)}, bf16[8320,128]{1,0:T(8,128)(2,1)}, u32[]{:S(2)}, u32[]{:S(2)}) collective-permute-start(bf16[8320,128]{1,0:T(8,128)(2,1)} %shard_map.247.refs_0_), channel_id=1, source_target_pairs={{0,8},{4,20},{8,0},{12,28},{16,24},{20,4},{24,16},{28,12},{1,9},{5... | collective-permute-start | bytes 6389768 | tf_op jit(solution)/shard_map/ppermute | solution.py:1338
  19.1 58.8 %all-to-all-start = ((bf16[8,16,9216]{2,1,0:T(8,128)(2,1)}), bf16[8,16,9216]{2,1,0:T(8,128)(2,1)S(1)}, u32[]{:S(2)}, u32[]{:S(2)}) async-start(bf16[8,16,9216]{2,1,0:T(8,128)(2,1)} %pad_maximum_fusion), calls=%async_computation | async-start | bytes 4718592 | tf_op jit(solution)/shard_map/all_to_all | solution.py:1525
  24.0 170.1 %reduce-scatter.2.cloned.1.call-start = ((), (), s32[]{:S(2)}) async-start(), calls=%async_computation.4 | async-start | bytes 2949120 | tf_op jit(solution)/shard_map/reduce_scatter | solution.py:1539
  63.4 16.2 %collective-permute-start.5 = (bf16[8320,128]{1,0:T(8,128)(2,1)}, bf16[8320,128]{1,0:T(8,128)(2,1)}, u32[]{:S(2)}, u32[]{:S(2)}) collective-permute-start(bf16[8320,128]{1,0:T(8,128)(2,1)} %collective-permute-done.1.refs_3_), channel_id=1, source_target_pairs={{0,4},{4,0},{8,12},{12,8},{16,20},{20,16},{24,28},{28,24},{1,5},{5... | collective-permute-start | bytes 6389768 | tf_op jit(solution)/shard_map/ppermute | solution.py:1340
  63.6 15.9 %collective-permute-start.4 = (bf16[8320,128]{1,0:T(8,128)(2,1)}, bf16[8320,128]{1,0:T(8,128)(2,1)}, u32[]{:S(2)}, u32[]{:S(2)}) collective-permute-start(bf16[8320,128]{1,0:T(8,128)(2,1)} %collective-permute-done.refs_2_), channel_id=1, source_target_pairs={{0,4},{4,0},{8,12},{12,8},{16,20},{20,16},{24,28},{28,24},{1,5},{5... | collective-permute-start | bytes 6389768 | tf_op jit(solution)/shard_map/ppermute | solution.py:1340
  63.9 26.7 %collective-permute-start.3 = (bf16[8320,128]{1,0:T(8,128)(2,1)}, bf16[8320,128]{1,0:T(8,128)(2,1)}, u32[]{:S(2)}, u32[]{:S(2)}) collective-permute-start(bf16[8320,128]{1,0:T(8,128)(2,1)} %collective-permute-done.refs_2_), channel_id=1, source_target_pairs={{0,16},{4,12},{8,24},{12,4},{16,0},{20,28},{24,8},{28,20},{1,17},{... | collective-permute-start | bytes 6389768 | tf_op jit(solution)/shard_map/ppermute | solution.py:1338
  77.9 12.7 %copy-start.14 = (s32[8]{0:T(128)S(1)}, s32[8]{0:T(128)}, u32[]{:S(2)}) copy-start(s32[8]{0:T(128)} %param.21) | copy-start | bytes 100
  77.9 12.8 %copy-start.15 = (s32[3]{0:T(128)S(1)}, s32[3]{0:T(128)}, u32[]{:S(2)}) copy-start(s32[3]{0:T(128)} %param.18) | copy-start | bytes 40
  90.6 4.4 %collective-permute-start.6 = (bf16[8320,128]{1,0:T(8,128)(2,1)}, bf16[8320,128]{1,0:T(8,128)(2,1)S(1)}, u32[]{:S(2)}, u32[]{:S(2)}) collective-permute-start(bf16[8320,128]{1,0:T(8,128)(2,1)} %collective-permute-done.3.refs_6_), channel_id=1, source_target_pairs={{0,4},{4,0},{8,12},{12,8},{16,20},{20,16},{24,28},{28,24},{1,5},{5... | collective-permute-start | bytes 6389768 | tf_op jit(solution)/shard_map/ppermute | solution.py:1340
  149.4 34.1 %all-to-all-start.1 = ((bf16[2,64,4608]{2,0,1:T(2,128)(2,1)}), bf16[2,64,4608]{2,0,1:T(2,128)(2,1)S(1)}, u32[]{:S(2)}, u32[]{:S(2)}) async-start(bf16[2,64,4608]{2,0,1:T(2,128)(2,1)} %copy.32), calls=%async_computation.1 | async-start | bytes 2359296 | tf_op jit(solution)/shard_map/all_to_all | solution.py:1518
  154.5 90.1 %all-reduce.2.cloned.1.call-start = ((), (), s32[]{:S(2)}) async-start(), calls=%async_computation.5 | async-start | bytes 655360 | tf_op jit(solution)/shard_map/psum | solution.py:1548
  185.3 8.7 %collective-permute-start.7 = (bf16[5120,128]{1,0:T(8,128)(2,1)}, bf16[5120,128]{1,0:T(8,128)(2,1)S(1)}, u32[]{:S(2)}, u32[]{:S(2)}) collective-permute-start(bf16[5120,128]{1,0:T(8,128)(2,1)} %get-tuple-element.235), channel_id=1, source_target_pairs={{0,4},{4,0},{8,12},{12,8},{16,20},{20,16},{24,28},{28,24},{1,5},{5... | collective-permute-start | bytes 3932168 | tf_op jit(solution)/shard_map/ppermute | solution.py:1410
  195.1 20.9 %collective-permute-start.11 = (bf16[3328,128]{1,0:T(8,128)(2,1)}, bf16[3328,128]{1,0:T(8,128)(2,1)S(1)}, u32[]{:S(2)}, u32[]{:S(2)}) collective-permute-start(bf16[3328,128]{1,0:T(8,128)(2,1)} %get-tuple-element.248), channel_id=1, source_target_pairs={{0,4},{4,0},{8,12},{12,8},{16,20},{20,16},{24,28},{28,24},{1,5},{5... | collective-permute-start | bytes 2555912 | tf_op jit(solution)/shard_map/ppermute | solution.py:1410
  198.2 16.1 %collective-permute-start.10 = (bf16[1280,128]{1,0:T(8,128)(2,1)}, bf16[1280,128]{1,0:T(8,128)(2,1)S(1)}, u32[]{:S(2)}, u32[]{:S(2)}) collective-permute-start(bf16[1280,128]{1,0:T(8,128)(2,1)} %get-tuple-element.324), channel_id=1, source_target_pairs={{0,24},{4,28},{8,16},{12,20},{16,8},{20,12},{24,0},{28,4},{1,25},{... | collective-permute-start | bytes 983048 | tf_op jit(solution)/shard_map/ppermute | solution.py:1413
  200.9 15.1 %collective-permute-start.9 = (bf16[1280,128]{1,0:T(8,128)(2,1)}, bf16[1280,128]{1,0:T(8,128)(2,1)S(1)}, u32[]{:S(2)}, u32[]{:S(2)}) collective-permute-start(bf16[1280,128]{1,0:T(8,128)(2,1)} %get-tuple-element.325), channel_id=1, source_target_pairs={{0,16},{4,20},{8,24},{12,28},{16,0},{20,4},{24,8},{28,12},{1,17},{... | collective-permute-start | bytes 983048 | tf_op jit(solution)/shard_map/ppermute | solution.py:1413
  201.3 14.7 %collective-permute-start.8 = (bf16[1280,128]{1,0:T(8,128)(2,1)S(1)}, bf16[1280,128]{1,0:T(8,128)(2,1)S(1)}, u32[]{:S(2)}, u32[]{:S(2)}) collective-permute-start(bf16[1280,128]{1,0:T(8,128)(2,1)S(1)} %get-tuple-element.326), channel_id=1, source_target_pairs={{0,8},{4,12},{8,0},{12,4},{16,24},{20,28},{24,16},{28,20},{1,9},{5... | collective-permute-start | bytes 983048 | tf_op jit(solution)/shard_map/ppermute | solution.py:1413
  201.7 107.7 %all-gather.2.cloned.1.call-start = ((), (), s32[]{:S(2)}) async-start(), calls=%async_computation.6 | async-start | bytes 2949120 | tf_op jit(solution)/shard_map/all_gather | solution.py:1558
  202.0 14.0 %copy-start.9 = (bf16[3328,128]{1,0:T(8,128)(2,1)S(1)}, bf16[3328,128]{1,0:T(8,128)(2,1)}, u32[]{:S(2)}) copy-start(bf16[3328,128]{1,0:T(8,128)(2,1)} %get-tuple-element.260) | copy-start | bytes 2555908
  216.3 12.9 %collective-permute-start.14 = (bf16[832,128]{1,0:T(8,128)(2,1)S(1)}, bf16[832,128]{1,0:T(8,128)(2,1)S(1)}, u32[]{:S(2)}, u32[]{:S(2)}) collective-permute-start(bf16[832,128]{1,0:T(8,128)(2,1)S(1)} %get-tuple-element.330), channel_id=1, source_target_pairs={{0,24},{4,28},{8,16},{12,20},{16,8},{20,12},{24,0},{28,4},{1,25},{... | collective-permute-start | bytes 638984 | tf_op jit(solution)/shard_map/ppermute | solution.py:1413
  218.1 11.1 %collective-permute-start.13 = (bf16[832,128]{1,0:T(8,128)(2,1)S(1)}, bf16[832,128]{1,0:T(8,128)(2,1)S(1)}, u32[]{:S(2)}, u32[]{:S(2)}) collective-permute-start(bf16[832,128]{1,0:T(8,128)(2,1)S(1)} %get-tuple-element.331), channel_id=1, source_target_pairs={{0,16},{4,20},{8,24},{12,28},{16,0},{20,4},{24,8},{28,12},{1,17},{... | collective-permute-start | bytes 638984 | tf_op jit(solution)/shard_map/ppermute | solution.py:1413
  219.6 9.6 %collective-permute-start.12 = (bf16[832,128]{1,0:T(8,128)(2,1)S(1)}, bf16[832,128]{1,0:T(8,128)(2,1)S(1)}, u32[]{:S(2)}, u32[]{:S(2)}) collective-permute-start(bf16[832,128]{1,0:T(8,128)(2,1)S(1)} %get-tuple-element.332), channel_id=1, source_target_pairs={{0,8},{4,12},{8,0},{12,4},{16,24},{20,28},{24,16},{28,20},{1,9},{5... | collective-permute-start | bytes 638984 | tf_op jit(solution)/shard_map/ppermute | solution.py:1413
  229.4 15.2 %collective-permute-start.15 = (bf16[528,128]{1,0:T(8,128)(2,1)S(1)}, bf16[528,128]{1,0:T(8,128)(2,1)S(1)}, u32[]{:S(2)}, u32[]{:S(2)}) collective-permute-start(bf16[528,128]{1,0:T(8,128)(2,1)S(1)} %pad_maximum_fusion.1), channel_id=1, source_target_pairs={{0,1},{1,0},{2,3},{3,2},{4,5},{5,4},{6,7},{7,6},{8,9},{9,8},{10,11... | collective-permute-start | bytes 405512 | tf_op jit(solution)/shard_map/ppermute | solution.py:1416
  229.5 15.1 %collective-permute-start.16 = (bf16[528,128]{1,0:T(8,128)(2,1)S(1)}, bf16[528,128]{1,0:T(8,128)(2,1)S(1)}, u32[]{:S(2)}, u32[]{:S(2)}) collective-permute-start(bf16[528,128]{1,0:T(8,128)(2,1)S(1)} %pad_maximum_fusion.2), channel_id=1, source_target_pairs={{0,2},{1,3},{2,0},{3,1},{4,6},{5,7},{6,4},{7,5},{8,10},{9,11},{10,... | collective-permute-start | bytes 405512 | tf_op jit(solution)/shard_map/ppermute | solution.py:1416
  231.8 12.8 %collective-permute-start.17 = (bf16[528,128]{1,0:T(8,128)(2,1)S(1)}, bf16[528,128]{1,0:T(8,128)(2,1)S(1)}, u32[]{:S(2)}, u32[]{:S(2)}) collective-permute-start(bf16[528,128]{1,0:T(8,128)(2,1)S(1)} %pad_maximum_fusion.3), channel_id=1, source_target_pairs={{0,3},{1,2},{2,1},{3,0},{4,7},{5,6},{6,5},{7,4},{8,11},{9,10},{10,... | collective-permute-start | bytes 405512 | tf_op jit(solution)/shard_map/ppermute | solution.py:1416
  244.6 2.7 collective-permute-start.18
  244.8 17.6 %collective-permute-start.24 = (bf16[528,128]{1,0:T(8,128)(2,1)S(1)}, bf16[528,128]{1,0:T(8,128)(2,1)S(1)}, u32[]{:S(2)}, u32[]{:S(2)}) collective-permute-start(bf16[528,128]{1,0:T(8,128)(2,1)S(1)} %add_convert_fusion.3.refs_0_), channel_id=1, source_target_pairs={{0,3},{1,2},{2,1},{3,0},{4,7},{5,6},{6,5},{7,4},{8,11},{9,10},{10,... | collective-permute-start | bytes 405512 | tf_op jit(solution)/shard_map/ppermute | solution.py:1416
  250.8 55.8 %all-to-all-start.2 = ((bf16[2,64,4608]{2,0,1:T(2,128)(2,1)}), bf16[2,64,4608]{2,0,1:T(2,128)(2,1)S(1)}, u32[]{:S(2)}, u32[]{:S(2)}) async-start(bf16[2,64,4608]{2,0,1:T(2,128)(2,1)} %copy.34), calls=%async_computation.3 | async-start | bytes 2359296 | tf_op jit(solution)/shard_map/all_to_all | solution.py:1518
  256.0 34.3 %collective-permute-start.21 = (bf16[832,128]{1,0:T(8,128)(2,1)S(1)}, bf16[832,128]{1,0:T(8,128)(2,1)S(1)}, u32[]{:S(2)}, u32[]{:S(2)}) collective-permute-start(bf16[832,128]{1,0:T(8,128)(2,1)S(1)} %get-tuple-element.327), channel_id=1, source_target_pairs={{0,24},{4,28},{8,16},{12,20},{16,8},{20,12},{24,0},{28,4},{1,25},{... | collective-permute-start | bytes 638984 | tf_op jit(solution)/shard_map/ppermute | solution.py:1413
  257.7 32.5 %collective-permute-start.20 = (bf16[832,128]{1,0:T(8,128)(2,1)S(1)}, bf16[832,128]{1,0:T(8,128)(2,1)S(1)}, u32[]{:S(2)}, u32[]{:S(2)}) collective-permute-start(bf16[832,128]{1,0:T(8,128)(2,1)S(1)} %get-tuple-element.328), channel_id=1, source_target_pairs={{0,16},{4,20},{8,24},{12,28},{16,0},{20,4},{24,8},{28,12},{1,17},{... | collective-permute-start | bytes 638984 | tf_op jit(solution)/shard_map/ppermute | solution.py:1413
  259.1 31.2 %collective-permute-start.19 = (bf16[832,128]{1,0:T(8,128)(2,1)S(1)}, bf16[832,128]{1,0:T(8,128)(2,1)S(1)}, u32[]{:S(2)}, u32[]{:S(2)}) collective-permute-start(bf16[832,128]{1,0:T(8,128)(2,1)S(1)} %get-tuple-element.329), channel_id=1, source_target_pairs={{0,8},{4,12},{8,0},{12,4},{16,24},{20,28},{24,16},{28,20},{1,9},{5... | collective-permute-start | bytes 638984 | tf_op jit(solution)/shard_map/ppermute | solution.py:1413
  259.5 30.8 %collective-permute-start.23 = (bf16[528,128]{1,0:T(8,128)(2,1)S(1)}, bf16[528,128]{1,0:T(8,128)(2,1)S(1)}, u32[]{:S(2)}, u32[]{:S(2)}) collective-permute-start(bf16[528,128]{1,0:T(8,128)(2,1)S(1)} %add_convert_fusion.3.refs_0_), channel_id=1, source_target_pairs={{0,2},{1,3},{2,0},{3,1},{4,6},{5,7},{6,4},{7,5},{8,10},{9,11},{10,... | collective-permute-start | bytes 405512 | tf_op jit(solution)/shard_map/ppermute | solution.py:1416
  262.4 27.8 %collective-permute-start.22 = (bf16[528,128]{1,0:T(8,128)(2,1)S(1)}, bf16[528,128]{1,0:T(8,128)(2,1)S(1)}, u32[]{:S(2)}, u32[]{:S(2)}) collective-permute-start(bf16[528,128]{1,0:T(8,128)(2,1)S(1)} %add_convert_fusion.3.refs_0_), channel_id=1, source_target_pairs={{0,1},{1,0},{2,3},{3,2},{4,5},{5,4},{6,7},{7,6},{8,9},{9,8},{10,11... | collective-permute-start | bytes 405512 | tf_op jit(solution)/shard_map/ppermute | solution.py:1416
  291.1 9.4 %collective-permute-start.28 = (bf16[2112,128]{1,0:T(8,128)(2,1)S(1)}, bf16[2112,128]{1,0:T(8,128)(2,1)S(1)}, u32[]{:S(2)}, u32[]{:S(2)}) collective-permute-start(bf16[2112,128]{1,0:T(8,128)(2,1)S(1)} %shard_map.256.refs_0_), channel_id=1, source_target_pairs={{0,8},{4,20},{8,0},{12,28},{16,24},{20,4},{24,16},{28,12},{1,9},{5... | collective-permute-start | bytes 1622024 | tf_op jit(solution)/shard_map/ppermute | solution.py:1446
  292.9 6.4 %collective-permute-start.27 = (bf16[208,128]{1,0:T(8,128)(2,1)S(1)}, bf16[208,128]{1,0:T(8,128)(2,1)S(1)}, u32[]{:S(2)}, u32[]{:S(2)}) collective-permute-start(bf16[208,128]{1,0:T(8,128)(2,1)S(1)} %get-tuple-element.337), channel_id=1, source_target_pairs={{0,3},{1,2},{2,1},{3,0},{4,7},{5,6},{6,5},{7,4},{8,11},{9,10},{10,... | collective-permute-start | bytes 159752 | tf_op jit(solution)/shard_map/ppermute | solution.py:1416
  294.9 5.6 %collective-permute-start.26 = (bf16[208,128]{1,0:T(8,128)(2,1)S(1)}, bf16[208,128]{1,0:T(8,128)(2,1)S(1)}, u32[]{:S(2)}, u32[]{:S(2)}) collective-permute-start(bf16[208,128]{1,0:T(8,128)(2,1)S(1)} %get-tuple-element.338), channel_id=1, source_target_pairs={{0,2},{1,3},{2,0},{3,1},{4,6},{5,7},{6,4},{7,5},{8,10},{9,11},{10,... | collective-permute-start | bytes 159752 | tf_op jit(solution)/shard_map/ppermute | solution.py:1416
  294.9 5.6 %collective-permute-start.25 = (bf16[208,128]{1,0:T(8,128)(2,1)S(1)}, bf16[208,128]{1,0:T(8,128)(2,1)S(1)}, u32[]{:S(2)}, u32[]{:S(2)}) collective-permute-start(bf16[208,128]{1,0:T(8,128)(2,1)S(1)} %get-tuple-element.339), channel_id=1, source_target_pairs={{0,1},{1,0},{2,3},{3,2},{4,5},{5,4},{6,7},{7,6},{8,9},{9,8},{10,11... | collective-permute-start | bytes 159752 | tf_op jit(solution)/shard_map/ppermute | solution.py:1416
  300.7 22.1 %collective-permute-start.35 = (bf16[4224,128]{1,0:T(8,128)(2,1)S(1)}, bf16[4224,128]{1,0:T(8,128)(2,1)S(1)}, u32[]{:S(2)}, u32[]{:S(2)}) collective-permute-start(bf16[4224,128]{1,0:T(8,128)(2,1)S(1)} %shard_map.258.refs_0_), channel_id=1, source_target_pairs={{0,16},{4,12},{8,24},{12,4},{16,0},{20,28},{24,8},{28,20},{1,17},{... | collective-permute-start | bytes 3244040 | tf_op jit(solution)/shard_map/ppermute | solution.py:1446
  302.2 6.3 %collective-permute-start.31 = (bf16[208,128]{1,0:T(8,128)(2,1)S(1)}, bf16[208,128]{1,0:T(8,128)(2,1)S(1)}, u32[]{:S(2)}, u32[]{:S(2)}) collective-permute-start(bf16[208,128]{1,0:T(8,128)(2,1)S(1)} %fusion.11.refs_0_), channel_id=1, source_target_pairs={{0,3},{1,2},{2,1},{3,0},{4,7},{5,6},{6,5},{7,4},{8,11},{9,10},{10,... | collective-permute-start | bytes 159752 | tf_op jit(solution)/shard_map/ppermute | solution.py:1416
  304.2 5.2 %collective-permute-start.30 = (bf16[208,128]{1,0:T(8,128)(2,1)S(1)}, bf16[208,128]{1,0:T(8,128)(2,1)S(1)}, u32[]{:S(2)}, u32[]{:S(2)}) collective-permute-start(bf16[208,128]{1,0:T(8,128)(2,1)S(1)} %fusion.11.refs_0_), channel_id=1, source_target_pairs={{0,2},{1,3},{2,0},{3,1},{4,6},{5,7},{6,4},{7,5},{8,10},{9,11},{10,... | collective-permute-start | bytes 159752 | tf_op jit(solution)/shard_map/ppermute | solution.py:1416
  304.2 5.2 %collective-permute-start.29 = (bf16[208,128]{1,0:T(8,128)(2,1)S(1)}, bf16[208,128]{1,0:T(8,128)(2,1)S(1)}, u32[]{:S(2)}, u32[]{:S(2)}) collective-permute-start(bf16[208,128]{1,0:T(8,128)(2,1)S(1)} %fusion.11.refs_0_), channel_id=1, source_target_pairs={{0,1},{1,0},{2,3},{3,2},{4,5},{5,4},{6,7},{7,6},{8,9},{9,8},{10,11... | collective-permute-start | bytes 159752 | tf_op jit(solution)/shard_map/ppermute | solution.py:1416
  309.8 12.9 %collective-permute-start.34 = (bf16[832,128]{1,0:T(8,128)(2,1)S(1)}, bf16[832,128]{1,0:T(8,128)(2,1)S(1)}, u32[]{:S(2)}, u32[]{:S(2)}) collective-permute-start(bf16[832,128]{1,0:T(8,128)(2,1)S(1)} %shard_map.257.refs_0_), channel_id=1, source_target_pairs={{0,24},{4,28},{8,16},{12,20},{16,8},{20,12},{24,0},{28,4},{1,25},{... | collective-permute-start | bytes 638984 | tf_op jit(solution)/shard_map/ppermute | solution.py:1413
  311.4 13.6 %collective-permute-start.33 = (bf16[832,128]{1,0:T(8,128)(2,1)S(1)}, bf16[832,128]{1,0:T(8,128)(2,1)S(1)}, u32[]{:S(2)}, u32[]{:S(2)}) collective-permute-start(bf16[832,128]{1,0:T(8,128)(2,1)S(1)} %shard_map.257.refs_0_), channel_id=1, source_target_pairs={{0,16},{4,20},{8,24},{12,28},{16,0},{20,4},{24,8},{28,12},{1,17},{... | collective-permute-start | bytes 638984 | tf_op jit(solution)/shard_map/ppermute | solution.py:1413
  312.2 12.8 %collective-permute-start.32 = (bf16[832,128]{1,0:T(8,128)(2,1)S(1)}, bf16[832,128]{1,0:T(8,128)(2,1)S(1)}, u32[]{:S(2)}, u32[]{:S(2)}) collective-permute-start(bf16[832,128]{1,0:T(8,128)(2,1)S(1)} %shard_map.257.refs_0_), channel_id=1, source_target_pairs={{0,8},{4,12},{8,0},{12,4},{16,24},{20,28},{24,16},{28,20},{1,9},{5... | collective-permute-start | bytes 638984 | tf_op jit(solution)/shard_map/ppermute | solution.py:1413
  325.3 5.5 %collective-permute-start.37 = (bf16[8448,128]{1,0:T(8,128)(2,1)S(1)}, bf16[8448,128]{1,0:T(8,128)(2,1)S(1)}, u32[]{:S(2)}, u32[]{:S(2)}) collective-permute-start(bf16[8448,128]{1,0:T(8,128)(2,1)S(1)} %shard_map.260.refs_3_), channel_id=1, source_target_pairs={{0,4},{4,0},{8,12},{12,8},{16,20},{20,16},{24,28},{28,24},{1,5},{5... | collective-permute-start | bytes 6488072 | tf_op jit(solution)/shard_map/ppermute | solution.py:1410
  326.5 4.3 %collective-permute-start.36 = (bf16[3328,128]{1,0:T(8,128)(2,1)S(1)}, bf16[3328,128]{1,0:T(8,128)(2,1)S(1)}, u32[]{:S(2)}, u32[]{:S(2)}) collective-permute-start(bf16[3328,128]{1,0:T(8,128)(2,1)S(1)} %shard_map.259.refs_1_), channel_id=1, source_target_pairs={{0,4},{4,0},{8,12},{12,8},{16,20},{20,16},{24,28},{28,24},{1,5},{5... | collective-permute-start | bytes 2555912 | tf_op jit(solution)/shard_map/ppermute | solution.py:1410
  (12 other events, 62.2 us)
Sparse Core Ops, SparseCore 0:
  145.9 45.4 reduce-scatter.1
  201.9 42.3 all-reduce.1
  246.1 31.2 all-gather.1

commit v5 on v4

--- a/solution.py
+++ b/solution.py
@@ -200,13 +200,14 @@
     return jnp.concatenate([ref[r, lanes(half)] for r in pair_rows], axis=1)
 
 
-def forward(dm, counts, w, io, res, scr):
+def forward(dm, counts, w, io, res, scr, ready):
     x = io.nodes[...].astype(F32)
     n, r = node_norm(x)
     res.node_n1[...] = n.astype(BF)
     res.node_r1[...] = jnp.broadcast_to(r, (dm.nodes, 128))
     hn = (n * w.nn[0:1, :] + w.nn[1:2, :]).astype(BF)
     res.qkv[...] = nn(hn, w.qkv[...]).astype(BF)
+    ready("node_n1", "node_r1", "qkv")
 
     @dm.each_pair
     def _(rows, pair):
@@ -221,6 +222,7 @@
         scr.scores[pair, :] = both[:, :256]
         res.gate[pair, :] = both[:, 256:]
 
+    ready("edge_n1", "edge_r1", "gate")
     t0 = 0
     for bucket in dm.buckets:
         @pl.loop(0, bucket.graphs * bucket.blocks, unroll=True)
@@ -274,6 +276,7 @@
 
         t0 += bucket.graphs * bucket.blocks
 
+    ready("low", "prob", "mixed")
     y = io.nodes[...].astype(F32) + nn(res.mixed[...], w.o[...])
     n, r = node_norm(y)
     res.node_n2[...] = n.astype(BF)
@@ -281,6 +284,7 @@
     z = (n * w.nn[2:3, :] + w.nn[3:4, :]).astype(BF)
     u = nn(z, w.up[...])
     res.node_u[...] = u
+    ready("node_n2", "node_r2", "node_u")
     io.nodes_out[...] = (y + nn(gelu_value(u).astype(BF), w.down[...])).astype(BF)
 
     @dm.each_pair
@@ -296,6 +300,8 @@
         mn = (n * w.en[2:3, :] + w.en[3:4, :]).astype(BF)
         ua = nn(mn, w.a[...])
         io.edges_out[rows, :] = (m + nn(gelu_value(ua).astype(BF), w.b[...])).astype(BF)
+
+    ready("edge_n2", "edge_r2")
 
 
 def put_strided(flat, first, value, parts):
@@ -807,6 +813,25 @@
     )
 
 
+class Leaving:
+    def __init__(self, names, held, outs, sems):
+        self.names, self.held, self.outs, self.sems = tuple(names), held, outs, sems
+        self.copies = []
+
+    def __call__(self, *names):
+        for k in names:
+            if k in self.names:
+                sem = self.sems.at[len(self.copies)]
+                self.copies.append(
+                    pltpu.make_async_copy(getattr(self.held, k), getattr(self.outs, k), sem)
+                )
+                self.copies[-1].start()
+
+    def wait(self):
+        assert len(self.copies) == len(self.names)
+        wait(self.copies)
+
+
 def first_forward(dm, counts, weights, small_nodes, small_edges, big):
     res = residual_shapes(dm)
     out = {"nodes_out": ((dm.nodes, D), BF), "edges_out": ((dm.edges, 256), BF), **res}
@@ -815,10 +840,11 @@
         **forward_scratch(dm),
         "nodes": ((dm.nodes, D), BF),
         "edges": ((dm.edges, 256), BF),
+        **res,
     }
 
     def body(*refs):
-        counts_ref, refs, sems = refs[0], refs[1:-1], refs[-1]
+        counts_ref, refs, sems, out_sems = refs[0], refs[1:-2], refs[-2], refs[-1]
         w, src, dst, s = split(refs, WEIGHTS, ("sn", "se", "big"), out, scr)
         copies = all_copies(
             dm, src.sn, src.se, src.big, 0, 2 * EDGE_LANES, s.nodes, s.edges, sems, False
@@ -829,11 +855,14 @@
             ("nodes", "edges", "nodes_out", "edges_out"),
             (s.nodes, s.edges, dst.nodes_out, dst.edges_out),
         )
+        leaving = Leaving(res, s, dst, out_sems)
         wait(copies)
-        forward(dm, counts_ref, w, io, dst, s)
+        forward(dm, counts_ref, w, io, s, s, leaving)
+        leaving.wait()
 
     inputs = take(weights, WEIGHTS) + [small_nodes, small_edges, big]
-    got = kernel(body, inputs, out, scr, 38, counts, 3, (), [copy_sems(dm)])
+    sems = [copy_sems(dm), pltpu.SemaphoreType.DMA((len(res),))]
+    got = kernel(body, inputs, out, scr, 16, counts, 3, tuple(res), sems)
     return got.nodes_out, got.edges_out, got
 
 
@@ -844,45 +873,44 @@
         "seo": ((dm.small.rows, dm.small.edge_lanes), BF),
         "bout": ((dm.big.rows, OUT_LANES), BF),
     }
-    node_res = [k for k in res if k in NODE_BACK]
     kept = {k: v for k, v in res.items() if k not in NODE_BACK}
     out = {**whole_outs, "edge_cot": ((dm.edges, 256), BF), **kept, **ffn}
     scr = {
         **mask_shapes(),
         **forward_scratch(dm),
         **ffn_scratch(),
-        **{k: res[k] for k in node_res},
+        **res,
         "nodes_out": ((dm.nodes, D), BF),
         "edges_out": ((dm.edges, 256), BF),
         "node_cot": ((dm.nodes, D), BF),
     }
 
     def body(*refs):
-        counts_ref, refs, in_sems, out_sems = refs[0], refs[1:-2], refs[-2], refs[-1]
+        counts_ref, refs, in_sems, out_sems, res_sems = refs[0], refs[1:-3], *refs[-3:]
         w, src, dst, s = split(refs, WEIGHTS, ("nodes", "edges", "snc", "sec", "big"), out, scr)
         copies = all_copies(
             dm, src.snc, src.sec, src.big, EDGE_LANES, 2 * EDGE_LANES + D, s.node_cot, dst.edge_cot, in_sems, False
         )
         start(copies)
         make_masks(s)
-        every = Group(
-            [*kept, *node_res], [getattr(dst, k) for k in kept] + [getattr(s, k) for k in node_res]
-        )
+        leaving = Leaving(kept, s, dst, res_sems)
         io = Group(
             ("nodes", "edges", "nodes_out", "edges_out"),
             (src.nodes, src.edges, s.nodes_out, s.edges_out),
         )
-        forward(dm, counts_ref, w, io, every, s)
+        forward(dm, counts_ref, w, io, s, s, leaving)
         outgoing = all_copies(
             dm, dst.sno, dst.seo, dst.bout, 0, EDGE_LANES, s.nodes_out, s.edges_out, out_sems, True
         )
         start(outgoing)
         wait(copies)
-        back_ffn(dm, w, Group(("nodes_cot", *ffn), (s.node_cot, *take(dst, ffn))), every, s)
+        back_ffn(dm, w, Group(("nodes_cot", *ffn), (s.node_cot, *take(dst, ffn))), s, s)
         wait(outgoing)
+        leaving.wait()
 
     inputs = take(weights, WEIGHTS) + [nodes, edges, small_node_cot, small_edge_cot, big]
-    got = kernel(body, inputs, out, scr, 46, counts, 3, tuple(whole_outs), [copy_sems(dm)] * 2)
+    sems = [copy_sems(dm), copy_sems(dm), pltpu.SemaphoreType.DMA((len(kept),))]
+    got = kernel(body, inputs, out, scr, 22, counts, 3, (*whole_outs, *kept), sems)
     return got.sno, got.seo, got.bout, None, got.edge_cot, got, got
 
 
@@ -1019,7 +1047,7 @@
     held = master.shape[0]
     count = owner.shape[0]
     padded = round_up(held + 15, 16)
-    step = 1664
+    step = round_up(-(-padded // 2), 16)
 
     def body(owner_ref, rows_ref, src, dst, window):
         i = pl.program_id(0)
@@ -1513,10 +1541,30 @@
     def flat2(v):
         return v.reshape(-1, v.shape[-1])
 
+    def packed(v, first, lanes):
+        v = v[:, first : first + lanes].reshape(share, n_row, NB // n_row, lanes)
+        return v.swapaxes(0, 1)
+
     def to_rows(v):
-        v = v.reshape(share, NB, OUT_LANES)
-        v = lax.all_to_all(v, "row", split_axis=1, concat_axis=0, tiled=True)
-        return v[..., EDGE_LANES:], v[..., :EDGE_LANES]
+        v = lax.all_to_all(v, "row", split_axis=0, concat_axis=0, tiled=True)
+        return v.reshape(n_row * share, NB // n_row, v.shape[-1])
+
+    row = lax.axis_index("row")
+
+    def row_pieces(v):
+        v = v.reshape(share, n_row, NB // n_row, OUT_LANES)
+        return [lax.dynamic_index_in_dim(v, row ^ k, 1, keepdims=False) for k in range(n_row)]
+
+    def send_pieces(pieces):
+        pairs = lambda k: [(i, i ^ k) for i in range(n_row)]
+        return pieces[:1] + [lax.ppermute(pieces[k], "row", pairs(k)) for k in range(1, n_row)]
+
+    def in_order(pieces, first, lanes):
+        pieces = [p[..., first : first + lanes] for p in pieces]
+        for k in range(n_row.bit_length() - 1):
+            odd = (row >> k) & 1 == 1
+            pieces = [jnp.where(odd, pieces[i ^ (1 << k)], p) for i, p in enumerate(pieces)]
+        return jnp.concatenate(pieces)
 
     def to_whole(first):
         big = (big_edges, big_edge_cot, big_nodes, big_node_cot)
@@ -1539,8 +1587,7 @@
     spread = lax.psum_scatter(ffn_two.upper, "dp", scatter_dimension=0, tiled=True)
     got = between(dm, two, one, kept_two, kept, ffn_two, edge_cot)
     names = tuple(vars(got))
-    outs = to_rows(bout)
-    *values, bno, beo = phase([], *take(got, names), *outs)
+    values, out_pieces = phase([], take(got, names), send_pieces(row_pieces(bout)))
     got = Group(names, values)
     middle = Chain(cube, False, (got.keep, got.send))
     rest = second_last(dm, two, kept_two, got)
@@ -1558,17 +1605,23 @@
     upper_two = lax.all_gather(spread, "dp", axis=0, tiled=True)
     last = Chain(cube, True, (keep, send))
     sent = middle.launch()
+    early = EDGE_LANES // 2
     bgrad, = phase([last], bgrad)
-    outs = to_rows(bgrad)
-    sent, = phase([last], sent)
+    one_part, two_part = packed(bgrad, 0, early), packed(bgrad, early, OUT_LANES - early)
+    one_part = to_rows(one_part)
+    sent, out_pieces = phase([last], sent, out_pieces)
+    bno, beo = in_order(out_pieces, EDGE_LANES, D), in_order(out_pieces, 0, EDGE_LANES)
     middle.land(sent)
     phase([last, middle])
     sent = middle.launch()
-    bng, beg, upper_two = phase([last], *outs, upper_two)
-    sent, = phase([last], sent)
+    one_part, upper_two, bno, beo = phase([last], one_part, upper_two, bno, beo)
+    sent, two_part = phase([last], sent, two_part)
     middle.land(sent)
     while not (last.done and middle.done):
-        phase([last, middle])
+        two_part, = phase([last, middle], two_part)
+    two_part = to_rows(two_part)
+    bng = two_part[..., EDGE_LANES - early :]
+    beg = jnp.concatenate([one_part, two_part[..., : EDGE_LANES - early]], axis=-1)
     blocks = last.blocks((0, 0)) + middle.blocks((0, 1), (1, 0))
     step_value = step_count[0].astype(F32)
     scales = jnp.stack(

time: 358 us -> 351 us (0.980)
  waiting for transfers between devices: 116 us -> 102 us
  other arithmetic: 5.37 us -> 13.6 us
    ppermute x12, waiting for transfers between devices: 30.5 us -> 9.42 us  [to_row(): return lax.ppermute(value, 'row', [(i, i ^ k) for i in range(self.rows)])]
    ppermute x12, waiting for transfers between devices: 3.91 us -> 9.08 us  [to_chip(): lax.ppermute(value, 'dp', [(i, i ^ k << 1) for i in range(2 * self.sides)])]
    ppermute x0 -> x3, starting transfers between devices: none -> 4.55 us  [send_pieces(): lax.ppermute(pieces[k], 'row', pairs(k))]
    reduce_scatter x1, waiting for transfers between devices: 0.02 us -> 4.24 us  [per_device(): lax.psum_scatter(ffn_two.upper, 'dp', scatter_dimension=0, tiled=True)]
    reshape x2, local copies, waits for them, and re-layouts: 5.8 us -> 1.71 us  [packed(): v = v[:, first:first + lanes].reshape(share, n_row, NB // n_row, lanes)]
    concatenate x0 -> x3, other arithmetic: none -> 3.88 us  [the longest x1 2.11 us: per_device(): jnp.concatenate([one_part, two_part[..., :EDGE_LANES - early]], axis=-1)]
  transfers between devices with their start and end apart: 44 -> 47, of which waited for: 15 -> 20; matrix products, arithmetic and copies ran while one was open for 5% -> 5% of each run, Pallas kernels for 20% -> 24%
where the time goes in v5:
time: 351 us; the launch traced here: 347 us
  Pallas kernels  136 us (39%)
  waiting for transfers between devices  102 us (29%)
  starting transfers between devices  62.7 us (18%)
  local copies, waits for them, and re-layouts  16.8 us (5%)
  between operations  15.3 us (4%)
  other arithmetic  13.6 us (4%)
    pallas_call x7, Pallas kernels, kernel(): pl.pallas_call(body, out_shape=structs(out), in_specs=[SMEM] * len(smem)...  104 us
    ppermute x3, waiting for transfers between devices, gather(): sent.append((0, used + (step,), lax.ppermute(v, 'dp', self.pairs(step))))  50.5 us
    ppermute x12, starting transfers between devices, to_row(): return lax.ppermute(value, 'row', [(i, i ^ k) for i in range(self.rows)])  19.9 us
    pallas_call x1, Pallas kernels, adam(): pl.pallas_call(body, grid=(pl.cdiv(held, step),), out_shape=[shape] * 3 +...  15 us
    ppermute x12, starting transfers between devices, to_chip(): lax.ppermute(value, 'dp', [(i, i ^ k << 1) for i in range(2 * self.sides)])  14.1 us
    all_to_all x1, waiting for transfers between devices, to_whole(): lax.all_to_all(big, 'row', split_axis=0, concat_axis=1, tiled=True)  12.3 us
    pallas_call x1, Pallas kernels, assemble(): pl.pallas_call(body, out_shape=structs(out), in_specs=[SMEM] * 2 + [HBM]...  10.6 us
    ppermute x12, waiting for transfers between devices, to_row(): return lax.ppermute(value, 'row', [(i, i ^ k) for i in range(self.rows)])  9.42 us
  transfers between devices with their start and end apart: 47, of which 20 were waited for; matrix products, arithmetic and copies ran while one was open for 5% of the time, Pallas kernels for 24%

profile of v5, /device:TPU:0, one launch (start us, length us, event | category | flops | bytes accessed | tf_op | source)
XLA Modules:
  0.0 346.7 jit_solution(800118787438220627)
XLA Ops:
  7.2 4.4 %shard_map.247.refs_0_ = bf16[8320,128]{1,0:T(8,128)(2,1)} custom-call(s32[8]{0:T(128)} %owner_ref.5, s32[8]{0:T(128)} %rows_ref.5, f32[8290,128]{1,0:T(8,128)} %refs_5_.1), custom_call_target="tpu_custom_call" | custom-call | tf_op jit(solution)/shard_map/pallas_call | solution.py:1068
  12.0 2.5 collective-permute-start.1
  14.5 1.5 collective-permute-start
  16.1 1.5 pad_maximum_fusion
  17.6 4.9 %all-to-all-start = ((bf16[8,16,9216]{2,1,0:T(8,128)(2,1)}), bf16[8,16,9216]{2,1,0:T(8,128)(2,1)S(1)}, u32[]{:S(2)}, u32[]{:S(2)}) async-start(bf16[8,16,9216]{2,1,0:T(8,128)(2,1)} %pad_maximum_fusion), calls=%async_computation | async-start | bytes 4718592 | tf_op jit(solution)/shard_map/all_to_all | solution.py:1573
  22.4 38.4 %collective-permute-done.1.refs_3_ = bf16[8320,128]{1,0:T(8,128)(2,1)} collective-permute-done((bf16[8320,128]{1,0:T(8,128)(2,1)}, bf16[8320,128]{1,0:T(8,128)(2,1)}, u32[]{:S(2)}, u32[]{:S(2)}) %collective-permute-start.1) | collective-permute-done | bytes 2129952 | tf_op jit(solution)/shard_map/ppermute | solution.py:1366
  62.4 1.7 collective-permute-start.3
  64.1 12.3 %all-to-all-done = bf16[8,16,9216]{2,1,0:T(8,128)(2,1)S(1)} async-done(((bf16[8,16,9216]{2,1,0:T(8,128)(2,1)}), bf16[8,16,9216]{2,1,0:T(8,128)(2,1)S(1)}, u32[]{:S(2)}, u32[]{:S(2)}) %all-to-all-start) | async-done | bytes 2359328 | tf_op jit(solution)/shard_map/all_to_all | solution.py:1573
  76.4 1.6 copy.31
  78.0 11.1 %collective-permute-done.3.refs_6_ = bf16[8320,128]{1,0:T(8,128)(2,1)} collective-permute-done((bf16[8320,128]{1,0:T(8,128)(2,1)}, bf16[8320,128]{1,0:T(8,128)(2,1)}, u32[]{:S(2)}, u32[]{:S(2)}) %collective-permute-start.3) | collective-permute-done | bytes 2129952 | tf_op jit(solution)/shard_map/ppermute | solution.py:1366
  89.7 3.7 %collective-permute-done.6.refs_7_ = bf16[8320,128]{1,0:T(8,128)(2,1)S(1)} collective-permute-done((bf16[8320,128]{1,0:T(8,128)(2,1)}, bf16[8320,128]{1,0:T(8,128)(2,1)S(1)}, u32[]{:S(2)}, u32[]{:S(2)}) %collective-permute-start.6) | collective-permute-done | bytes 2129952 | tf_op jit(solution)/shard_map/ppermute | solution.py:1368
  94.8 10.6 %shard_map.248 = (bf16[512,1536]{1,0:T(8,128)(2,1)}, bf16[512,512]{1,0:T(8,128)(2,1)}, bf16[512,1024]{1,0:T(8,128)(2,1)}, bf16[1024,512]{1,0:T(8,128)(2,1)}, bf1...) custom-call(s32[8]{0:T(128)} %owner_ref.5, ...), custom_call_target="tpu_custom_call" | custom-call | bytes 34000000 | tf_op jit(solution)/shard_map/pallas_call | solution.py:1147
  105.4 17.0 %shard_map.249 = (bf16[224,512]{1,0:T(8,128)(2,1)}, bf16[2816,256]{1,0:T(8,128)(2,1)}, bf16[224,512]{1,0:T(8,128)(2,1)}, f32[224,128]{1,0:T(8,128)}, bf16[224,15...) custom-call(s32[5]{0:T(128)} %pad_add_fusion.refs_0_, ...), custom_call_target="tpu_custom_call" | custom-call | bytes 54400000 | tf_op jit(solution)/shard_map/pallas_call | solution.py:804
  122.4 20.0 %shard_map.250 = (bf16[96,512]{1,0:T(8,128)(2,1)}, bf16[96,2048]{1,0:T(8,128)(2,1)}, bf16[128,4608]{1,0:T(8,128)(2,1)}, bf16[2816,256]{1,0:T(8,128)(2,1)}, bf16[...) custom-call(s32[5]{0:T(128)} %pad_add_fusion.refs_0_, ...), custom_call_target="tpu_custom_call" | custom-call | bytes 74800000 | tf_op jit(solution)/shard_map/pallas_call | solution.py:804
  143.8 3.9 %collective-permute-start.9 = (bf16[2,16,4608]{2,1,0:T(8,128)(2,1)S(1)}, bf16[2,16,4608]{2,1,0:T(8,128)(2,1)S(1)}, u32[]{:S(2)}, u32[]{:S(2)}) collective-permute-start(bf16[2,16,4608]{2,1,0:T(8,128)(2,1)S(1)} %get-tuple-element.353), channel_id=1, source_target_pairs={{0,3},{1,2},{2,1},{3,0},{4,7},{5,6},{6,5},{7,4},{8,11},{9,10},{10,... | collective-permute-start | bytes 884744 | tf_op jit(solution)/shard_map/ppermute | solution.py:1560
  148.4 25.7 %shard_map.251 = (bf16[2816,256]{1,0:T(8,128)(2,1)}, f32[256,128]{1,0:T(8,128)}, bf16[1408,512]{1,0:T(8,128)(2,1)}, bf16[224,1536]{1,0:T(8,128)(2,1)}, f32[8,128...) custom-call(bf16[512,1536]{1,0:T(8,128)(2,1)} %get-tuple-element.189, ...), custom_call_target="tpu_custom_call" | custom-call | bytes 85000000 | tf_op jit(solution)/shard_map/pallas_call | solution.py:804
  175.0 8.8 %shard_map.252 = (bf16[2816,256]{1,0:T(8,128)(2,1)}, bf16[3328,128]{1,0:T(8,128)(2,1)}, bf16[3328,128]{1,0:T(8,128)(2,1)}) custom-call(bf16[512,512]{1,0:T(8,128)(2,1)} %get-tuple-element.193.refs_5_.refs_0_, f32[4,512]{1,0:T(4,128)} %get-tuple-element.197.refs_9_.refs_5_.refs_1_, f32[4,256]{1,0:T(4,128)} %get-tuple-element.198.refs_10_.refs_4_.refs_2_, ...), custom_call_target="tpu_custom_call" | custom-call | bytes 30600000 | tf_op jit(solution)/shard_map/pallas_call | solution.py:804
  183.8 4.2 %reduce-scatter.2.cloned.1.call-done = bf16[1280,128]{1,0:T(8,128)(2,1)} async-done(((bf16[10240,128]{1,0:T(8,128)(2,1)}), bf16[1280,128]{1,0:T(8,128)(2,1)}) %reduce-scatter.2.cloned.1.call-update) | async-done | bytes 327696 | tf_op jit(solution)/shard_map/reduce_scatter | solution.py:1587
  188.1 1.7 add_convert_fusion
  190.7 1.5 collective-permute-start.13
  194.7 12.4 %shard_map.253 = (bf16[2816,256]{1,0:T(8,128)(2,1)}, f32[1408,256]{1,0:T(8,128)}, f32[256,128]{1,0:T(8,128)}) custom-call(bf16[256,512]{1,0:T(8,128)(2,1)} %get-tuple-element.204.refs_6_.refs_0_, bf16[256,512]{1,0:T(8,128)(2,1)} %get-tuple-element.205.refs_7_.refs_1_, bf16[512,256]{1,0:T(8,128)(2,1)} %get-tuple-element.206.refs_8_.refs_2_, ...), custom_call_target="tpu_custom_call" | custom-call | bytes 54400000 | tf_op jit(solution)/shard_map/pallas_call | solution.py:804
  207.1 1.9 collective-permute-done.12
  210.4 1.5 collective-permute-start.17
  214.1 9.1 %shard_map.254 = (bf16[1408,512]{1,0:T(8,128)(2,1)}, bf16[224,1536]{1,0:T(8,128)(2,1)}) custom-call(bf16[224,1536]{1,0:T(8,128)(2,1)} %get-tuple-element.269.refs_0_, bf16[1408,256]{1,0:T(8,128)(2,1)} %get-tuple-element.270.refs_1_, f32[1408,256]{1,0:T(8,128)} %get-tuple-element.271.refs_2_, bf16[224,512]{1,0:T(8,128)(2,1)} %get-tuple-element.272.refs_3_, ...), custom_call_target="tpu_custom_call" | custom-call | bytes 47600000 | tf_op jit(solution)/shard_map/pallas_call | solution.py:804
  223.5 1.6 collective-permute-start.18
  225.1 2.5 collective-permute-start.19
  228.1 10.5 %shard_map.255 = (bf16[96,512]{1,0:T(8,128)(2,1)}, bf16[96,2048]{1,0:T(8,128)(2,1)}, bf16[128,4608]{1,0:T(8,128)(2,1)}, bf16[3328,128]{1,0:T(8,128)(2,1)}, bf16[3328,128]{1,0:T(8,128)(2,1)}) custom-call(bf16[512,1536]{1,0:T(8,128)(2,1)} %get-tuple-element.199.refs_1_.refs_0_, bf16[512,512]{1,0:T(8,128)(2,1)} %get-tuple-element.203.refs_5_.refs_1_, ...), custom_call_target="tpu_custom_call" | custom-call | bytes 44200000 | tf_op jit(solution)/shard_map/pallas_call | solution.py:804
  238.8 3.4 collective-permute-start.27
  247.9 2.6 collective-permute-start.26
  252.8 3.6 %all-to-all-start.1 = ((bf16[4,2,16,2048]{3,2,1,0:T(8,128)(2,1)}), bf16[4,2,16,2048]{3,2,1,0:T(8,128)(2,1)S(1)}, u32[]{:S(2)}, u32[]{:S(2)}) async-start(bf16[4,2,16,2048]{3,2,1,0:T(8,128)(2,1)} %bitcast.88), calls=%async_computation.2 | async-start | bytes 1048576 | tf_op jit(solution)/shard_map/all_to_all | solution.py:1549
  256.9 4.2 %collective-permute-done.23 = bf16[832,128]{1,0:T(8,128)(2,1)} collective-permute-done((bf16[832,128]{1,0:T(8,128)(2,1)}, bf16[832,128]{1,0:T(8,128)(2,1)}, u32[]{:S(2)}, u32[]{:S(2)}) %collective-permute-start.23) | collective-permute-done | bytes 213024 | tf_op jit(solution)/shard_map/ppermute | solution.py:1441
  262.4 2.4 collective-permute-start.30
  267.6 1.5 collective-permute-start.31
  269.2 1.6 collective-permute-done.30
  270.8 4.1 %collective-permute-done.29 = bf16[208,128]{1,0:T(8,128)(2,1)S(1)} collective-permute-done((bf16[208,128]{1,0:T(8,128)(2,1)S(1)}, bf16[208,128]{1,0:T(8,128)(2,1)S(1)}, u32[]{:S(2)}, u32[]{:S(2)}) %collective-permute-start.29) | collective-permute-done | bytes 53280 | tf_op jit(solution)/shard_map/ppermute | solution.py:1444
  274.9 5.2 %collective-permute-done.31.refs_1_ = bf16[2112,128]{1,0:T(8,128)(2,1)S(1)} collective-permute-done((bf16[2112,128]{1,0:T(8,128)(2,1)S(1)}, bf16[2112,128]{1,0:T(8,128)(2,1)S(1)}, u32[]{:S(2)}, u32[]{:S(2)}) %collective-permute-start.31) | collective-permute-done | bytes 540704 | tf_op jit(solution)/shard_map/ppermute | solution.py:1474
  280.3 1.5 collective-permute-start.38
  283.7 3.4 collective-permute-start.34
  290.1 2.0 collective-permute-done.33.refs_2_
  293.1 1.5 collective-permute-start.36
  294.6 1.5 collective-permute-start.35
  298.1 2.7 collective-permute-done.38.refs_1_
  301.7 2.9 collective-permute-done.36.refs_2_
  307.9 3.8 %collective-permute-done.39.refs_2_ = bf16[3328,128]{1,0:T(8,128)(2,1)S(1)} collective-permute-done((bf16[3328,128]{1,0:T(8,128)(2,1)S(1)}, bf16[3328,128]{1,0:T(8,128)(2,1)S(1)}, u32[]{:S(2)}, u32[]{:S(2)}) %collective-permute-start.39) | collective-permute-done | bytes 852000 | tf_op jit(solution)/shard_map/ppermute | solution.py:1438
  312.6 4.8 %all-to-all-start.2 = ((bf16[4,2,16,2560]{3,2,1,0:T(8,128)(2,1)}), bf16[4,2,16,2560]{3,2,1,0:T(8,128)(2,1)}, u32[]{:S(2)}, u32[]{:S(2)}) async-start(bf16[4,2,16,2560]{3,2,1,0:T(8,128)(2,1)} %bitcast.98), calls=%async_computation.3 | async-start | bytes 1310720 | tf_op jit(solution)/shard_map/all_to_all | solution.py:1549
  318.9 15.0 %shard_map.261 = (f32[8290,128]{1,0:T(8,128)}, f32[8290,128]{1,0:T(8,128)}, f32[8290,128]{1,0:T(8,128)}, f32[8,576]{1,0:T(8,128)}) custom-call(s32[8]{0:T(128)} %owner_ref.5, s32[8]{0:T(128)} %rows_ref.5, f32[2]{0:T(128)} %pad_maximum_fusion.7.scale_ref, bf16[10240,128]{1,0:T(8,128)(2,1)} %all-gather.2.cloned.1.call-done.refs_0_, ...), custom_call_target="tpu_custom_call" | custom-call | bytes 34000000 | tf_op jit(solution)/shard_map/pallas_call | solution.py:1305
  335.1 1.6 slice.49
  337.8 2.1 pad_maximum_fusion.2
  (144 shorter events, 43.6 us)
Async XLA Ops:
  11.6 10.9 %collective-permute-start.2 = (bf16[8320,128]{1,0:T(8,128)(2,1)}, bf16[8320,128]{1,0:T(8,128)(2,1)}, u32[]{:S(2)}, u32[]{:S(2)}) collective-permute-start(bf16[8320,128]{1,0:T(8,128)(2,1)} %shard_map.247.refs_0_), channel_id=1, source_target_pairs={{0,4},{4,0},{8,12},{12,8},{16,20},{20,16},{24,28},{28,24},{1,5},{5... | collective-permute-start | bytes 6389768 | tf_op jit(solution)/shard_map/ppermute | solution.py:1368
  12.0 48.8 %collective-permute-start.1 = (bf16[8320,128]{1,0:T(8,128)(2,1)}, bf16[8320,128]{1,0:T(8,128)(2,1)}, u32[]{:S(2)}, u32[]{:S(2)}) collective-permute-start(bf16[8320,128]{1,0:T(8,128)(2,1)} %shard_map.247.refs_0_), channel_id=1, source_target_pairs={{0,16},{4,12},{8,24},{12,4},{16,0},{20,28},{24,8},{28,20},{1,17},{... | collective-permute-start | bytes 6389768 | tf_op jit(solution)/shard_map/ppermute | solution.py:1366
  14.5 47.3 %collective-permute-start = (bf16[8320,128]{1,0:T(8,128)(2,1)}, bf16[8320,128]{1,0:T(8,128)(2,1)}, u32[]{:S(2)}, u32[]{:S(2)}) collective-permute-start(bf16[8320,128]{1,0:T(8,128)(2,1)} %shard_map.247.refs_0_), channel_id=1, source_target_pairs={{0,8},{4,20},{8,0},{12,28},{16,24},{20,4},{24,16},{28,12},{1,9},{5... | collective-permute-start | bytes 6389768 | tf_op jit(solution)/shard_map/ppermute | solution.py:1366
  17.6 58.8 %all-to-all-start = ((bf16[8,16,9216]{2,1,0:T(8,128)(2,1)}), bf16[8,16,9216]{2,1,0:T(8,128)(2,1)S(1)}, u32[]{:S(2)}, u32[]{:S(2)}) async-start(bf16[8,16,9216]{2,1,0:T(8,128)(2,1)} %pad_maximum_fusion), calls=%async_computation | async-start | bytes 4718592 | tf_op jit(solution)/shard_map/all_to_all | solution.py:1573
  22.4 165.6 %reduce-scatter.2.cloned.1.call-start = ((), (), s32[]{:S(2)}) async-start(), calls=%async_computation.4 | async-start | bytes 2949120 | tf_op jit(solution)/shard_map/reduce_scatter | solution.py:1587
  61.8 16.2 %collective-permute-start.5 = (bf16[8320,128]{1,0:T(8,128)(2,1)}, bf16[8320,128]{1,0:T(8,128)(2,1)}, u32[]{:S(2)}, u32[]{:S(2)}) collective-permute-start(bf16[8320,128]{1,0:T(8,128)(2,1)} %collective-permute-done.1.refs_3_), channel_id=1, source_target_pairs={{0,4},{4,0},{8,12},{12,8},{16,20},{20,16},{24,28},{28,24},{1,5},{5... | collective-permute-start | bytes 6389768 | tf_op jit(solution)/shard_map/ppermute | solution.py:1368
  62.0 16.0 %collective-permute-start.4 = (bf16[8320,128]{1,0:T(8,128)(2,1)}, bf16[8320,128]{1,0:T(8,128)(2,1)}, u32[]{:S(2)}, u32[]{:S(2)}) collective-permute-start(bf16[8320,128]{1,0:T(8,128)(2,1)} %collective-permute-done.refs_2_), channel_id=1, source_target_pairs={{0,4},{4,0},{8,12},{12,8},{16,20},{20,16},{24,28},{28,24},{1,5},{5... | collective-permute-start | bytes 6389768 | tf_op jit(solution)/shard_map/ppermute | solution.py:1368
  62.4 26.7 %collective-permute-start.3 = (bf16[8320,128]{1,0:T(8,128)(2,1)}, bf16[8320,128]{1,0:T(8,128)(2,1)}, u32[]{:S(2)}, u32[]{:S(2)}) collective-permute-start(bf16[8320,128]{1,0:T(8,128)(2,1)} %collective-permute-done.refs_2_), channel_id=1, source_target_pairs={{0,16},{4,12},{8,24},{12,4},{16,0},{20,28},{24,8},{28,20},{1,17},{... | collective-permute-start | bytes 6389768 | tf_op jit(solution)/shard_map/ppermute | solution.py:1366
  89.1 4.4 %collective-permute-start.6 = (bf16[8320,128]{1,0:T(8,128)(2,1)}, bf16[8320,128]{1,0:T(8,128)(2,1)S(1)}, u32[]{:S(2)}, u32[]{:S(2)}) collective-permute-start(bf16[8320,128]{1,0:T(8,128)(2,1)} %collective-permute-done.3.refs_6_), channel_id=1, source_target_pairs={{0,4},{4,0},{8,12},{12,8},{16,20},{20,16},{24,28},{28,24},{1,5},{5... | collective-permute-start | bytes 6389768 | tf_op jit(solution)/shard_map/ppermute | solution.py:1368
  142.5 96.1 %all-reduce.2.cloned.1.call-start = ((), (), s32[]{:S(2)}) async-start(), calls=%async_computation.5 | async-start | bytes 655360 | tf_op jit(solution)/shard_map/psum | solution.py:1595
  143.8 30.3 %collective-permute-start.9 = (bf16[2,16,4608]{2,1,0:T(8,128)(2,1)S(1)}, bf16[2,16,4608]{2,1,0:T(8,128)(2,1)S(1)}, u32[]{:S(2)}, u32[]{:S(2)}) collective-permute-start(bf16[2,16,4608]{2,1,0:T(8,128)(2,1)S(1)} %get-tuple-element.353), channel_id=1, source_target_pairs={{0,3},{1,2},{2,1},{3,0},{4,7},{5,6},{6,5},{7,4},{8,11},{9,10},{10,... | collective-permute-start | bytes 884744 | tf_op jit(solution)/shard_map/ppermute | solution.py:1560
  147.7 26.4 %collective-permute-start.8 = (bf16[2,16,4608]{2,1,0:T(8,128)(2,1)S(1)}, bf16[2,16,4608]{2,1,0:T(8,128)(2,1)S(1)}, u32[]{:S(2)}, u32[]{:S(2)}) collective-permute-start(bf16[2,16,4608]{2,1,0:T(8,128)(2,1)S(1)} %get-tuple-element.354), channel_id=1, source_target_pairs={{0,2},{1,3},{2,0},{3,1},{4,6},{5,7},{6,4},{7,5},{8,10},{9,11},{10,... | collective-permute-start | bytes 884744 | tf_op jit(solution)/shard_map/ppermute | solution.py:1560
  147.7 26.4 %collective-permute-start.7 = (bf16[2,16,4608]{2,1,0:T(8,128)(2,1)S(1)}, bf16[2,16,4608]{2,1,0:T(8,128)(2,1)S(1)}, u32[]{:S(2)}, u32[]{:S(2)}) collective-permute-start(bf16[2,16,4608]{2,1,0:T(8,128)(2,1)S(1)} %get-tuple-element.355), channel_id=1, source_target_pairs={{0,1},{1,0},{2,3},{3,2},{4,5},{5,4},{6,7},{7,6},{8,9},{9,8},{10,11... | collective-permute-start | bytes 884744 | tf_op jit(solution)/shard_map/ppermute | solution.py:1560
  174.9 8.9 %collective-permute-start.10 = (bf16[5120,128]{1,0:T(8,128)(2,1)}, bf16[5120,128]{1,0:T(8,128)(2,1)S(1)}, u32[]{:S(2)}, u32[]{:S(2)}) collective-permute-start(bf16[5120,128]{1,0:T(8,128)(2,1)} %get-tuple-element.242), channel_id=1, source_target_pairs={{0,4},{4,0},{8,12},{12,8},{16,20},{20,16},{24,28},{28,24},{1,5},{5... | collective-permute-start | bytes 3932168 | tf_op jit(solution)/shard_map/ppermute | solution.py:1438
  188.1 20.9 %collective-permute-start.14 = (bf16[3328,128]{1,0:T(8,128)(2,1)}, bf16[3328,128]{1,0:T(8,128)(2,1)}, u32[]{:S(2)}, u32[]{:S(2)}) collective-permute-start(bf16[3328,128]{1,0:T(8,128)(2,1)} %get-tuple-element.255), channel_id=1, source_target_pairs={{0,4},{4,0},{8,12},{12,8},{16,20},{20,16},{24,28},{28,24},{1,5},{5... | collective-permute-start | bytes 2555912 | tf_op jit(solution)/shard_map/ppermute | solution.py:1438
  190.7 16.4 %collective-permute-start.13 = (bf16[1280,128]{1,0:T(8,128)(2,1)}, bf16[1280,128]{1,0:T(8,128)(2,1)S(1)}, u32[]{:S(2)}, u32[]{:S(2)}) collective-permute-start(bf16[1280,128]{1,0:T(8,128)(2,1)} %get-tuple-element.342), channel_id=1, source_target_pairs={{0,24},{4,28},{8,16},{12,20},{16,8},{20,12},{24,0},{28,4},{1,25},{... | collective-permute-start | bytes 983048 | tf_op jit(solution)/shard_map/ppermute | solution.py:1441
  192.2 16.8 %collective-permute-start.12 = (bf16[1280,128]{1,0:T(8,128)(2,1)}, bf16[1280,128]{1,0:T(8,128)(2,1)S(1)}, u32[]{:S(2)}, u32[]{:S(2)}) collective-permute-start(bf16[1280,128]{1,0:T(8,128)(2,1)} %get-tuple-element.343), channel_id=1, source_target_pairs={{0,16},{4,20},{8,24},{12,28},{16,0},{20,4},{24,8},{28,12},{1,17},{... | collective-permute-start | bytes 983048 | tf_op jit(solution)/shard_map/ppermute | solution.py:1441
  193.6 15.4 %collective-permute-start.11 = (bf16[1280,128]{1,0:T(8,128)(2,1)}, bf16[1280,128]{1,0:T(8,128)(2,1)S(1)}, u32[]{:S(2)}, u32[]{:S(2)}) collective-permute-start(bf16[1280,128]{1,0:T(8,128)(2,1)} %get-tuple-element.344), channel_id=1, source_target_pairs={{0,8},{4,12},{8,0},{12,4},{16,24},{20,28},{24,16},{28,20},{1,9},{5... | collective-permute-start | bytes 983048 | tf_op jit(solution)/shard_map/ppermute | solution.py:1441
  194.2 98.0 %all-gather.2.cloned.1.call-start = ((), (), s32[]{:S(2)}) async-start(), calls=%async_computation.6 | async-start | bytes 2949120 | tf_op jit(solution)/shard_map/all_gather | solution.py:1605
  210.4 12.9 %collective-permute-start.17 = (bf16[832,128]{1,0:T(8,128)(2,1)S(1)}, bf16[832,128]{1,0:T(8,128)(2,1)S(1)}, u32[]{:S(2)}, u32[]{:S(2)}) collective-permute-start(bf16[832,128]{1,0:T(8,128)(2,1)S(1)} %get-tuple-element.360), channel_id=1, source_target_pairs={{0,24},{4,28},{8,16},{12,20},{16,8},{20,12},{24,0},{28,4},{1,25},{... | collective-permute-start | bytes 638984 | tf_op jit(solution)/shard_map/ppermute | solution.py:1441
  211.9 11.3 %collective-permute-start.16 = (bf16[832,128]{1,0:T(8,128)(2,1)S(1)}, bf16[832,128]{1,0:T(8,128)(2,1)S(1)}, u32[]{:S(2)}, u32[]{:S(2)}) collective-permute-start(bf16[832,128]{1,0:T(8,128)(2,1)S(1)} %get-tuple-element.361), channel_id=1, source_target_pairs={{0,16},{4,20},{8,24},{12,28},{16,0},{20,4},{24,8},{28,12},{1,17},{... | collective-permute-start | bytes 638984 | tf_op jit(solution)/shard_map/ppermute | solution.py:1441
  213.4 9.9 %collective-permute-start.15 = (bf16[832,128]{1,0:T(8,128)(2,1)S(1)}, bf16[832,128]{1,0:T(8,128)(2,1)S(1)}, u32[]{:S(2)}, u32[]{:S(2)}) collective-permute-start(bf16[832,128]{1,0:T(8,128)(2,1)S(1)} %get-tuple-element.362), channel_id=1, source_target_pairs={{0,8},{4,12},{8,0},{12,4},{16,24},{20,28},{24,16},{28,20},{1,9},{5... | collective-permute-start | bytes 638984 | tf_op jit(solution)/shard_map/ppermute | solution.py:1441
  223.5 15.1 %collective-permute-start.18 = (bf16[528,128]{1,0:T(8,128)(2,1)S(1)}, bf16[528,128]{1,0:T(8,128)(2,1)S(1)}, u32[]{:S(2)}, u32[]{:S(2)}) collective-permute-start(bf16[528,128]{1,0:T(8,128)(2,1)S(1)} %pad_maximum_fusion.3), channel_id=1, source_target_pairs={{0,1},{1,0},{2,3},{3,2},{4,5},{5,4},{6,7},{7,6},{8,9},{9,8},{10,11... | collective-permute-start | bytes 405512 | tf_op jit(solution)/shard_map/ppermute | solution.py:1444
  225.1 13.6 %collective-permute-start.19 = (bf16[528,128]{1,0:T(8,128)(2,1)S(1)}, bf16[528,128]{1,0:T(8,128)(2,1)S(1)}, u32[]{:S(2)}, u32[]{:S(2)}) collective-permute-start(bf16[528,128]{1,0:T(8,128)(2,1)S(1)} %pad_maximum_fusion.4), channel_id=1, source_target_pairs={{0,2},{1,3},{2,0},{3,1},{4,6},{5,7},{6,4},{7,5},{8,10},{9,11},{10,... | collective-permute-start | bytes 405512 | tf_op jit(solution)/shard_map/ppermute | solution.py:1444
  227.5 11.1 %collective-permute-start.20 = (bf16[528,128]{1,0:T(8,128)(2,1)S(1)}, bf16[528,128]{1,0:T(8,128)(2,1)S(1)}, u32[]{:S(2)}, u32[]{:S(2)}) collective-permute-start(bf16[528,128]{1,0:T(8,128)(2,1)S(1)} %pad_maximum_fusion.5), channel_id=1, source_target_pairs={{0,3},{1,2},{2,1},{3,0},{4,7},{5,6},{6,5},{7,4},{8,11},{9,10},{10,... | collective-permute-start | bytes 405512 | tf_op jit(solution)/shard_map/ppermute | solution.py:1444
  238.7 3.6 %collective-permute-start.21 = (bf16[3328,128]{1,0:T(8,128)(2,1)}, bf16[3328,128]{1,0:T(8,128)(2,1)S(1)}, u32[]{:S(2)}, u32[]{:S(2)}) collective-permute-start(bf16[3328,128]{1,0:T(8,128)(2,1)} %get-tuple-element.295), channel_id=1, source_target_pairs={{0,4},{4,0},{8,12},{12,8},{16,20},{20,16},{24,28},{28,24},{1,5},{5... | collective-permute-start | bytes 2555912 | tf_op jit(solution)/shard_map/ppermute | solution.py:1438
  238.8 11.7 %collective-permute-start.27 = (bf16[528,128]{1,0:T(8,128)(2,1)S(1)}, bf16[528,128]{1,0:T(8,128)(2,1)S(1)}, u32[]{:S(2)}, u32[]{:S(2)}) collective-permute-start(bf16[528,128]{1,0:T(8,128)(2,1)S(1)} %add_convert_fusion.3.refs_0_), channel_id=1, source_target_pairs={{0,3},{1,2},{2,1},{3,0},{4,7},{5,6},{6,5},{7,4},{8,11},{9,10},{10,... | collective-permute-start | bytes 405512 | tf_op jit(solution)/shard_map/ppermute | solution.py:1444
  244.4 12.5 %collective-permute-start.24 = (bf16[832,128]{1,0:T(8,128)(2,1)}, bf16[832,128]{1,0:T(8,128)(2,1)}, u32[]{:S(2)}, u32[]{:S(2)}) collective-permute-start(bf16[832,128]{1,0:T(8,128)(2,1)} %get-tuple-element.357), channel_id=1, source_target_pairs={{0,24},{4,28},{8,16},{12,20},{16,8},{20,12},{24,0},{28,4},{1,25},{... | collective-permute-start | bytes 638984 | tf_op jit(solution)/shard_map/ppermute | solution.py:1441
  245.9 15.2 %collective-permute-start.23 = (bf16[832,128]{1,0:T(8,128)(2,1)}, bf16[832,128]{1,0:T(8,128)(2,1)}, u32[]{:S(2)}, u32[]{:S(2)}) collective-permute-start(bf16[832,128]{1,0:T(8,128)(2,1)} %get-tuple-element.358), channel_id=1, source_target_pairs={{0,16},{4,20},{8,24},{12,28},{16,0},{20,4},{24,8},{28,12},{1,17},{... | collective-permute-start | bytes 638984 | tf_op jit(solution)/shard_map/ppermute | solution.py:1441
  247.3 13.8 %collective-permute-start.22 = (bf16[832,128]{1,0:T(8,128)(2,1)S(1)}, bf16[832,128]{1,0:T(8,128)(2,1)}, u32[]{:S(2)}, u32[]{:S(2)}) collective-permute-start(bf16[832,128]{1,0:T(8,128)(2,1)S(1)} %get-tuple-element.359), channel_id=1, source_target_pairs={{0,8},{4,12},{8,0},{12,4},{16,24},{20,28},{24,16},{28,20},{1,9},{5... | collective-permute-start | bytes 638984 | tf_op jit(solution)/shard_map/ppermute | solution.py:1441
  247.9 8.7 %collective-permute-start.26 = (bf16[528,128]{1,0:T(8,128)(2,1)S(1)}, bf16[528,128]{1,0:T(8,128)(2,1)S(1)}, u32[]{:S(2)}, u32[]{:S(2)}) collective-permute-start(bf16[528,128]{1,0:T(8,128)(2,1)S(1)} %add_convert_fusion.3.refs_0_), channel_id=1, source_target_pairs={{0,2},{1,3},{2,0},{3,1},{4,6},{5,7},{6,4},{7,5},{8,10},{9,11},{10,... | collective-permute-start | bytes 405512 | tf_op jit(solution)/shard_map/ppermute | solution.py:1444
  250.5 6.3 %collective-permute-start.25 = (bf16[528,128]{1,0:T(8,128)(2,1)S(1)}, bf16[528,128]{1,0:T(8,128)(2,1)S(1)}, u32[]{:S(2)}, u32[]{:S(2)}) collective-permute-start(bf16[528,128]{1,0:T(8,128)(2,1)S(1)} %add_convert_fusion.3.refs_0_), channel_id=1, source_target_pairs={{0,1},{1,0},{2,3},{3,2},{4,5},{5,4},{6,7},{7,6},{8,9},{9,8},{10,11... | collective-permute-start | bytes 405512 | tf_op jit(solution)/shard_map/ppermute | solution.py:1444
  252.8 16.2 %copy-start.18 = (bf16[2,16,4608]{2,1,0:T(8,128)(2,1)S(1)}, bf16[2,16,4608]{2,1,0:T(8,128)(2,1)}, u32[]{:S(2)}) copy-start(bf16[2,16,4608]{2,1,0:T(8,128)(2,1)} %copy-done.17) | copy-start | bytes 884740
  252.8 36.0 %all-to-all-start.1 = ((bf16[4,2,16,2048]{3,2,1,0:T(8,128)(2,1)}), bf16[4,2,16,2048]{3,2,1,0:T(8,128)(2,1)S(1)}, u32[]{:S(2)}, u32[]{:S(2)}) async-start(bf16[4,2,16,2048]{3,2,1,0:T(8,128)(2,1)} %bitcast.88), calls=%async_computation.2 | async-start | bytes 1048576 | tf_op jit(solution)/shard_map/all_to_all | solution.py:1549
  262.4 8.4 %collective-permute-start.30 = (bf16[208,128]{1,0:T(8,128)(2,1)S(1)}, bf16[208,128]{1,0:T(8,128)(2,1)S(1)}, u32[]{:S(2)}, u32[]{:S(2)}) collective-permute-start(bf16[208,128]{1,0:T(8,128)(2,1)S(1)} %get-tuple-element.367), channel_id=1, source_target_pairs={{0,3},{1,2},{2,1},{3,0},{4,7},{5,6},{6,5},{7,4},{8,11},{9,10},{10,... | collective-permute-start | bytes 159752 | tf_op jit(solution)/shard_map/ppermute | solution.py:1444
  264.8 10.1 %collective-permute-start.29 = (bf16[208,128]{1,0:T(8,128)(2,1)S(1)}, bf16[208,128]{1,0:T(8,128)(2,1)S(1)}, u32[]{:S(2)}, u32[]{:S(2)}) collective-permute-start(bf16[208,128]{1,0:T(8,128)(2,1)S(1)} %get-tuple-element.368), channel_id=1, source_target_pairs={{0,2},{1,3},{2,0},{3,1},{4,6},{5,7},{6,4},{7,5},{8,10},{9,11},{10,... | collective-permute-start | bytes 159752 | tf_op jit(solution)/shard_map/ppermute | solution.py:1444
  265.6 9.3 %collective-permute-start.28 = (bf16[208,128]{1,0:T(8,128)(2,1)S(1)}, bf16[208,128]{1,0:T(8,128)(2,1)S(1)}, u32[]{:S(2)}, u32[]{:S(2)}) collective-permute-start(bf16[208,128]{1,0:T(8,128)(2,1)S(1)} %get-tuple-element.369), channel_id=1, source_target_pairs={{0,1},{1,0},{2,3},{3,2},{4,5},{5,4},{6,7},{7,6},{8,9},{9,8},{10,11... | collective-permute-start | bytes 159752 | tf_op jit(solution)/shard_map/ppermute | solution.py:1444
  267.6 12.5 %collective-permute-start.31 = (bf16[2112,128]{1,0:T(8,128)(2,1)S(1)}, bf16[2112,128]{1,0:T(8,128)(2,1)S(1)}, u32[]{:S(2)}, u32[]{:S(2)}) collective-permute-start(bf16[2112,128]{1,0:T(8,128)(2,1)S(1)} %shard_map.256.refs_0_), channel_id=1, source_target_pairs={{0,8},{4,20},{8,0},{12,28},{16,24},{20,4},{24,16},{28,12},{1,9},{5... | collective-permute-start | bytes 1622024 | tf_op jit(solution)/shard_map/ppermute | solution.py:1474
  280.3 20.5 %collective-permute-start.38 = (bf16[4224,128]{1,0:T(8,128)(2,1)S(1)}, bf16[4224,128]{1,0:T(8,128)(2,1)S(1)}, u32[]{:S(2)}, u32[]{:S(2)}) collective-permute-start(bf16[4224,128]{1,0:T(8,128)(2,1)S(1)} %shard_map.258.refs_0_), channel_id=1, source_target_pairs={{0,16},{4,12},{8,24},{12,4},{16,0},{20,28},{24,8},{28,20},{1,17},{... | collective-permute-start | bytes 3244040 | tf_op jit(solution)/shard_map/ppermute | solution.py:1474
  283.7 6.4 %collective-permute-start.34 = (bf16[208,128]{1,0:T(8,128)(2,1)S(1)}, bf16[208,128]{1,0:T(8,128)(2,1)S(1)}, u32[]{:S(2)}, u32[]{:S(2)}) collective-permute-start(bf16[208,128]{1,0:T(8,128)(2,1)S(1)} %fusion.11.refs_0_), channel_id=1, source_target_pairs={{0,3},{1,2},{2,1},{3,0},{4,7},{5,6},{6,5},{7,4},{8,11},{9,10},{10,... | collective-permute-start | bytes 159752 | tf_op jit(solution)/shard_map/ppermute | solution.py:1444
  287.1 5.0 %collective-permute-start.33 = (bf16[208,128]{1,0:T(8,128)(2,1)S(1)}, bf16[208,128]{1,0:T(8,128)(2,1)S(1)}, u32[]{:S(2)}, u32[]{:S(2)}) collective-permute-start(bf16[208,128]{1,0:T(8,128)(2,1)S(1)} %fusion.11.refs_0_), channel_id=1, source_target_pairs={{0,2},{1,3},{2,0},{3,1},{4,6},{5,7},{6,4},{7,5},{8,10},{9,11},{10,... | collective-permute-start | bytes 159752 | tf_op jit(solution)/shard_map/ppermute | solution.py:1444
  287.1 5.0 %collective-permute-start.32 = (bf16[208,128]{1,0:T(8,128)(2,1)S(1)}, bf16[208,128]{1,0:T(8,128)(2,1)S(1)}, u32[]{:S(2)}, u32[]{:S(2)}) collective-permute-start(bf16[208,128]{1,0:T(8,128)(2,1)S(1)} %fusion.11.refs_0_), channel_id=1, source_target_pairs={{0,1},{1,0},{2,3},{3,2},{4,5},{5,4},{6,7},{7,6},{8,9},{9,8},{10,11... | collective-permute-start | bytes 159752 | tf_op jit(solution)/shard_map/ppermute | solution.py:1444
  292.5 9.2 %collective-permute-start.37 = (bf16[832,128]{1,0:T(8,128)(2,1)S(1)}, bf16[832,128]{1,0:T(8,128)(2,1)S(1)}, u32[]{:S(2)}, u32[]{:S(2)}) collective-permute-start(bf16[832,128]{1,0:T(8,128)(2,1)S(1)} %shard_map.257.refs_0_), channel_id=1, source_target_pairs={{0,24},{4,28},{8,16},{12,20},{16,8},{20,12},{24,0},{28,4},{1,25},{... | collective-permute-start | bytes 638984 | tf_op jit(solution)/shard_map/ppermute | solution.py:1441
  293.1 11.5 %collective-permute-start.36 = (bf16[832,128]{1,0:T(8,128)(2,1)S(1)}, bf16[832,128]{1,0:T(8,128)(2,1)S(1)}, u32[]{:S(2)}, u32[]{:S(2)}) collective-permute-start(bf16[832,128]{1,0:T(8,128)(2,1)S(1)} %shard_map.257.refs_0_), channel_id=1, source_target_pairs={{0,16},{4,20},{8,24},{12,28},{16,0},{20,4},{24,8},{28,12},{1,17},{... | collective-permute-start | bytes 638984 | tf_op jit(solution)/shard_map/ppermute | solution.py:1441
  294.6 10.0 %collective-permute-start.35 = (bf16[832,128]{1,0:T(8,128)(2,1)S(1)}, bf16[832,128]{1,0:T(8,128)(2,1)S(1)}, u32[]{:S(2)}, u32[]{:S(2)}) collective-permute-start(bf16[832,128]{1,0:T(8,128)(2,1)S(1)} %shard_map.257.refs_0_), channel_id=1, source_target_pairs={{0,8},{4,12},{8,0},{12,4},{16,24},{20,28},{24,16},{28,20},{1,9},{5... | collective-permute-start | bytes 638984 | tf_op jit(solution)/shard_map/ppermute | solution.py:1441
  306.1 6.5 %collective-permute-start.40 = (bf16[8448,128]{1,0:T(8,128)(2,1)S(1)}, bf16[8448,128]{1,0:T(8,128)(2,1)}, u32[]{:S(2)}, u32[]{:S(2)}) collective-permute-start(bf16[8448,128]{1,0:T(8,128)(2,1)S(1)} %shard_map.260.refs_3_), channel_id=1, source_target_pairs={{0,4},{4,0},{8,12},{12,8},{16,20},{20,16},{24,28},{28,24},{1,5},{5... | collective-permute-start | bytes 6488072 | tf_op jit(solution)/shard_map/ppermute | solution.py:1438
  307.4 4.3 %collective-permute-start.39 = (bf16[3328,128]{1,0:T(8,128)(2,1)S(1)}, bf16[3328,128]{1,0:T(8,128)(2,1)S(1)}, u32[]{:S(2)}, u32[]{:S(2)}) collective-permute-start(bf16[3328,128]{1,0:T(8,128)(2,1)S(1)} %shard_map.259.refs_1_), channel_id=1, source_target_pairs={{0,4},{4,0},{8,12},{12,8},{16,20},{20,16},{24,28},{28,24},{1,5},{5... | collective-permute-start | bytes 2555912 | tf_op jit(solution)/shard_map/ppermute | solution.py:1438
  312.6 22.5 %all-to-all-start.2 = ((bf16[4,2,16,2560]{3,2,1,0:T(8,128)(2,1)}), bf16[4,2,16,2560]{3,2,1,0:T(8,128)(2,1)}, u32[]{:S(2)}, u32[]{:S(2)}) async-start(bf16[4,2,16,2560]{3,2,1,0:T(8,128)(2,1)} %bitcast.98), calls=%async_computation.3 | async-start | bytes 1310720 | tf_op jit(solution)/shard_map/all_to_all | solution.py:1549
  (22 other events, 173.3 us)
Sparse Core Ops, SparseCore 0:
  142.6 45.4 reduce-scatter.1
  194.3 37.8 all-reduce.1
  238.8 39.7 all-gather.1

commit v6 on v5

--- a/solution.py
+++ b/solution.py
@@ -900,7 +900,7 @@
         )
         forward(dm, counts_ref, w, io, s, s, leaving)
         outgoing = all_copies(
-            dm, dst.sno, dst.seo, dst.bout, 0, EDGE_LANES, s.nodes_out, s.edges_out, out_sems, True
+            dm, dst.sno, dst.seo, dst.bout, D, 0, s.nodes_out, s.edges_out, out_sems, True
         )
         start(outgoing)
         wait(copies)
@@ -1020,7 +1020,7 @@
         back_nodes(dm, w, io, res, s)
         back_last(dm, w, io, res, s)
         outgoing = all_copies(
-            dm, dst.sng, dst.seg, dst.bgrad, 0, EDGE_LANES, s.nodes_grad, s.edges_grad, sems, True
+            dm, dst.sng, dst.seg, dst.bgrad, D, 0, s.nodes_grad, s.edges_grad, sems, True
         )
         start(outgoing)
         wait(outgoing)
@@ -1605,23 +1605,23 @@
     upper_two = lax.all_gather(spread, "dp", axis=0, tiled=True)
     last = Chain(cube, True, (keep, send))
     sent = middle.launch()
-    early = EDGE_LANES // 2
+    early = D + EDGE_LANES // 2
     bgrad, = phase([last], bgrad)
     one_part, two_part = packed(bgrad, 0, early), packed(bgrad, early, OUT_LANES - early)
     one_part = to_rows(one_part)
     sent, out_pieces = phase([last], sent, out_pieces)
-    bno, beo = in_order(out_pieces, EDGE_LANES, D), in_order(out_pieces, 0, EDGE_LANES)
+    bno, beo = in_order(out_pieces, 0, D), in_order(out_pieces, D, EDGE_LANES)
     middle.land(sent)
     phase([last, middle])
     sent = middle.launch()
     one_part, upper_two, bno, beo = phase([last], one_part, upper_two, bno, beo)
-    sent, two_part = phase([last], sent, two_part)
+    bng, head = one_part[..., :D], one_part[..., D:]
+    sent, two_part, bng, head = phase([last], sent, two_part, bng, head)
     middle.land(sent)
     while not (last.done and middle.done):
         two_part, = phase([last, middle], two_part)
     two_part = to_rows(two_part)
-    bng = two_part[..., EDGE_LANES - early :]
-    beg = jnp.concatenate([one_part, two_part[..., : EDGE_LANES - early]], axis=-1)
+    beg = jnp.concatenate([head, two_part], axis=-1)
     blocks = last.blocks((0, 0)) + middle.blocks((0, 1), (1, 0))
     step_value = step_count[0].astype(F32)
     scales = jnp.stack(

time: 351 us -> 347 us (0.989)
    ppermute x2, waiting for transfers between devices: 7.89 us -> 4.05 us  [launch(): return [lax.ppermute(self.value, 'dp', self.cube.pairs(self.step - 5))]]
  transfers between devices with their start and end apart: 47 -> 47, of which waited for: 20 -> 20; matrix products, arithmetic and copies ran while one was open for 5% -> 6% of each run, Pallas kernels for 24% -> 24%
where the time goes in v6:
time: 347 us; the launch traced here: 343 us
  Pallas kernels  136 us (39%)
  waiting for transfers between devices  100 us (29%)
  starting transfers between devices  62.8 us (18%)
  between operations  15.3 us (4%)
  other arithmetic  14.7 us (4%)
  local copies, waits for them, and re-layouts  14.5 us (4%)
    pallas_call x7, Pallas kernels, kernel(): pl.pallas_call(body, out_shape=structs(out), in_specs=[SMEM] * len(smem)...  104 us
    ppermute x3, waiting for transfers between devices, gather(): sent.append((0, used + (step,), lax.ppermute(v, 'dp', self.pairs(step))))  50.5 us
    ppermute x12, starting transfers between devices, to_row(): return lax.ppermute(value, 'row', [(i, i ^ k) for i in range(self.rows)])  19.9 us
    pallas_call x1, Pallas kernels, adam(): pl.pallas_call(body, grid=(pl.cdiv(held, step),), out_shape=[shape] * 3 +...  14.6 us
    ppermute x12, starting transfers between devices, to_chip(): lax.ppermute(value, 'dp', [(i, i ^ k << 1) for i in range(2 * self.sides)])  14.1 us
    all_to_all x1, waiting for transfers between devices, to_whole(): lax.all_to_all(big, 'row', split_axis=0, concat_axis=1, tiled=True)  12.2 us
    ppermute x12, waiting for transfers between devices, to_row(): return lax.ppermute(value, 'row', [(i, i ^ k) for i in range(self.rows)])  12.1 us
    pallas_call x1, Pallas kernels, assemble(): pl.pallas_call(body, out_shape=structs(out), in_specs=[SMEM] * 2 + [HBM]...  10.6 us
  transfers between devices with their start and end apart: 47, of which 20 were waited for; matrix products, arithmetic and copies ran while one was open for 6% of the time, Pallas kernels for 24%

profile of v6, /device:TPU:0, one launch (start us, length us, event | category | flops | bytes accessed | tf_op | source)
XLA Modules:
  0.0 343.1 jit_solution(14452184332791257688)
XLA Ops:
  7.2 4.3 %shard_map.247.refs_0_ = bf16[8320,128]{1,0:T(8,128)(2,1)} custom-call(s32[8]{0:T(128)} %owner_ref.5, s32[8]{0:T(128)} %rows_ref.5, f32[8290,128]{1,0:T(8,128)} %refs_5_.1), custom_call_target="tpu_custom_call" | custom-call | tf_op jit(solution)/shard_map/pallas_call | solution.py:1068
  12.0 2.5 collective-permute-start.1
  14.6 1.5 collective-permute-start
  16.0 1.5 pad_maximum_fusion
  17.5 4.9 %all-to-all-start = ((bf16[8,16,9216]{2,1,0:T(8,128)(2,1)}), bf16[8,16,9216]{2,1,0:T(8,128)(2,1)S(1)}, u32[]{:S(2)}, u32[]{:S(2)}) async-start(bf16[8,16,9216]{2,1,0:T(8,128)(2,1)} %pad_maximum_fusion), calls=%async_computation | async-start | bytes 4718592 | tf_op jit(solution)/shard_map/all_to_all | solution.py:1573
  22.4 38.5 %collective-permute-done.1.refs_3_ = bf16[8320,128]{1,0:T(8,128)(2,1)} collective-permute-done((bf16[8320,128]{1,0:T(8,128)(2,1)}, bf16[8320,128]{1,0:T(8,128)(2,1)}, u32[]{:S(2)}, u32[]{:S(2)}) %collective-permute-start.1) | collective-permute-done | bytes 2129952 | tf_op jit(solution)/shard_map/ppermute | solution.py:1366
  62.3 1.8 collective-permute-start.3
  64.1 12.2 %all-to-all-done = bf16[8,16,9216]{2,1,0:T(8,128)(2,1)S(1)} async-done(((bf16[8,16,9216]{2,1,0:T(8,128)(2,1)}), bf16[8,16,9216]{2,1,0:T(8,128)(2,1)S(1)}, u32[]{:S(2)}, u32[]{:S(2)}) %all-to-all-start) | async-done | bytes 2359328 | tf_op jit(solution)/shard_map/all_to_all | solution.py:1573
  76.3 1.6 copy.31
  78.0 11.1 %collective-permute-done.3.refs_6_ = bf16[8320,128]{1,0:T(8,128)(2,1)} collective-permute-done((bf16[8320,128]{1,0:T(8,128)(2,1)}, bf16[8320,128]{1,0:T(8,128)(2,1)}, u32[]{:S(2)}, u32[]{:S(2)}) %collective-permute-start.3) | collective-permute-done | bytes 2129952 | tf_op jit(solution)/shard_map/ppermute | solution.py:1366
  89.7 3.7 %collective-permute-done.6.refs_7_ = bf16[8320,128]{1,0:T(8,128)(2,1)S(1)} collective-permute-done((bf16[8320,128]{1,0:T(8,128)(2,1)}, bf16[8320,128]{1,0:T(8,128)(2,1)S(1)}, u32[]{:S(2)}, u32[]{:S(2)}) %collective-permute-start.6) | collective-permute-done | bytes 2129952 | tf_op jit(solution)/shard_map/ppermute | solution.py:1368
  94.8 10.6 %shard_map.248 = (bf16[512,1536]{1,0:T(8,128)(2,1)}, bf16[512,512]{1,0:T(8,128)(2,1)}, bf16[512,1024]{1,0:T(8,128)(2,1)}, bf16[1024,512]{1,0:T(8,128)(2,1)}, bf1...) custom-call(s32[8]{0:T(128)} %owner_ref.5, ...), custom_call_target="tpu_custom_call" | custom-call | bytes 34000000 | tf_op jit(solution)/shard_map/pallas_call | solution.py:1147
  105.4 17.0 %shard_map.249 = (bf16[224,512]{1,0:T(8,128)(2,1)}, bf16[2816,256]{1,0:T(8,128)(2,1)}, bf16[224,512]{1,0:T(8,128)(2,1)}, f32[224,128]{1,0:T(8,128)}, bf16[224,15...) custom-call(s32[5]{0:T(128)} %pad_add_fusion.refs_0_, ...), custom_call_target="tpu_custom_call" | custom-call | bytes 54400000 | tf_op jit(solution)/shard_map/pallas_call | solution.py:804
  122.4 20.0 %shard_map.250 = (bf16[96,512]{1,0:T(8,128)(2,1)}, bf16[96,2048]{1,0:T(8,128)(2,1)}, bf16[128,4608]{1,0:T(8,128)(2,1)}, bf16[2816,256]{1,0:T(8,128)(2,1)}, bf16[...) custom-call(s32[5]{0:T(128)} %pad_add_fusion.refs_0_, ...), custom_call_target="tpu_custom_call" | custom-call | bytes 74800000 | tf_op jit(solution)/shard_map/pallas_call | solution.py:804
  143.8 3.9 %collective-permute-start.9 = (bf16[2,16,4608]{2,1,0:T(8,128)(2,1)S(1)}, bf16[2,16,4608]{2,1,0:T(8,128)(2,1)S(1)}, u32[]{:S(2)}, u32[]{:S(2)}) collective-permute-start(bf16[2,16,4608]{2,1,0:T(8,128)(2,1)S(1)} %get-tuple-element.357), channel_id=1, source_target_pairs={{0,3},{1,2},{2,1},{3,0},{4,7},{5,6},{6,5},{7,4},{8,11},{9,10},{10,... | collective-permute-start | bytes 884744 | tf_op jit(solution)/shard_map/ppermute | solution.py:1560
  148.4 25.7 %shard_map.251 = (bf16[2816,256]{1,0:T(8,128)(2,1)}, f32[256,128]{1,0:T(8,128)}, bf16[1408,512]{1,0:T(8,128)(2,1)}, bf16[224,1536]{1,0:T(8,128)(2,1)}, f32[8,128...) custom-call(bf16[512,1536]{1,0:T(8,128)(2,1)} %get-tuple-element.191, ...), custom_call_target="tpu_custom_call" | custom-call | bytes 85000000 | tf_op jit(solution)/shard_map/pallas_call | solution.py:804
  174.9 8.8 %shard_map.252 = (bf16[2816,256]{1,0:T(8,128)(2,1)}, bf16[3328,128]{1,0:T(8,128)(2,1)}, bf16[3328,128]{1,0:T(8,128)(2,1)}) custom-call(bf16[512,512]{1,0:T(8,128)(2,1)} %get-tuple-element.195.refs_5_.refs_0_, f32[4,512]{1,0:T(4,128)} %get-tuple-element.199.refs_9_.refs_5_.refs_1_, f32[4,256]{1,0:T(4,128)} %get-tuple-element.200.refs_10_.refs_4_.refs_2_, ...), custom_call_target="tpu_custom_call" | custom-call | bytes 30600000 | tf_op jit(solution)/shard_map/pallas_call | solution.py:804
  183.8 4.5 %reduce-scatter.2.cloned.1.call-done = bf16[1280,128]{1,0:T(8,128)(2,1)} async-done(((bf16[10240,128]{1,0:T(8,128)(2,1)}), bf16[1280,128]{1,0:T(8,128)(2,1)}) %reduce-scatter.2.cloned.1.call-update) | async-done | bytes 327696 | tf_op jit(solution)/shard_map/reduce_scatter | solution.py:1587
  188.2 1.7 add_convert_fusion
  190.9 1.5 collective-permute-start.13
  192.3 1.4 collective-permute-start.12
  194.8 12.4 %shard_map.253 = (bf16[2816,256]{1,0:T(8,128)(2,1)}, f32[1408,256]{1,0:T(8,128)}, f32[256,128]{1,0:T(8,128)}) custom-call(bf16[256,512]{1,0:T(8,128)(2,1)} %get-tuple-element.206.refs_6_.refs_0_, bf16[256,512]{1,0:T(8,128)(2,1)} %get-tuple-element.207.refs_7_.refs_1_, bf16[512,256]{1,0:T(8,128)(2,1)} %get-tuple-element.208.refs_8_.refs_2_, ...), custom_call_target="tpu_custom_call" | custom-call | bytes 54400000 | tf_op jit(solution)/shard_map/pallas_call | solution.py:804
  207.2 1.9 collective-permute-done.12
  210.7 1.6 collective-permute-start.17
  215.4 9.1 %shard_map.254 = (bf16[1408,512]{1,0:T(8,128)(2,1)}, bf16[224,1536]{1,0:T(8,128)(2,1)}) custom-call(bf16[224,1536]{1,0:T(8,128)(2,1)} %get-tuple-element.271.refs_0_, bf16[1408,256]{1,0:T(8,128)(2,1)} %get-tuple-element.272.refs_1_, f32[1408,256]{1,0:T(8,128)} %get-tuple-element.273.refs_2_, bf16[224,512]{1,0:T(8,128)(2,1)} %get-tuple-element.274.refs_3_, ...), custom_call_target="tpu_custom_call" | custom-call | bytes 47600000 | tf_op jit(solution)/shard_map/pallas_call | solution.py:804
  224.7 1.6 collective-permute-start.18
  226.3 2.5 collective-permute-start.19
  229.3 10.5 %shard_map.255 = (bf16[96,512]{1,0:T(8,128)(2,1)}, bf16[96,2048]{1,0:T(8,128)(2,1)}, bf16[128,4608]{1,0:T(8,128)(2,1)}, bf16[3328,128]{1,0:T(8,128)(2,1)}, bf16[3328,128]{1,0:T(8,128)(2,1)}) custom-call(bf16[512,1536]{1,0:T(8,128)(2,1)} %get-tuple-element.201.refs_1_.refs_0_, bf16[512,512]{1,0:T(8,128)(2,1)} %get-tuple-element.205.refs_5_.refs_1_, ...), custom_call_target="tpu_custom_call" | custom-call | bytes 44200000 | tf_op jit(solution)/shard_map/pallas_call | solution.py:804
  240.1 3.4 collective-permute-start.27
  245.7 1.4 collective-permute-start.24
  249.2 1.7 collective-permute-start.26
  253.1 3.6 %all-to-all-start.1 = ((bf16[4,2,16,2560]{3,2,1,0:T(8,128)(2,1)}), bf16[4,2,16,2560]{3,2,1,0:T(8,128)(2,1)S(1)}, u32[]{:S(2)}, u32[]{:S(2)}) async-start(bf16[4,2,16,2560]{3,2,1,0:T(8,128)(2,1)} %bitcast.87), calls=%async_computation.2 | async-start | bytes 1310720 | tf_op jit(solution)/shard_map/all_to_all | solution.py:1549
  258.5 3.9 %collective-permute-done.23 = bf16[832,128]{1,0:T(8,128)(2,1)} collective-permute-done((bf16[832,128]{1,0:T(8,128)(2,1)}, bf16[832,128]{1,0:T(8,128)(2,1)}, u32[]{:S(2)}, u32[]{:S(2)}) %collective-permute-start.23) | collective-permute-done | bytes 213024 | tf_op jit(solution)/shard_map/ppermute | solution.py:1441
  263.6 2.4 collective-permute-start.30
  266.0 2.1 collective-permute-start.28
  270.3 2.5 collective-permute-done.30
  272.9 4.8 %collective-permute-done.29 = bf16[208,128]{1,0:T(8,128)(2,1)S(1)} collective-permute-done((bf16[208,128]{1,0:T(8,128)(2,1)S(1)}, bf16[208,128]{1,0:T(8,128)(2,1)S(1)}, u32[]{:S(2)}, u32[]{:S(2)}) %collective-permute-start.29) | collective-permute-done | bytes 53280 | tf_op jit(solution)/shard_map/ppermute | solution.py:1444
  277.7 3.0 collective-permute-done.31.refs_1_
  280.9 1.5 collective-permute-start.38
  284.4 3.4 collective-permute-start.34
  290.8 2.0 collective-permute-done.33.refs_2_
  293.8 1.5 collective-permute-start.36
  295.3 1.5 collective-permute-start.35
  302.2 3.1 collective-permute-done.36.refs_2_
  308.5 3.8 %collective-permute-done.39.refs_2_ = bf16[3328,128]{1,0:T(8,128)(2,1)S(1)} collective-permute-done((bf16[3328,128]{1,0:T(8,128)(2,1)S(1)}, bf16[3328,128]{1,0:T(8,128)(2,1)S(1)}, u32[]{:S(2)}, u32[]{:S(2)}) %collective-permute-start.39) | collective-permute-done | bytes 852000 | tf_op jit(solution)/shard_map/ppermute | solution.py:1438
  313.2 4.8 %all-to-all-start.2 = ((bf16[4,2,16,2048]{3,2,1,0:T(8,128)(2,1)}), bf16[4,2,16,2048]{3,2,1,0:T(8,128)(2,1)}, u32[]{:S(2)}, u32[]{:S(2)}) async-start(bf16[4,2,16,2048]{3,2,1,0:T(8,128)(2,1)} %bitcast.101), calls=%async_computation.3 | async-start | bytes 1048576 | tf_op jit(solution)/shard_map/all_to_all | solution.py:1549
  319.5 14.6 %shard_map.261 = (f32[8290,128]{1,0:T(8,128)}, f32[8290,128]{1,0:T(8,128)}, f32[8290,128]{1,0:T(8,128)}, f32[8,576]{1,0:T(8,128)}) custom-call(s32[8]{0:T(128)} %owner_ref.5, s32[8]{0:T(128)} %rows_ref.5, f32[2]{0:T(128)} %pad_maximum_fusion.7.scale_ref, bf16[10240,128]{1,0:T(8,128)(2,1)} %all-gather.2.cloned.1.call-done.refs_0_, ...), custom_call_target="tpu_custom_call" | custom-call | bytes 34000000 | tf_op jit(solution)/shard_map/pallas_call | solution.py:1305
  334.0 2.3 pad_maximum_fusion.2
  (144 shorter events, 42.3 us)
Async XLA Ops:
  11.6 10.9 %collective-permute-start.2 = (bf16[8320,128]{1,0:T(8,128)(2,1)}, bf16[8320,128]{1,0:T(8,128)(2,1)}, u32[]{:S(2)}, u32[]{:S(2)}) collective-permute-start(bf16[8320,128]{1,0:T(8,128)(2,1)} %shard_map.247.refs_0_), channel_id=1, source_target_pairs={{0,4},{4,0},{8,12},{12,8},{16,20},{20,16},{24,28},{28,24},{1,5},{5... | collective-permute-start | bytes 6389768 | tf_op jit(solution)/shard_map/ppermute | solution.py:1368
  12.0 48.9 %collective-permute-start.1 = (bf16[8320,128]{1,0:T(8,128)(2,1)}, bf16[8320,128]{1,0:T(8,128)(2,1)}, u32[]{:S(2)}, u32[]{:S(2)}) collective-permute-start(bf16[8320,128]{1,0:T(8,128)(2,1)} %shard_map.247.refs_0_), channel_id=1, source_target_pairs={{0,16},{4,12},{8,24},{12,4},{16,0},{20,28},{24,8},{28,20},{1,17},{... | collective-permute-start | bytes 6389768 | tf_op jit(solution)/shard_map/ppermute | solution.py:1366
  14.6 47.3 %collective-permute-start = (bf16[8320,128]{1,0:T(8,128)(2,1)}, bf16[8320,128]{1,0:T(8,128)(2,1)}, u32[]{:S(2)}, u32[]{:S(2)}) collective-permute-start(bf16[8320,128]{1,0:T(8,128)(2,1)} %shard_map.247.refs_0_), channel_id=1, source_target_pairs={{0,8},{4,20},{8,0},{12,28},{16,24},{20,4},{24,16},{28,12},{1,9},{5... | collective-permute-start | bytes 6389768 | tf_op jit(solution)/shard_map/ppermute | solution.py:1366
  17.5 58.8 %all-to-all-start = ((bf16[8,16,9216]{2,1,0:T(8,128)(2,1)}), bf16[8,16,9216]{2,1,0:T(8,128)(2,1)S(1)}, u32[]{:S(2)}, u32[]{:S(2)}) async-start(bf16[8,16,9216]{2,1,0:T(8,128)(2,1)} %pad_maximum_fusion), calls=%async_computation | async-start | bytes 4718592 | tf_op jit(solution)/shard_map/all_to_all | solution.py:1573
  22.4 165.8 %reduce-scatter.2.cloned.1.call-start = ((), (), s32[]{:S(2)}) async-start(), calls=%async_computation.4 | async-start | bytes 2949120 | tf_op jit(solution)/shard_map/reduce_scatter | solution.py:1587
  61.8 16.2 %collective-permute-start.5 = (bf16[8320,128]{1,0:T(8,128)(2,1)}, bf16[8320,128]{1,0:T(8,128)(2,1)}, u32[]{:S(2)}, u32[]{:S(2)}) collective-permute-start(bf16[8320,128]{1,0:T(8,128)(2,1)} %collective-permute-done.1.refs_3_), channel_id=1, source_target_pairs={{0,4},{4,0},{8,12},{12,8},{16,20},{20,16},{24,28},{28,24},{1,5},{5... | collective-permute-start | bytes 6389768 | tf_op jit(solution)/shard_map/ppermute | solution.py:1368
  62.1 15.9 %collective-permute-start.4 = (bf16[8320,128]{1,0:T(8,128)(2,1)}, bf16[8320,128]{1,0:T(8,128)(2,1)}, u32[]{:S(2)}, u32[]{:S(2)}) collective-permute-start(bf16[8320,128]{1,0:T(8,128)(2,1)} %collective-permute-done.refs_2_), channel_id=1, source_target_pairs={{0,4},{4,0},{8,12},{12,8},{16,20},{20,16},{24,28},{28,24},{1,5},{5... | collective-permute-start | bytes 6389768 | tf_op jit(solution)/shard_map/ppermute | solution.py:1368
  62.3 26.7 %collective-permute-start.3 = (bf16[8320,128]{1,0:T(8,128)(2,1)}, bf16[8320,128]{1,0:T(8,128)(2,1)}, u32[]{:S(2)}, u32[]{:S(2)}) collective-permute-start(bf16[8320,128]{1,0:T(8,128)(2,1)} %collective-permute-done.refs_2_), channel_id=1, source_target_pairs={{0,16},{4,12},{8,24},{12,4},{16,0},{20,28},{24,8},{28,20},{1,17},{... | collective-permute-start | bytes 6389768 | tf_op jit(solution)/shard_map/ppermute | solution.py:1366
  89.0 4.4 %collective-permute-start.6 = (bf16[8320,128]{1,0:T(8,128)(2,1)}, bf16[8320,128]{1,0:T(8,128)(2,1)S(1)}, u32[]{:S(2)}, u32[]{:S(2)}) collective-permute-start(bf16[8320,128]{1,0:T(8,128)(2,1)} %collective-permute-done.3.refs_6_), channel_id=1, source_target_pairs={{0,4},{4,0},{8,12},{12,8},{16,20},{20,16},{24,28},{28,24},{1,5},{5... | collective-permute-start | bytes 6389768 | tf_op jit(solution)/shard_map/ppermute | solution.py:1368
  142.5 97.4 %all-reduce.2.cloned.1.call-start = ((), (), s32[]{:S(2)}) async-start(), calls=%async_computation.5 | async-start | bytes 655360 | tf_op jit(solution)/shard_map/psum | solution.py:1595
  143.8 30.3 %collective-permute-start.9 = (bf16[2,16,4608]{2,1,0:T(8,128)(2,1)S(1)}, bf16[2,16,4608]{2,1,0:T(8,128)(2,1)S(1)}, u32[]{:S(2)}, u32[]{:S(2)}) collective-permute-start(bf16[2,16,4608]{2,1,0:T(8,128)(2,1)S(1)} %get-tuple-element.357), channel_id=1, source_target_pairs={{0,3},{1,2},{2,1},{3,0},{4,7},{5,6},{6,5},{7,4},{8,11},{9,10},{10,... | collective-permute-start | bytes 884744 | tf_op jit(solution)/shard_map/ppermute | solution.py:1560
  147.7 26.4 %collective-permute-start.8 = (bf16[2,16,4608]{2,1,0:T(8,128)(2,1)S(1)}, bf16[2,16,4608]{2,1,0:T(8,128)(2,1)S(1)}, u32[]{:S(2)}, u32[]{:S(2)}) collective-permute-start(bf16[2,16,4608]{2,1,0:T(8,128)(2,1)S(1)} %get-tuple-element.358), channel_id=1, source_target_pairs={{0,2},{1,3},{2,0},{3,1},{4,6},{5,7},{6,4},{7,5},{8,10},{9,11},{10,... | collective-permute-start | bytes 884744 | tf_op jit(solution)/shard_map/ppermute | solution.py:1560
  147.7 26.4 %collective-permute-start.7 = (bf16[2,16,4608]{2,1,0:T(8,128)(2,1)S(1)}, bf16[2,16,4608]{2,1,0:T(8,128)(2,1)S(1)}, u32[]{:S(2)}, u32[]{:S(2)}) collective-permute-start(bf16[2,16,4608]{2,1,0:T(8,128)(2,1)S(1)} %get-tuple-element.359), channel_id=1, source_target_pairs={{0,1},{1,0},{2,3},{3,2},{4,5},{5,4},{6,7},{7,6},{8,9},{9,8},{10,11... | collective-permute-start | bytes 884744 | tf_op jit(solution)/shard_map/ppermute | solution.py:1560
  174.2 9.6 %collective-permute-start.10 = (bf16[5120,128]{1,0:T(8,128)(2,1)}, bf16[5120,128]{1,0:T(8,128)(2,1)S(1)}, u32[]{:S(2)}, u32[]{:S(2)}) collective-permute-start(bf16[5120,128]{1,0:T(8,128)(2,1)} %get-tuple-element.244), channel_id=1, source_target_pairs={{0,4},{4,0},{8,12},{12,8},{16,20},{20,16},{24,28},{28,24},{1,5},{5... | collective-permute-start | bytes 3932168 | tf_op jit(solution)/shard_map/ppermute | solution.py:1438
  188.2 21.0 %collective-permute-start.14 = (bf16[3328,128]{1,0:T(8,128)(2,1)}, bf16[3328,128]{1,0:T(8,128)(2,1)}, u32[]{:S(2)}, u32[]{:S(2)}) collective-permute-start(bf16[3328,128]{1,0:T(8,128)(2,1)} %get-tuple-element.257), channel_id=1, source_target_pairs={{0,4},{4,0},{8,12},{12,8},{16,20},{20,16},{24,28},{28,24},{1,5},{5... | collective-permute-start | bytes 2555912 | tf_op jit(solution)/shard_map/ppermute | solution.py:1438
  190.9 16.4 %collective-permute-start.13 = (bf16[1280,128]{1,0:T(8,128)(2,1)}, bf16[1280,128]{1,0:T(8,128)(2,1)S(1)}, u32[]{:S(2)}, u32[]{:S(2)}) collective-permute-start(bf16[1280,128]{1,0:T(8,128)(2,1)} %get-tuple-element.346), channel_id=1, source_target_pairs={{0,24},{4,28},{8,16},{12,20},{16,8},{20,12},{24,0},{28,4},{1,25},{... | collective-permute-start | bytes 983048 | tf_op jit(solution)/shard_map/ppermute | solution.py:1441
  192.3 16.8 %collective-permute-start.12 = (bf16[1280,128]{1,0:T(8,128)(2,1)}, bf16[1280,128]{1,0:T(8,128)(2,1)S(1)}, u32[]{:S(2)}, u32[]{:S(2)}) collective-permute-start(bf16[1280,128]{1,0:T(8,128)(2,1)} %get-tuple-element.347), channel_id=1, source_target_pairs={{0,16},{4,20},{8,24},{12,28},{16,0},{20,4},{24,8},{28,12},{1,17},{... | collective-permute-start | bytes 983048 | tf_op jit(solution)/shard_map/ppermute | solution.py:1441
  193.8 15.4 %collective-permute-start.11 = (bf16[1280,128]{1,0:T(8,128)(2,1)}, bf16[1280,128]{1,0:T(8,128)(2,1)}, u32[]{:S(2)}, u32[]{:S(2)}) collective-permute-start(bf16[1280,128]{1,0:T(8,128)(2,1)} %get-tuple-element.348), channel_id=1, source_target_pairs={{0,8},{4,12},{8,0},{12,4},{16,24},{20,28},{24,16},{28,20},{1,9},{5... | collective-permute-start | bytes 983048 | tf_op jit(solution)/shard_map/ppermute | solution.py:1441
  194.4 98.5 %all-gather.2.cloned.1.call-start = ((), (), s32[]{:S(2)}) async-start(), calls=%async_computation.6 | async-start | bytes 2949120 | tf_op jit(solution)/shard_map/all_gather | solution.py:1605
  210.7 13.8 %collective-permute-start.17 = (bf16[832,128]{1,0:T(8,128)(2,1)S(1)}, bf16[832,128]{1,0:T(8,128)(2,1)S(1)}, u32[]{:S(2)}, u32[]{:S(2)}) collective-permute-start(bf16[832,128]{1,0:T(8,128)(2,1)S(1)} %get-tuple-element.364), channel_id=1, source_target_pairs={{0,24},{4,28},{8,16},{12,20},{16,8},{20,12},{24,0},{28,4},{1,25},{... | collective-permute-start | bytes 638984 | tf_op jit(solution)/shard_map/ppermute | solution.py:1441
  212.2 12.3 %collective-permute-start.16 = (bf16[832,128]{1,0:T(8,128)(2,1)S(1)}, bf16[832,128]{1,0:T(8,128)(2,1)S(1)}, u32[]{:S(2)}, u32[]{:S(2)}) collective-permute-start(bf16[832,128]{1,0:T(8,128)(2,1)S(1)} %get-tuple-element.365), channel_id=1, source_target_pairs={{0,16},{4,20},{8,24},{12,28},{16,0},{20,4},{24,8},{28,12},{1,17},{... | collective-permute-start | bytes 638984 | tf_op jit(solution)/shard_map/ppermute | solution.py:1441
  213.5 11.0 %collective-permute-start.15 = (bf16[832,128]{1,0:T(8,128)(2,1)S(1)}, bf16[832,128]{1,0:T(8,128)(2,1)S(1)}, u32[]{:S(2)}, u32[]{:S(2)}) collective-permute-start(bf16[832,128]{1,0:T(8,128)(2,1)S(1)} %get-tuple-element.366), channel_id=1, source_target_pairs={{0,8},{4,12},{8,0},{12,4},{16,24},{20,28},{24,16},{28,20},{1,9},{5... | collective-permute-start | bytes 638984 | tf_op jit(solution)/shard_map/ppermute | solution.py:1441
  224.7 15.1 %collective-permute-start.18 = (bf16[528,128]{1,0:T(8,128)(2,1)S(1)}, bf16[528,128]{1,0:T(8,128)(2,1)S(1)}, u32[]{:S(2)}, u32[]{:S(2)}) collective-permute-start(bf16[528,128]{1,0:T(8,128)(2,1)S(1)} %pad_maximum_fusion.3), channel_id=1, source_target_pairs={{0,1},{1,0},{2,3},{3,2},{4,5},{5,4},{6,7},{7,6},{8,9},{9,8},{10,11... | collective-permute-start | bytes 405512 | tf_op jit(solution)/shard_map/ppermute | solution.py:1444
  226.3 13.6 %collective-permute-start.19 = (bf16[528,128]{1,0:T(8,128)(2,1)S(1)}, bf16[528,128]{1,0:T(8,128)(2,1)S(1)}, u32[]{:S(2)}, u32[]{:S(2)}) collective-permute-start(bf16[528,128]{1,0:T(8,128)(2,1)S(1)} %pad_maximum_fusion.4), channel_id=1, source_target_pairs={{0,2},{1,3},{2,0},{3,1},{4,6},{5,7},{6,4},{7,5},{8,10},{9,11},{10,... | collective-permute-start | bytes 405512 | tf_op jit(solution)/shard_map/ppermute | solution.py:1444
  228.8 11.1 %collective-permute-start.20 = (bf16[528,128]{1,0:T(8,128)(2,1)S(1)}, bf16[528,128]{1,0:T(8,128)(2,1)S(1)}, u32[]{:S(2)}, u32[]{:S(2)}) collective-permute-start(bf16[528,128]{1,0:T(8,128)(2,1)S(1)} %pad_maximum_fusion.5), channel_id=1, source_target_pairs={{0,3},{1,2},{2,1},{3,0},{4,7},{5,6},{6,5},{7,4},{8,11},{9,10},{10,... | collective-permute-start | bytes 405512 | tf_op jit(solution)/shard_map/ppermute | solution.py:1444
  239.9 3.6 %collective-permute-start.21 = (bf16[3328,128]{1,0:T(8,128)(2,1)}, bf16[3328,128]{1,0:T(8,128)(2,1)S(1)}, u32[]{:S(2)}, u32[]{:S(2)}) collective-permute-start(bf16[3328,128]{1,0:T(8,128)(2,1)} %get-tuple-element.297), channel_id=1, source_target_pairs={{0,4},{4,0},{8,12},{12,8},{16,20},{20,16},{24,28},{28,24},{1,5},{5... | collective-permute-start | bytes 2555912 | tf_op jit(solution)/shard_map/ppermute | solution.py:1438
  240.1 10.8 %collective-permute-start.27 = (bf16[528,128]{1,0:T(8,128)(2,1)S(1)}, bf16[528,128]{1,0:T(8,128)(2,1)S(1)}, u32[]{:S(2)}, u32[]{:S(2)}) collective-permute-start(bf16[528,128]{1,0:T(8,128)(2,1)S(1)} %add_convert_fusion.3.refs_0_), channel_id=1, source_target_pairs={{0,3},{1,2},{2,1},{3,0},{4,7},{5,6},{6,5},{7,4},{8,11},{9,10},{10,... | collective-permute-start | bytes 405512 | tf_op jit(solution)/shard_map/ppermute | solution.py:1444
  245.7 12.8 %collective-permute-start.24 = (bf16[832,128]{1,0:T(8,128)(2,1)}, bf16[832,128]{1,0:T(8,128)(2,1)}, u32[]{:S(2)}, u32[]{:S(2)}) collective-permute-start(bf16[832,128]{1,0:T(8,128)(2,1)} %get-tuple-element.361), channel_id=1, source_target_pairs={{0,24},{4,28},{8,16},{12,20},{16,8},{20,12},{24,0},{28,4},{1,25},{... | collective-permute-start | bytes 638984 | tf_op jit(solution)/shard_map/ppermute | solution.py:1441
  247.1 15.2 %collective-permute-start.23 = (bf16[832,128]{1,0:T(8,128)(2,1)}, bf16[832,128]{1,0:T(8,128)(2,1)}, u32[]{:S(2)}, u32[]{:S(2)}) collective-permute-start(bf16[832,128]{1,0:T(8,128)(2,1)} %get-tuple-element.362), channel_id=1, source_target_pairs={{0,16},{4,20},{8,24},{12,28},{16,0},{20,4},{24,8},{28,12},{1,17},{... | collective-permute-start | bytes 638984 | tf_op jit(solution)/shard_map/ppermute | solution.py:1441
  248.5 13.9 %collective-permute-start.22 = (bf16[832,128]{1,0:T(8,128)(2,1)S(1)}, bf16[832,128]{1,0:T(8,128)(2,1)}, u32[]{:S(2)}, u32[]{:S(2)}) collective-permute-start(bf16[832,128]{1,0:T(8,128)(2,1)S(1)} %get-tuple-element.363), channel_id=1, source_target_pairs={{0,8},{4,12},{8,0},{12,4},{16,24},{20,28},{24,16},{28,20},{1,9},{5... | collective-permute-start | bytes 638984 | tf_op jit(solution)/shard_map/ppermute | solution.py:1441
  249.2 8.7 %collective-permute-start.26 = (bf16[528,128]{1,0:T(8,128)(2,1)S(1)}, bf16[528,128]{1,0:T(8,128)(2,1)S(1)}, u32[]{:S(2)}, u32[]{:S(2)}) collective-permute-start(bf16[528,128]{1,0:T(8,128)(2,1)S(1)} %add_convert_fusion.3.refs_0_), channel_id=1, source_target_pairs={{0,2},{1,3},{2,0},{3,1},{4,6},{5,7},{6,4},{7,5},{8,10},{9,11},{10,... | collective-permute-start | bytes 405512 | tf_op jit(solution)/shard_map/ppermute | solution.py:1444
  250.9 7.2 %collective-permute-start.25 = (bf16[528,128]{1,0:T(8,128)(2,1)S(1)}, bf16[528,128]{1,0:T(8,128)(2,1)S(1)}, u32[]{:S(2)}, u32[]{:S(2)}) collective-permute-start(bf16[528,128]{1,0:T(8,128)(2,1)S(1)} %add_convert_fusion.3.refs_0_), channel_id=1, source_target_pairs={{0,1},{1,0},{2,3},{3,2},{4,5},{5,4},{6,7},{7,6},{8,9},{9,8},{10,11... | collective-permute-start | bytes 405512 | tf_op jit(solution)/shard_map/ppermute | solution.py:1444
  253.1 17.2 %copy-start.18 = (bf16[2,16,4608]{2,1,0:T(8,128)(2,1)S(1)}, bf16[2,16,4608]{2,1,0:T(8,128)(2,1)}, u32[]{:S(2)}) copy-start(bf16[2,16,4608]{2,1,0:T(8,128)(2,1)} %copy-done.17) | copy-start | bytes 884740
  253.1 39.7 %all-to-all-start.1 = ((bf16[4,2,16,2560]{3,2,1,0:T(8,128)(2,1)}), bf16[4,2,16,2560]{3,2,1,0:T(8,128)(2,1)S(1)}, u32[]{:S(2)}, u32[]{:S(2)}) async-start(bf16[4,2,16,2560]{3,2,1,0:T(8,128)(2,1)} %bitcast.87), calls=%async_computation.2 | async-start | bytes 1310720 | tf_op jit(solution)/shard_map/all_to_all | solution.py:1549
  263.6 9.2 %collective-permute-start.30 = (bf16[208,128]{1,0:T(8,128)(2,1)S(1)}, bf16[208,128]{1,0:T(8,128)(2,1)S(1)}, u32[]{:S(2)}, u32[]{:S(2)}) collective-permute-start(bf16[208,128]{1,0:T(8,128)(2,1)S(1)} %get-tuple-element.371), channel_id=1, source_target_pairs={{0,3},{1,2},{2,1},{3,0},{4,7},{5,6},{6,5},{7,4},{8,11},{9,10},{10,... | collective-permute-start | bytes 159752 | tf_op jit(solution)/shard_map/ppermute | solution.py:1444
  266.0 11.7 %collective-permute-start.29 = (bf16[208,128]{1,0:T(8,128)(2,1)S(1)}, bf16[208,128]{1,0:T(8,128)(2,1)S(1)}, u32[]{:S(2)}, u32[]{:S(2)}) collective-permute-start(bf16[208,128]{1,0:T(8,128)(2,1)S(1)} %get-tuple-element.372), channel_id=1, source_target_pairs={{0,2},{1,3},{2,0},{3,1},{4,6},{5,7},{6,4},{7,5},{8,10},{9,11},{10,... | collective-permute-start | bytes 159752 | tf_op jit(solution)/shard_map/ppermute | solution.py:1444
  266.0 11.7 %collective-permute-start.28 = (bf16[208,128]{1,0:T(8,128)(2,1)S(1)}, bf16[208,128]{1,0:T(8,128)(2,1)S(1)}, u32[]{:S(2)}, u32[]{:S(2)}) collective-permute-start(bf16[208,128]{1,0:T(8,128)(2,1)S(1)} %get-tuple-element.373), channel_id=1, source_target_pairs={{0,1},{1,0},{2,3},{3,2},{4,5},{5,4},{6,7},{7,6},{8,9},{9,8},{10,11... | collective-permute-start | bytes 159752 | tf_op jit(solution)/shard_map/ppermute | solution.py:1444
  268.8 11.9 %collective-permute-start.31 = (bf16[2112,128]{1,0:T(8,128)(2,1)S(1)}, bf16[2112,128]{1,0:T(8,128)(2,1)S(1)}, u32[]{:S(2)}, u32[]{:S(2)}) collective-permute-start(bf16[2112,128]{1,0:T(8,128)(2,1)S(1)} %shard_map.256.refs_0_), channel_id=1, source_target_pairs={{0,8},{4,20},{8,0},{12,28},{16,24},{20,4},{24,16},{28,12},{1,9},{5... | collective-permute-start | bytes 1622024 | tf_op jit(solution)/shard_map/ppermute | solution.py:1474
  280.9 20.3 %collective-permute-start.38 = (bf16[4224,128]{1,0:T(8,128)(2,1)S(1)}, bf16[4224,128]{1,0:T(8,128)(2,1)S(1)}, u32[]{:S(2)}, u32[]{:S(2)}) collective-permute-start(bf16[4224,128]{1,0:T(8,128)(2,1)S(1)} %shard_map.258.refs_0_), channel_id=1, source_target_pairs={{0,16},{4,12},{8,24},{12,4},{16,0},{20,28},{24,8},{28,20},{1,17},{... | collective-permute-start | bytes 3244040 | tf_op jit(solution)/shard_map/ppermute | solution.py:1474
  284.4 6.4 %collective-permute-start.34 = (bf16[208,128]{1,0:T(8,128)(2,1)S(1)}, bf16[208,128]{1,0:T(8,128)(2,1)S(1)}, u32[]{:S(2)}, u32[]{:S(2)}) collective-permute-start(bf16[208,128]{1,0:T(8,128)(2,1)S(1)} %fusion.11.refs_0_), channel_id=1, source_target_pairs={{0,3},{1,2},{2,1},{3,0},{4,7},{5,6},{6,5},{7,4},{8,11},{9,10},{10,... | collective-permute-start | bytes 159752 | tf_op jit(solution)/shard_map/ppermute | solution.py:1444
  287.8 5.0 %collective-permute-start.33 = (bf16[208,128]{1,0:T(8,128)(2,1)S(1)}, bf16[208,128]{1,0:T(8,128)(2,1)S(1)}, u32[]{:S(2)}, u32[]{:S(2)}) collective-permute-start(bf16[208,128]{1,0:T(8,128)(2,1)S(1)} %fusion.11.refs_0_), channel_id=1, source_target_pairs={{0,2},{1,3},{2,0},{3,1},{4,6},{5,7},{6,4},{7,5},{8,10},{9,11},{10,... | collective-permute-start | bytes 159752 | tf_op jit(solution)/shard_map/ppermute | solution.py:1444
  287.8 5.0 %collective-permute-start.32 = (bf16[208,128]{1,0:T(8,128)(2,1)S(1)}, bf16[208,128]{1,0:T(8,128)(2,1)S(1)}, u32[]{:S(2)}, u32[]{:S(2)}) collective-permute-start(bf16[208,128]{1,0:T(8,128)(2,1)S(1)} %fusion.11.refs_0_), channel_id=1, source_target_pairs={{0,1},{1,0},{2,3},{3,2},{4,5},{5,4},{6,7},{7,6},{8,9},{9,8},{10,11... | collective-permute-start | bytes 159752 | tf_op jit(solution)/shard_map/ppermute | solution.py:1444
  293.2 9.0 %collective-permute-start.37 = (bf16[832,128]{1,0:T(8,128)(2,1)S(1)}, bf16[832,128]{1,0:T(8,128)(2,1)S(1)}, u32[]{:S(2)}, u32[]{:S(2)}) collective-permute-start(bf16[832,128]{1,0:T(8,128)(2,1)S(1)} %shard_map.257.refs_0_), channel_id=1, source_target_pairs={{0,24},{4,28},{8,16},{12,20},{16,8},{20,12},{24,0},{28,4},{1,25},{... | collective-permute-start | bytes 638984 | tf_op jit(solution)/shard_map/ppermute | solution.py:1441
  293.8 11.4 %collective-permute-start.36 = (bf16[832,128]{1,0:T(8,128)(2,1)S(1)}, bf16[832,128]{1,0:T(8,128)(2,1)S(1)}, u32[]{:S(2)}, u32[]{:S(2)}) collective-permute-start(bf16[832,128]{1,0:T(8,128)(2,1)S(1)} %shard_map.257.refs_0_), channel_id=1, source_target_pairs={{0,16},{4,20},{8,24},{12,28},{16,0},{20,4},{24,8},{28,12},{1,17},{... | collective-permute-start | bytes 638984 | tf_op jit(solution)/shard_map/ppermute | solution.py:1441
  295.3 10.0 %collective-permute-start.35 = (bf16[832,128]{1,0:T(8,128)(2,1)S(1)}, bf16[832,128]{1,0:T(8,128)(2,1)S(1)}, u32[]{:S(2)}, u32[]{:S(2)}) collective-permute-start(bf16[832,128]{1,0:T(8,128)(2,1)S(1)} %shard_map.257.refs_0_), channel_id=1, source_target_pairs={{0,8},{4,12},{8,0},{12,4},{16,24},{20,28},{24,16},{28,20},{1,9},{5... | collective-permute-start | bytes 638984 | tf_op jit(solution)/shard_map/ppermute | solution.py:1441
  306.7 6.5 %collective-permute-start.40 = (bf16[8448,128]{1,0:T(8,128)(2,1)S(1)}, bf16[8448,128]{1,0:T(8,128)(2,1)}, u32[]{:S(2)}, u32[]{:S(2)}) collective-permute-start(bf16[8448,128]{1,0:T(8,128)(2,1)S(1)} %shard_map.260.refs_3_), channel_id=1, source_target_pairs={{0,4},{4,0},{8,12},{12,8},{16,20},{20,16},{24,28},{28,24},{1,5},{5... | collective-permute-start | bytes 6488072 | tf_op jit(solution)/shard_map/ppermute | solution.py:1438
  308.0 4.3 %collective-permute-start.39 = (bf16[3328,128]{1,0:T(8,128)(2,1)S(1)}, bf16[3328,128]{1,0:T(8,128)(2,1)S(1)}, u32[]{:S(2)}, u32[]{:S(2)}) collective-permute-start(bf16[3328,128]{1,0:T(8,128)(2,1)S(1)} %shard_map.259.refs_1_), channel_id=1, source_target_pairs={{0,4},{4,0},{8,12},{12,8},{16,20},{20,16},{24,28},{28,24},{1,5},{5... | collective-permute-start | bytes 2555912 | tf_op jit(solution)/shard_map/ppermute | solution.py:1438
  313.2 20.8 %all-to-all-start.2 = ((bf16[4,2,16,2048]{3,2,1,0:T(8,128)(2,1)}), bf16[4,2,16,2048]{3,2,1,0:T(8,128)(2,1)}, u32[]{:S(2)}, u32[]{:S(2)}) async-start(bf16[4,2,16,2048]{3,2,1,0:T(8,128)(2,1)} %bitcast.101), calls=%async_computation.3 | async-start | bytes 1048576 | tf_op jit(solution)/shard_map/all_to_all | solution.py:1549
  (22 other events, 180.5 us)
Sparse Core Ops, SparseCore 0:
  142.6 45.5 reduce-scatter.1
  194.5 37.1 all-reduce.1
  240.0 38.7 all-gather.1

commit v7 on v6

--- a/solution.py
+++ b/solution.py
@@ -1605,7 +1605,7 @@
     upper_two = lax.all_gather(spread, "dp", axis=0, tiled=True)
     last = Chain(cube, True, (keep, send))
     sent = middle.launch()
-    early = D + EDGE_LANES // 2
+    early = D + 3 * EDGE_LANES // 8
     bgrad, = phase([last], bgrad)
     one_part, two_part = packed(bgrad, 0, early), packed(bgrad, early, OUT_LANES - early)
     one_part = to_rows(one_part)

time: 347 us -> 348 us (level)
  transfers between devices with their start and end apart: 47 -> 47, of which waited for: 20 -> 21; matrix products, arithmetic and copies ran while one was open for 6% -> 6% of each run, Pallas kernels for 24% -> 24%
where the time goes in v7:
time: 348 us; the launch traced here: 344 us
  Pallas kernels  136 us (39%)
  waiting for transfers between devices  101 us (29%)
  starting transfers between devices  62.7 us (18%)
  local copies, waits for them, and re-layouts  15.7 us (5%)
  between operations  15.2 us (4%)
  other arithmetic  13.7 us (4%)
    pallas_call x7, Pallas kernels, kernel(): pl.pallas_call(body, out_shape=structs(out), in_specs=[SMEM] * len(smem)...  104 us
    ppermute x3, waiting for transfers between devices, gather(): sent.append((0, used + (step,), lax.ppermute(v, 'dp', self.pairs(step))))  50.4 us
    ppermute x12, starting transfers between devices, to_row(): return lax.ppermute(value, 'row', [(i, i ^ k) for i in range(self.rows)])  19.8 us
    pallas_call x1, Pallas kernels, adam(): pl.pallas_call(body, grid=(pl.cdiv(held, step),), out_shape=[shape] * 3 +...  14.7 us
    ppermute x12, starting transfers between devices, to_chip(): lax.ppermute(value, 'dp', [(i, i ^ k << 1) for i in range(2 * self.sides)])  14.1 us
    all_to_all x1, waiting for transfers between devices, to_whole(): lax.all_to_all(big, 'row', split_axis=0, concat_axis=1, tiled=True)  12.3 us
    pallas_call x1, Pallas kernels, assemble(): pl.pallas_call(body, out_shape=structs(out), in_specs=[SMEM] * 2 + [HBM]...  10.8 us
    ppermute x12, waiting for transfers between devices, to_row(): return lax.ppermute(value, 'row', [(i, i ^ k) for i in range(self.rows)])  9.56 us
  transfers between devices with their start and end apart: 47, of which 21 were waited for; matrix products, arithmetic and copies ran while one was open for 6% of the time, Pallas kernels for 24%

profile of v7, /device:TPU:0, one launch (start us, length us, event | category | flops | bytes accessed | tf_op | source)
XLA Modules:
  0.0 344.2 jit_solution(13677152615033042809)
XLA Ops:
  7.2 4.3 %shard_map.247.refs_0_ = bf16[8320,128]{1,0:T(8,128)(2,1)} custom-call(s32[8]{0:T(128)} %owner_ref.5, s32[8]{0:T(128)} %rows_ref.5, f32[8290,128]{1,0:T(8,128)} %refs_5_.1), custom_call_target="tpu_custom_call" | custom-call | tf_op jit(solution)/shard_map/pallas_call | solution.py:1068
  12.0 2.5 collective-permute-start.1
  14.5 1.5 collective-permute-start
  16.1 1.5 pad_maximum_fusion
  17.6 4.9 %all-to-all-start = ((bf16[8,16,9216]{2,1,0:T(8,128)(2,1)}), bf16[8,16,9216]{2,1,0:T(8,128)(2,1)S(1)}, u32[]{:S(2)}, u32[]{:S(2)}) async-start(bf16[8,16,9216]{2,1,0:T(8,128)(2,1)} %pad_maximum_fusion), calls=%async_computation | async-start | bytes 4718592 | tf_op jit(solution)/shard_map/all_to_all | solution.py:1573
  22.4 38.4 %collective-permute-done.1.refs_3_ = bf16[8320,128]{1,0:T(8,128)(2,1)} collective-permute-done((bf16[8320,128]{1,0:T(8,128)(2,1)}, bf16[8320,128]{1,0:T(8,128)(2,1)}, u32[]{:S(2)}, u32[]{:S(2)}) %collective-permute-start.1) | collective-permute-done | bytes 2129952 | tf_op jit(solution)/shard_map/ppermute | solution.py:1366
  62.3 1.8 collective-permute-start.3
  64.1 12.3 %all-to-all-done = bf16[8,16,9216]{2,1,0:T(8,128)(2,1)S(1)} async-done(((bf16[8,16,9216]{2,1,0:T(8,128)(2,1)}), bf16[8,16,9216]{2,1,0:T(8,128)(2,1)S(1)}, u32[]{:S(2)}, u32[]{:S(2)}) %all-to-all-start) | async-done | bytes 2359328 | tf_op jit(solution)/shard_map/all_to_all | solution.py:1573
  76.4 1.6 copy.31
  78.0 11.0 %collective-permute-done.3.refs_6_ = bf16[8320,128]{1,0:T(8,128)(2,1)} collective-permute-done((bf16[8320,128]{1,0:T(8,128)(2,1)}, bf16[8320,128]{1,0:T(8,128)(2,1)}, u32[]{:S(2)}, u32[]{:S(2)}) %collective-permute-start.3) | collective-permute-done | bytes 2129952 | tf_op jit(solution)/shard_map/ppermute | solution.py:1366
  89.7 3.7 %collective-permute-done.6.refs_7_ = bf16[8320,128]{1,0:T(8,128)(2,1)S(1)} collective-permute-done((bf16[8320,128]{1,0:T(8,128)(2,1)}, bf16[8320,128]{1,0:T(8,128)(2,1)S(1)}, u32[]{:S(2)}, u32[]{:S(2)}) %collective-permute-start.6) | collective-permute-done | bytes 2129952 | tf_op jit(solution)/shard_map/ppermute | solution.py:1368
  94.8 10.8 %shard_map.248 = (bf16[512,1536]{1,0:T(8,128)(2,1)}, bf16[512,512]{1,0:T(8,128)(2,1)}, bf16[512,1024]{1,0:T(8,128)(2,1)}, bf16[1024,512]{1,0:T(8,128)(2,1)}, bf1...) custom-call(s32[8]{0:T(128)} %owner_ref.5, ...), custom_call_target="tpu_custom_call" | custom-call | bytes 34000000 | tf_op jit(solution)/shard_map/pallas_call | solution.py:1147
  105.5 17.0 %shard_map.249 = (bf16[224,512]{1,0:T(8,128)(2,1)}, bf16[2816,256]{1,0:T(8,128)(2,1)}, bf16[224,512]{1,0:T(8,128)(2,1)}, f32[224,128]{1,0:T(8,128)}, bf16[224,15...) custom-call(s32[5]{0:T(128)} %pad_add_fusion.refs_0_, ...), custom_call_target="tpu_custom_call" | custom-call | bytes 54400000 | tf_op jit(solution)/shard_map/pallas_call | solution.py:804
  122.6 20.0 %shard_map.250 = (bf16[96,512]{1,0:T(8,128)(2,1)}, bf16[96,2048]{1,0:T(8,128)(2,1)}, bf16[128,4608]{1,0:T(8,128)(2,1)}, bf16[2816,256]{1,0:T(8,128)(2,1)}, bf16[...) custom-call(s32[5]{0:T(128)} %pad_add_fusion.refs_0_, ...), custom_call_target="tpu_custom_call" | custom-call | bytes 74800000 | tf_op jit(solution)/shard_map/pallas_call | solution.py:804
  144.0 3.9 %collective-permute-start.9 = (bf16[2,16,4608]{2,1,0:T(8,128)(2,1)S(1)}, bf16[2,16,4608]{2,1,0:T(8,128)(2,1)S(1)}, u32[]{:S(2)}, u32[]{:S(2)}) collective-permute-start(bf16[2,16,4608]{2,1,0:T(8,128)(2,1)S(1)} %get-tuple-element.357), channel_id=1, source_target_pairs={{0,3},{1,2},{2,1},{3,0},{4,7},{5,6},{6,5},{7,4},{8,11},{9,10},{10,... | collective-permute-start | bytes 884744 | tf_op jit(solution)/shard_map/ppermute | solution.py:1560
  148.5 25.7 %shard_map.251 = (bf16[2816,256]{1,0:T(8,128)(2,1)}, f32[256,128]{1,0:T(8,128)}, bf16[1408,512]{1,0:T(8,128)(2,1)}, bf16[224,1536]{1,0:T(8,128)(2,1)}, f32[8,128...) custom-call(bf16[512,1536]{1,0:T(8,128)(2,1)} %get-tuple-element.191, ...), custom_call_target="tpu_custom_call" | custom-call | bytes 85000000 | tf_op jit(solution)/shard_map/pallas_call | solution.py:804
  175.2 8.8 %shard_map.252 = (bf16[2816,256]{1,0:T(8,128)(2,1)}, bf16[3328,128]{1,0:T(8,128)(2,1)}, bf16[3328,128]{1,0:T(8,128)(2,1)}) custom-call(bf16[512,512]{1,0:T(8,128)(2,1)} %get-tuple-element.195.refs_5_.refs_0_, f32[4,512]{1,0:T(4,128)} %get-tuple-element.199.refs_9_.refs_5_.refs_1_, f32[4,256]{1,0:T(4,128)} %get-tuple-element.200.refs_10_.refs_4_.refs_2_, ...), custom_call_target="tpu_custom_call" | custom-call | bytes 30600000 | tf_op jit(solution)/shard_map/pallas_call | solution.py:804
  184.0 4.1 %reduce-scatter.2.cloned.1.call-done = bf16[1280,128]{1,0:T(8,128)(2,1)} async-done(((bf16[10240,128]{1,0:T(8,128)(2,1)}), bf16[1280,128]{1,0:T(8,128)(2,1)}) %reduce-scatter.2.cloned.1.call-update) | async-done | bytes 327696 | tf_op jit(solution)/shard_map/reduce_scatter | solution.py:1587
  188.1 1.7 add_convert_fusion
  190.8 1.5 collective-permute-start.13
  194.7 12.4 %shard_map.253 = (bf16[2816,256]{1,0:T(8,128)(2,1)}, f32[1408,256]{1,0:T(8,128)}, f32[256,128]{1,0:T(8,128)}) custom-call(bf16[256,512]{1,0:T(8,128)(2,1)} %get-tuple-element.206.refs_6_.refs_0_, bf16[256,512]{1,0:T(8,128)(2,1)} %get-tuple-element.207.refs_7_.refs_1_, bf16[512,256]{1,0:T(8,128)(2,1)} %get-tuple-element.208.refs_8_.refs_2_, ...), custom_call_target="tpu_custom_call" | custom-call | bytes 54400000 | tf_op jit(solution)/shard_map/pallas_call | solution.py:804
  207.1 1.9 collective-permute-done.12
  210.5 1.5 collective-permute-start.17
  214.2 9.1 %shard_map.254 = (bf16[1408,512]{1,0:T(8,128)(2,1)}, bf16[224,1536]{1,0:T(8,128)(2,1)}) custom-call(bf16[224,1536]{1,0:T(8,128)(2,1)} %get-tuple-element.271.refs_0_, bf16[1408,256]{1,0:T(8,128)(2,1)} %get-tuple-element.272.refs_1_, f32[1408,256]{1,0:T(8,128)} %get-tuple-element.273.refs_2_, bf16[224,512]{1,0:T(8,128)(2,1)} %get-tuple-element.274.refs_3_, ...), custom_call_target="tpu_custom_call" | custom-call | bytes 47600000 | tf_op jit(solution)/shard_map/pallas_call | solution.py:804
  223.6 1.6 collective-permute-start.18
  225.1 2.5 collective-permute-start.19
  228.2 10.5 %shard_map.255 = (bf16[96,512]{1,0:T(8,128)(2,1)}, bf16[96,2048]{1,0:T(8,128)(2,1)}, bf16[128,4608]{1,0:T(8,128)(2,1)}, bf16[3328,128]{1,0:T(8,128)(2,1)}, bf16[3328,128]{1,0:T(8,128)(2,1)}) custom-call(bf16[512,1536]{1,0:T(8,128)(2,1)} %get-tuple-element.201.refs_1_.refs_0_, bf16[512,512]{1,0:T(8,128)(2,1)} %get-tuple-element.205.refs_5_.refs_1_, ...), custom_call_target="tpu_custom_call" | custom-call | bytes 44200000 | tf_op jit(solution)/shard_map/pallas_call | solution.py:804
  239.0 3.3 collective-permute-start.27
  244.5 1.4 collective-permute-start.24
  248.0 2.6 collective-permute-start.26
  252.9 3.6 %all-to-all-start.1 = ((bf16[4,2,16,2048]{3,2,1,0:T(8,128)(2,1)}), bf16[4,2,16,2048]{3,2,1,0:T(8,128)(2,1)S(1)}, u32[]{:S(2)}, u32[]{:S(2)}) async-start(bf16[4,2,16,2048]{3,2,1,0:T(8,128)(2,1)} %bitcast.88), calls=%async_computation.2 | async-start | bytes 1048576 | tf_op jit(solution)/shard_map/all_to_all | solution.py:1549
  257.0 4.2 %collective-permute-done.23 = bf16[832,128]{1,0:T(8,128)(2,1)} collective-permute-done((bf16[832,128]{1,0:T(8,128)(2,1)}, bf16[832,128]{1,0:T(8,128)(2,1)}, u32[]{:S(2)}, u32[]{:S(2)}) %collective-permute-start.23) | collective-permute-done | bytes 213024 | tf_op jit(solution)/shard_map/ppermute | solution.py:1441
  262.5 2.4 collective-permute-start.30
  267.7 1.5 collective-permute-start.31
  269.3 1.7 collective-permute-done.30
  270.9 4.1 %collective-permute-done.29 = bf16[208,128]{1,0:T(8,128)(2,1)S(1)} collective-permute-done((bf16[208,128]{1,0:T(8,128)(2,1)S(1)}, bf16[208,128]{1,0:T(8,128)(2,1)S(1)}, u32[]{:S(2)}, u32[]{:S(2)}) %collective-permute-start.29) | collective-permute-done | bytes 53280 | tf_op jit(solution)/shard_map/ppermute | solution.py:1444
  275.1 5.1 %collective-permute-done.31.refs_1_ = bf16[2112,128]{1,0:T(8,128)(2,1)S(1)} collective-permute-done((bf16[2112,128]{1,0:T(8,128)(2,1)S(1)}, bf16[2112,128]{1,0:T(8,128)(2,1)S(1)}, u32[]{:S(2)}, u32[]{:S(2)}) %collective-permute-start.31) | collective-permute-done | bytes 540704 | tf_op jit(solution)/shard_map/ppermute | solution.py:1474
  280.4 1.5 collective-permute-start.38
  283.8 3.4 collective-permute-start.34
  290.2 2.0 collective-permute-done.33.refs_2_
  293.2 1.5 collective-permute-start.36
  294.7 1.5 collective-permute-start.35
  301.8 2.9 collective-permute-done.36.refs_2_
  308.0 3.8 %collective-permute-done.39.refs_2_ = bf16[3328,128]{1,0:T(8,128)(2,1)S(1)} collective-permute-done((bf16[3328,128]{1,0:T(8,128)(2,1)S(1)}, bf16[3328,128]{1,0:T(8,128)(2,1)S(1)}, u32[]{:S(2)}, u32[]{:S(2)}) %collective-permute-start.39) | collective-permute-done | bytes 852000 | tf_op jit(solution)/shard_map/ppermute | solution.py:1438
  312.7 4.8 %all-to-all-start.2 = ((bf16[4,2,16,2560]{3,2,1,0:T(8,128)(2,1)}), bf16[4,2,16,2560]{3,2,1,0:T(8,128)(2,1)}, u32[]{:S(2)}, u32[]{:S(2)}) async-start(bf16[4,2,16,2560]{3,2,1,0:T(8,128)(2,1)} %bitcast.98), calls=%async_computation.3 | async-start | bytes 1310720 | tf_op jit(solution)/shard_map/all_to_all | solution.py:1549
  318.9 14.7 %shard_map.261 = (f32[8290,128]{1,0:T(8,128)}, f32[8290,128]{1,0:T(8,128)}, f32[8290,128]{1,0:T(8,128)}, f32[8,576]{1,0:T(8,128)}) custom-call(s32[8]{0:T(128)} %owner_ref.5, s32[8]{0:T(128)} %rows_ref.5, f32[2]{0:T(128)} %pad_maximum_fusion.7.scale_ref, bf16[10240,128]{1,0:T(8,128)(2,1)} %all-gather.2.cloned.1.call-done.refs_0_, ...), custom_call_target="tpu_custom_call" | custom-call | bytes 34000000 | tf_op jit(solution)/shard_map/pallas_call | solution.py:1305
  333.6 1.6 all-to-all-done.2
  335.2 2.3 pad_maximum_fusion.2
  (142 shorter events, 42.6 us)
Async XLA Ops:
  11.6 10.9 %collective-permute-start.2 = (bf16[8320,128]{1,0:T(8,128)(2,1)}, bf16[8320,128]{1,0:T(8,128)(2,1)}, u32[]{:S(2)}, u32[]{:S(2)}) collective-permute-start(bf16[8320,128]{1,0:T(8,128)(2,1)} %shard_map.247.refs_0_), channel_id=1, source_target_pairs={{0,4},{4,0},{8,12},{12,8},{16,20},{20,16},{24,28},{28,24},{1,5},{5... | collective-permute-start | bytes 6389768 | tf_op jit(solution)/shard_map/ppermute | solution.py:1368
  12.0 48.8 %collective-permute-start.1 = (bf16[8320,128]{1,0:T(8,128)(2,1)}, bf16[8320,128]{1,0:T(8,128)(2,1)}, u32[]{:S(2)}, u32[]{:S(2)}) collective-permute-start(bf16[8320,128]{1,0:T(8,128)(2,1)} %shard_map.247.refs_0_), channel_id=1, source_target_pairs={{0,16},{4,12},{8,24},{12,4},{16,0},{20,28},{24,8},{28,20},{1,17},{... | collective-permute-start | bytes 6389768 | tf_op jit(solution)/shard_map/ppermute | solution.py:1366
  14.5 47.3 %collective-permute-start = (bf16[8320,128]{1,0:T(8,128)(2,1)}, bf16[8320,128]{1,0:T(8,128)(2,1)}, u32[]{:S(2)}, u32[]{:S(2)}) collective-permute-start(bf16[8320,128]{1,0:T(8,128)(2,1)} %shard_map.247.refs_0_), channel_id=1, source_target_pairs={{0,8},{4,20},{8,0},{12,28},{16,24},{20,4},{24,16},{28,12},{1,9},{5... | collective-permute-start | bytes 6389768 | tf_op jit(solution)/shard_map/ppermute | solution.py:1366
  17.6 58.8 %all-to-all-start = ((bf16[8,16,9216]{2,1,0:T(8,128)(2,1)}), bf16[8,16,9216]{2,1,0:T(8,128)(2,1)S(1)}, u32[]{:S(2)}, u32[]{:S(2)}) async-start(bf16[8,16,9216]{2,1,0:T(8,128)(2,1)} %pad_maximum_fusion), calls=%async_computation | async-start | bytes 4718592 | tf_op jit(solution)/shard_map/all_to_all | solution.py:1573
  22.4 165.7 %reduce-scatter.2.cloned.1.call-start = ((), (), s32[]{:S(2)}) async-start(), calls=%async_computation.4 | async-start | bytes 2949120 | tf_op jit(solution)/shard_map/reduce_scatter | solution.py:1587
  61.8 16.2 %collective-permute-start.5 = (bf16[8320,128]{1,0:T(8,128)(2,1)}, bf16[8320,128]{1,0:T(8,128)(2,1)}, u32[]{:S(2)}, u32[]{:S(2)}) collective-permute-start(bf16[8320,128]{1,0:T(8,128)(2,1)} %collective-permute-done.1.refs_3_), channel_id=1, source_target_pairs={{0,4},{4,0},{8,12},{12,8},{16,20},{20,16},{24,28},{28,24},{1,5},{5... | collective-permute-start | bytes 6389768 | tf_op jit(solution)/shard_map/ppermute | solution.py:1368
  62.0 16.0 %collective-permute-start.4 = (bf16[8320,128]{1,0:T(8,128)(2,1)}, bf16[8320,128]{1,0:T(8,128)(2,1)}, u32[]{:S(2)}, u32[]{:S(2)}) collective-permute-start(bf16[8320,128]{1,0:T(8,128)(2,1)} %collective-permute-done.refs_2_), channel_id=1, source_target_pairs={{0,4},{4,0},{8,12},{12,8},{16,20},{20,16},{24,28},{28,24},{1,5},{5... | collective-permute-start | bytes 6389768 | tf_op jit(solution)/shard_map/ppermute | solution.py:1368
  62.3 26.7 %collective-permute-start.3 = (bf16[8320,128]{1,0:T(8,128)(2,1)}, bf16[8320,128]{1,0:T(8,128)(2,1)}, u32[]{:S(2)}, u32[]{:S(2)}) collective-permute-start(bf16[8320,128]{1,0:T(8,128)(2,1)} %collective-permute-done.refs_2_), channel_id=1, source_target_pairs={{0,16},{4,12},{8,24},{12,4},{16,0},{20,28},{24,8},{28,20},{1,17},{... | collective-permute-start | bytes 6389768 | tf_op jit(solution)/shard_map/ppermute | solution.py:1366
  89.0 4.4 %collective-permute-start.6 = (bf16[8320,128]{1,0:T(8,128)(2,1)}, bf16[8320,128]{1,0:T(8,128)(2,1)S(1)}, u32[]{:S(2)}, u32[]{:S(2)}) collective-permute-start(bf16[8320,128]{1,0:T(8,128)(2,1)} %collective-permute-done.3.refs_6_), channel_id=1, source_target_pairs={{0,4},{4,0},{8,12},{12,8},{16,20},{20,16},{24,28},{28,24},{1,5},{5... | collective-permute-start | bytes 6389768 | tf_op jit(solution)/shard_map/ppermute | solution.py:1368
  142.6 96.0 %all-reduce.2.cloned.1.call-start = ((), (), s32[]{:S(2)}) async-start(), calls=%async_computation.5 | async-start | bytes 655360 | tf_op jit(solution)/shard_map/psum | solution.py:1595
  144.0 30.3 %collective-permute-start.9 = (bf16[2,16,4608]{2,1,0:T(8,128)(2,1)S(1)}, bf16[2,16,4608]{2,1,0:T(8,128)(2,1)S(1)}, u32[]{:S(2)}, u32[]{:S(2)}) collective-permute-start(bf16[2,16,4608]{2,1,0:T(8,128)(2,1)S(1)} %get-tuple-element.357), channel_id=1, source_target_pairs={{0,3},{1,2},{2,1},{3,0},{4,7},{5,6},{6,5},{7,4},{8,11},{9,10},{10,... | collective-permute-start | bytes 884744 | tf_op jit(solution)/shard_map/ppermute | solution.py:1560
  147.9 26.4 %collective-permute-start.8 = (bf16[2,16,4608]{2,1,0:T(8,128)(2,1)S(1)}, bf16[2,16,4608]{2,1,0:T(8,128)(2,1)S(1)}, u32[]{:S(2)}, u32[]{:S(2)}) collective-permute-start(bf16[2,16,4608]{2,1,0:T(8,128)(2,1)S(1)} %get-tuple-element.358), channel_id=1, source_target_pairs={{0,2},{1,3},{2,0},{3,1},{4,6},{5,7},{6,4},{7,5},{8,10},{9,11},{10,... | collective-permute-start | bytes 884744 | tf_op jit(solution)/shard_map/ppermute | solution.py:1560
  147.9 26.4 %collective-permute-start.7 = (bf16[2,16,4608]{2,1,0:T(8,128)(2,1)S(1)}, bf16[2,16,4608]{2,1,0:T(8,128)(2,1)S(1)}, u32[]{:S(2)}, u32[]{:S(2)}) collective-permute-start(bf16[2,16,4608]{2,1,0:T(8,128)(2,1)S(1)} %get-tuple-element.359), channel_id=1, source_target_pairs={{0,1},{1,0},{2,3},{3,2},{4,5},{5,4},{6,7},{7,6},{8,9},{9,8},{10,11... | collective-permute-start | bytes 884744 | tf_op jit(solution)/shard_map/ppermute | solution.py:1560
  175.1 8.9 %collective-permute-start.10 = (bf16[5120,128]{1,0:T(8,128)(2,1)}, bf16[5120,128]{1,0:T(8,128)(2,1)S(1)}, u32[]{:S(2)}, u32[]{:S(2)}) collective-permute-start(bf16[5120,128]{1,0:T(8,128)(2,1)} %get-tuple-element.244), channel_id=1, source_target_pairs={{0,4},{4,0},{8,12},{12,8},{16,20},{20,16},{24,28},{28,24},{1,5},{5... | collective-permute-start | bytes 3932168 | tf_op jit(solution)/shard_map/ppermute | solution.py:1438
  188.1 20.9 %collective-permute-start.14 = (bf16[3328,128]{1,0:T(8,128)(2,1)}, bf16[3328,128]{1,0:T(8,128)(2,1)}, u32[]{:S(2)}, u32[]{:S(2)}) collective-permute-start(bf16[3328,128]{1,0:T(8,128)(2,1)} %get-tuple-element.257), channel_id=1, source_target_pairs={{0,4},{4,0},{8,12},{12,8},{16,20},{20,16},{24,28},{28,24},{1,5},{5... | collective-permute-start | bytes 2555912 | tf_op jit(solution)/shard_map/ppermute | solution.py:1438
  190.8 16.4 %collective-permute-start.13 = (bf16[1280,128]{1,0:T(8,128)(2,1)}, bf16[1280,128]{1,0:T(8,128)(2,1)S(1)}, u32[]{:S(2)}, u32[]{:S(2)}) collective-permute-start(bf16[1280,128]{1,0:T(8,128)(2,1)} %get-tuple-element.346), channel_id=1, source_target_pairs={{0,24},{4,28},{8,16},{12,20},{16,8},{20,12},{24,0},{28,4},{1,25},{... | collective-permute-start | bytes 983048 | tf_op jit(solution)/shard_map/ppermute | solution.py:1441
  192.2 16.8 %collective-permute-start.12 = (bf16[1280,128]{1,0:T(8,128)(2,1)}, bf16[1280,128]{1,0:T(8,128)(2,1)S(1)}, u32[]{:S(2)}, u32[]{:S(2)}) collective-permute-start(bf16[1280,128]{1,0:T(8,128)(2,1)} %get-tuple-element.347), channel_id=1, source_target_pairs={{0,16},{4,20},{8,24},{12,28},{16,0},{20,4},{24,8},{28,12},{1,17},{... | collective-permute-start | bytes 983048 | tf_op jit(solution)/shard_map/ppermute | solution.py:1441
  193.7 15.4 %collective-permute-start.11 = (bf16[1280,128]{1,0:T(8,128)(2,1)}, bf16[1280,128]{1,0:T(8,128)(2,1)S(1)}, u32[]{:S(2)}, u32[]{:S(2)}) collective-permute-start(bf16[1280,128]{1,0:T(8,128)(2,1)} %get-tuple-element.348), channel_id=1, source_target_pairs={{0,8},{4,12},{8,0},{12,4},{16,24},{20,28},{24,16},{28,20},{1,9},{5... | collective-permute-start | bytes 983048 | tf_op jit(solution)/shard_map/ppermute | solution.py:1441
  194.3 98.0 %all-gather.2.cloned.1.call-start = ((), (), s32[]{:S(2)}) async-start(), calls=%async_computation.6 | async-start | bytes 2949120 | tf_op jit(solution)/shard_map/all_gather | solution.py:1605
  210.5 12.9 %collective-permute-start.17 = (bf16[832,128]{1,0:T(8,128)(2,1)S(1)}, bf16[832,128]{1,0:T(8,128)(2,1)S(1)}, u32[]{:S(2)}, u32[]{:S(2)}) collective-permute-start(bf16[832,128]{1,0:T(8,128)(2,1)S(1)} %get-tuple-element.364), channel_id=1, source_target_pairs={{0,24},{4,28},{8,16},{12,20},{16,8},{20,12},{24,0},{28,4},{1,25},{... | collective-permute-start | bytes 638984 | tf_op jit(solution)/shard_map/ppermute | solution.py:1441
  212.0 11.3 %collective-permute-start.16 = (bf16[832,128]{1,0:T(8,128)(2,1)S(1)}, bf16[832,128]{1,0:T(8,128)(2,1)S(1)}, u32[]{:S(2)}, u32[]{:S(2)}) collective-permute-start(bf16[832,128]{1,0:T(8,128)(2,1)S(1)} %get-tuple-element.365), channel_id=1, source_target_pairs={{0,16},{4,20},{8,24},{12,28},{16,0},{20,4},{24,8},{28,12},{1,17},{... | collective-permute-start | bytes 638984 | tf_op jit(solution)/shard_map/ppermute | solution.py:1441
  213.4 9.9 %collective-permute-start.15 = (bf16[832,128]{1,0:T(8,128)(2,1)S(1)}, bf16[832,128]{1,0:T(8,128)(2,1)S(1)}, u32[]{:S(2)}, u32[]{:S(2)}) collective-permute-start(bf16[832,128]{1,0:T(8,128)(2,1)S(1)} %get-tuple-element.366), channel_id=1, source_target_pairs={{0,8},{4,12},{8,0},{12,4},{16,24},{20,28},{24,16},{28,20},{1,9},{5... | collective-permute-start | bytes 638984 | tf_op jit(solution)/shard_map/ppermute | solution.py:1441
  223.6 15.1 %collective-permute-start.18 = (bf16[528,128]{1,0:T(8,128)(2,1)S(1)}, bf16[528,128]{1,0:T(8,128)(2,1)S(1)}, u32[]{:S(2)}, u32[]{:S(2)}) collective-permute-start(bf16[528,128]{1,0:T(8,128)(2,1)S(1)} %pad_maximum_fusion.3), channel_id=1, source_target_pairs={{0,1},{1,0},{2,3},{3,2},{4,5},{5,4},{6,7},{7,6},{8,9},{9,8},{10,11... | collective-permute-start | bytes 405512 | tf_op jit(solution)/shard_map/ppermute | solution.py:1444
  225.1 13.7 %collective-permute-start.19 = (bf16[528,128]{1,0:T(8,128)(2,1)S(1)}, bf16[528,128]{1,0:T(8,128)(2,1)S(1)}, u32[]{:S(2)}, u32[]{:S(2)}) collective-permute-start(bf16[528,128]{1,0:T(8,128)(2,1)S(1)} %pad_maximum_fusion.4), channel_id=1, source_target_pairs={{0,2},{1,3},{2,0},{3,1},{4,6},{5,7},{6,4},{7,5},{8,10},{9,11},{10,... | collective-permute-start | bytes 405512 | tf_op jit(solution)/shard_map/ppermute | solution.py:1444
  227.6 11.2 %collective-permute-start.20 = (bf16[528,128]{1,0:T(8,128)(2,1)S(1)}, bf16[528,128]{1,0:T(8,128)(2,1)S(1)}, u32[]{:S(2)}, u32[]{:S(2)}) collective-permute-start(bf16[528,128]{1,0:T(8,128)(2,1)S(1)} %pad_maximum_fusion.5), channel_id=1, source_target_pairs={{0,3},{1,2},{2,1},{3,0},{4,7},{5,6},{6,5},{7,4},{8,11},{9,10},{10,... | collective-permute-start | bytes 405512 | tf_op jit(solution)/shard_map/ppermute | solution.py:1444
  238.8 3.5 %collective-permute-start.21 = (bf16[3328,128]{1,0:T(8,128)(2,1)}, bf16[3328,128]{1,0:T(8,128)(2,1)S(1)}, u32[]{:S(2)}, u32[]{:S(2)}) collective-permute-start(bf16[3328,128]{1,0:T(8,128)(2,1)} %get-tuple-element.297), channel_id=1, source_target_pairs={{0,4},{4,0},{8,12},{12,8},{16,20},{20,16},{24,28},{28,24},{1,5},{5... | collective-permute-start | bytes 2555912 | tf_op jit(solution)/shard_map/ppermute | solution.py:1438
  239.0 11.6 %collective-permute-start.27 = (bf16[528,128]{1,0:T(8,128)(2,1)S(1)}, bf16[528,128]{1,0:T(8,128)(2,1)S(1)}, u32[]{:S(2)}, u32[]{:S(2)}) collective-permute-start(bf16[528,128]{1,0:T(8,128)(2,1)S(1)} %add_convert_fusion.3.refs_0_), channel_id=1, source_target_pairs={{0,3},{1,2},{2,1},{3,0},{4,7},{5,6},{6,5},{7,4},{8,11},{9,10},{10,... | collective-permute-start | bytes 405512 | tf_op jit(solution)/shard_map/ppermute | solution.py:1444
  244.5 12.4 %collective-permute-start.24 = (bf16[832,128]{1,0:T(8,128)(2,1)}, bf16[832,128]{1,0:T(8,128)(2,1)}, u32[]{:S(2)}, u32[]{:S(2)}) collective-permute-start(bf16[832,128]{1,0:T(8,128)(2,1)} %get-tuple-element.361), channel_id=1, source_target_pairs={{0,24},{4,28},{8,16},{12,20},{16,8},{20,12},{24,0},{28,4},{1,25},{... | collective-permute-start | bytes 638984 | tf_op jit(solution)/shard_map/ppermute | solution.py:1441
  246.0 15.2 %collective-permute-start.23 = (bf16[832,128]{1,0:T(8,128)(2,1)}, bf16[832,128]{1,0:T(8,128)(2,1)}, u32[]{:S(2)}, u32[]{:S(2)}) collective-permute-start(bf16[832,128]{1,0:T(8,128)(2,1)} %get-tuple-element.362), channel_id=1, source_target_pairs={{0,16},{4,20},{8,24},{12,28},{16,0},{20,4},{24,8},{28,12},{1,17},{... | collective-permute-start | bytes 638984 | tf_op jit(solution)/shard_map/ppermute | solution.py:1441
  247.4 13.8 %collective-permute-start.22 = (bf16[832,128]{1,0:T(8,128)(2,1)S(1)}, bf16[832,128]{1,0:T(8,128)(2,1)}, u32[]{:S(2)}, u32[]{:S(2)}) collective-permute-start(bf16[832,128]{1,0:T(8,128)(2,1)S(1)} %get-tuple-element.363), channel_id=1, source_target_pairs={{0,8},{4,12},{8,0},{12,4},{16,24},{20,28},{24,16},{28,20},{1,9},{5... | collective-permute-start | bytes 638984 | tf_op jit(solution)/shard_map/ppermute | solution.py:1441
  248.0 8.7 %collective-permute-start.26 = (bf16[528,128]{1,0:T(8,128)(2,1)S(1)}, bf16[528,128]{1,0:T(8,128)(2,1)S(1)}, u32[]{:S(2)}, u32[]{:S(2)}) collective-permute-start(bf16[528,128]{1,0:T(8,128)(2,1)S(1)} %add_convert_fusion.3.refs_0_), channel_id=1, source_target_pairs={{0,2},{1,3},{2,0},{3,1},{4,6},{5,7},{6,4},{7,5},{8,10},{9,11},{10,... | collective-permute-start | bytes 405512 | tf_op jit(solution)/shard_map/ppermute | solution.py:1444
  250.6 6.3 %collective-permute-start.25 = (bf16[528,128]{1,0:T(8,128)(2,1)S(1)}, bf16[528,128]{1,0:T(8,128)(2,1)S(1)}, u32[]{:S(2)}, u32[]{:S(2)}) collective-permute-start(bf16[528,128]{1,0:T(8,128)(2,1)S(1)} %add_convert_fusion.3.refs_0_), channel_id=1, source_target_pairs={{0,1},{1,0},{2,3},{3,2},{4,5},{5,4},{6,7},{7,6},{8,9},{9,8},{10,11... | collective-permute-start | bytes 405512 | tf_op jit(solution)/shard_map/ppermute | solution.py:1444
  252.9 16.3 %copy-start.17 = (bf16[2,16,4608]{2,1,0:T(8,128)(2,1)S(1)}, bf16[2,16,4608]{2,1,0:T(8,128)(2,1)}, u32[]{:S(2)}) copy-start(bf16[2,16,4608]{2,1,0:T(8,128)(2,1)} %copy-done.16) | copy-start | bytes 884740
  252.9 36.1 %all-to-all-start.1 = ((bf16[4,2,16,2048]{3,2,1,0:T(8,128)(2,1)}), bf16[4,2,16,2048]{3,2,1,0:T(8,128)(2,1)S(1)}, u32[]{:S(2)}, u32[]{:S(2)}) async-start(bf16[4,2,16,2048]{3,2,1,0:T(8,128)(2,1)} %bitcast.88), calls=%async_computation.2 | async-start | bytes 1048576 | tf_op jit(solution)/shard_map/all_to_all | solution.py:1549
  262.5 8.5 %collective-permute-start.30 = (bf16[208,128]{1,0:T(8,128)(2,1)S(1)}, bf16[208,128]{1,0:T(8,128)(2,1)S(1)}, u32[]{:S(2)}, u32[]{:S(2)}) collective-permute-start(bf16[208,128]{1,0:T(8,128)(2,1)S(1)} %get-tuple-element.371), channel_id=1, source_target_pairs={{0,3},{1,2},{2,1},{3,0},{4,7},{5,6},{6,5},{7,4},{8,11},{9,10},{10,... | collective-permute-start | bytes 159752 | tf_op jit(solution)/shard_map/ppermute | solution.py:1444
  264.9 10.2 %collective-permute-start.29 = (bf16[208,128]{1,0:T(8,128)(2,1)S(1)}, bf16[208,128]{1,0:T(8,128)(2,1)S(1)}, u32[]{:S(2)}, u32[]{:S(2)}) collective-permute-start(bf16[208,128]{1,0:T(8,128)(2,1)S(1)} %get-tuple-element.372), channel_id=1, source_target_pairs={{0,2},{1,3},{2,0},{3,1},{4,6},{5,7},{6,4},{7,5},{8,10},{9,11},{10,... | collective-permute-start | bytes 159752 | tf_op jit(solution)/shard_map/ppermute | solution.py:1444
  265.7 9.4 %collective-permute-start.28 = (bf16[208,128]{1,0:T(8,128)(2,1)S(1)}, bf16[208,128]{1,0:T(8,128)(2,1)S(1)}, u32[]{:S(2)}, u32[]{:S(2)}) collective-permute-start(bf16[208,128]{1,0:T(8,128)(2,1)S(1)} %get-tuple-element.373), channel_id=1, source_target_pairs={{0,1},{1,0},{2,3},{3,2},{4,5},{5,4},{6,7},{7,6},{8,9},{9,8},{10,11... | collective-permute-start | bytes 159752 | tf_op jit(solution)/shard_map/ppermute | solution.py:1444
  267.7 12.5 %collective-permute-start.31 = (bf16[2112,128]{1,0:T(8,128)(2,1)S(1)}, bf16[2112,128]{1,0:T(8,128)(2,1)S(1)}, u32[]{:S(2)}, u32[]{:S(2)}) collective-permute-start(bf16[2112,128]{1,0:T(8,128)(2,1)S(1)} %shard_map.256.refs_0_), channel_id=1, source_target_pairs={{0,8},{4,20},{8,0},{12,28},{16,24},{20,4},{24,16},{28,12},{1,9},{5... | collective-permute-start | bytes 1622024 | tf_op jit(solution)/shard_map/ppermute | solution.py:1474
  280.4 20.5 %collective-permute-start.38 = (bf16[4224,128]{1,0:T(8,128)(2,1)S(1)}, bf16[4224,128]{1,0:T(8,128)(2,1)S(1)}, u32[]{:S(2)}, u32[]{:S(2)}) collective-permute-start(bf16[4224,128]{1,0:T(8,128)(2,1)S(1)} %shard_map.258.refs_0_), channel_id=1, source_target_pairs={{0,16},{4,12},{8,24},{12,4},{16,0},{20,28},{24,8},{28,20},{1,17},{... | collective-permute-start | bytes 3244040 | tf_op jit(solution)/shard_map/ppermute | solution.py:1474
  283.8 6.4 %collective-permute-start.34 = (bf16[208,128]{1,0:T(8,128)(2,1)S(1)}, bf16[208,128]{1,0:T(8,128)(2,1)S(1)}, u32[]{:S(2)}, u32[]{:S(2)}) collective-permute-start(bf16[208,128]{1,0:T(8,128)(2,1)S(1)} %fusion.11.refs_0_), channel_id=1, source_target_pairs={{0,3},{1,2},{2,1},{3,0},{4,7},{5,6},{6,5},{7,4},{8,11},{9,10},{10,... | collective-permute-start | bytes 159752 | tf_op jit(solution)/shard_map/ppermute | solution.py:1444
  287.2 5.0 %collective-permute-start.33 = (bf16[208,128]{1,0:T(8,128)(2,1)S(1)}, bf16[208,128]{1,0:T(8,128)(2,1)S(1)}, u32[]{:S(2)}, u32[]{:S(2)}) collective-permute-start(bf16[208,128]{1,0:T(8,128)(2,1)S(1)} %fusion.11.refs_0_), channel_id=1, source_target_pairs={{0,2},{1,3},{2,0},{3,1},{4,6},{5,7},{6,4},{7,5},{8,10},{9,11},{10,... | collective-permute-start | bytes 159752 | tf_op jit(solution)/shard_map/ppermute | solution.py:1444
  287.2 5.0 %collective-permute-start.32 = (bf16[208,128]{1,0:T(8,128)(2,1)S(1)}, bf16[208,128]{1,0:T(8,128)(2,1)S(1)}, u32[]{:S(2)}, u32[]{:S(2)}) collective-permute-start(bf16[208,128]{1,0:T(8,128)(2,1)S(1)} %fusion.11.refs_0_), channel_id=1, source_target_pairs={{0,1},{1,0},{2,3},{3,2},{4,5},{5,4},{6,7},{7,6},{8,9},{9,8},{10,11... | collective-permute-start | bytes 159752 | tf_op jit(solution)/shard_map/ppermute | solution.py:1444
  292.6 9.2 %collective-permute-start.37 = (bf16[832,128]{1,0:T(8,128)(2,1)S(1)}, bf16[832,128]{1,0:T(8,128)(2,1)S(1)}, u32[]{:S(2)}, u32[]{:S(2)}) collective-permute-start(bf16[832,128]{1,0:T(8,128)(2,1)S(1)} %shard_map.257.refs_0_), channel_id=1, source_target_pairs={{0,24},{4,28},{8,16},{12,20},{16,8},{20,12},{24,0},{28,4},{1,25},{... | collective-permute-start | bytes 638984 | tf_op jit(solution)/shard_map/ppermute | solution.py:1441
  293.2 11.5 %collective-permute-start.36 = (bf16[832,128]{1,0:T(8,128)(2,1)S(1)}, bf16[832,128]{1,0:T(8,128)(2,1)S(1)}, u32[]{:S(2)}, u32[]{:S(2)}) collective-permute-start(bf16[832,128]{1,0:T(8,128)(2,1)S(1)} %shard_map.257.refs_0_), channel_id=1, source_target_pairs={{0,16},{4,20},{8,24},{12,28},{16,0},{20,4},{24,8},{28,12},{1,17},{... | collective-permute-start | bytes 638984 | tf_op jit(solution)/shard_map/ppermute | solution.py:1441
  294.7 10.0 %collective-permute-start.35 = (bf16[832,128]{1,0:T(8,128)(2,1)S(1)}, bf16[832,128]{1,0:T(8,128)(2,1)S(1)}, u32[]{:S(2)}, u32[]{:S(2)}) collective-permute-start(bf16[832,128]{1,0:T(8,128)(2,1)S(1)} %shard_map.257.refs_0_), channel_id=1, source_target_pairs={{0,8},{4,12},{8,0},{12,4},{16,24},{20,28},{24,16},{28,20},{1,9},{5... | collective-permute-start | bytes 638984 | tf_op jit(solution)/shard_map/ppermute | solution.py:1441
  306.2 6.5 %collective-permute-start.40 = (bf16[8448,128]{1,0:T(8,128)(2,1)S(1)}, bf16[8448,128]{1,0:T(8,128)(2,1)}, u32[]{:S(2)}, u32[]{:S(2)}) collective-permute-start(bf16[8448,128]{1,0:T(8,128)(2,1)S(1)} %shard_map.260.refs_3_), channel_id=1, source_target_pairs={{0,4},{4,0},{8,12},{12,8},{16,20},{20,16},{24,28},{28,24},{1,5},{5... | collective-permute-start | bytes 6488072 | tf_op jit(solution)/shard_map/ppermute | solution.py:1438
  307.4 4.3 %collective-permute-start.39 = (bf16[3328,128]{1,0:T(8,128)(2,1)S(1)}, bf16[3328,128]{1,0:T(8,128)(2,1)S(1)}, u32[]{:S(2)}, u32[]{:S(2)}) collective-permute-start(bf16[3328,128]{1,0:T(8,128)(2,1)S(1)} %shard_map.259.refs_1_), channel_id=1, source_target_pairs={{0,4},{4,0},{8,12},{12,8},{16,20},{20,16},{24,28},{28,24},{1,5},{5... | collective-permute-start | bytes 2555912 | tf_op jit(solution)/shard_map/ppermute | solution.py:1438
  312.7 22.5 %all-to-all-start.2 = ((bf16[4,2,16,2560]{3,2,1,0:T(8,128)(2,1)}), bf16[4,2,16,2560]{3,2,1,0:T(8,128)(2,1)}, u32[]{:S(2)}, u32[]{:S(2)}) async-start(bf16[4,2,16,2560]{3,2,1,0:T(8,128)(2,1)} %bitcast.98), calls=%async_computation.3 | async-start | bytes 1310720 | tf_op jit(solution)/shard_map/all_to_all | solution.py:1549
  (21 other events, 157.2 us)
Sparse Core Ops, SparseCore 0:
  142.8 45.2 reduce-scatter.1
  194.4 37.7 all-reduce.1
  238.9 39.6 all-gather.1
